TPU v7x, 32 devices: a whole 2x2x4 slice. The times are simulated.
32 devices in a mesh: row: 8 (over z, x), col: 4 (over y, core).
Axes of the slice: x: 2, y: 2, z: 4, core: 2. Of those that a mesh axis runs over, the one named last changes fastest.
Arguments:
- features: bfloat16 [4, 1024, 2048], P('col', 'row'), may hold values from -6 to 6
- weight: bfloat16 [2048, 2048], P(('row', 'col')), may hold values from -0.125 to 0.125
- bias: bfloat16 [2048], P(('row', 'col')), may hold values from -3 to 3
- node_mask: int32 [8, 512], P('row', 'col'), may hold values 0 or 1
- neighbour_tiles: int32 [8, 4, 4, 3], P('row', 'col'), may hold values from -1 to 7, as said below
- tile_weights: bfloat16 [8, 4, 4, 3, 128, 128], P('row', 'col'), may hold values from -0.3125 to 0.3125
- out_grad: bfloat16 [8, 512, 2048], P('row', 'col'), may hold values from -6 to 6
Outputs:
- activations: bfloat16 [8, 512, 2048], P('row', 'col')
- input_grad: bfloat16 [4, 1024, 2048], P('col', 'row')
- weight_grad: float32 [2048, 2048], P(('row', 'col'))
- bias_grad: float32 [2048], P(('row', 'col'))
Inputs may be any that keep to these rules, and one draw needn't show every extreme that they name: `neighbour_tiles`: in each destination tile the first 1 to 3 slots list distinct source tiles and the rest hold -1; destination tile 0 of block (0, 0) lists 3 tiles, the first of them 8 - 1.
All inputs are finite; a program needn't handle non-finite values. No bound on the sum of `node_mask` on one device may be relied on, other than what follows from the above.
Results may differ from a plain program's by a relative error of at most 0.0064.
Values may be sent and summed in bfloat16 or wider, within the bound.
No kernel may reach another device: no remote copies, remote signals or barrier semaphores. Data moves between devices by JAX's collectives and lax.ppermute only.
A program may use at most 128 MiB of HBM per device.

v0:
```python
import jax
import jax.numpy as jnp
from jax import lax
from jax.sharding import PartitionSpec as P


def fetch_weights(weight, bias):
    return (
        lax.all_gather(weight, ("row", "col"), axis=0, tiled=True),
        lax.all_gather(bias, ("row", "col"), axis=0, tiled=True),
    )


def body(features, weight, bias, node_mask, neighbour_tiles, tile_weights, out_grad):
    tile = tile_weights.shape[-1]
    dest_count = neighbour_tiles.shape[2]
    slot_count = neighbour_tiles.shape[3]
    lists = neighbour_tiles[0, 0]
    valid = lists >= 0
    blocks = jnp.where(valid[:, :, None, None], tile_weights[0, 0], jnp.zeros((), jnp.bfloat16))
    group = 4
    turns = dest_count // group
    full_weight, full_bias = fetch_weights(weight, bias)
    source = lax.all_gather(features, "row", axis=1, tiled=True)[0]
    width = source.shape[-1]
    source_count = source.shape[0] // tile
    source_index = jnp.arange(source_count, dtype=jnp.int32)
    selector = ((lists[:, :, None] == source_index[None, None, :]) & valid[:, :, None]).astype(
        jnp.bfloat16
    )
    grouped_selector = selector.reshape(turns, group, slot_count, source_count)
    grouped_blocks = blocks.reshape(turns, group, slot_count, tile, tile)

    def dense_strip(group_selector, group_blocks):
        strip = jnp.einsum(
            "gsj,gsik->gijk", group_selector, group_blocks, preferred_element_type=jnp.float32
        )
        return strip.astype(jnp.bfloat16).reshape(group * tile, source_count * tile)

    def aggregate_group(pieces):
        group_selector, group_blocks = pieces
        strip = dense_strip(group_selector, group_blocks)
        return jnp.dot(strip, source, preferred_element_type=jnp.float32)

    partial_value = lax.map(aggregate_group, (grouped_selector, grouped_blocks)).reshape(-1, width)
    summed = lax.psum_scatter(partial_value, "col", scatter_dimension=0, tiled=True)
    aggregate = summed.astype(jnp.bfloat16)
    pre = jnp.dot(aggregate, full_weight, preferred_element_type=jnp.float32) + full_bias.astype(
        jnp.float32
    )
    keep = node_mask[0].astype(jnp.float32)[:, None]
    sigmoid_pre = jax.nn.sigmoid(pre)
    activations = (keep * (pre * sigmoid_pre)).astype(jnp.bfloat16)[None]
    slope = sigmoid_pre * (1.0 + pre * (1.0 - sigmoid_pre))
    pre_grad = (out_grad[0].astype(jnp.float32) * keep * slope).astype(jnp.bfloat16)
    weight_term = lax.dot_general(
        aggregate, pre_grad, (((0,), (0,)), ((), ())), preferred_element_type=jnp.float32
    )
    bias_term = jnp.sum(pre_grad.astype(jnp.float32), axis=0)
    weight_grad, bias_grad = (
        lax.psum_scatter(weight_term, ("row", "col"), scatter_dimension=0, tiled=True),
        lax.psum_scatter(bias_term, ("row", "col"), scatter_dimension=0, tiled=True),
    )
    aggregate_grad = lax.dot_general(
        pre_grad, full_weight, (((1,), (1,)), ((), ())), preferred_element_type=jnp.float32
    ).astype(jnp.bfloat16)
    dest_rows = lax.all_gather(aggregate_grad, "col", axis=0, tiled=True)
    grouped_grads = dest_rows.reshape(turns, group * tile, width)

    def spread_group(totals, pieces):
        group_selector, group_blocks, group_grads = pieces
        strip = dense_strip(group_selector, group_blocks)
        terms = lax.dot_general(
            strip, group_grads, (((0,), (0,)), ((), ())), preferred_element_type=jnp.float32
        )
        return (totals + terms, None)

    initial = jnp.zeros((source_count * tile, width), jnp.float32)
    source_terms, unused = lax.scan(
        spread_group, initial, (grouped_selector, grouped_blocks, grouped_grads)
    )
    input_grad = lax.psum_scatter(source_terms, "row", scatter_dimension=0, tiled=True)
    input_grad = input_grad.astype(jnp.bfloat16)[None]
    return (activations, input_grad, weight_grad, bias_grad)


def solution(mesh):
    return jax.shard_map(
        body,
        mesh=mesh,
        in_specs=(
            P("col", "row", None),
            P(("row", "col"), None),
            P(("row", "col")),
            P("row", "col"),
            P("row", "col", None, None),
            P("row", "col", None, None, None, None),
            P("row", "col", None),
        ),
        out_specs=(
            P("row", "col", None),
            P("col", "row", None),
            P(("row", "col"), None),
            P(("row", "col")),
        ),
        check_vma=False,
    )
```

profile of v0, /device:TPU:0, one launch (start us, length us, event | category | flops | bytes accessed | tf_op | source)
XLA Modules:
  0.0 563.8 jit_solution(1888923242660247010)
XLA Ops:
  8.0 0.0 all-gather.4.cloned.1.call-start
  8.0 0.7 all-gather.4.cloned.1.call-update
  8.7 0.0 reduce-scatter.4.cloned.1.call-start
  8.8 0.8 copy.13
  9.6 1.1 bitcast_select_fusion
  10.7 0.6 convolution_convert_fusion.1
  11.2 75.8 %all-gather.4.cloned.1.call-done = bf16[1,1024,2048]{2,1,0:T(8,128)(2,1)} async-done(((bf16[1,128,2048]{2,1,0:T(8,128)(2,1)}), bf16[1,1024,2048]{2,1,0:T(8,128)(2,1)}) %all-gather.4.cloned.1.call-update) | async-done | bytes 4194320 | tf_op jit(solution)/shard_map/all_gather | solution.py:24
  87.1 6.6 %fusion = f32[512,2048]{1,0:T(8,128)} fusion(bf16[1,1024,2048]{2,1,0:T(8,128)(2,1)} %all-gather.4.cloned.1.call-done, bf16[64,8,8,128]{3,2,1,0:T(8,128)(2,1)S(1)} %bitcast.36), kind=kOutput, calls=%fused_computation | convolution fusion | flops 2147483648 | bytes 9437184 | tf_op jit(solution)/shard_map/while/body/eval_jaxpr/dot_general | solution.py:43
  93.6 0.0 reduce-scatter.4.cloned.1.call-update
  93.7 0.0 all-gather.6.cloned.1.call-start
  93.7 0.5 all-gather.6.cloned.1.call-update
  94.2 0.0 all-gather.8.cloned.1.call-start
  94.3 0.0 copy-done.3
  94.3 0.2 dynamic-update-slice
  94.6 39.1 %all-reduce = bf16[2048]{0:T(1024)(128)(2,1)S(1)} all-reduce(bf16[2048]{0:T(1024)(128)(2,1)S(1)} %dynamic-update-slice), channel_id=1, replica_groups=mesh['row'=8,'col'=4] {'row','col'}, use_global_device_ids=true, to_apply=%add | all-reduce | flops 2048 | bytes 8192
  133.7 3.9 reduce-scatter.4.cloned.1.call-done
  137.6 45.4 %all-gather.6.cloned.1.call-done = bf16[2048,2048]{1,0:T(8,128)(2,1)} async-done(((bf16[64,2048]{1,0:T(8,128)(2,1)}), bf16[2048,2048]{1,0:T(8,128)(2,1)}) %all-gather.6.cloned.1.call-update) | async-done | bytes 8388624 | tf_op jit(solution)/shard_map/all_gather | solution.py:9
  182.9 6.5 %convert_reduce_fusion = (f32[2048]{0:T(1024)S(1)}, bf16[128,2048]{1,0:T(8,128)(2,1)S(1)}, bf16[1,128,2048]{2,1,0:T(8,128)(2,1)}) fusion(f32[128]{0:T(128)S(1)} %convert_bitcast_fusion.1, bf16[1,128,2048]{2,1,0:T(8,128)(2,1)S(1)} %copy-done.2, f32[2048]{0:T(1024)S(1)} %convert_element_type.52, bf16[2048,2048]{1,0:T(8,128)(2,1)} %all-gather.6.cloned.1.call-done, ...), kind=kOutput, calls=%fused_computation.11 | convolution fusion | flops 1078458368 | bytes 11026944 | tf_op jit(solution)/shard_map/dot_general | solution.py:48
  189.4 3.7 convolution_convert_fusion
  193.1 0.0 all-gather.8.cloned.1.call-update
  193.2 0.0 reduce-scatter.6.cloned.1.call-start
  193.2 21.3 %all-gather.8.cloned.1.call-done = bf16[512,2048]{1,0:T(8,128)(2,1)} async-done(((bf16[128,2048]{1,0:T(8,128)(2,1)}), bf16[512,2048]{1,0:T(8,128)(2,1)}) %all-gather.8.cloned.1.call-update) | async-done | bytes 2097168 | tf_op jit(solution)/shard_map/all_gather | solution.py:67
  214.5 7.2 %fusion.2 = f32[1024,2048]{1,0:T(8,128)} fusion(bf16[512,2048]{1,0:T(8,128)(2,1)} %all-gather.8.cloned.1.call-done, bf16[64,8,8,128]{3,2,1,0:T(8,128)(2,1)S(1)} %bitcast.37), kind=kOutput, calls=%fused_computation.5 | convolution fusion | flops 2147483648 | bytes 11534336 | tf_op jit(solution)/shard_map/while/body/eval_jaxpr/dot_general | solution.py:73
  221.7 0.0 reduce-scatter.6.cloned.1.call-update
  221.7 0.0 reduce-scatter.8.cloned.1.call-start
  221.8 8.7 %fusion.11 = f32[2048,2048]{1,0:T(8,128)} fusion(bf16[128,2048]{1,0:T(8,128)(2,1)S(1)} %get-tuple-element.30, f32[128,2048]{1,0:T(8,128)S(1)} %copy-done.1), kind=kOutput, calls=%fused_computation.20 | convolution fusion | flops 1074003968 | bytes 18350080 | tf_op jit(solution)/shard_map/dot_general | solution.py:56
  230.5 0.0 reduce-scatter.8.cloned.1.call-update
  230.5 42.4 %all-reduce.1 = f32[2048]{0:T(1024)S(1)} all-reduce(f32[2048]{0:T(1024)S(1)} %get-tuple-element.24), channel_id=5, replica_groups=mesh['row'=8,'col'=4] {'row','col'}, use_global_device_ids=true, to_apply=%region_4.5.clone | all-reduce | flops 2048 | bytes 16384
  272.9 0.6 dynamic-slice.3
  273.5 98.4 %reduce-scatter.6.cloned.1.call-done = f32[128,2048]{1,0:T(8,128)} async-done(((f32[1024,2048]{1,0:T(8,128)}), f32[128,2048]{1,0:T(8,128)}) %reduce-scatter.6.cloned.1.call-update) | async-done | bytes 1048592 | tf_op jit(solution)/shard_map/reduce_scatter | solution.py:82
  371.9 2.1 convert_bitcast_fusion
  374.0 182.7 %reduce-scatter.8.cloned.1.call-done = f32[64,2048]{1,0:T(8,128)} async-done(((f32[2048,2048]{1,0:T(8,128)}), f32[64,2048]{1,0:T(8,128)}) %reduce-scatter.8.cloned.1.call-update) | async-done | bytes 524304 | tf_op jit(solution)/shard_map/reduce_scatter | solution.py:61
  (13 shorter events, 0.0 us)
Async XLA Ops:
  8.0 79.1 %all-gather.4.cloned.1.call-start = ((), (), s32[]{:S(2)}) async-start(), calls=%async_computation.3 | async-start | bytes 4718592 | tf_op jit(solution)/shard_map/all_gather | solution.py:24
  8.7 128.8 %reduce-scatter.4.cloned.1.call-start = ((), (), s32[]{:S(2)}) async-start(), calls=%async_computation.4 | async-start | bytes 5242880 | tf_op jit(solution)/shard_map/reduce_scatter | solution.py:46
  87.1 7.2 %copy-start.3 = (bf16[64]{0:T(256)(128)(2,1)S(1)}, bf16[64]{0:T(256)(128)(2,1)}, u32[]{:S(2)}) copy-start(bf16[64]{0:T(256)(128)(2,1)} %param.9) | copy-start | bytes 388
  87.1 46.6 %copy-start.4 = (s32[1,128]{1,0:T(1,128)S(1)}, s32[1,128]{1,0:T(1,128)}, u32[]{:S(2)}) copy-start(s32[1,128]{1,0:T(1,128)} %param.10) | copy-start | bytes 1540
  87.1 95.8 %copy-start.2 = (bf16[1,128,2048]{2,1,0:T(8,128)(2,1)S(1)}, bf16[1,128,2048]{2,1,0:T(8,128)(2,1)}, u32[]{:S(2)}) copy-start(bf16[1,128,2048]{2,1,0:T(8,128)(2,1)} %param.13) | copy-start | bytes 1572868
  93.7 89.3 %all-gather.6.cloned.1.call-start = ((), (), s32[]{:S(2)}) async-start(), calls=%async_computation.5 | async-start | bytes 8650752 | tf_op jit(solution)/shard_map/all_gather | solution.py:9
  94.2 120.3 %all-gather.8.cloned.1.call-start = ((), (), s32[]{:S(2)}) async-start(), calls=%async_computation.6 | async-start | bytes 2621440 | tf_op jit(solution)/shard_map/all_gather | solution.py:67
  182.9 6.5 %copy-start = (bf16[2048,2048]{1,0:T(8,128)(2,1)S(1)}, bf16[2048,2048]{1,0:T(8,128)(2,1)}, u32[]{:S(2)}) copy-start(bf16[2048,2048]{1,0:T(8,128)(2,1)} %all-gather.6.cloned.1.call-done) | copy-start | bytes 25165828
  193.1 28.7 %copy-start.1 = (f32[128,2048]{1,0:T(8,128)S(1)}, f32[128,2048]{1,0:T(8,128)}, u32[]{:S(2)}) copy-start(f32[128,2048]{1,0:T(8,128)} %reduce-scatter.4.cloned.1.call-done) | copy-start | bytes 3145732
  193.2 178.7 %reduce-scatter.6.cloned.1.call-start = ((), (), s32[]{:S(2)}) async-start(), calls=%async_computation.7 | async-start | bytes 9437184 | tf_op jit(solution)/shard_map/reduce_scatter | solution.py:82
  221.7 334.9 %reduce-scatter.8.cloned.1.call-start = ((), (), s32[]{:S(2)}) async-start(), calls=%async_computation.8 | async-start | bytes 17301504 | tf_op jit(solution)/shard_map/reduce_scatter | solution.py:61
Sparse Core Ops, SparseCore 0:
  11.0 76.0 all-gather.3
  93.8 43.7 reduce-scatter.3
  193.3 21.2 all-gather.7
  221.9 149.9 reduce-scatter.5
  374.6 182.0 reduce-scatter.7
Sparse Core Ops, SparseCore 1:
  97.0 85.8 all-gather.5
where the time goes:
time: 565 us; the launch traced here: 564 us
  waiting for transfers between devices  429 us (76%)
  blocking collectives  81.5 us (14%)
  matrix products  33.2 us (6%)
  between operations  15.3 us (3%)
    reduce_scatter x1, waiting for transfers between devices, body(): lax.psum_scatter(weight_term, ('row', 'col'), scatter_dimension=0, tiled=...  183 us
    reduce_scatter x1, waiting for transfers between devices, body(): lax.psum_scatter(source_terms, 'row', scatter_dimension=0, tiled=True)  98.4 us
    unnamed x2, blocking collectives  81.5 us
    all_gather x1, waiting for transfers between devices, body(): source = lax.all_gather(features, 'row', axis=1, tiled=True)[0]  75.8 us
    all_gather x1, waiting for transfers between devices, fetch_weights(): lax.all_gather(weight, ('row', 'col'), axis=0, tiled=True)  45.4 us
    all_gather x1, waiting for transfers between devices, body(): dest_rows = lax.all_gather(aggregate_grad, 'col', axis=0, tiled=True)  21.3 us
  transfers between devices with their start and end apart: 6, of which 6 were waited for; matrix products, arithmetic and copies ran while one was open for 2% of the time, Pallas kernels for 0%

commit v1 on v0

--- a/solution.py
+++ b/solution.py
@@ -1,9 +1,303 @@
+import functools
+
 import jax
 import jax.numpy as jnp
 from jax import lax
+from jax.experimental import pallas as pl
+from jax.experimental.pallas import tpu as pltpu
 from jax.sharding import PartitionSpec as P
 
-
+BOTH = ("row", "col")
+F32 = jnp.float32
+BF16 = jnp.bfloat16
+VMEM = pl.BlockSpec(memory_space=pltpu.VMEM)
+SMEM = pl.BlockSpec(memory_space=pltpu.SMEM)
+CORE, Y, X, Z = 1, 2, 4, 8
+GROUP = 4
+
+
+def swap(value, mask, total=32):
+    return lax.ppermute(value, BOTH, [(i, i ^ mask) for i in range(total)])
+
+
+def call(kernel, outs, *operands, scratch=(), smem=1, flops=0):
+    moved = sum(o.size * o.dtype.itemsize for o in operands)
+    moved += sum(o.size * o.dtype.itemsize for o in outs)
+    return pl.pallas_call(
+        kernel,
+        out_shape=outs,
+        in_specs=[SMEM] * smem + [VMEM] * (len(operands) - smem),
+        out_specs=[VMEM] * len(outs),
+        scratch_shapes=list(scratch),
+        compiler_params=pltpu.CompilerParams(vmem_limit_bytes=48 * 2**20),
+        cost_estimate=pl.CostEstimate(flops=flops, bytes_accessed=moved, transcendentals=0),
+    )(*operands)
+
+
+def shape(dims, dtype):
+    return jax.ShapeDtypeStruct(dims, dtype)
+
+
+def gather_kernel(ids, l0, l1, l2, l3, a0, a1, a2, a3, source, keep, send):
+    member, core = ids[0], ids[1]
+    for i, (lists, tiles) in enumerate(zip((l0, l1, l2, l3), (a0, a1, a2, a3))):
+        dests, slots = tiles.shape[0], tiles.shape[1]
+        for pair in range(dests // 2):
+            for other in range(2):
+                m = pair * 2 + (core if other == 0 else 1 - core)
+                left, right = [], []
+                for s in range(slots):
+                    listed = lists[m, s]
+                    block = tiles[m, s]
+                    left.append(jnp.where(listed >= 0, block, jnp.zeros_like(block)))
+                    right.append(source[jnp.maximum(listed, 0)])
+                total = jnp.dot(
+                    jnp.concatenate(left, axis=1),
+                    jnp.concatenate(right, axis=0),
+                    preferred_element_type=F32,
+                )
+                if other == 0:
+                    keep[member ^ i, pair] = total
+                else:
+                    send[member ^ i, pair] = total.astype(BF16)
+
+
+def aggregate_kernel(ids, terms, full, s1, s2, s3):
+    place = ids[2]
+    quarter = terms.shape[-1]
+    for part in range(GROUP):
+        total = terms[2 * part].astype(F32) + terms[2 * part + 1].astype(F32)
+        full[:, part * quarter : (part + 1) * quarter] = total.astype(BF16)
+    block = quarter // GROUP
+    for i, piece in ((1, s1), (2, s2), (3, s3)):
+        for part in range(GROUP):
+            start = pl.multiple_of(part * quarter + (place ^ i) * block, block)
+            piece[:, part * block : (part + 1) * block] = full[:, pl.ds(start, block)]
+
+
+def dense_kernel(ids, own, other, bias, grad_own, grad_other, *rest):
+    chips = 16
+    weights = rest[:chips]
+    act_own, act_other, pre_grad, back_own, back_other, bias_sum, left = rest[chips:]
+    chip = ids[3]
+    nodes, width = own.shape
+    block = width // chips
+    half = pre_grad.shape[1]
+    for i in range(chips):
+        start = pl.multiple_of((chip ^ i) * block, block)
+        left[:nodes, i * block : (i + 1) * block] = own[:, pl.ds(start, block)]
+        left[nodes:, i * block : (i + 1) * block] = other[:, pl.ds(start, block)]
+    step = 256
+    for n in range(half // step):
+        cols = slice(n * step, (n + 1) * step)
+        matrix = jnp.concatenate([w[:, cols] for w in weights], axis=0)
+        pre = jnp.dot(left[...], matrix, preferred_element_type=F32) + bias[:, cols]
+        sigmoid = 1.0 / (1.0 + jnp.exp(-pre))
+        act = (pre * sigmoid).astype(BF16)
+        act_own[:, cols] = act[:nodes]
+        act_other[:, cols] = act[nodes:]
+        slope = sigmoid * (1.0 + pre * (1.0 - sigmoid))
+        og = jnp.concatenate([grad_own[:, cols], grad_other[:, cols]], axis=0).astype(F32)
+        grad = (og * slope).astype(BF16)
+        pre_grad[:, cols] = grad
+        bias_sum[:, cols] = jnp.sum(grad.astype(F32), axis=0, keepdims=True)
+    for i in range(0, chips, 2):
+        matrix = jnp.concatenate([weights[i][...], weights[i + 1][...]], axis=0)
+        back = lax.dot_general(
+            pre_grad[...], matrix, (((1,), (1,)), ((), ())), preferred_element_type=F32
+        )
+        for j in range(2):
+            start = pl.multiple_of((chip ^ (i + j)) * block, block)
+            back_own[:, pl.ds(start, block)] = back[:nodes, j * block : (j + 1) * block]
+            back_other[:, pl.ds(start, block)] = back[nodes:, j * block : (j + 1) * block].astype(BF16)
+
+
+def pieces_kernel(own, received, pieces):
+    quarter = pieces.shape[-1]
+    for part in range(GROUP):
+        cols = slice(part * quarter, (part + 1) * quarter)
+        total = (own[:, cols] + received[:, cols].astype(F32)).astype(BF16)
+        pieces[2 * part] = total
+        pieces[2 * part + 1] = total
+
+
+def spread_kernel(ids, l0, l1, l2, l3, a0, a1, a2, a3, same, cross, out, total):
+    member, core = ids[0], ids[1]
+    total[...] = jnp.zeros_like(total)
+    for i, (lists, tiles) in enumerate(zip((l0, l1, l2, l3), (a0, a1, a2, a3))):
+        dests, slots, tile = tiles.shape[0], tiles.shape[1], tiles.shape[2]
+        for pair in range(dests // 2):
+            for other in range(2):
+                m = pair * 2 + (core if other == 0 else 1 - core)
+                grads = (same if other == 0 else cross)[(member ^ i) * 2 + pair]
+                left = []
+                for s in range(slots):
+                    block = tiles[m, s]
+                    left.append(jnp.where(lists[m, s] >= 0, block, jnp.zeros_like(block)))
+                terms = lax.dot_general(
+                    jnp.concatenate(left, axis=1), grads, (((0,), (0,)), ((), ())),
+                    preferred_element_type=F32,
+                )
+                for s in range(slots):
+                    at = jnp.maximum(lists[m, s], 0)
+                    total[at] += terms[s * tile : (s + 1) * tile]
+    out[...] = total[...].astype(BF16)
+
+
+def finish_kernel(terms, out):
+    quarter = terms.shape[-1]
+    for part in range(GROUP):
+        total = terms[part].astype(F32) + terms[part + GROUP].astype(F32)
+        out[:, part * quarter : (part + 1) * quarter] = total.astype(BF16)
+
+
+def weight_grad_kernel(ids, own, other, r1, r2, r3, c1, c2, c3, g0, g1, g2, g3, mine, s1, s2, s3, total):
+    place, depth = ids[2], ids[4]
+    nodes, width = own.shape
+    quarter = width // GROUP
+    block = quarter // GROUP
+    first = []
+    for part in range(GROUP):
+        start = pl.multiple_of(part * quarter + place * block, block)
+        first.append(jnp.concatenate([own[:, pl.ds(start, block)], other[:, pl.ds(start, block)]], axis=0))
+    lefts = [jnp.concatenate(first, axis=1)]
+    for a, b in ((r1, c1), (r2, c2), (r3, c3)):
+        lefts.append(jnp.concatenate([a[...], b[...]], axis=0))
+    total[...] = lax.dot_general(
+        jnp.concatenate(lefts, axis=0),
+        jnp.concatenate([g0[...], g1[...], g2[...], g3[...]], axis=0),
+        (((0,), (0,)), ((), ())),
+        preferred_element_type=F32,
+    )
+    for i, out in enumerate((mine, s1, s2, s3)):
+        start = pl.multiple_of((depth ^ i) * block, block)
+        out[...] = total[pl.ds(start, block), :].astype(out.dtype)
+
+
+def weight_sum_kernel(mine, r1, r2, r3, out):
+    out[...] = mine[...] + r1[...].astype(F32) + r2[...].astype(F32) + r3[...].astype(F32)
+
+
+def halves(value, core):
+    width = value.shape[1] // 2
+    mine = lax.dynamic_slice_in_dim(value, core * width, width, axis=1)
+    rest = lax.dynamic_slice_in_dim(value, (1 - core) * width, width, axis=1)
+    return mine, rest
+
+
+def in_order(mine, received, core, axis):
+    return jnp.where(
+        core == 0,
+        jnp.concatenate([mine, received], axis=axis),
+        jnp.concatenate([received, mine], axis=axis),
+    )
+
+
+def chip_body(features, weight, bias, node_mask, neighbour_tiles, tile_weights, out_grad):
+    rows, cols = lax.axis_size("row"), lax.axis_size("col")
+    devices = rows * cols
+    r, c = lax.axis_index("row"), lax.axis_index("col")
+    core = c & 1
+    ids = jnp.stack([r & 3, core, (r & 1) * 2 + (c >> 1), r * 2 + (c >> 1), r >> 1]).astype(jnp.int32)
+    nodes, width = features.shape[1:]
+    half, quarter = width // 2, width // GROUP
+    lists, tiles = neighbour_tiles[0, 0], tile_weights[0, 0]
+    dests, slots, tile = tiles.shape[0], tiles.shape[1], tiles.shape[2]
+    sources = rows
+    groups = [
+        [((zh * GROUP + g) * cols + y * 2 + k) for g in range(GROUP) for y in range(cols // 2)]
+        for zh in range(rows // GROUP)
+        for k in range(2)
+    ]
+
+    quarters = features[0].reshape(nodes, GROUP, quarter).transpose(1, 0, 2)
+    source = lax.all_to_all(
+        jnp.concatenate([quarters] * (rows // GROUP), axis=0), "row", 0, 0, tiled=True
+    )
+    lists_of = [lists] + [swap(lists, m) for m in (X, Z, X | Z)]
+    tiles_of = [tiles, swap(tiles, X), swap(tiles, Z)]
+    tiles_of.append(swap(tiles_of[2], X))
+
+    mine, rest = halves(weight, core)
+    block = in_order(mine, swap(rest, CORE), core, 0)
+    along_z = [block, swap(block, Z), swap(block, 2 * Z), swap(block, 3 * Z)]
+    weights = []
+    for value in along_z:
+        across = swap(value, X)
+        weights += [value, swap(value, Y), across, swap(across, Y)]
+    gathered = lax.all_to_all(
+        jnp.broadcast_to(bias[None], (devices, bias.shape[0])), BOTH, 0, 0, tiled=True
+    )
+    bias_half = lax.dynamic_slice_in_dim(gathered.reshape(1, width), core * half, half, axis=1).astype(F32)
+
+    keep_mask = node_mask[0][:, None]
+    masked = out_grad[0] * keep_mask.astype(BF16)
+    grad_own, grad_rest = halves(masked, core)
+    grad_other = swap(grad_rest, CORE)
+
+    piece = (GROUP, dests // 2, tile, quarter)
+    kept, sent = call(
+        gather_kernel, [shape(piece, F32), shape(piece, BF16)],
+        ids, *lists_of, *tiles_of, source,
+        smem=5, flops=2 * GROUP * dests * slots * tile * tile * quarter,
+    )
+    partial = (kept + swap(sent, CORE).astype(F32)).astype(BF16).reshape(-1, tile, quarter)
+    terms = lax.all_to_all(partial, BOTH, 0, 0, axis_index_groups=groups, tiled=True)
+    aggregate, p1, p2, p3 = call(
+        aggregate_kernel,
+        [shape((nodes, width), BF16)] + [shape((nodes, quarter), BF16)] * 3,
+        ids, terms,
+    )
+    aggregate_other = swap(aggregate, CORE)
+
+    act_own, act_other, pre_grad, back_own, back_other, bias_sum = call(
+        dense_kernel,
+        [shape((nodes, half), BF16)] * 2
+        + [shape((2 * nodes, half), BF16), shape((nodes, width), F32), shape((nodes, width), BF16), shape((1, half), F32)],
+        ids, aggregate, aggregate_other, bias_half, grad_own, grad_other, *weights,
+        scratch=[pltpu.VMEM((2 * nodes, width), BF16)],
+        flops=8 * nodes * half * width,
+    )
+    act = in_order(act_own, swap(act_other, CORE), core, 1)
+    activations = jnp.where(keep_mask != 0, act, jnp.zeros_like(act))[None]
+
+    (pieces,) = call(
+        pieces_kernel, [shape((2 * GROUP, nodes, quarter), BF16)], back_own, swap(back_other, CORE), smem=0
+    )
+    same = lax.all_to_all(pieces, BOTH, 0, 0, axis_index_groups=groups, tiled=True)
+    cross = swap(same, CORE)
+    (spread,) = call(
+        spread_kernel, [shape((sources, tile, quarter), BF16)],
+        ids, *lists_of, *tiles_of, same, cross,
+        scratch=[pltpu.VMEM((sources, tile, quarter), F32)],
+        smem=5, flops=2 * GROUP * dests * slots * tile * tile * quarter,
+    )
+    grads = lax.all_to_all(spread, "row", 0, 0, tiled=True)
+    (input_grad,) = call(finish_kernel, [shape((nodes, width), BF16)], grads, smem=0)
+
+    received = [swap(p1, Y), swap(p2, X), swap(p3, X | Y)]
+    crossed = [swap(p, CORE) for p in received]
+    pre_grads = [pre_grad, swap(pre_grad, Y), swap(pre_grad, X), swap(pre_grad, X | Y)]
+    mine, w1, w2, w3 = call(
+        weight_grad_kernel,
+        [shape((tile, half), F32)] + [shape((tile, half), BF16)] * 3,
+        ids, aggregate, aggregate_other, *received, *crossed, *pre_grads,
+        scratch=[pltpu.VMEM((quarter, half), F32)],
+        flops=2 * quarter * half * 8 * nodes,
+    )
+    (summed,) = call(
+        weight_sum_kernel, [shape((tile, half), F32)],
+        mine, swap(w1, Z), swap(w2, 2 * Z), swap(w3, 3 * Z), smem=0,
+    )
+    own_rows = weight.shape[0]
+    mine = lax.dynamic_slice_in_dim(summed, core * own_rows, own_rows, axis=0)
+    rest = lax.dynamic_slice_in_dim(summed, (1 - core) * own_rows, own_rows, axis=0)
+    weight_grad = in_order(mine, swap(rest, CORE), core, 1)
+
+    nothing = jnp.zeros_like(bias_sum)
+    placed = in_order(bias_sum, nothing, core, 1).reshape(devices, -1)
+    bias_grad = jnp.sum(lax.all_to_all(placed, BOTH, 0, 0, tiled=True), axis=0)
+    return activations, input_grad[None], weight_grad, bias_grad
 def fetch_weights(weight, bias):
     return (
         lax.all_gather(weight, ("row", "col"), axis=0, tiled=True),
@@ -85,8 +379,9 @@
 
 
 def solution(mesh):
+    chips = mesh.shape["row"] == 8 and mesh.shape["col"] == 4
     return jax.shard_map(
-        body,
+        chip_body if chips else body,
         mesh=mesh,
         in_specs=(
             P("col", "row", None),

time: 565 us -> 261 us (0.46)
  waiting for transfers between devices: 429 us -> 118 us
  starting transfers between devices: 0.25 us -> 62.6 us
  blocking collectives: 81.5 us -> 35 us
  matrix products: 33.2 us -> 0 us
  local copies, waits for them, and re-layouts: 1.62 us -> 18.7 us
  Pallas kernels: 0 us -> 16.6 us
  between operations: 15.3 us -> 1.02 us
    reduce_scatter x3 -> x0, waiting for transfers between devices: 285 us -> none  [the longest x1 183 us: body(): lax.psum_scatter(weight_term, ('row', 'col'), scatter_dimension=0, tiled=...]
    all_gather x3 -> x0, waiting for transfers between devices: 143 us -> none  [the longest x1 75.8 us: body(): source = lax.all_gather(features, 'row', axis=1, tiled=True)[0]]
    ppermute x0 -> x41, waiting for transfers between devices: none -> 116 us  [swap(): return lax.ppermute(value, BOTH, [(i, i ^ mask) for i in range(total)])]
    unnamed x2 -> x0, blocking collectives: 81.5 us -> none
    ppermute x0 -> x41, starting transfers between devices: none -> 43.7 us  [swap(): return lax.ppermute(value, BOTH, [(i, i ^ mask) for i in range(total)])]
    all_to_all x0 -> x2, blocking collectives: none -> 35 us  [the longest x1 18 us: chip_body(): lax.all_to_all(pieces, BOTH, 0, 0, axis_index_groups=groups, tiled=True)]
    dot_general x6 -> x0, matrix products: 33.2 us -> none  [the longest x1 8.66 us: body(): lax.dot_general(aggregate, pre_grad, (((0,), (0,)), ((), ())), preferred_...]
    all_to_all x0 -> x4, starting transfers between devices: none -> 18.9 us  [the longest x1 7.25 us: chip_body(): lax.all_to_all(jnp.concatenate([quarters] * (rows // GROUP), axis=0), 'ro...]
  transfers between devices with their start and end apart: 6 -> 45, of which waited for: 6 -> 20; matrix products, arithmetic and copies ran while one was open for 2% -> 2% of each run, Pallas kernels for 0% -> 3%
where the time goes in v1:
time: 261 us; the launch traced here: 258 us
  waiting for transfers between devices  118 us (45%)
  starting transfers between devices  62.6 us (24%)
  blocking collectives  35 us (13%)
  local copies, waits for them, and re-layouts  18.7 us (7%)
  Pallas kernels  16.6 us (6%)
  other arithmetic  6.33 us (2%)
    ppermute x41, waiting for transfers between devices, swap(): return lax.ppermute(value, BOTH, [(i, i ^ mask) for i in range(total)])  116 us
    ppermute x41, starting transfers between devices, swap(): return lax.ppermute(value, BOTH, [(i, i ^ mask) for i in range(total)])  43.7 us
    all_to_all x1, blocking collectives, chip_body(): lax.all_to_all(pieces, BOTH, 0, 0, axis_index_groups=groups, tiled=True)  18 us
    all_to_all x1, blocking collectives, chip_body(): lax.all_to_all(jnp.broadcast_to(bias[None], (devices, bias.shape[0])), BO...  16.9 us
    pallas_call x8, Pallas kernels, call(): pl.pallas_call(kernel, out_shape=outs, in_specs=[SMEM] * smem + [VMEM] *...  16.6 us
    unnamed x70, local copies, waits for them, and re-layouts  15.5 us
    all_to_all x1, starting transfers between devices, chip_body(): lax.all_to_all(jnp.concatenate([quarters] * (rows // GROUP), axis=0), 'ro...  7.25 us
  transfers between devices with their start and end apart: 45, of which 20 were waited for; matrix products, arithmetic and copies ran while one was open for 2% of the time, Pallas kernels for 3%

profile of v1, /device:TPU:0, one launch (start us, length us, event | category | flops | bytes accessed | tf_op | source)
XLA Modules:
  0.0 258.1 jit_solution(3491502145955745679)
XLA Ops:
  3.3 7.3 %all-to-all-start = ((bf16[8,128,512]{2,1,0:T(8,128)(2,1)}), bf16[8,128,512]{2,1,0:T(8,128)(2,1)S(1)}, u32[]{:S(2)}, u32[]{:S(2)}) async-start(bf16[8,128,512]{2,1,0:T(8,128)(2,1)} %pad_maximum_fusion), calls=%async_computation | async-start | bytes 2097152 | tf_op jit(solution)/shard_map/all_to_all | solution.py:214
  10.5 2.0 collective-permute-start.4
  14.0 24.2 %collective-permute-done.4.a2 = bf16[4,3,128,128]{3,2,1,0:T(8,128)(2,1)S(1)} collective-permute-done((bf16[4,3,128,128]{3,2,1,0:T(8,128)(2,1)S(1)}, bf16[4,3,128,128]{3,2,1,0:T(8,128)(2,1)S(1)}, u32[]{:S(2)}, u32[]{:S(2)}) %collective-permute-start.4) | collective-permute-done | bytes 393248 | tf_op jit(solution)/shard_map/ppermute | solution.py:20
  40.7 2.6 collective-permute-start.2
  43.3 4.8 %collective-permute-done.l1 = s32[4,3]{1,0:T(4,128)S(1)} collective-permute-done((s32[4,3]{1,0:T(4,128)S(1)}, s32[4,3]{1,0:T(4,128)S(1)}, u32[]{:S(2)}, u32[]{:S(2)}) %collective-permute-start) | collective-permute-done | bytes 80 | tf_op jit(solution)/shard_map/ppermute | solution.py:20
  50.1 2.6 %collective-permute-done.6 = bf16[4,2,128,512]{3,2,1,0:T(8,128)(2,1)S(1)} collective-permute-done((bf16[4,2,128,512]{3,2,1,0:T(8,128)(2,1)S(1)}, bf16[4,2,128,512]{3,2,1,0:T(8,128)(2,1)S(1)}, u32[]{:S(2)}, u32[]{:S(2)}) %collective-permute-start.6) | collective-permute-done | bytes 1048608 | tf_op jit(solution)/shard_map/ppermute | solution.py:20
  54.2 4.1 %all-to-all-start.1 = ((bf16[8,128,512]{2,1,0:T(8,128)(2,1)}), bf16[8,128,512]{2,1,0:T(8,128)(2,1)S(1)}, u32[]{:S(2)}, u32[]{:S(2)}) async-start(bf16[8,128,512]{2,1,0:T(8,128)(2,1)} %bitcast.30), calls=%async_computation.1 | async-start | bytes 2097152 | tf_op jit(solution)/shard_map/all_to_all | solution.py:245
  60.6 2.1 collective-permute-start.13
  62.7 2.2 collective-permute-start.17
  68.5 15.1 %collective-permute-done.13.rest_4_ = bf16[128,1024]{1,0:T(8,128)(2,1)} collective-permute-done((bf16[128,1024]{1,0:T(8,128)(2,1)S(1)}, bf16[128,1024]{1,0:T(8,128)(2,1)}, u32[]{:S(2)}, u32[]{:S(2)}) %collective-permute-start.13) | collective-permute-done | bytes 262176 | tf_op jit(solution)/shard_map/ppermute | solution.py:20
  88.4 2.4 collective-permute-done.21.rest_12_
  95.8 3.0 %collective-permute-done.19.rest_10_ = bf16[128,1024]{1,0:T(8,128)(2,1)} collective-permute-done((bf16[128,1024]{1,0:T(8,128)(2,1)}, bf16[128,1024]{1,0:T(8,128)(2,1)}, u32[]{:S(2)}, u32[]{:S(2)}) %collective-permute-start.19) | collective-permute-done | bytes 262176 | tf_op jit(solution)/shard_map/ppermute | solution.py:20
  98.8 3.5 %collective-permute-done.23.rest_14_ = bf16[128,1024]{1,0:T(8,128)(2,1)S(1)} collective-permute-done((bf16[128,1024]{1,0:T(8,128)(2,1)}, bf16[128,1024]{1,0:T(8,128)(2,1)S(1)}, u32[]{:S(2)}, u32[]{:S(2)}) %collective-permute-start.23) | collective-permute-done | bytes 262176 | tf_op jit(solution)/shard_map/ppermute | solution.py:20
  105.0 2.3 collective-permute-done.18.rest_9_
  109.5 3.5 %collective-permute-done.22.rest_13_ = bf16[128,1024]{1,0:T(8,128)(2,1)S(1)} collective-permute-done((bf16[128,1024]{1,0:T(8,128)(2,1)}, bf16[128,1024]{1,0:T(8,128)(2,1)S(1)}, u32[]{:S(2)}, u32[]{:S(2)}) %collective-permute-start.22) | collective-permute-done | bytes 262176 | tf_op jit(solution)/shard_map/ppermute | solution.py:20
  116.6 16.9 %all_to_all.35 = bf16[32,1,64]{2,1,0:T(2,128)(2,1)S(1)} all-to-all(bf16[32,1,64]{2,1,0:T(2,128)(2,1)S(1)} %broadcast_in_dim.23), channel_id=1, replica_groups=mesh['row'=8,'col'=4] {'row','col'}, dimensions={0} | all-to-all | bytes 8192 | tf_op jit(solution)/shard_map/all_to_all | solution.py:228
  139.3 6.2 %shard_map.104 = (bf16[128,1024]{1,0:T(8,128)(2,1)S(1)}, bf16[128,1024]{1,0:T(8,128)(2,1)S(1)}, bf16[256,1024]{1,0:T(8,128)(2,1)S(1)}, f32[128,2048]{1,0:T(8,128...) custom-call(s32[5]{0:T(128)S(1)} %stack.23.ids, bf16[128,2048]{1,0:T(8,128)(2,1)} %copy-done.6, ...), custom_call_target="tpu_custom_call" | custom-call | flops 2147483648 | bytes 8396820 | tf_op jit(solution)/shard_map/pallas_call | solution.py:26
  146.4 2.0 collective-permute-done.26.received
  149.8 18.0 %all_to_all.36.same = bf16[8,128,512]{2,1,0:T(8,128)(2,1)S(1)} all-to-all(bf16[8,128,512]{2,1,0:T(8,128)(2,1)S(1)} %shard_map.105), channel_id=1, replica_groups={{0,2,4,6,8,10,12,14},{1,3,5,7,9,11,13,15},{16,18,20,22,24,26,28,30},{17..., dimensions={0} | all-to-all | bytes 2097152 | tf_op jit(solution)/shard_map/all_to_all | solution.py:267
  169.8 3.2 %all-to-all-start.5 = ((f32[32,1,64]{2,1,0:T(1,128)}), f32[32,1,64]{2,1,0:T(1,128)}, u32[]{:S(2)}, u32[]{:S(2)}) async-start(f32[32,1,64]{2,1,0:T(1,128)} %bitcast.35), calls=%async_computation.5 | async-start | bytes 32768 | tf_op jit(solution)/shard_map/all_to_all | solution.py:299
  174.6 3.7 %shard_map.106 = bf16[8,128,512]{2,1,0:T(8,128)(2,1)} custom-call(s32[5]{0:T(128)S(1)} %stack.23.ids, s32[4,3]{1,0:T(4,128)S(1)} %bitcast.29, s32[4,3]{1,0:T(4,128)S(1)} %collective-permute-done.l1, s32[4,3]{1,0:T(4,128)S(1)} %collective-permute-done.1.l2, s32[4,3]{1,0:T(4,128)S(1)} %copy-done.5, bf16[4,3,128,128]{3,2,1,0:T(8,128)(2,1)S(1)} %bitcast.23, ...), custom_call_target="tpu_custom_call" | custom-call | flops 805306368 | bytes 4718804 | tf_op jit(solution)/shard_map/pallas_call | solution.py:26
  179.9 4.4 %all-to-all-start.4 = ((bf16[8,128,512]{2,1,0:T(8,128)(2,1)}), bf16[8,128,512]{2,1,0:T(8,128)(2,1)S(1)}, u32[]{:S(2)}, u32[]{:S(2)}) async-start(bf16[8,128,512]{2,1,0:T(8,128)(2,1)} %shard_map.106), calls=%async_computation.4 | async-start | bytes 2097152 | tf_op jit(solution)/shard_map/all_to_all | solution.py:275
  185.8 2.0 collective-permute-start.35
  189.3 2.0 collective-permute-start.29
  191.3 9.5 %collective-permute-done.28.r1 = bf16[128,512]{1,0:T(8,128)(2,1)S(1)} collective-permute-done((bf16[128,512]{1,0:T(8,128)(2,1)S(1)}, bf16[128,512]{1,0:T(8,128)(2,1)S(1)}, u32[]{:S(2)}, u32[]{:S(2)}) %collective-permute-start.28) | collective-permute-done | bytes 131104 | tf_op jit(solution)/shard_map/ppermute | solution.py:20
  200.9 2.7 %collective-permute-start.30 = (bf16[128,512]{1,0:T(8,128)(2,1)S(1)}, bf16[128,512]{1,0:T(8,128)(2,1)S(1)}, u32[]{:S(2)}, u32[]{:S(2)}) collective-permute-start(bf16[128,512]{1,0:T(8,128)(2,1)S(1)} %copy-done.24), channel_id=1, source_target_pairs={{0,6},{1,7},{2,4},{3,5},{4,2},{5,3},{6,0},{7,1},{8,14},{9,15},{10,... | collective-permute-start | bytes 393224 | tf_op jit(solution)/shard_map/ppermute | solution.py:20
  203.5 21.0 %collective-permute-done.29.r2 = bf16[128,512]{1,0:T(8,128)(2,1)S(1)} collective-permute-done((bf16[128,512]{1,0:T(8,128)(2,1)S(1)}, bf16[128,512]{1,0:T(8,128)(2,1)S(1)}, u32[]{:S(2)}, u32[]{:S(2)}) %collective-permute-start.29) | collective-permute-done | bytes 131104 | tf_op jit(solution)/shard_map/ppermute | solution.py:20
  224.6 2.6 %collective-permute-done.30.r3 = bf16[128,512]{1,0:T(8,128)(2,1)S(1)} collective-permute-done((bf16[128,512]{1,0:T(8,128)(2,1)S(1)}, bf16[128,512]{1,0:T(8,128)(2,1)S(1)}, u32[]{:S(2)}, u32[]{:S(2)}) %collective-permute-start.30) | collective-permute-done | bytes 131104 | tf_op jit(solution)/shard_map/ppermute | solution.py:20
  228.7 2.8 %shard_map.108 = (f32[128,1024]{1,0:T(8,128)S(1)}, bf16[128,1024]{1,0:T(8,128)(2,1)}, bf16[128,1024]{1,0:T(8,128)(2,1)}, bf16[128,1024]{1,0:T(8,128)(2,1)}) custom-call(s32[5]{0:T(128)S(1)} %stack.23.ids, bf16[128,2048]{1,0:T(8,128)(2,1)S(1)} %copy-done.7, bf16[128,2048]{1,0:T(8,128)(2,1)S(1)} %copy-done.9, bf16[128,512]{1,0:T(8,128)(2,1)S(1)} %collective-permute-done.28.r1, ...), custom_call_target="tpu_custom_call" | custom-call | flops 1073741824 | bytes 5242900 | tf_op jit(solution)/shard_map/pallas_call | solution.py:26
  233.0 2.4 collective-permute-start.38
  237.2 8.1 %collective-permute-done.37.r1 = bf16[128,1024]{1,0:T(8,128)(2,1)S(1)} collective-permute-done((bf16[128,1024]{1,0:T(8,128)(2,1)}, bf16[128,1024]{1,0:T(8,128)(2,1)S(1)}, u32[]{:S(2)}, u32[]{:S(2)}) %collective-permute-start.37) | collective-permute-done | bytes 262176 | tf_op jit(solution)/shard_map/ppermute | solution.py:20
  245.3 9.2 %collective-permute-done.38.r2 = bf16[128,1024]{1,0:T(8,128)(2,1)S(1)} collective-permute-done((bf16[128,1024]{1,0:T(8,128)(2,1)}, bf16[128,1024]{1,0:T(8,128)(2,1)S(1)}, u32[]{:S(2)}, u32[]{:S(2)}) %collective-permute-start.38) | collective-permute-done | bytes 262176 | tf_op jit(solution)/shard_map/ppermute | solution.py:20
  (158 shorter events, 58.7 us)
Async XLA Ops:
  3.3 44.8 %all-to-all-start = ((bf16[8,128,512]{2,1,0:T(8,128)(2,1)}), bf16[8,128,512]{2,1,0:T(8,128)(2,1)S(1)}, u32[]{:S(2)}, u32[]{:S(2)}) async-start(bf16[8,128,512]{2,1,0:T(8,128)(2,1)} %pad_maximum_fusion), calls=%async_computation | async-start | bytes 2097152 | tf_op jit(solution)/shard_map/all_to_all | solution.py:214
  10.5 27.7 %collective-permute-start.4 = (bf16[4,3,128,128]{3,2,1,0:T(8,128)(2,1)S(1)}, bf16[4,3,128,128]{3,2,1,0:T(8,128)(2,1)S(1)}, u32[]{:S(2)}, u32[]{:S(2)}) collective-permute-start(bf16[4,3,128,128]{3,2,1,0:T(8,128)(2,1)S(1)} %bitcast.20), channel_id=1, source_target_pairs={{0,8},{1,9},{2,10},{3,11},{4,12},{5,13},{6,14},{7,15},{8,0},{9,1},... | collective-permute-start | bytes 1179656 | tf_op jit(solution)/shard_map/ppermute | solution.py:20
  12.6 35.5 %collective-permute-start.3 = (bf16[4,3,128,128]{3,2,1,0:T(8,128)(2,1)S(1)}, bf16[4,3,128,128]{3,2,1,0:T(8,128)(2,1)S(1)}, u32[]{:S(2)}, u32[]{:S(2)}) collective-permute-start(bf16[4,3,128,128]{3,2,1,0:T(8,128)(2,1)S(1)} %bitcast.21), channel_id=1, source_target_pairs={{0,4},{1,5},{2,6},{3,7},{4,0},{5,1},{6,2},{7,3},{8,12},{9,13},{10,... | collective-permute-start | bytes 1179656 | tf_op jit(solution)/shard_map/ppermute | solution.py:20
  54.2 31.5 %all-to-all-start.1 = ((bf16[8,128,512]{2,1,0:T(8,128)(2,1)}), bf16[8,128,512]{2,1,0:T(8,128)(2,1)S(1)}, u32[]{:S(2)}, u32[]{:S(2)}) async-start(bf16[8,128,512]{2,1,0:T(8,128)(2,1)} %bitcast.30), calls=%async_computation.1 | async-start | bytes 2097152 | tf_op jit(solution)/shard_map/all_to_all | solution.py:245
  60.6 23.0 %collective-permute-start.13 = (bf16[128,1024]{1,0:T(8,128)(2,1)S(1)}, bf16[128,1024]{1,0:T(8,128)(2,1)}, u32[]{:S(2)}, u32[]{:S(2)}) collective-permute-start(bf16[128,1024]{1,0:T(8,128)(2,1)S(1)} %maximum_select_fusion.2.rest_0_), channel_id=1, source_target_pairs={{0,8},{1,9},{2,10},{3,11},{4,12},{5,13},{6,14},{7,15},{8,0},{9,1},... | collective-permute-start | bytes 786440 | tf_op jit(solution)/shard_map/ppermute | solution.py:20
  62.7 22.4 %collective-permute-start.17 = (bf16[128,1024]{1,0:T(8,128)(2,1)S(1)}, bf16[128,1024]{1,0:T(8,128)(2,1)}, u32[]{:S(2)}, u32[]{:S(2)}) collective-permute-start(bf16[128,1024]{1,0:T(8,128)(2,1)S(1)} %maximum_select_fusion.2.rest_0_), channel_id=1, source_target_pairs={{0,16},{1,17},{2,18},{3,19},{4,20},{5,21},{6,22},{7,23},{8,24},{9,... | collective-permute-start | bytes 786440 | tf_op jit(solution)/shard_map/ppermute | solution.py:20
  64.8 26.0 %collective-permute-start.21 = (bf16[128,1024]{1,0:T(8,128)(2,1)S(1)}, bf16[128,1024]{1,0:T(8,128)(2,1)}, u32[]{:S(2)}, u32[]{:S(2)}) collective-permute-start(bf16[128,1024]{1,0:T(8,128)(2,1)S(1)} %maximum_select_fusion.2.rest_0_), channel_id=1, source_target_pairs={{0,24},{1,25},{2,26},{3,27},{4,28},{5,29},{6,30},{7,31},{8,16},{9,... | collective-permute-start | bytes 786440 | tf_op jit(solution)/shard_map/ppermute | solution.py:20
  65.1 27.2 %collective-permute-start.11 = (bf16[128,1024]{1,0:T(8,128)(2,1)S(1)}, bf16[128,1024]{1,0:T(8,128)(2,1)}, u32[]{:S(2)}, u32[]{:S(2)}) collective-permute-start(bf16[128,1024]{1,0:T(8,128)(2,1)S(1)} %maximum_select_fusion.2.rest_0_), channel_id=1, source_target_pairs={{0,4},{1,5},{2,6},{3,7},{4,0},{5,1},{6,2},{7,3},{8,12},{9,13},{10,... | collective-permute-start | bytes 786440 | tf_op jit(solution)/shard_map/ppermute | solution.py:20
  67.1 26.7 %collective-permute-start.10 = (bf16[128,1024]{1,0:T(8,128)(2,1)S(1)}, bf16[128,1024]{1,0:T(8,128)(2,1)}, u32[]{:S(2)}, u32[]{:S(2)}) collective-permute-start(bf16[128,1024]{1,0:T(8,128)(2,1)S(1)} %maximum_select_fusion.2.rest_0_), channel_id=1, source_target_pairs={{0,2},{1,3},{2,0},{3,1},{4,6},{5,7},{6,4},{7,5},{8,10},{9,11},{10,... | collective-permute-start | bytes 786440 | tf_op jit(solution)/shard_map/ppermute | solution.py:20
  83.6 10.7 %collective-permute-start.15 = (bf16[128,1024]{1,0:T(8,128)(2,1)}, bf16[128,1024]{1,0:T(8,128)(2,1)}, u32[]{:S(2)}, u32[]{:S(2)}) collective-permute-start(bf16[128,1024]{1,0:T(8,128)(2,1)} %collective-permute-done.13.rest_4_), channel_id=1, source_target_pairs={{0,4},{1,5},{2,6},{3,7},{4,0},{5,1},{6,2},{7,3},{8,12},{9,13},{10,... | collective-permute-start | bytes 786440 | tf_op jit(solution)/shard_map/ppermute | solution.py:20
  85.1 13.7 %collective-permute-start.19 = (bf16[128,1024]{1,0:T(8,128)(2,1)}, bf16[128,1024]{1,0:T(8,128)(2,1)}, u32[]{:S(2)}, u32[]{:S(2)}) collective-permute-start(bf16[128,1024]{1,0:T(8,128)(2,1)} %collective-permute-done.17.rest_8_), channel_id=1, source_target_pairs={{0,4},{1,5},{2,6},{3,7},{4,0},{5,1},{6,2},{7,3},{8,12},{9,13},{10,... | collective-permute-start | bytes 786440 | tf_op jit(solution)/shard_map/ppermute | solution.py:20
  90.8 11.5 %collective-permute-start.23 = (bf16[128,1024]{1,0:T(8,128)(2,1)}, bf16[128,1024]{1,0:T(8,128)(2,1)S(1)}, u32[]{:S(2)}, u32[]{:S(2)}) collective-permute-start(bf16[128,1024]{1,0:T(8,128)(2,1)} %collective-permute-done.21.rest_12_), channel_id=1, source_target_pairs={{0,4},{1,5},{2,6},{3,7},{4,0},{5,1},{6,2},{7,3},{8,12},{9,13},{10,... | collective-permute-start | bytes 786440 | tf_op jit(solution)/shard_map/ppermute | solution.py:20
  92.3 11.5 %collective-permute-start.14 = (bf16[128,1024]{1,0:T(8,128)(2,1)}, bf16[128,1024]{1,0:T(8,128)(2,1)S(1)}, u32[]{:S(2)}, u32[]{:S(2)}) collective-permute-start(bf16[128,1024]{1,0:T(8,128)(2,1)} %collective-permute-done.13.rest_4_), channel_id=1, source_target_pairs={{0,2},{1,3},{2,0},{3,1},{4,6},{5,7},{6,4},{7,5},{8,10},{9,11},{10,... | collective-permute-start | bytes 786440 | tf_op jit(solution)/shard_map/ppermute | solution.py:20
  93.8 13.6 %collective-permute-start.18 = (bf16[128,1024]{1,0:T(8,128)(2,1)}, bf16[128,1024]{1,0:T(8,128)(2,1)S(1)}, u32[]{:S(2)}, u32[]{:S(2)}) collective-permute-start(bf16[128,1024]{1,0:T(8,128)(2,1)} %collective-permute-done.17.rest_8_), channel_id=1, source_target_pairs={{0,2},{1,3},{2,0},{3,1},{4,6},{5,7},{6,4},{7,5},{8,10},{9,11},{10,... | collective-permute-start | bytes 786440 | tf_op jit(solution)/shard_map/ppermute | solution.py:20
  94.3 18.7 %collective-permute-start.22 = (bf16[128,1024]{1,0:T(8,128)(2,1)}, bf16[128,1024]{1,0:T(8,128)(2,1)S(1)}, u32[]{:S(2)}, u32[]{:S(2)}) collective-permute-start(bf16[128,1024]{1,0:T(8,128)(2,1)} %collective-permute-done.21.rest_12_), channel_id=1, source_target_pairs={{0,2},{1,3},{2,0},{3,1},{4,6},{5,7},{6,4},{7,5},{8,10},{9,11},{10,... | collective-permute-start | bytes 786440 | tf_op jit(solution)/shard_map/ppermute | solution.py:20
  98.8 34.9 %collective-permute-start.7 = (bf16[128,2048]{1,0:T(8,128)(2,1)S(1)}, bf16[128,2048]{1,0:T(8,128)(2,1)S(1)}, u32[]{:S(2)}, u32[]{:S(2)}) collective-permute-start(bf16[128,2048]{1,0:T(8,128)(2,1)S(1)} %get-tuple-element.22.own), channel_id=1, source_target_pairs={{0,1},{1,0},{2,3},{3,2},{4,5},{5,4},{6,7},{7,6},{8,9},{9,8},{10,11... | collective-permute-start | bytes 1572872 | tf_op jit(solution)/shard_map/ppermute | solution.py:20
  102.3 31.4 %collective-permute-start.12 = (bf16[128,1024]{1,0:T(8,128)(2,1)}, bf16[128,1024]{1,0:T(8,128)(2,1)}, u32[]{:S(2)}, u32[]{:S(2)}) collective-permute-start(bf16[128,1024]{1,0:T(8,128)(2,1)} %collective-permute-done.11.rest_2_), channel_id=1, source_target_pairs={{0,2},{1,3},{2,0},{3,1},{4,6},{5,7},{6,4},{7,5},{8,10},{9,11},{10,... | collective-permute-start | bytes 786440 | tf_op jit(solution)/shard_map/ppermute | solution.py:20
  104.5 29.1 %collective-permute-start.16 = (bf16[128,1024]{1,0:T(8,128)(2,1)}, bf16[128,1024]{1,0:T(8,128)(2,1)}, u32[]{:S(2)}, u32[]{:S(2)}) collective-permute-start(bf16[128,1024]{1,0:T(8,128)(2,1)} %collective-permute-done.15.rest_6_), channel_id=1, source_target_pairs={{0,2},{1,3},{2,0},{3,1},{4,6},{5,7},{6,4},{7,5},{8,10},{9,11},{10,... | collective-permute-start | bytes 786440 | tf_op jit(solution)/shard_map/ppermute | solution.py:20
  108.1 25.6 %collective-permute-start.20 = (bf16[128,1024]{1,0:T(8,128)(2,1)}, bf16[128,1024]{1,0:T(8,128)(2,1)}, u32[]{:S(2)}, u32[]{:S(2)}) collective-permute-start(bf16[128,1024]{1,0:T(8,128)(2,1)} %collective-permute-done.19.rest_10_), channel_id=1, source_target_pairs={{0,2},{1,3},{2,0},{3,1},{4,6},{5,7},{6,4},{7,5},{8,10},{9,11},{10,... | collective-permute-start | bytes 786440 | tf_op jit(solution)/shard_map/ppermute | solution.py:20
  113.7 20.0 %collective-permute-start.24 = (bf16[128,1024]{1,0:T(8,128)(2,1)S(1)}, bf16[128,1024]{1,0:T(8,128)(2,1)}, u32[]{:S(2)}, u32[]{:S(2)}) collective-permute-start(bf16[128,1024]{1,0:T(8,128)(2,1)S(1)} %collective-permute-done.23.rest_14_), channel_id=1, source_target_pairs={{0,2},{1,3},{2,0},{3,1},{4,6},{5,7},{6,4},{7,5},{8,10},{9,11},{10,... | collective-permute-start | bytes 786440 | tf_op jit(solution)/shard_map/ppermute | solution.py:20
  169.8 10.1 %all-to-all-start.5 = ((f32[32,1,64]{2,1,0:T(1,128)}), f32[32,1,64]{2,1,0:T(1,128)}, u32[]{:S(2)}, u32[]{:S(2)}) async-start(f32[32,1,64]{2,1,0:T(1,128)} %bitcast.35), calls=%async_computation.5 | async-start | bytes 32768 | tf_op jit(solution)/shard_map/all_to_all | solution.py:299
  179.9 77.3 %all-to-all-start.4 = ((bf16[8,128,512]{2,1,0:T(8,128)(2,1)}), bf16[8,128,512]{2,1,0:T(8,128)(2,1)S(1)}, u32[]{:S(2)}, u32[]{:S(2)}) async-start(bf16[8,128,512]{2,1,0:T(8,128)(2,1)} %shard_map.106), calls=%async_computation.4 | async-start | bytes 2097152 | tf_op jit(solution)/shard_map/all_to_all | solution.py:275
  184.3 44.4 %collective-permute-start.34 = (bf16[256,1024]{1,0:T(8,128)(2,1)S(1)}, bf16[256,1024]{1,0:T(8,128)(2,1)S(1)}, u32[]{:S(2)}, u32[]{:S(2)}) collective-permute-start(bf16[256,1024]{1,0:T(8,128)(2,1)S(1)} %copy-done.11), channel_id=1, source_target_pairs={{0,2},{1,3},{2,0},{3,1},{4,6},{5,7},{6,4},{7,5},{8,10},{9,11},{10,... | collective-permute-start | bytes 1572872 | tf_op jit(solution)/shard_map/ppermute | solution.py:20
  185.8 42.9 %collective-permute-start.35 = (bf16[256,1024]{1,0:T(8,128)(2,1)S(1)}, bf16[256,1024]{1,0:T(8,128)(2,1)S(1)}, u32[]{:S(2)}, u32[]{:S(2)}) collective-permute-start(bf16[256,1024]{1,0:T(8,128)(2,1)S(1)} %copy-done.11), channel_id=1, source_target_pairs={{0,4},{1,5},{2,6},{3,7},{4,0},{5,1},{6,2},{7,3},{8,12},{9,13},{10,... | collective-permute-start | bytes 1572872 | tf_op jit(solution)/shard_map/ppermute | solution.py:20
  187.8 40.9 %collective-permute-start.36 = (bf16[256,1024]{1,0:T(8,128)(2,1)S(1)}, bf16[256,1024]{1,0:T(8,128)(2,1)S(1)}, u32[]{:S(2)}, u32[]{:S(2)}) collective-permute-start(bf16[256,1024]{1,0:T(8,128)(2,1)S(1)} %copy-done.11), channel_id=1, source_target_pairs={{0,6},{1,7},{2,4},{3,5},{4,2},{5,3},{6,0},{7,1},{8,14},{9,15},{10,... | collective-permute-start | bytes 1572872 | tf_op jit(solution)/shard_map/ppermute | solution.py:20
  187.9 13.0 %collective-permute-start.28 = (bf16[128,512]{1,0:T(8,128)(2,1)S(1)}, bf16[128,512]{1,0:T(8,128)(2,1)S(1)}, u32[]{:S(2)}, u32[]{:S(2)}) collective-permute-start(bf16[128,512]{1,0:T(8,128)(2,1)S(1)} %copy-done.28), channel_id=1, source_target_pairs={{0,2},{1,3},{2,0},{3,1},{4,6},{5,7},{6,4},{7,5},{8,10},{9,11},{10,... | collective-permute-start | bytes 393224 | tf_op jit(solution)/shard_map/ppermute | solution.py:20
  189.3 35.2 %collective-permute-start.29 = (bf16[128,512]{1,0:T(8,128)(2,1)S(1)}, bf16[128,512]{1,0:T(8,128)(2,1)S(1)}, u32[]{:S(2)}, u32[]{:S(2)}) collective-permute-start(bf16[128,512]{1,0:T(8,128)(2,1)S(1)} %copy-done.26), channel_id=1, source_target_pairs={{0,4},{1,5},{2,6},{3,7},{4,0},{5,1},{6,2},{7,3},{8,12},{9,13},{10,... | collective-permute-start | bytes 393224 | tf_op jit(solution)/shard_map/ppermute | solution.py:20
  200.9 26.3 %collective-permute-start.30 = (bf16[128,512]{1,0:T(8,128)(2,1)S(1)}, bf16[128,512]{1,0:T(8,128)(2,1)S(1)}, u32[]{:S(2)}, u32[]{:S(2)}) collective-permute-start(bf16[128,512]{1,0:T(8,128)(2,1)S(1)} %copy-done.24), channel_id=1, source_target_pairs={{0,6},{1,7},{2,4},{3,5},{4,2},{5,3},{6,0},{7,1},{8,14},{9,15},{10,... | collective-permute-start | bytes 393224 | tf_op jit(solution)/shard_map/ppermute | solution.py:20
  231.5 13.8 %collective-permute-start.37 = (bf16[128,1024]{1,0:T(8,128)(2,1)}, bf16[128,1024]{1,0:T(8,128)(2,1)S(1)}, u32[]{:S(2)}, u32[]{:S(2)}) collective-permute-start(bf16[128,1024]{1,0:T(8,128)(2,1)} %get-tuple-element.32), channel_id=1, source_target_pairs={{0,8},{1,9},{2,10},{3,11},{4,12},{5,13},{6,14},{7,15},{8,0},{9,1},... | collective-permute-start | bytes 786440 | tf_op jit(solution)/shard_map/ppermute | solution.py:20
  233.0 21.6 %collective-permute-start.38 = (bf16[128,1024]{1,0:T(8,128)(2,1)}, bf16[128,1024]{1,0:T(8,128)(2,1)S(1)}, u32[]{:S(2)}, u32[]{:S(2)}) collective-permute-start(bf16[128,1024]{1,0:T(8,128)(2,1)} %get-tuple-element.33), channel_id=1, source_target_pairs={{0,16},{1,17},{2,18},{3,19},{4,20},{5,21},{6,22},{7,23},{8,24},{9,... | collective-permute-start | bytes 786440 | tf_op jit(solution)/shard_map/ppermute | solution.py:20
  235.4 19.2 %collective-permute-start.39 = (bf16[128,1024]{1,0:T(8,128)(2,1)}, bf16[128,1024]{1,0:T(8,128)(2,1)S(1)}, u32[]{:S(2)}, u32[]{:S(2)}) collective-permute-start(bf16[128,1024]{1,0:T(8,128)(2,1)} %get-tuple-element.34), channel_id=1, source_target_pairs={{0,24},{1,25},{2,26},{3,27},{4,28},{5,29},{6,30},{7,31},{8,16},{9,... | collective-permute-start | bytes 786440 | tf_op jit(solution)/shard_map/ppermute | solution.py:20
  235.9 18.9 %collective-permute-start.25 = (bf16[128,1024]{1,0:T(8,128)(2,1)}, bf16[128,1024]{1,0:T(8,128)(2,1)S(1)}, u32[]{:S(2)}, u32[]{:S(2)}) collective-permute-start(bf16[128,1024]{1,0:T(8,128)(2,1)} %copy-done.12), channel_id=1, source_target_pairs={{0,1},{1,0},{2,3},{3,2},{4,5},{5,4},{6,7},{7,6},{8,9},{9,8},{10,11... | collective-permute-start | bytes 786440 | tf_op jit(solution)/shard_map/ppermute | solution.py:20
  (47 other events, 480.6 us)

commit v2 on v0

--- a/solution.py
+++ b/solution.py
@@ -1,7 +1,456 @@
 import jax
 import jax.numpy as jnp
 from jax import lax
+from jax.experimental import pallas as pl
+from jax.experimental.pallas import tpu as pltpu
 from jax.sharding import PartitionSpec as P
+
+BOTH = ("row", "col")
+F32 = jnp.float32
+BF16 = jnp.bfloat16
+VMEM = pl.BlockSpec(memory_space=pltpu.VMEM)
+SMEM = pl.BlockSpec(memory_space=pltpu.SMEM)
+CORE, Y, X, Z = 1, 2, 4, 8
+GROUP = 4
+SLOTS = 3
+ROWS = 16
+
+
+def swap(value, mask, total=32):
+    return lax.ppermute(value, BOTH, [(i, i ^ mask) for i in range(total)])
+
+
+def after(value, *others):
+    return lax.optimization_barrier((value,) + others)[0]
+
+
+def shape(dims, dtype):
+    return jax.ShapeDtypeStruct(dims, dtype)
+
+
+def call(kernel, outs, *operands, scratch=(), smem=1, flops=0, vmem=24):
+    moved = sum(o.size * o.dtype.itemsize for o in operands)
+    moved += sum(o.size * o.dtype.itemsize for o in outs)
+    return pl.pallas_call(
+        kernel,
+        out_shape=outs,
+        in_specs=[SMEM] * smem + [VMEM] * (len(operands) - smem),
+        out_specs=[VMEM] * len(outs),
+        scratch_shapes=list(scratch),
+        compiler_params=pltpu.CompilerParams(vmem_limit_bytes=vmem * 2**20),
+        cost_estimate=pl.CostEstimate(flops=flops, bytes_accessed=moved, transcendentals=0),
+    )(*operands)
+
+
+def split_kernel(ids, value, row, *pieces):
+    part = pieces[0].shape[-1]
+    for i, piece in enumerate(pieces):
+        piece[:-ROWS] = value[:, pl.ds(pl.multiple_of((ids[7] ^ i) * part, part), part)]
+        piece[-ROWS:] = row[...]
+
+
+def split_masked_kernel(ids, mask, value, *pieces):
+    part, lanes = pieces[0].shape[-1], mask.shape[-1]
+    for i, piece in enumerate(pieces):
+        start = pl.multiple_of((ids[7] ^ i) * part, part)
+        for j in range(part // lanes):
+            cols = pl.ds(start + j * lanes, lanes)
+            piece[:, j * lanes : (j + 1) * lanes] = value[:, cols] * mask[...]
+
+
+def block_kernel(ids, p0, p1, p2, p3, block):
+    rows = p0.shape[0] - ROWS
+    for i, piece in enumerate((p0, p1, p2, p3)):
+        block[pl.ds(pl.multiple_of((ids[7] ^ i) * rows, rows), rows), :] = piece[:rows]
+    block[4 * rows :] = p0[rows:] + p1[rows:] + p2[rows:] + p3[rows:]
+
+
+def columns_kernel(ids, own, far, *pieces):
+    member = ids[0]
+    part, half = pieces[0].shape[-1] // 2, far.shape[-1] // 2
+    for i, piece in enumerate(pieces):
+        for j in range(2):
+            cols = pl.ds(pl.multiple_of(j * half + (member ^ i) * part, part), part)
+            piece[0, :, j * part : (j + 1) * part] = own[0, :, cols]
+            piece[1, :, j * part : (j + 1) * part] = far[:, cols]
+
+
+def gather_kernel(ids, lists, a0, a1, a2, a3, h0, h1, h2, h3, keep, send, source):
+    member, core, row = ids[0], ids[1], ids[8]
+    tile, dests = keep.shape[2], 2 * keep.shape[1]
+    for i, piece in enumerate((h0, h1, h2, h3)):
+        source[row ^ i] = piece[0]
+        source[row ^ i ^ GROUP] = piece[1]
+    for i, tiles in enumerate((a0, a1, a2, a3)):
+        for pair in range(dests // 2):
+            for other in range(2):
+                m = pair * 2 + (core if other == 0 else 1 - core)
+                left, right = [], []
+                for s in range(SLOTS):
+                    slot = m * SLOTS + s
+                    listed = lists[i, slot]
+                    block = tiles[pl.ds(pl.multiple_of(slot * tile, tile), tile), :]
+                    left.append(jnp.where(listed >= 0, block, jnp.zeros_like(block)))
+                    right.append(source[jnp.maximum(listed, 0)])
+                total = jnp.dot(
+                    jnp.concatenate(left, axis=1),
+                    jnp.concatenate(right, axis=0),
+                    preferred_element_type=F32,
+                )
+                if other == 0:
+                    keep[member ^ i, pair] = total
+                else:
+                    send[member ^ i, pair] = total.astype(BF16)
+
+
+def pair_sum_kernel(ids, kept, received, mine, send):
+    y = ids[2]
+    for g in range(GROUP):
+        mine[g] = kept[g, y] + received[g, y].astype(F32)
+        send[g] = (kept[g, 1 - y] + received[g, 1 - y].astype(F32)).astype(BF16)
+
+
+def group_kernel(ids, mine, received, near, far):
+    low = ids[6]
+    for out, z in ((near, low), (far, 1 - low)):
+        for x in range(2):
+            out[x] = (mine[2 * z + x] + received[2 * z + x].astype(F32)).astype(BF16)
+
+
+def aggregate_kernel(ids, own, rx, rz, rxz, full, away):
+    member, y = ids[0], ids[2]
+    nodes, part, half = own.shape[1], own.shape[2] // 2, full.shape[1] // 2
+    for i, term in enumerate((own, rx, rz, rxz)):
+        for j in range(2):
+            cols = pl.ds(pl.multiple_of(j * half + (member ^ i) * part, part), part)
+            for x in range(2):
+                full[x * nodes : (x + 1) * nodes, cols] = term[x, :, j * part : (j + 1) * part]
+    block = full.shape[1] // 16
+    for i in range(8):
+        cols = pl.ds(pl.multiple_of((2 * i + 1 - y) * block, block), block)
+        away[:, i * block : (i + 1) * block] = full[:, cols]
+
+
+def dense_kernel(ids, own, other, o0, o1, o2, o3, *rest):
+    weights = rest[:8]
+    a0, a1, a2, a3, pre_grad, back_own, back_other, left, grads, acts = rest[8:]
+    y, z, x = ids[2], ids[3], ids[5]
+    pair, width = own.shape
+    nodes, block = pair // 2, width // 16
+    part = pre_grad.shape[1]
+
+    def chip(i, other_x):
+        return pl.multiple_of(((z ^ (i >> 1)) * 4 + other_x * 2 + (y ^ (i & 1))) * block, block)
+
+    def place(i):
+        return pl.ds(pl.multiple_of((i & 1) * pair + (x ^ (i >> 1)) * nodes, nodes), nodes)
+
+    for i in range(8):
+        for j in range(2):
+            cols = slice((2 * i + j) * block, (2 * i + j + 1) * block)
+            left[:pair, cols] = own[:, pl.ds(chip(i, j), block)]
+            left[pair:, cols] = other[:, pl.ds(chip(i, j), block)]
+    for i, piece in enumerate((o0, o1, o2, o3)):
+        grads[place(i), :] = piece[...]
+    many = 2 * block
+    bias = sum(
+        w[many:, :].astype(F32) * (z ^ (i >> 1) == ids[7]).astype(F32) for i, w in enumerate(weights)
+    )[:1]
+    step = 256
+    for n in range(part // step):
+        cols = slice(n * step, (n + 1) * step)
+        matrix = jnp.concatenate([w[:many, cols] for w in weights], axis=0)
+        pre = jnp.dot(left[...], matrix, preferred_element_type=F32) + bias[:, cols]
+        sigmoid = 1.0 / (1.0 + jnp.exp(-pre))
+        acts[:, cols] = (pre * sigmoid).astype(BF16)
+        slope = sigmoid * (1.0 + pre * (1.0 - sigmoid))
+        grad = (grads[:, cols].astype(F32) * slope).astype(BF16)
+        pre_grad[:, cols] = grad
+    for i, piece in enumerate((a0, a1, a2, a3)):
+        piece[...] = acts[place(i), :]
+    for i, weight in enumerate(weights):
+        back = lax.dot_general(
+            pre_grad[...], weight[:many, :], (((1,), (1,)), ((), ())), preferred_element_type=F32
+        )
+        for j in range(2):
+            cols = pl.ds(chip(i, j), block)
+            back_own[:, cols] = back[:pair, j * block : (j + 1) * block]
+            back_other[:, cols] = back[pair:, j * block : (j + 1) * block].astype(BF16)
+
+
+def back_kernel(ids, own, received, v0, v1, v2, v3):
+    member = ids[0]
+    nodes, part, half = v0.shape[1], v0.shape[2] // 2, own.shape[1] // 2
+    for i, out in enumerate((v0, v1, v2, v3)):
+        for j in range(2):
+            cols = pl.ds(pl.multiple_of(j * half + (member ^ i) * part, part), part)
+            for x in range(2):
+                rows = slice(x * nodes, (x + 1) * nodes)
+                total = own[rows, cols] + received[rows, cols].astype(F32)
+                out[x, :, j * part : (j + 1) * part] = total.astype(out.dtype)
+
+
+def add_kernel(v0, vx, vz, vxz, out):
+    out[:2] = (v0[...] + vx[...].astype(F32)).astype(BF16)
+    out[2:] = (vz[...].astype(F32) + vxz[...].astype(F32)).astype(BF16)
+
+
+def spread_kernel(ids, lists, a0, a1, a2, a3, *rest):
+    grads, (out, total) = rest[:4], rest[4:]
+    core, y, x = ids[1], ids[2], ids[5]
+    tile = out.shape[1]
+    total[...] = jnp.zeros_like(total)
+    for i, tiles in enumerate((a0, a1, a2, a3)):
+        for away in range(4):
+            m = (y ^ (away >> 1)) * 2 + (core ^ (away & 1))
+            left = []
+            for s in range(SLOTS):
+                slot = m * SLOTS + s
+                block = tiles[pl.ds(pl.multiple_of(slot * tile, tile), tile), :]
+                left.append(jnp.where(lists[i, slot] >= 0, block, jnp.zeros_like(block)))
+            terms = lax.dot_general(
+                jnp.concatenate(left, axis=1), grads[away][2 * (i >> 1) + (x ^ (i & 1))],
+                (((0,), (0,)), ((), ())), preferred_element_type=F32,
+            )
+            for s in range(SLOTS):
+                at = jnp.maximum(lists[i, m * SLOTS + s], 0)
+                total[at] += terms[s * tile : (s + 1) * tile]
+    out[...] = total[...].astype(BF16)
+
+
+def finish_kernel(terms, out):
+    part, half = terms.shape[-1] // 2, out.shape[-1] // 2
+    for g in range(GROUP):
+        total = sum(terms[i].astype(F32) for i in range(g, terms.shape[0], GROUP)).astype(BF16)
+        out[:, g * part : (g + 1) * part] = total[:, :part]
+        out[:, half + g * part : half + (g + 1) * part] = total[:, part:]
+
+
+def act_kernel(ids, mask, a0, a1, a2, a3, out):
+    part, lanes = a0.shape[-1], mask.shape[-1]
+    for i, piece in enumerate((a0, a1, a2, a3)):
+        start = pl.multiple_of((ids[7] ^ i) * part, part)
+        for j in range(part // lanes):
+            out[:, pl.ds(start + j * lanes, lanes)] = piece[:, j * lanes : (j + 1) * lanes] * mask[...]
+
+
+def weight_grad_kernel(ids, own, other, away, away_other, g0, g1, keep, send, row, left, total):
+    y, high, low = ids[2], ids[4], ids[6]
+    pair, block = own.shape[0], keep.shape[1]
+    for i in range(8):
+        take = pl.ds(pl.multiple_of((2 * i + y) * block, block), block)
+        cols = slice(i * block, (i + 1) * block)
+        left[:pair, cols] = own[:, take]
+        left[pair : 2 * pair, cols] = other[:, take]
+    left[2 * pair : 3 * pair, :] = away[...]
+    left[3 * pair :, :] = away_other[...]
+    total[...] = lax.dot_general(
+        left[...], jnp.concatenate([g0[...], g1[...]], axis=0),
+        (((0,), (0,)), ((), ())), preferred_element_type=F32,
+    )
+    for j in range(2):
+        for i in range(2):
+            for out, flip in ((keep, 0), (send, 1)):
+                at = (high ^ j) * 4 + (low ^ flip) * 2 + i
+                rows = pl.ds(pl.multiple_of(at * block, block), block)
+                value = total[rows, :].astype(out.dtype)
+                if flip:
+                    out[(2 * j + i) * block : (2 * j + i + 1) * block, :] = value
+                else:
+                    out[2 * j + i] = value
+    sums = sum(jnp.sum(g[...].astype(F32), axis=0, keepdims=True) for g in (g0, g1))
+    row[...] = jnp.broadcast_to(sums, row.shape)
+    send[4 * block :, :] = row[...].astype(send.dtype)
+
+
+def fold_low_kernel(ids, keep, row, received, own, send, both):
+    x, block = ids[5], keep.shape[1]
+    for i in range(4):
+        total = keep[i] + received[i * block : (i + 1) * block, :].astype(F32)
+        place = jnp.int32(i & 1) == x
+        j = i >> 1
+
+        @pl.when(place)
+        def _():
+            own[j] = total
+
+        @pl.when(jnp.logical_not(place))
+        def _():
+            send[j * block : (j + 1) * block, :] = total.astype(BF16)
+
+    both[...] = row[...] + received[4 * block :, :].astype(F32)
+    send[2 * block :, :] = both[...].astype(BF16)
+
+
+def fold_x_kernel(own, row, received, mine, rows, send):
+    block = own.shape[1]
+    mine[0] = own[0]
+    mine[1] = received[:block, :].astype(F32)
+    send[:block, :] = own[1].astype(BF16)
+    send[block : 2 * block, :] = received[block : 2 * block, :]
+    rows[0] = row[...]
+    rows[1] = received[2 * block :, :].astype(F32)
+    send[2 * block : 2 * block + ROWS, :] = row[...].astype(BF16)
+    send[2 * block + ROWS :, :] = received[2 * block :, :]
+
+
+def fold_high_kernel(ids, own, rows, received, mine, sums, send):
+    core, block = ids[1], own.shape[1]
+    many = mine.shape[1]
+    for i in range(2):
+        for out, k in ((mine, core), (send, 1 - core)):
+            at = pl.multiple_of(k * many, many)
+            take = pl.ds(pl.multiple_of(i * block + k * many, many), many)
+            value = own[i, pl.ds(at, many), :] + received[take, :].astype(F32)
+            if out is mine:
+                out[i] = value
+            else:
+                out[i * many : (i + 1) * many, :] = value
+        first = 2 * block + i * ROWS
+        sums[i] = rows[i] + received[first : first + ROWS, :].astype(F32)
+        send[2 * many + i * ROWS : 2 * many + (i + 1) * ROWS, :] = sums[i]
+
+
+def weight_out_kernel(ids, mine, sums, received, out, bias):
+    many, part = mine.shape[1:]
+    block = 2 * many
+    for i in range(2):
+        cols = pl.ds(pl.multiple_of((ids[7] ^ (2 * i)) * part, part), part)
+        out[:, cols] = mine[i]
+        cols = pl.ds(pl.multiple_of((ids[7] ^ (2 * i + 1)) * part, part), part)
+        out[:, cols] = received[i * many : (i + 1) * many, :]
+    quarters = (
+        sums[0], received[block : block + ROWS, :], sums[1], received[block + ROWS :, :],
+    )
+    bias[...] = sum(q * (ids[3] ^ ids[7] == i).astype(F32) for i, q in enumerate(quarters))
+
+
+def chip_body(features, weight, bias, node_mask, neighbour_tiles, tile_weights, out_grad):
+    rows, cols = lax.axis_size("row"), lax.axis_size("col")
+    devices = rows * cols
+    r, c = lax.axis_index("row"), lax.axis_index("col")
+    core, z = c & 1, r >> 1
+    place = (r & 1) * 2 + core
+    ids = jnp.stack([r & 3, core, c >> 1, z, r >> 2, r & 1, z & 1, place, r]).astype(jnp.int32)
+    nodes, width = features.shape[1:]
+    half, quarter = width // 2, width // GROUP
+    lists, tiles = neighbour_tiles[0, 0], tile_weights[0, 0]
+    dests, slots, tile = tiles.shape[0], tiles.shape[1], tiles.shape[2]
+    masks = (X, Z, X | Z)
+    shares = (CORE, X, X | CORE)
+
+    lists = jnp.pad(lists.reshape(1, -1), ((0, 15), (0, tile - dests * slots))).astype(BF16)
+    tiles = jnp.concatenate([tiles.reshape(-1, tile), lists], axis=0)
+    tiles_of = [tiles, swap(tiles, X), swap(tiles, Z)]
+    tiles_of.append(swap(tiles_of[2], X))
+    lists_of = jnp.stack([t[-16, : dests * slots] for t in tiles_of]).astype(jnp.int32)
+
+    own_rows = weight.shape[0]
+    at = (r & 1) * (quarter // 2) + c * own_rows
+    row = lax.dynamic_update_slice(jnp.zeros((ROWS, quarter), BF16), bias[None], (0, at))
+    pieces = call(split_kernel, [shape((own_rows + ROWS, quarter), BF16)] * 4, ids, weight, row)
+    pieces = [pieces[0]] + [swap(p, m) for p, m in zip(pieces[1:], shares)]
+    pieces[0] = after(pieces[0], tiles_of[1])
+    (block,) = call(block_kernel, [shape((4 * own_rows + ROWS, quarter), BF16)], ids, *pieces)
+
+    columns = call(
+        columns_kernel, [shape((2, nodes, quarter), BF16)] * 4, ids, features, swap(features[0], 2 * Z)
+    )
+    source = [columns[0]] + [swap(value, m) for value, m in zip(columns[1:], masks)]
+    y0, z1, z2 = [swap(block, m) for m in (Y, Z, 2 * Z)]
+    z3 = swap(z2, Z)
+    y1, y2, y3 = [swap(value, Y) for value in (z1, z2, z3)]
+    weights = [block, y0, z1, y1, z2, y2, z3, y3]
+
+    lanes = jnp.broadcast_to(node_mask[0][:, None].astype(BF16), (nodes, 128))
+    grads = call(split_masked_kernel, [shape((nodes, quarter), BF16)] * 4, ids, lanes, out_grad[0])
+    grads = [grads[0]] + [swap(g, m) for g, m in zip(grads[1:], shares)]
+
+    source[0] = after(source[0], y0, z1, z2)
+    piece = (GROUP, dests // 2, tile, quarter)
+    kept, sent = call(
+        gather_kernel, [shape(piece, F32), shape(piece, BF16)],
+        ids, lists_of, *tiles_of, *source,
+        scratch=[pltpu.VMEM((rows, tile, quarter), BF16)],
+        smem=2, flops=2 * GROUP * dests * slots * tile * tile * quarter,
+    )
+    mine, send = call(
+        pair_sum_kernel, [shape((GROUP, tile, quarter), F32), shape((GROUP, tile, quarter), BF16)],
+        ids, kept, swap(after(sent, y1), CORE),
+    )
+    received = after(swap(send, Y), z3, y2, grads[2], grads[3])
+    near, far = call(group_kernel, [shape((2, tile, quarter), BF16)] * 2, ids, mine, received)
+    aggregate, away = call(
+        aggregate_kernel, [shape((2 * nodes, width), BF16), shape((2 * nodes, half), BF16)],
+        ids, after(near, y3), swap(near, X), swap(far, Z), swap(far, X | Z),
+    )
+    aggregate_other = swap(aggregate, CORE)
+    away = swap(away, Y)
+    away_other = swap(away, CORE)
+
+    *acts, pre_grad, back_own, back_other = call(
+        dense_kernel,
+        [shape((nodes, quarter), BF16)] * 4
+        + [shape((4 * nodes, quarter), BF16)]
+        + [shape((2 * nodes, width), F32), shape((2 * nodes, width), BF16)],
+        ids, aggregate, aggregate_other, *grads, *weights,
+        scratch=[pltpu.VMEM((4 * nodes, width), BF16)] + [pltpu.VMEM((4 * nodes, quarter), BF16)] * 2,
+        flops=16 * nodes * quarter * width, vmem=56,
+    )
+
+    v0, *others = call(
+        back_kernel, [shape((2, nodes, quarter), F32)] + [shape((2, nodes, quarter), BF16)] * 3,
+        ids, back_own, swap(back_other, CORE),
+    )
+    vx, vz, vxz = [swap(v, m) for v, m in zip(others, masks)]
+    pre_grad_y = swap(pre_grad, Y)
+    grads_own = call(add_kernel, [shape((4, nodes, quarter), BF16)], v0, vx, vz, vxz, smem=0)[0]
+    grads_away = swap(grads_own, Y)
+    keep, send, row = call(
+        weight_grad_kernel,
+        [shape((4, tile, quarter), F32), shape((4 * tile + ROWS, quarter), BF16), shape((ROWS, quarter), F32)],
+        ids, aggregate, aggregate_other, away, away_other, pre_grad, pre_grad_y,
+        scratch=[pltpu.VMEM((8 * nodes, half), BF16), pltpu.VMEM((half, quarter), F32)],
+        flops=16 * nodes * quarter * half,
+    )
+    grads_away, send = lax.optimization_barrier((grads_away, send))
+    (spread,) = call(
+        spread_kernel, [shape((rows, tile, quarter), BF16)],
+        ids, lists_of, *tiles_of,
+        grads_own, swap(grads_own, CORE), grads_away, swap(grads_away, CORE),
+        scratch=[pltpu.VMEM((rows, tile, quarter), F32)],
+        smem=2, flops=2 * GROUP * dests * slots * tile * tile * quarter,
+    )
+
+    acts = [acts[0]] + [swap(a, m) for a, m in zip(acts[1:], shares)]
+    received = swap(send, Z)
+    spread = after(spread, received)
+    spread_all = lax.all_to_all(spread, "row", 0, 0, tiled=True)
+    own, send, row = call(
+        fold_low_kernel,
+        [shape((2, tile, quarter), F32), shape((2 * tile + ROWS, quarter), BF16), shape((ROWS, quarter), F32)],
+        ids, keep, row, received,
+    )
+    own, rows_of, send = call(
+        fold_x_kernel,
+        [shape((2, tile, quarter), F32), shape((2, ROWS, quarter), F32), shape((2 * tile + 2 * ROWS, quarter), BF16)],
+        own, row, swap(send, X), smem=0,
+    )
+    own = after(own, *acts[1:])
+    own, rows_of, send = call(
+        fold_high_kernel,
+        [shape((2, own_rows, quarter), F32), shape((2, ROWS, quarter), F32), shape((2 * own_rows + 2 * ROWS, quarter), F32)],
+        ids, own, rows_of, swap(send, 2 * Z),
+    )
+    weight_grad, row = call(
+        weight_out_kernel, [shape((own_rows, width), F32), shape((ROWS, quarter), F32)],
+        ids, own, rows_of, swap(send, CORE),
+    )
+    bias_grad = lax.dynamic_slice_in_dim(row[0], at, own_rows)
+
+    (activations,) = call(act_kernel, [shape((nodes, width), BF16)], ids, lanes, *acts)
+    (input_grad,) = call(finish_kernel, [shape((nodes, width), BF16)], spread_all, smem=0)
+    return activations[None], input_grad[None], weight_grad, bias_grad
 
 
 def fetch_weights(weight, bias):
@@ -85,8 +534,9 @@
 
 
 def solution(mesh):
+    chips = mesh.shape["row"] == 8 and mesh.shape["col"] == 4
     return jax.shard_map(
-        body,
+        chip_body if chips else body,
         mesh=mesh,
         in_specs=(
             P("col", "row", None),

time: 565 us -> 209 us (0.37)
  waiting for transfers between devices: 429 us -> 123 us
  blocking collectives: 81.5 us -> 0 us
  starting transfers between devices: 0.25 us -> 52.6 us
  matrix products: 33.2 us -> 0 us
  Pallas kernels: 0 us -> 25.7 us
  between operations: 15.3 us -> 1.03 us
    reduce_scatter x3 -> x0, waiting for transfers between devices: 285 us -> none  [the longest x1 183 us: body(): lax.psum_scatter(weight_term, ('row', 'col'), scatter_dimension=0, tiled=...]
    all_gather x3 -> x0, waiting for transfers between devices: 143 us -> none  [the longest x1 75.8 us: body(): source = lax.all_gather(features, 'row', axis=1, tiled=True)[0]]
    ppermute x0 -> x43, waiting for transfers between devices: none -> 123 us  [swap(): return lax.ppermute(value, BOTH, [(i, i ^ mask) for i in range(total)])]
    unnamed x2 -> x0, blocking collectives: 81.5 us -> none
    ppermute x0 -> x43, starting transfers between devices: none -> 45.3 us  [swap(): return lax.ppermute(value, BOTH, [(i, i ^ mask) for i in range(total)])]
    dot_general x6 -> x0, matrix products: 33.2 us -> none  [the longest x1 8.66 us: body(): lax.dot_general(aggregate, pre_grad, (((0,), (0,)), ((), ())), preferred_...]
    pallas_call x0 -> x19, Pallas kernels: none -> 25.7 us  [call(): pl.pallas_call(kernel, out_shape=outs, in_specs=[SMEM] * smem + [VMEM] *...]
    all_to_all x0 -> x1, starting transfers between devices: none -> 7.3 us  [chip_body(): spread_all = lax.all_to_all(spread, 'row', 0, 0, tiled=True)]
  transfers between devices with their start and end apart: 6 -> 44, of which waited for: 6 -> 31; matrix products, arithmetic and copies ran while one was open for 2% -> 1% of each run, Pallas kernels for 0% -> 8%
where the time goes in v2:
time: 209 us
  waiting for transfers between devices  123 us (59%)
  starting transfers between devices  52.6 us (25%)
  Pallas kernels  25.7 us (12%)
  local copies, waits for them, and re-layouts  5.34 us (3%)
    ppermute x43, waiting for transfers between devices, swap(): return lax.ppermute(value, BOTH, [(i, i ^ mask) for i in range(total)])  123 us
    ppermute x43, starting transfers between devices, swap(): return lax.ppermute(value, BOTH, [(i, i ^ mask) for i in range(total)])  45.3 us
    pallas_call x19, Pallas kernels, call(): pl.pallas_call(kernel, out_shape=outs, in_specs=[SMEM] * smem + [VMEM] *...  25.7 us
    all_to_all x1, starting transfers between devices, chip_body(): spread_all = lax.all_to_all(spread, 'row', 0, 0, tiled=True)  7.3 us
  transfers between devices with their start and end apart: 44, of which 31 were waited for; matrix products, arithmetic and copies ran while one was open for 1% of the time, Pallas kernels for 8%

profile of v2, /device:TPU:0, one launch (start us, length us, event | category | flops | bytes accessed | tf_op | source)
XLA Modules:
  0.0 209.0 jit_solution(14140994789883665458)
XLA Ops:
  2.6 3.0 %collective-permute-start = (bf16[1552,128]{1,0:T(8,128)(2,1)S(1)}, bf16[1552,128]{1,0:T(8,128)(2,1)S(1)}, u32[]{:S(2)}, u32[]{:S(2)}) collective-permute-start(bf16[1552,128]{1,0:T(8,128)(2,1)S(1)} %fusion.1.a0), channel_id=1, source_target_pairs={{0,4},{1,5},{2,6},{3,7},{4,0},{5,1},{6,2},{7,3},{8,12},{9,13},{10,... | collective-permute-start | bytes 1191944 | tf_op jit(solution)/shard_map/ppermute | solution.py:20
  7.2 2.6 %collective-permute-start.3 = (bf16[128,2048]{1,0:T(8,128)(2,1)}, bf16[128,2048]{1,0:T(8,128)(2,1)S(1)}, u32[]{:S(2)}, u32[]{:S(2)}) collective-permute-start(bf16[128,2048]{1,0:T(8,128)(2,1)} %bitcast.20), channel_id=1, source_target_pairs={{0,16},{1,17},{2,18},{3,19},{4,20},{5,21},{6,22},{7,23},{8,24},{9,... | collective-permute-start | bytes 1572872 | tf_op jit(solution)/shard_map/ppermute | solution.py:20
  19.3 2.1 %collective-permute-start.7 = (bf16[272,512]{1,0:T(8,128)(2,1)S(1)}, bf16[272,512]{1,0:T(8,128)(2,1)S(1)}, u32[]{:S(2)}, u32[]{:S(2)}) collective-permute-start(bf16[272,512]{1,0:T(8,128)(2,1)S(1)} %shard_map.104.rest_0_), channel_id=1, source_target_pairs={{0,2},{1,3},{2,0},{3,1},{4,6},{5,7},{6,4},{7,5},{8,10},{9,11},{10,... | collective-permute-start | bytes 835592 | tf_op jit(solution)/shard_map/ppermute | solution.py:20
  21.4 2.8 %collective-permute-start.8 = (bf16[272,512]{1,0:T(8,128)(2,1)S(1)}, bf16[272,512]{1,0:T(8,128)(2,1)S(1)}, u32[]{:S(2)}, u32[]{:S(2)}) collective-permute-start(bf16[272,512]{1,0:T(8,128)(2,1)S(1)} %shard_map.104.rest_0_), channel_id=1, source_target_pairs={{0,8},{1,9},{2,10},{3,11},{4,12},{5,13},{6,14},{7,15},{8,0},{9,1},... | collective-permute-start | bytes 835592 | tf_op jit(solution)/shard_map/ppermute | solution.py:20
  25.0 2.6 %collective-permute-start.9 = (bf16[272,512]{1,0:T(8,128)(2,1)S(1)}, bf16[272,512]{1,0:T(8,128)(2,1)S(1)}, u32[]{:S(2)}, u32[]{:S(2)}) collective-permute-start(bf16[272,512]{1,0:T(8,128)(2,1)S(1)} %shard_map.104.rest_0_), channel_id=1, source_target_pairs={{0,16},{1,17},{2,18},{3,19},{4,20},{5,21},{6,22},{7,23},{8,24},{9,... | collective-permute-start | bytes 835592 | tf_op jit(solution)/shard_map/ppermute | solution.py:20
  27.6 7.2 %collective-permute-done.3.far = bf16[128,2048]{1,0:T(8,128)(2,1)S(1)} collective-permute-done((bf16[128,2048]{1,0:T(8,128)(2,1)}, bf16[128,2048]{1,0:T(8,128)(2,1)S(1)}, u32[]{:S(2)}, u32[]{:S(2)}) %collective-permute-start.3) | collective-permute-done | bytes 524320 | tf_op jit(solution)/shard_map/ppermute | solution.py:20
  39.1 5.7 %collective-permute-done.9.rest_4_ = bf16[272,512]{1,0:T(8,128)(2,1)S(1)} collective-permute-done((bf16[272,512]{1,0:T(8,128)(2,1)S(1)}, bf16[272,512]{1,0:T(8,128)(2,1)S(1)}, u32[]{:S(2)}, u32[]{:S(2)}) %collective-permute-start.9) | collective-permute-done | bytes 278560 | tf_op jit(solution)/shard_map/ppermute | solution.py:20
  46.3 2.1 collective-permute-done.11.h2
  48.4 2.3 %collective-permute-done.12.h3 = bf16[2,128,512]{2,1,0:T(8,128)(2,1)S(1)} collective-permute-done((bf16[2,128,512]{2,1,0:T(8,128)(2,1)S(1)}, bf16[2,128,512]{2,1,0:T(8,128)(2,1)S(1)}, u32[]{:S(2)}, u32[]{:S(2)}) %collective-permute-start.12) | collective-permute-done | bytes 262176 | tf_op jit(solution)/shard_map/ppermute | solution.py:20
  52.7 2.6 %collective-permute-done.14.received = bf16[4,2,128,512]{3,2,1,0:T(8,128)(2,1)S(1)} collective-permute-done((bf16[4,2,128,512]{3,2,1,0:T(8,128)(2,1)S(1)}, bf16[4,2,128,512]{3,2,1,0:T(8,128)(2,1)S(1)}, u32[]{:S(2)}, u32[]{:S(2)}) %collective-permute-start.14) | collective-permute-done | bytes 1048608 | tf_op jit(solution)/shard_map/ppermute | solution.py:20
  62.2 3.9 %collective-permute-done.16.rest_6_ = bf16[272,512]{1,0:T(8,128)(2,1)S(1)} collective-permute-done((bf16[272,512]{1,0:T(8,128)(2,1)S(1)}, bf16[272,512]{1,0:T(8,128)(2,1)S(1)}, u32[]{:S(2)}, u32[]{:S(2)}) %collective-permute-start.16) | collective-permute-done | bytes 278560 | tf_op jit(solution)/shard_map/ppermute | solution.py:20
  68.0 8.9 %collective-permute-done.17.rest_5_ = bf16[272,512]{1,0:T(8,128)(2,1)S(1)} collective-permute-done((bf16[272,512]{1,0:T(8,128)(2,1)S(1)}, bf16[272,512]{1,0:T(8,128)(2,1)S(1)}, u32[]{:S(2)}, u32[]{:S(2)}) %collective-permute-start.17) | collective-permute-done | bytes 278560 | tf_op jit(solution)/shard_map/ppermute | solution.py:20
  77.6 2.1 collective-permute-start.21
  82.1 3.8 %collective-permute-done.21.rx = bf16[2,128,512]{2,1,0:T(8,128)(2,1)S(1)} collective-permute-done((bf16[2,128,512]{2,1,0:T(8,128)(2,1)S(1)}, bf16[2,128,512]{2,1,0:T(8,128)(2,1)S(1)}, u32[]{:S(2)}, u32[]{:S(2)}) %collective-permute-start.21) | collective-permute-done | bytes 262176 | tf_op jit(solution)/shard_map/ppermute | solution.py:20
  85.9 3.0 %collective-permute-done.22.rz = bf16[2,128,512]{2,1,0:T(8,128)(2,1)S(1)} collective-permute-done((bf16[2,128,512]{2,1,0:T(8,128)(2,1)S(1)}, bf16[2,128,512]{2,1,0:T(8,128)(2,1)S(1)}, u32[]{:S(2)}, u32[]{:S(2)}) %collective-permute-start.22) | collective-permute-done | bytes 262176 | tf_op jit(solution)/shard_map/ppermute | solution.py:20
  88.9 2.6 %collective-permute-done.23.rxz = bf16[2,128,512]{2,1,0:T(8,128)(2,1)S(1)} collective-permute-done((bf16[2,128,512]{2,1,0:T(8,128)(2,1)S(1)}, bf16[2,128,512]{2,1,0:T(8,128)(2,1)S(1)}, u32[]{:S(2)}, u32[]{:S(2)}) %collective-permute-start.23) | collective-permute-done | bytes 262176 | tf_op jit(solution)/shard_map/ppermute | solution.py:20
  92.9 2.3 %collective-permute-done.25.o1 = bf16[128,512]{1,0:T(8,128)(2,1)S(1)} collective-permute-done((bf16[128,512]{1,0:T(8,128)(2,1)S(1)}, bf16[128,512]{1,0:T(8,128)(2,1)S(1)}, u32[]{:S(2)}, u32[]{:S(2)}) %collective-permute-start.25) | collective-permute-done | bytes 131104 | tf_op jit(solution)/shard_map/ppermute | solution.py:20
  96.3 7.3 %shard_map.110 = (bf16[128,512]{1,0:T(8,128)(2,1)}, bf16[128,512]{1,0:T(8,128)(2,1)}, bf16[128,512]{1,0:T(8,128)(2,1)}, bf16[128,512]{1,0:T(8,128)(2,1)}, bf16[5...) custom-call(s32[9]{0:T(128)} %copy-done.11, bf16[256,2048]{1,0:T(8,128)(2,1)} %copy-done.1, ...), custom_call_target="tpu_custom_call" | custom-call | flops 2147483648 | bytes 9044004 | tf_op jit(solution)/shard_map/pallas_call | solution.py:34
  112.4 5.5 %collective-permute-done.35.away = bf16[256,1024]{1,0:T(8,128)(2,1)S(1)} collective-permute-done((bf16[256,1024]{1,0:T(8,128)(2,1)S(1)}, bf16[256,1024]{1,0:T(8,128)(2,1)S(1)}, u32[]{:S(2)}, u32[]{:S(2)}) %collective-permute-start.35) | collective-permute-done | bytes 524320 | tf_op jit(solution)/shard_map/ppermute | solution.py:20
  119.8 4.3 %collective-permute-done.32.vxz = bf16[2,128,512]{2,1,0:T(8,128)(2,1)S(1)} collective-permute-done((bf16[2,128,512]{2,1,0:T(8,128)(2,1)S(1)}, bf16[2,128,512]{2,1,0:T(8,128)(2,1)S(1)}, u32[]{:S(2)}, u32[]{:S(2)}) %collective-permute-start.32) | collective-permute-done | bytes 262176 | tf_op jit(solution)/shard_map/ppermute | solution.py:20
  125.5 7.2 %collective-permute-done.37.g1 = bf16[512,512]{1,0:T(8,128)(2,1)S(1)} collective-permute-done((bf16[512,512]{1,0:T(8,128)(2,1)S(1)}, bf16[512,512]{1,0:T(8,128)(2,1)S(1)}, u32[]{:S(2)}, u32[]{:S(2)}) %collective-permute-start.37) | collective-permute-done | bytes 524320 | tf_op jit(solution)/shard_map/ppermute | solution.py:20
  132.6 2.2 %shard_map.114 = (f32[4,128,512]{2,1,0:T(8,128)S(1)}, bf16[528,512]{1,0:T(8,128)(2,1)S(1)}, f32[16,512]{1,0:T(8,128)S(1)}) custom-call(s32[9]{0:T(128)S(1)} %copy-done.12, bf16[256,2048]{1,0:T(8,128)(2,1)S(1)} %copy-done.2, bf16[256,2048]{1,0:T(8,128)(2,1)S(1)} %copy-done.4, bf16[256,1024]{1,0:T(8,128)(2,1)S(1)} %collective-permute-done.35.away, ...), custom_call_target="tpu_custom_call" | custom-call | flops 1073741824 | bytes 5816356 | tf_op jit(solution)/shard_map/pallas_call | solution.py:34
  134.9 8.6 %collective-permute-done.34.rest_2_ = bf16[4,128,512]{2,1,0:T(8,128)(2,1)S(1)} collective-permute-done((bf16[4,128,512]{2,1,0:T(8,128)(2,1)S(1)}, bf16[4,128,512]{2,1,0:T(8,128)(2,1)S(1)}, u32[]{:S(2)}, u32[]{:S(2)}) %collective-permute-start.34) | collective-permute-done | bytes 524320 | tf_op jit(solution)/shard_map/ppermute | solution.py:20
  145.4 3.6 %shard_map.115 = bf16[8,128,512]{2,1,0:T(8,128)(2,1)} custom-call(s32[9]{0:T(128)S(1)} %copy-done.12, s32[4,12]{1,0:T(4,128)S(1)} %maximum_convert_fusion.lists, bf16[1552,128]{1,0:T(8,128)(2,1)S(1)} %fusion.1.a0, bf16[1552,128]{1,0:T(8,128)(2,1)S(1)} %collective-permute-done.a1, bf16[1552,128]{1,0:T(8,128)(2,1)S(1)} %collective-permute-done.1.a2, ...), custom_call_target="tpu_custom_call" | custom-call | flops 805306368 | bytes 4735204 | tf_op jit(solution)/shard_map/pallas_call | solution.py:34
  149.0 9.2 %collective-permute-done.39.received = bf16[528,512]{1,0:T(8,128)(2,1)S(1)} collective-permute-done((bf16[528,512]{1,0:T(8,128)(2,1)S(1)}, bf16[528,512]{1,0:T(8,128)(2,1)S(1)}, u32[]{:S(2)}, u32[]{:S(2)}) %collective-permute-start.39) | collective-permute-done | bytes 540704 | tf_op jit(solution)/shard_map/ppermute | solution.py:20
  158.2 7.3 %all-to-all-start = ((bf16[8,128,512]{2,1,0:T(8,128)(2,1)}), bf16[8,128,512]{2,1,0:T(8,128)(2,1)S(1)}, u32[]{:S(2)}, u32[]{:S(2)}) async-start(bf16[8,128,512]{2,1,0:T(8,128)(2,1)} %shard_map.115), calls=%async_computation | async-start | bytes 2097152 | tf_op jit(solution)/shard_map/all_to_all | solution.py:428
  166.2 2.1 collective-permute-start.40
  168.3 15.5 %collective-permute-done.40.received = bf16[272,512]{1,0:T(8,128)(2,1)S(1)} collective-permute-done((bf16[272,512]{1,0:T(8,128)(2,1)S(1)}, bf16[272,512]{1,0:T(8,128)(2,1)S(1)}, u32[]{:S(2)}, u32[]{:S(2)}) %collective-permute-start.40) | collective-permute-done | bytes 278560 | tf_op jit(solution)/shard_map/ppermute | solution.py:20
  185.5 2.5 %collective-permute-start.27 = (bf16[128,512]{1,0:T(8,128)(2,1)S(1)}, bf16[128,512]{1,0:T(8,128)(2,1)S(1)}, u32[]{:S(2)}, u32[]{:S(2)}) collective-permute-start(bf16[128,512]{1,0:T(8,128)(2,1)S(1)} %copy-done.22), channel_id=1, source_target_pairs={{0,4},{1,5},{2,6},{3,7},{4,0},{5,1},{6,2},{7,3},{8,12},{9,13},{10,... | collective-permute-start | bytes 393224 | tf_op jit(solution)/shard_map/ppermute | solution.py:20
  188.2 4.2 %collective-permute-done.27.a2 = bf16[128,512]{1,0:T(8,128)(2,1)S(1)} collective-permute-done((bf16[128,512]{1,0:T(8,128)(2,1)S(1)}, bf16[128,512]{1,0:T(8,128)(2,1)S(1)}, u32[]{:S(2)}, u32[]{:S(2)}) %collective-permute-start.27) | collective-permute-done | bytes 131104 | tf_op jit(solution)/shard_map/ppermute | solution.py:20
  192.4 2.7 %collective-permute-done.28.a3 = bf16[128,512]{1,0:T(8,128)(2,1)S(1)} collective-permute-done((bf16[128,512]{1,0:T(8,128)(2,1)S(1)}, bf16[128,512]{1,0:T(8,128)(2,1)S(1)}, u32[]{:S(2)}, u32[]{:S(2)}) %collective-permute-start.28) | collective-permute-done | bytes 131104 | tf_op jit(solution)/shard_map/ppermute | solution.py:20
  195.1 8.7 %collective-permute-done.41.received = bf16[288,512]{1,0:T(8,128)(2,1)S(1)} collective-permute-done((bf16[288,512]{1,0:T(8,128)(2,1)S(1)}, bf16[288,512]{1,0:T(8,128)(2,1)S(1)}, u32[]{:S(2)}, u32[]{:S(2)}) %collective-permute-start.41) | collective-permute-done | bytes 294944 | tf_op jit(solution)/shard_map/ppermute | solution.py:20
  (146 shorter events, 57.6 us)
Async XLA Ops:
  2.6 12.2 %collective-permute-start = (bf16[1552,128]{1,0:T(8,128)(2,1)S(1)}, bf16[1552,128]{1,0:T(8,128)(2,1)S(1)}, u32[]{:S(2)}, u32[]{:S(2)}) collective-permute-start(bf16[1552,128]{1,0:T(8,128)(2,1)S(1)} %fusion.1.a0), channel_id=1, source_target_pairs={{0,4},{1,5},{2,6},{3,7},{4,0},{5,1},{6,2},{7,3},{8,12},{9,13},{10,... | collective-permute-start | bytes 1191944 | tf_op jit(solution)/shard_map/ppermute | solution.py:20
  5.6 18.9 %collective-permute-start.1 = (bf16[1552,128]{1,0:T(8,128)(2,1)S(1)}, bf16[1552,128]{1,0:T(8,128)(2,1)S(1)}, u32[]{:S(2)}, u32[]{:S(2)}) collective-permute-start(bf16[1552,128]{1,0:T(8,128)(2,1)S(1)} %fusion.1.a0), channel_id=1, source_target_pairs={{0,8},{1,9},{2,10},{3,11},{4,12},{5,13},{6,14},{7,15},{8,0},{9,1},... | collective-permute-start | bytes 1191944 | tf_op jit(solution)/shard_map/ppermute | solution.py:20
  7.2 27.6 %collective-permute-start.3 = (bf16[128,2048]{1,0:T(8,128)(2,1)}, bf16[128,2048]{1,0:T(8,128)(2,1)S(1)}, u32[]{:S(2)}, u32[]{:S(2)}) collective-permute-start(bf16[128,2048]{1,0:T(8,128)(2,1)} %bitcast.20), channel_id=1, source_target_pairs={{0,16},{1,17},{2,18},{3,19},{4,20},{5,21},{6,22},{7,23},{8,24},{9,... | collective-permute-start | bytes 1572872 | tf_op jit(solution)/shard_map/ppermute | solution.py:20
  19.3 16.8 %collective-permute-start.7 = (bf16[272,512]{1,0:T(8,128)(2,1)S(1)}, bf16[272,512]{1,0:T(8,128)(2,1)S(1)}, u32[]{:S(2)}, u32[]{:S(2)}) collective-permute-start(bf16[272,512]{1,0:T(8,128)(2,1)S(1)} %shard_map.104.rest_0_), channel_id=1, source_target_pairs={{0,2},{1,3},{2,0},{3,1},{4,6},{5,7},{6,4},{7,5},{8,10},{9,11},{10,... | collective-permute-start | bytes 835592 | tf_op jit(solution)/shard_map/ppermute | solution.py:20
  21.4 16.2 %collective-permute-start.8 = (bf16[272,512]{1,0:T(8,128)(2,1)S(1)}, bf16[272,512]{1,0:T(8,128)(2,1)S(1)}, u32[]{:S(2)}, u32[]{:S(2)}) collective-permute-start(bf16[272,512]{1,0:T(8,128)(2,1)S(1)} %shard_map.104.rest_0_), channel_id=1, source_target_pairs={{0,8},{1,9},{2,10},{3,11},{4,12},{5,13},{6,14},{7,15},{8,0},{9,1},... | collective-permute-start | bytes 835592 | tf_op jit(solution)/shard_map/ppermute | solution.py:20
  24.5 21.8 %collective-permute-start.2 = (bf16[1552,128]{1,0:T(8,128)(2,1)S(1)}, bf16[1552,128]{1,0:T(8,128)(2,1)S(1)}, u32[]{:S(2)}, u32[]{:S(2)}) collective-permute-start(bf16[1552,128]{1,0:T(8,128)(2,1)S(1)} %collective-permute-done.1.a2), channel_id=1, source_target_pairs={{0,4},{1,5},{2,6},{3,7},{4,0},{5,1},{6,2},{7,3},{8,12},{9,13},{10,... | collective-permute-start | bytes 1191944 | tf_op jit(solution)/shard_map/ppermute | solution.py:20
  25.0 19.7 %collective-permute-start.9 = (bf16[272,512]{1,0:T(8,128)(2,1)S(1)}, bf16[272,512]{1,0:T(8,128)(2,1)S(1)}, u32[]{:S(2)}, u32[]{:S(2)}) collective-permute-start(bf16[272,512]{1,0:T(8,128)(2,1)S(1)} %shard_map.104.rest_0_), channel_id=1, source_target_pairs={{0,16},{1,17},{2,18},{3,19},{4,20},{5,21},{6,22},{7,23},{8,24},{9,... | collective-permute-start | bytes 835592 | tf_op jit(solution)/shard_map/ppermute | solution.py:20
  35.5 10.8 %collective-permute-start.10 = (bf16[2,128,512]{2,1,0:T(8,128)(2,1)S(1)}, bf16[2,128,512]{2,1,0:T(8,128)(2,1)S(1)}, u32[]{:S(2)}, u32[]{:S(2)}) collective-permute-start(bf16[2,128,512]{2,1,0:T(8,128)(2,1)S(1)} %get-tuple-element.65), channel_id=1, source_target_pairs={{0,4},{1,5},{2,6},{3,7},{4,0},{5,1},{6,2},{7,3},{8,12},{9,13},{10,... | collective-permute-start | bytes 786440 | tf_op jit(solution)/shard_map/ppermute | solution.py:20
  36.1 12.3 %collective-permute-start.11 = (bf16[2,128,512]{2,1,0:T(8,128)(2,1)S(1)}, bf16[2,128,512]{2,1,0:T(8,128)(2,1)S(1)}, u32[]{:S(2)}, u32[]{:S(2)}) collective-permute-start(bf16[2,128,512]{2,1,0:T(8,128)(2,1)S(1)} %get-tuple-element.66), channel_id=1, source_target_pairs={{0,8},{1,9},{2,10},{3,11},{4,12},{5,13},{6,14},{7,15},{8,0},{9,1},... | collective-permute-start | bytes 786440 | tf_op jit(solution)/shard_map/ppermute | solution.py:20
  37.6 13.1 %collective-permute-start.12 = (bf16[2,128,512]{2,1,0:T(8,128)(2,1)S(1)}, bf16[2,128,512]{2,1,0:T(8,128)(2,1)S(1)}, u32[]{:S(2)}, u32[]{:S(2)}) collective-permute-start(bf16[2,128,512]{2,1,0:T(8,128)(2,1)S(1)} %get-tuple-element.67), channel_id=1, source_target_pairs={{0,12},{1,13},{2,14},{3,15},{4,8},{5,9},{6,10},{7,11},{8,4},{9,5},... | collective-permute-start | bytes 786440 | tf_op jit(solution)/shard_map/ppermute | solution.py:20
  44.8 7.9 %collective-permute-start.13 = (bf16[272,512]{1,0:T(8,128)(2,1)S(1)}, bf16[272,512]{1,0:T(8,128)(2,1)S(1)}, u32[]{:S(2)}, u32[]{:S(2)}) collective-permute-start(bf16[272,512]{1,0:T(8,128)(2,1)S(1)} %collective-permute-done.8.rest_2_), channel_id=1, source_target_pairs={{0,2},{1,3},{2,0},{3,1},{4,6},{5,7},{6,4},{7,5},{8,10},{9,11},{10,... | collective-permute-start | bytes 835592 | tf_op jit(solution)/shard_map/ppermute | solution.py:20
  56.1 20.8 %collective-permute-start.15 = (bf16[4,128,512]{2,1,0:T(8,128)(2,1)S(1)}, bf16[4,128,512]{2,1,0:T(8,128)(2,1)S(1)}, u32[]{:S(2)}, u32[]{:S(2)}) collective-permute-start(bf16[4,128,512]{2,1,0:T(8,128)(2,1)S(1)} %get-tuple-element.72), channel_id=1, source_target_pairs={{0,2},{1,3},{2,0},{3,1},{4,6},{5,7},{6,4},{7,5},{8,10},{9,11},{10,... | collective-permute-start | bytes 1572872 | tf_op jit(solution)/shard_map/ppermute | solution.py:20
  57.7 8.4 %collective-permute-start.16 = (bf16[272,512]{1,0:T(8,128)(2,1)S(1)}, bf16[272,512]{1,0:T(8,128)(2,1)S(1)}, u32[]{:S(2)}, u32[]{:S(2)}) collective-permute-start(bf16[272,512]{1,0:T(8,128)(2,1)S(1)} %collective-permute-done.9.rest_4_), channel_id=1, source_target_pairs={{0,8},{1,9},{2,10},{3,11},{4,12},{5,13},{6,14},{7,15},{8,0},{9,1},... | collective-permute-start | bytes 835592 | tf_op jit(solution)/shard_map/ppermute | solution.py:20
  59.3 17.6 %collective-permute-start.17 = (bf16[272,512]{1,0:T(8,128)(2,1)S(1)}, bf16[272,512]{1,0:T(8,128)(2,1)S(1)}, u32[]{:S(2)}, u32[]{:S(2)}) collective-permute-start(bf16[272,512]{1,0:T(8,128)(2,1)S(1)} %collective-permute-done.9.rest_4_), channel_id=1, source_target_pairs={{0,2},{1,3},{2,0},{3,1},{4,6},{5,7},{6,4},{7,5},{8,10},{9,11},{10,... | collective-permute-start | bytes 835592 | tf_op jit(solution)/shard_map/ppermute | solution.py:20
  66.1 16.0 %collective-permute-start.20 = (bf16[272,512]{1,0:T(8,128)(2,1)S(1)}, bf16[272,512]{1,0:T(8,128)(2,1)S(1)}, u32[]{:S(2)}, u32[]{:S(2)}) collective-permute-start(bf16[272,512]{1,0:T(8,128)(2,1)S(1)} %collective-permute-done.16.rest_6_), channel_id=1, source_target_pairs={{0,2},{1,3},{2,0},{3,1},{4,6},{5,7},{6,4},{7,5},{8,10},{9,11},{10,... | collective-permute-start | bytes 835592 | tf_op jit(solution)/shard_map/ppermute | solution.py:20
  77.6 8.3 %collective-permute-start.21 = (bf16[2,128,512]{2,1,0:T(8,128)(2,1)S(1)}, bf16[2,128,512]{2,1,0:T(8,128)(2,1)S(1)}, u32[]{:S(2)}, u32[]{:S(2)}) collective-permute-start(bf16[2,128,512]{2,1,0:T(8,128)(2,1)S(1)} %get-tuple-element.77.own), channel_id=1, source_target_pairs={{0,4},{1,5},{2,6},{3,7},{4,0},{5,1},{6,2},{7,3},{8,12},{9,13},{10,... | collective-permute-start | bytes 786440 | tf_op jit(solution)/shard_map/ppermute | solution.py:20
  79.7 9.2 %collective-permute-start.22 = (bf16[2,128,512]{2,1,0:T(8,128)(2,1)S(1)}, bf16[2,128,512]{2,1,0:T(8,128)(2,1)S(1)}, u32[]{:S(2)}, u32[]{:S(2)}) collective-permute-start(bf16[2,128,512]{2,1,0:T(8,128)(2,1)S(1)} %get-tuple-element.78), channel_id=1, source_target_pairs={{0,8},{1,9},{2,10},{3,11},{4,12},{5,13},{6,14},{7,15},{8,0},{9,1},... | collective-permute-start | bytes 786440 | tf_op jit(solution)/shard_map/ppermute | solution.py:20
  80.8 10.7 %collective-permute-start.23 = (bf16[2,128,512]{2,1,0:T(8,128)(2,1)S(1)}, bf16[2,128,512]{2,1,0:T(8,128)(2,1)S(1)}, u32[]{:S(2)}, u32[]{:S(2)}) collective-permute-start(bf16[2,128,512]{2,1,0:T(8,128)(2,1)S(1)} %get-tuple-element.78), channel_id=1, source_target_pairs={{0,12},{1,13},{2,14},{3,15},{4,8},{5,9},{6,10},{7,11},{8,4},{9,5},... | collective-permute-start | bytes 786440 | tf_op jit(solution)/shard_map/ppermute | solution.py:20
  103.7 14.2 %collective-permute-start.35 = (bf16[256,1024]{1,0:T(8,128)(2,1)S(1)}, bf16[256,1024]{1,0:T(8,128)(2,1)S(1)}, u32[]{:S(2)}, u32[]{:S(2)}) collective-permute-start(bf16[256,1024]{1,0:T(8,128)(2,1)S(1)} %get-tuple-element.92), channel_id=1, source_target_pairs={{0,2},{1,3},{2,0},{3,1},{4,6},{5,7},{6,4},{7,5},{8,10},{9,11},{10,... | collective-permute-start | bytes 1572872 | tf_op jit(solution)/shard_map/ppermute | solution.py:20
  108.9 10.2 %collective-permute-start.30 = (bf16[2,128,512]{2,1,0:T(8,128)(2,1)S(1)}, bf16[2,128,512]{2,1,0:T(8,128)(2,1)S(1)}, u32[]{:S(2)}, u32[]{:S(2)}) collective-permute-start(bf16[2,128,512]{2,1,0:T(8,128)(2,1)S(1)} %get-tuple-element.89), channel_id=1, source_target_pairs={{0,4},{1,5},{2,6},{3,7},{4,0},{5,1},{6,2},{7,3},{8,12},{9,13},{10,... | collective-permute-start | bytes 786440 | tf_op jit(solution)/shard_map/ppermute | solution.py:20
  110.6 9.2 %collective-permute-start.31 = (bf16[2,128,512]{2,1,0:T(8,128)(2,1)S(1)}, bf16[2,128,512]{2,1,0:T(8,128)(2,1)S(1)}, u32[]{:S(2)}, u32[]{:S(2)}) collective-permute-start(bf16[2,128,512]{2,1,0:T(8,128)(2,1)S(1)} %get-tuple-element.90), channel_id=1, source_target_pairs={{0,8},{1,9},{2,10},{3,11},{4,12},{5,13},{6,14},{7,15},{8,0},{9,1},... | collective-permute-start | bytes 786440 | tf_op jit(solution)/shard_map/ppermute | solution.py:20
  111.6 12.4 %collective-permute-start.32 = (bf16[2,128,512]{2,1,0:T(8,128)(2,1)S(1)}, bf16[2,128,512]{2,1,0:T(8,128)(2,1)S(1)}, u32[]{:S(2)}, u32[]{:S(2)}) collective-permute-start(bf16[2,128,512]{2,1,0:T(8,128)(2,1)S(1)} %get-tuple-element.91), channel_id=1, source_target_pairs={{0,12},{1,13},{2,14},{3,15},{4,8},{5,9},{6,10},{7,11},{8,4},{9,5},... | collective-permute-start | bytes 786440 | tf_op jit(solution)/shard_map/ppermute | solution.py:20
  117.9 7.6 %collective-permute-start.36 = (bf16[256,1024]{1,0:T(8,128)(2,1)S(1)}, bf16[256,1024]{1,0:T(8,128)(2,1)S(1)}, u32[]{:S(2)}, u32[]{:S(2)}) collective-permute-start(bf16[256,1024]{1,0:T(8,128)(2,1)S(1)} %collective-permute-done.35.away), channel_id=1, source_target_pairs={{0,1},{1,0},{2,3},{3,2},{4,5},{5,4},{6,7},{7,6},{8,9},{9,8},{10,11... | collective-permute-start | bytes 1572872 | tf_op jit(solution)/shard_map/ppermute | solution.py:20
  117.9 14.7 %collective-permute-start.37 = (bf16[512,512]{1,0:T(8,128)(2,1)S(1)}, bf16[512,512]{1,0:T(8,128)(2,1)S(1)}, u32[]{:S(2)}, u32[]{:S(2)}) collective-permute-start(bf16[512,512]{1,0:T(8,128)(2,1)S(1)} %copy-done.5), channel_id=1, source_target_pairs={{0,2},{1,3},{2,0},{3,1},{4,6},{5,7},{6,4},{7,5},{8,10},{9,11},{10,... | collective-permute-start | bytes 1572872 | tf_op jit(solution)/shard_map/ppermute | solution.py:20
  124.2 19.3 %collective-permute-start.34 = (bf16[4,128,512]{2,1,0:T(8,128)(2,1)S(1)}, bf16[4,128,512]{2,1,0:T(8,128)(2,1)S(1)}, u32[]{:S(2)}, u32[]{:S(2)}) collective-permute-start(bf16[4,128,512]{2,1,0:T(8,128)(2,1)S(1)} %shard_map.113.rest_0_), channel_id=1, source_target_pairs={{0,2},{1,3},{2,0},{3,1},{4,6},{5,7},{6,4},{7,5},{8,10},{9,11},{10,... | collective-permute-start | bytes 1572872 | tf_op jit(solution)/shard_map/ppermute | solution.py:20
  134.8 9.9 %collective-permute-start.33 = (bf16[4,128,512]{2,1,0:T(8,128)(2,1)S(1)}, bf16[4,128,512]{2,1,0:T(8,128)(2,1)S(1)}, u32[]{:S(2)}, u32[]{:S(2)}) collective-permute-start(bf16[4,128,512]{2,1,0:T(8,128)(2,1)S(1)} %shard_map.113.rest_0_), channel_id=1, source_target_pairs={{0,1},{1,0},{2,3},{3,2},{4,5},{5,4},{6,7},{7,6},{8,9},{9,8},{10,11... | collective-permute-start | bytes 1572872 | tf_op jit(solution)/shard_map/ppermute | solution.py:20
  143.5 14.7 %collective-permute-start.39 = (bf16[528,512]{1,0:T(8,128)(2,1)S(1)}, bf16[528,512]{1,0:T(8,128)(2,1)S(1)}, u32[]{:S(2)}, u32[]{:S(2)}) collective-permute-start(bf16[528,512]{1,0:T(8,128)(2,1)S(1)} %get-tuple-element.96), channel_id=1, source_target_pairs={{0,8},{1,9},{2,10},{3,11},{4,12},{5,13},{6,14},{7,15},{8,0},{9,1},... | collective-permute-start | bytes 1622024 | tf_op jit(solution)/shard_map/ppermute | solution.py:20
  158.2 49.9 %all-to-all-start = ((bf16[8,128,512]{2,1,0:T(8,128)(2,1)}), bf16[8,128,512]{2,1,0:T(8,128)(2,1)S(1)}, u32[]{:S(2)}, u32[]{:S(2)}) async-start(bf16[8,128,512]{2,1,0:T(8,128)(2,1)} %shard_map.115), calls=%async_computation | async-start | bytes 2097152 | tf_op jit(solution)/shard_map/all_to_all | solution.py:428
  166.2 17.6 %collective-permute-start.40 = (bf16[272,512]{1,0:T(8,128)(2,1)S(1)}, bf16[272,512]{1,0:T(8,128)(2,1)S(1)}, u32[]{:S(2)}, u32[]{:S(2)}) collective-permute-start(bf16[272,512]{1,0:T(8,128)(2,1)S(1)} %get-tuple-element.102), channel_id=1, source_target_pairs={{0,4},{1,5},{2,6},{3,7},{4,0},{5,1},{6,2},{7,3},{8,12},{9,13},{10,... | collective-permute-start | bytes 835592 | tf_op jit(solution)/shard_map/ppermute | solution.py:20
  183.8 20.0 %collective-permute-start.41 = (bf16[288,512]{1,0:T(8,128)(2,1)S(1)}, bf16[288,512]{1,0:T(8,128)(2,1)S(1)}, u32[]{:S(2)}, u32[]{:S(2)}) collective-permute-start(bf16[288,512]{1,0:T(8,128)(2,1)S(1)} %get-tuple-element.106), channel_id=1, source_target_pairs={{0,16},{1,17},{2,18},{3,19},{4,20},{5,21},{6,22},{7,23},{8,24},{9,... | collective-permute-start | bytes 884744 | tf_op jit(solution)/shard_map/ppermute | solution.py:20
  185.5 6.9 %collective-permute-start.27 = (bf16[128,512]{1,0:T(8,128)(2,1)S(1)}, bf16[128,512]{1,0:T(8,128)(2,1)S(1)}, u32[]{:S(2)}, u32[]{:S(2)}) collective-permute-start(bf16[128,512]{1,0:T(8,128)(2,1)S(1)} %copy-done.22), channel_id=1, source_target_pairs={{0,4},{1,5},{2,6},{3,7},{4,0},{5,1},{6,2},{7,3},{8,12},{9,13},{10,... | collective-permute-start | bytes 393224 | tf_op jit(solution)/shard_map/ppermute | solution.py:20
  188.1 7.0 %collective-permute-start.28 = (bf16[128,512]{1,0:T(8,128)(2,1)S(1)}, bf16[128,512]{1,0:T(8,128)(2,1)S(1)}, u32[]{:S(2)}, u32[]{:S(2)}) collective-permute-start(bf16[128,512]{1,0:T(8,128)(2,1)S(1)} %copy-done.21), channel_id=1, source_target_pairs={{0,5},{1,4},{2,7},{3,6},{4,1},{5,0},{6,3},{7,2},{8,13},{9,12},{10,... | collective-permute-start | bytes 393224 | tf_op jit(solution)/shard_map/ppermute | solution.py:20
  (40 other events, 647.8 us)

commit v3 on v2

--- a/solution.py
+++ b/solution.py
@@ -1,3 +1,5 @@
+import functools
+
 import jax
 import jax.numpy as jnp
 from jax import lax
@@ -114,21 +116,20 @@
     low = ids[6]
     for out, z in ((near, low), (far, 1 - low)):
         for x in range(2):
-            out[x] = (mine[2 * z + x] + received[2 * z + x].astype(F32)).astype(BF16)
-
-
-def aggregate_kernel(ids, own, rx, rz, rxz, full, away):
-    member, y = ids[0], ids[2]
-    nodes, part, half = own.shape[1], own.shape[2] // 2, full.shape[1] // 2
+            nodes = mine.shape[1]
+            total = mine[2 * z + x] + received[2 * z + x].astype(F32)
+            out[x * nodes : (x + 1) * nodes, :] = total.astype(BF16)
+        out[2 * nodes :, :] = jnp.zeros((out.shape[0] - 2 * nodes, out.shape[1]), BF16)
+
+
+def aggregate_kernel(ids, own, rx, rz, rxz, full):
+    member = ids[0]
+    nodes, part, half = full.shape[0] // 2, own.shape[1] // 2, full.shape[1] // 2
     for i, term in enumerate((own, rx, rz, rxz)):
         for j in range(2):
             cols = pl.ds(pl.multiple_of(j * half + (member ^ i) * part, part), part)
             for x in range(2):
-                full[x * nodes : (x + 1) * nodes, cols] = term[x, :, j * part : (j + 1) * part]
-    block = full.shape[1] // 16
-    for i in range(8):
-        cols = pl.ds(pl.multiple_of((2 * i + 1 - y) * block, block), block)
-        away[:, i * block : (i + 1) * block] = full[:, cols]
+                full[x * nodes : (x + 1) * nodes, cols] = term[x * nodes : (x + 1) * nodes, j * part : (j + 1) * part]
 
 
 def dense_kernel(ids, own, other, o0, o1, o2, o3, *rest):
@@ -234,80 +235,67 @@
             out[:, pl.ds(start + j * lanes, lanes)] = piece[:, j * lanes : (j + 1) * lanes] * mask[...]
 
 
-def weight_grad_kernel(ids, own, other, away, away_other, g0, g1, keep, send, row, left, total):
-    y, high, low = ids[2], ids[4], ids[6]
-    pair, block = own.shape[0], keep.shape[1]
-    for i in range(8):
-        take = pl.ds(pl.multiple_of((2 * i + y) * block, block), block)
-        cols = slice(i * block, (i + 1) * block)
-        left[:pair, cols] = own[:, take]
-        left[pair : 2 * pair, cols] = other[:, take]
-    left[2 * pair : 3 * pair, :] = away[...]
-    left[3 * pair :, :] = away_other[...]
-    total[...] = lax.dot_general(
-        left[...], jnp.concatenate([g0[...], g1[...]], axis=0),
-        (((0,), (0,)), ((), ())), preferred_element_type=F32,
-    )
+def weight_grad_kernel(far, ids, own, other, grads, keep, send, *rest):
+    y, low = ids[2], ids[6]
+    block = keep.shape[1]
+    row, total = rest if far else (None,) + rest
+    z = 1 - low if far else low
     for j in range(2):
-        for i in range(2):
-            for out, flip in ((keep, 0), (send, 1)):
-                at = (high ^ j) * 4 + (low ^ flip) * 2 + i
-                rows = pl.ds(pl.multiple_of(at * block, block), block)
-                value = total[rows, :].astype(out.dtype)
-                if flip:
-                    out[(2 * j + i) * block : (2 * j + i + 1) * block, :] = value
-                else:
-                    out[2 * j + i] = value
-    sums = sum(jnp.sum(g[...].astype(F32), axis=0, keepdims=True) for g in (g0, g1))
-    row[...] = jnp.broadcast_to(sums, row.shape)
-    send[4 * block :, :] = row[...].astype(send.dtype)
-
-
-def fold_low_kernel(ids, keep, row, received, own, send, both):
-    x, block = ids[5], keep.shape[1]
+        cols = pl.ds(pl.multiple_of((j * 8 + z * 4) * block, block), 4 * block)
+        total[4 * j * block : 4 * (j + 1) * block, :] = lax.dot_general(
+            jnp.concatenate([own[:, cols], other[:, cols]], axis=0), grads[...],
+            (((0,), (0,)), ((), ())), preferred_element_type=F32,
+        )
     for i in range(4):
-        total = keep[i] + received[i * block : (i + 1) * block, :].astype(F32)
-        place = jnp.int32(i & 1) == x
-        j = i >> 1
-
-        @pl.when(place)
-        def _():
-            own[j] = total
-
-        @pl.when(jnp.logical_not(place))
-        def _():
-            send[j * block : (j + 1) * block, :] = total.astype(BF16)
-
+        keep[i] = total[pl.ds(pl.multiple_of((2 * i + y) * block, block), block), :]
+        value = total[pl.ds(pl.multiple_of((2 * i + 1 - y) * block, block), block), :]
+        send[i * block : (i + 1) * block, :] = value.astype(BF16)
+    if far:
+        sums = jnp.sum(grads[...].astype(F32), axis=0, keepdims=True)
+        row[...] = jnp.broadcast_to(sums, row.shape)
+        send[4 * block :, :] = row[...].astype(BF16)
+
+
+def fold_y_kernel(keep, row, received, send, both):
+    block = keep.shape[1]
+    for i in range(4):
+        rows = slice(i * block, (i + 1) * block)
+        send[rows, :] = (keep[i] + received[rows, :].astype(F32)).astype(BF16)
     both[...] = row[...] + received[4 * block :, :].astype(F32)
-    send[2 * block :, :] = both[...].astype(BF16)
-
-
-def fold_x_kernel(own, row, received, mine, rows, send):
-    block = own.shape[1]
-    mine[0] = own[0]
-    mine[1] = received[:block, :].astype(F32)
-    send[:block, :] = own[1].astype(BF16)
-    send[block : 2 * block, :] = received[block : 2 * block, :]
-    rows[0] = row[...]
-    rows[1] = received[2 * block :, :].astype(F32)
-    send[2 * block : 2 * block + ROWS, :] = row[...].astype(BF16)
-    send[2 * block + ROWS :, :] = received[2 * block :, :]
-
-
-def fold_high_kernel(ids, own, rows, received, mine, sums, send):
-    core, block = ids[1], own.shape[1]
+    send[4 * block :, :] = both[...].astype(BF16)
+
+
+def fold_low_kernel(ids, keep, row, from_y, from_z, own, sums, s1, s2, s3):
+    high, x, block = ids[4], ids[5], keep.shape[1]
+    sums[...] = row[...] + from_z[4 * block :, :].astype(F32)
+    for i, out in enumerate((own, s1, s2, s3)):
+        at = (high ^ (i >> 1)) * 2 + (x ^ (i & 1))
+        rows = pl.ds(pl.multiple_of(at * block, block), block)
+        total = keep[at] + from_y[rows, :].astype(F32) + from_z[rows, :].astype(F32)
+        if out is own:
+            own[...] = total
+        else:
+            out[:block, :] = total.astype(BF16)
+            out[block:, :] = sums[...].astype(BF16)
+
+
+def fold_high_kernel(ids, own, row, r1, r2, r3, mine, sums, send):
+    core, block = ids[1], own.shape[0]
     many = mine.shape[1]
     for i in range(2):
         for out, k in ((mine, core), (send, 1 - core)):
-            at = pl.multiple_of(k * many, many)
-            take = pl.ds(pl.multiple_of(i * block + k * many, many), many)
-            value = own[i, pl.ds(at, many), :] + received[take, :].astype(F32)
+            at = pl.ds(pl.multiple_of(k * many, many), many)
+            if i == 0:
+                value = own[at, :] + r2[at, :].astype(F32)
+            else:
+                value = r1[at, :].astype(F32) + r3[at, :].astype(F32)
             if out is mine:
                 out[i] = value
             else:
                 out[i * many : (i + 1) * many, :] = value
-        first = 2 * block + i * ROWS
-        sums[i] = rows[i] + received[first : first + ROWS, :].astype(F32)
+    sums[0] = row[...] + r2[block:, :].astype(F32)
+    sums[1] = r1[block:, :].astype(F32) + r3[block:, :].astype(F32)
+    for i in range(2):
         send[2 * many + i * ROWS : 2 * many + (i + 1) * ROWS, :] = sums[i]
 
 
@@ -322,7 +310,12 @@
     quarters = (
         sums[0], received[block : block + ROWS, :], sums[1], received[block + ROWS :, :],
     )
-    bias[...] = sum(q * (ids[3] ^ ids[7] == i).astype(F32) for i, q in enumerate(quarters))
+    total = sum(q * (ids[3] ^ ids[7] == i).astype(F32) for i, q in enumerate(quarters))
+    step = 2 * many
+    picked = sum(
+        total[:1, i * step : (i + 1) * step] * ((ids[5] * 2 + ids[2]) == i).astype(F32) for i in range(4)
+    )
+    bias[...] = jnp.where(ids[1] == 0, picked[:, :many], picked[:, many:])
 
 
 def chip_body(features, weight, bias, node_mask, neighbour_tiles, tile_weights, out_grad):
@@ -339,34 +332,35 @@
     masks = (X, Z, X | Z)
     shares = (CORE, X, X | CORE)
 
-    lists = jnp.pad(lists.reshape(1, -1), ((0, 15), (0, tile - dests * slots))).astype(BF16)
-    tiles = jnp.concatenate([tiles.reshape(-1, tile), lists], axis=0)
-    tiles_of = [tiles, swap(tiles, X), swap(tiles, Z)]
-    tiles_of.append(swap(tiles_of[2], X))
-    lists_of = jnp.stack([t[-16, : dests * slots] for t in tiles_of]).astype(jnp.int32)
-
     own_rows = weight.shape[0]
     at = (r & 1) * (quarter // 2) + c * own_rows
     row = lax.dynamic_update_slice(jnp.zeros((ROWS, quarter), BF16), bias[None], (0, at))
     pieces = call(split_kernel, [shape((own_rows + ROWS, quarter), BF16)] * 4, ids, weight, row)
     pieces = [pieces[0]] + [swap(p, m) for p, m in zip(pieces[1:], shares)]
-    pieces[0] = after(pieces[0], tiles_of[1])
     (block,) = call(block_kernel, [shape((4 * own_rows + ROWS, quarter), BF16)], ids, *pieces)
 
+    lists = jnp.pad(lists.reshape(1, -1), ((0, 15), (0, tile - dests * slots))).astype(BF16)
+    tiles, lists = lax.optimization_barrier((tiles, lists, pieces[1]))[:2]
+    tiles = jnp.concatenate([tiles.reshape(-1, tile), lists], axis=0)
+    tiles_of = [tiles, swap(after(tiles, *pieces[2:]), X), swap(tiles, Z)]
+    tiles_of.append(swap(tiles_of[2], X))
+    lists_of = jnp.stack([t[-16, : dests * slots] for t in tiles_of]).astype(jnp.int32)
+
     columns = call(
-        columns_kernel, [shape((2, nodes, quarter), BF16)] * 4, ids, features, swap(features[0], 2 * Z)
+        columns_kernel, [shape((2, nodes, quarter), BF16)] * 4, ids, features, after(swap(features[0], 2 * Z), tiles_of[1])
     )
     source = [columns[0]] + [swap(value, m) for value, m in zip(columns[1:], masks)]
-    y0, z1, z2 = [swap(block, m) for m in (Y, Z, 2 * Z)]
-    z3 = swap(z2, Z)
-    y1, y2, y3 = [swap(value, Y) for value in (z1, z2, z3)]
-    weights = [block, y0, z1, y1, z2, y2, z3, y3]
-
     lanes = jnp.broadcast_to(node_mask[0][:, None].astype(BF16), (nodes, 128))
     grads = call(split_masked_kernel, [shape((nodes, quarter), BF16)] * 4, ids, lanes, out_grad[0])
     grads = [grads[0]] + [swap(g, m) for g, m in zip(grads[1:], shares)]
 
-    source[0] = after(source[0], y0, z1, z2)
+    y0, z1 = swap(block, Y), swap(block, Z)
+    z2 = swap(after(block, y0, z1), 2 * Z)
+    z3 = swap(after(z2, *grads[2:]), Z)
+    y1, y2, y3 = [swap(value, Y) for value in (z1, z2, z3)]
+    weights = [block, y0, z1, y1, z2, y2, z3, y3]
+
+    source[0] = after(source[0], y0, z1)
     piece = (GROUP, dests // 2, tile, quarter)
     kept, sent = call(
         gather_kernel, [shape(piece, F32), shape(piece, BF16)],
@@ -378,15 +372,13 @@
         pair_sum_kernel, [shape((GROUP, tile, quarter), F32), shape((GROUP, tile, quarter), BF16)],
         ids, kept, swap(after(sent, y1), CORE),
     )
-    received = after(swap(send, Y), z3, y2, grads[2], grads[3])
-    near, far = call(group_kernel, [shape((2, tile, quarter), BF16)] * 2, ids, mine, received)
-    aggregate, away = call(
-        aggregate_kernel, [shape((2 * nodes, width), BF16), shape((2 * nodes, half), BF16)],
-        ids, after(near, y3), swap(near, X), swap(far, Z), swap(far, X | Z),
+    received = after(swap(send, Y), y1, z2, grads[1])
+    near, far = call(group_kernel, [shape((2 * tile + 2 * ROWS, quarter), BF16)] * 2, ids, mine, received)
+    (aggregate,) = call(
+        aggregate_kernel, [shape((2 * nodes, width), BF16)],
+        ids, after(near, y2, y3), swap(near, X), swap(far, Z), swap(far, X | Z),
     )
     aggregate_other = swap(aggregate, CORE)
-    away = swap(away, Y)
-    away_other = swap(away, CORE)
 
     *acts, pre_grad, back_own, back_other = call(
         dense_kernel,
@@ -398,22 +390,35 @@
         flops=16 * nodes * quarter * width, vmem=56,
     )
 
+    far, send_far, row = call(
+        functools.partial(weight_grad_kernel, True),
+        [shape((4, tile, quarter), F32), shape((4 * tile + ROWS, quarter), BF16), shape((ROWS, quarter), F32)],
+        ids, aggregate, aggregate_other, pre_grad,
+        scratch=[pltpu.VMEM((half, quarter), F32)], flops=4 * nodes * quarter * width, vmem=56,
+    )
     v0, *others = call(
         back_kernel, [shape((2, nodes, quarter), F32)] + [shape((2, nodes, quarter), BF16)] * 3,
-        ids, back_own, swap(back_other, CORE),
+        ids, back_own, after(swap(back_other, CORE), send_far),
     )
     vx, vz, vxz = [swap(v, m) for v, m in zip(others, masks)]
-    pre_grad_y = swap(pre_grad, Y)
+    from_y = swap(send_far, Y)
+    near, send_near = call(
+        functools.partial(weight_grad_kernel, False),
+        [shape((4, tile, quarter), F32), shape((4 * tile, quarter), BF16)],
+        ids, aggregate, aggregate_other, after(pre_grad, v0),
+        scratch=[pltpu.VMEM((half, quarter), F32)], flops=4 * nodes * quarter * width, vmem=56,
+    )
+    vx, from_y, near = lax.optimization_barrier((vx, from_y, near))
     grads_own = call(add_kernel, [shape((4, nodes, quarter), BF16)], v0, vx, vz, vxz, smem=0)[0]
     grads_away = swap(grads_own, Y)
-    keep, send, row = call(
-        weight_grad_kernel,
-        [shape((4, tile, quarter), F32), shape((4 * tile + ROWS, quarter), BF16), shape((ROWS, quarter), F32)],
-        ids, aggregate, aggregate_other, away, away_other, pre_grad, pre_grad_y,
-        scratch=[pltpu.VMEM((8 * nodes, half), BF16), pltpu.VMEM((half, quarter), F32)],
-        flops=16 * nodes * quarter * half,
-    )
-    grads_away, send = lax.optimization_barrier((grads_away, send))
+    send, row = call(
+        fold_y_kernel, [shape((4 * tile + ROWS, quarter), BF16), shape((ROWS, quarter), F32)],
+        far, row, from_y, smem=0,
+    )
+    from_z = swap(send, Z)
+    grads_away = after(grads_away, from_z)
+    from_y = swap(after(send_near, grads_own), Y)
+    acts = [acts[0]] + [swap(after(a, grads_own), m) for a, m in zip(acts[1:], shares)]
     (spread,) = call(
         spread_kernel, [shape((rows, tile, quarter), BF16)],
         ids, lists_of, *tiles_of,
@@ -422,34 +427,28 @@
         smem=2, flops=2 * GROUP * dests * slots * tile * tile * quarter,
     )
 
-    acts = [acts[0]] + [swap(a, m) for a, m in zip(acts[1:], shares)]
-    received = swap(send, Z)
-    spread = after(spread, received)
+    pass
     spread_all = lax.all_to_all(spread, "row", 0, 0, tiled=True)
-    own, send, row = call(
+    own, row, *send = call(
         fold_low_kernel,
-        [shape((2, tile, quarter), F32), shape((2 * tile + ROWS, quarter), BF16), shape((ROWS, quarter), F32)],
-        ids, keep, row, received,
-    )
-    own, rows_of, send = call(
-        fold_x_kernel,
-        [shape((2, tile, quarter), F32), shape((2, ROWS, quarter), F32), shape((2 * tile + 2 * ROWS, quarter), BF16)],
-        own, row, swap(send, X), smem=0,
-    )
-    own = after(own, *acts[1:])
+        [shape((tile, quarter), F32), shape((ROWS, quarter), F32)] + [shape((tile + ROWS, quarter), BF16)] * 3,
+        ids, near, row, from_y, from_z,
+    )
+    received = [swap(s, m) for s, m in zip(send, (X, 2 * Z, 2 * Z | X))]
+    (input_grad,) = call(finish_kernel, [shape((nodes, width), BF16)], spread_all, smem=0)
+    (activations,) = call(act_kernel, [shape((nodes, width), BF16)], ids, lanes, *acts)
+    own = after(own, input_grad, activations)
     own, rows_of, send = call(
         fold_high_kernel,
         [shape((2, own_rows, quarter), F32), shape((2, ROWS, quarter), F32), shape((2 * own_rows + 2 * ROWS, quarter), F32)],
-        ids, own, rows_of, swap(send, 2 * Z),
+        ids, own, row, *received,
     )
     weight_grad, row = call(
-        weight_out_kernel, [shape((own_rows, width), F32), shape((ROWS, quarter), F32)],
+        weight_out_kernel, [shape((own_rows, width), F32), shape((1, own_rows), F32)],
         ids, own, rows_of, swap(send, CORE),
     )
-    bias_grad = lax.dynamic_slice_in_dim(row[0], at, own_rows)
-
-    (activations,) = call(act_kernel, [shape((nodes, width), BF16)], ids, lanes, *acts)
-    (input_grad,) = call(finish_kernel, [shape((nodes, width), BF16)], spread_all, smem=0)
+    bias_grad = row.reshape(own_rows)
+
     return activations[None], input_grad[None], weight_grad, bias_grad
 
 

time: 209 us -> 189 us (0.904)
  waiting for transfers between devices: 123 us -> 105 us
  starting transfers between devices: 52.6 us -> 46.1 us
  Pallas kernels: 25.7 us -> 31.5 us
  local copies, waits for them, and re-layouts: 5.34 us -> 3.19 us
    ppermute x43, waiting for transfers between devices: 123 us -> 100 us  [swap(): return lax.ppermute(value, BOTH, [(i, i ^ mask) for i in range(total)])]
    pallas_call x19 -> x20, Pallas kernels: 25.7 us -> 31.5 us  [call(): pl.pallas_call(kernel, out_shape=outs, in_specs=[SMEM] * smem + [VMEM] *...]
    all_to_all x1, waiting for transfers between devices: 0.01 us -> 4.82 us  [chip_body(): spread_all = lax.all_to_all(spread, 'row', 0, 0, tiled=True)]
    ppermute x43, starting transfers between devices: 45.3 us -> 41.4 us  [swap(): return lax.ppermute(value, BOTH, [(i, i ^ mask) for i in range(total)])]
    all_to_all x1, starting transfers between devices: 7.3 us -> 4.7 us  [chip_body(): spread_all = lax.all_to_all(spread, 'row', 0, 0, tiled=True)]
  transfers between devices with their start and end apart: 44 -> 44, of which waited for: 31 -> 29; matrix products, arithmetic and copies ran while one was open for 1% -> 1% of each run, Pallas kernels for 8% -> 9%
where the time goes in v3:
time: 189 us; the launch traced here: 188 us
  waiting for transfers between devices  105 us (56%)
  starting transfers between devices  46.1 us (24%)
  Pallas kernels  31.5 us (17%)
  local copies, waits for them, and re-layouts  3.19 us (2%)
    ppermute x43, waiting for transfers between devices, swap(): return lax.ppermute(value, BOTH, [(i, i ^ mask) for i in range(total)])  100 us
    ppermute x43, starting transfers between devices, swap(): return lax.ppermute(value, BOTH, [(i, i ^ mask) for i in range(total)])  41.4 us
    pallas_call x20, Pallas kernels, call(): pl.pallas_call(kernel, out_shape=outs, in_specs=[SMEM] * smem + [VMEM] *...  31.5 us
    all_to_all x1, waiting for transfers between devices, chip_body(): spread_all = lax.all_to_all(spread, 'row', 0, 0, tiled=True)  4.82 us
    all_to_all x1, starting transfers between devices, chip_body(): spread_all = lax.all_to_all(spread, 'row', 0, 0, tiled=True)  4.7 us
  transfers between devices with their start and end apart: 44, of which 29 were waited for; matrix products, arithmetic and copies ran while one was open for 1% of the time, Pallas kernels for 9%

profile of v3, /device:TPU:0, one launch (start us, length us, event | category | flops | bytes accessed | tf_op | source)
XLA Modules:
  0.0 188.5 jit_solution(7768748600314634907)
XLA Ops:
  5.7 2.9 %collective-permute-start.4 = (bf16[1552,128]{1,0:T(8,128)(2,1)S(1)}, bf16[1552,128]{1,0:T(8,128)(2,1)S(1)}, u32[]{:S(2)}, u32[]{:S(2)}) collective-permute-start(bf16[1552,128]{1,0:T(8,128)(2,1)S(1)} %pad_maximum_fusion.a0), channel_id=1, source_target_pairs={{0,8},{1,9},{2,10},{3,11},{4,12},{5,13},{6,14},{7,15},{8,0},{9,1},... | collective-permute-start | bytes 1191944 | tf_op jit(solution)/shard_map/ppermute | solution.py:22
  8.6 2.6 %collective-permute-start.6 = (bf16[128,2048]{1,0:T(8,128)(2,1)}, bf16[128,2048]{1,0:T(8,128)(2,1)S(1)}, u32[]{:S(2)}, u32[]{:S(2)}) collective-permute-start(bf16[128,2048]{1,0:T(8,128)(2,1)} %bitcast.20), channel_id=1, source_target_pairs={{0,16},{1,17},{2,18},{3,19},{4,20},{5,21},{6,22},{7,23},{8,24},{9,... | collective-permute-start | bytes 1572872 | tf_op jit(solution)/shard_map/ppermute | solution.py:22
  12.6 2.9 %collective-permute-done.1.p2 = bf16[80,512]{1,0:T(8,128)(2,1)S(1)} collective-permute-done((bf16[80,512]{1,0:T(8,128)(2,1)S(1)}, bf16[80,512]{1,0:T(8,128)(2,1)S(1)}, u32[]{:S(2)}, u32[]{:S(2)}) %collective-permute-start.1) | collective-permute-done | bytes 81952 | tf_op jit(solution)/shard_map/ppermute | solution.py:22
  19.0 7.7 %collective-permute-done.4.a2 = bf16[1552,128]{1,0:T(8,128)(2,1)S(1)} collective-permute-done((bf16[1552,128]{1,0:T(8,128)(2,1)S(1)}, bf16[1552,128]{1,0:T(8,128)(2,1)S(1)}, u32[]{:S(2)}, u32[]{:S(2)}) %collective-permute-start.4) | collective-permute-done | bytes 397344 | tf_op jit(solution)/shard_map/ppermute | solution.py:22
  26.7 2.0 %collective-permute-start.5 = (bf16[1552,128]{1,0:T(8,128)(2,1)S(1)}, bf16[1552,128]{1,0:T(8,128)(2,1)S(1)}, u32[]{:S(2)}, u32[]{:S(2)}) collective-permute-start(bf16[1552,128]{1,0:T(8,128)(2,1)S(1)} %collective-permute-done.4.a2), channel_id=1, source_target_pairs={{0,4},{1,5},{2,6},{3,7},{4,0},{5,1},{6,2},{7,3},{8,12},{9,13},{10,... | collective-permute-start | bytes 1191944 | tf_op jit(solution)/shard_map/ppermute | solution.py:22
  30.2 4.5 %collective-permute-done.6.far = bf16[128,2048]{1,0:T(8,128)(2,1)S(1)} collective-permute-done((bf16[128,2048]{1,0:T(8,128)(2,1)}, bf16[128,2048]{1,0:T(8,128)(2,1)S(1)}, u32[]{:S(2)}, u32[]{:S(2)}) %collective-permute-start.6) | collective-permute-done | bytes 524320 | tf_op jit(solution)/shard_map/ppermute | solution.py:22
  37.0 2.0 %collective-permute-start.11 = (bf16[2,128,512]{2,1,0:T(8,128)(2,1)S(1)}, bf16[2,128,512]{2,1,0:T(8,128)(2,1)S(1)}, u32[]{:S(2)}, u32[]{:S(2)}) collective-permute-start(bf16[2,128,512]{2,1,0:T(8,128)(2,1)S(1)} %get-tuple-element.83), channel_id=1, source_target_pairs={{0,12},{1,13},{2,14},{3,15},{4,8},{5,9},{6,10},{7,11},{8,4},{9,5},... | collective-permute-start | bytes 786440 | tf_op jit(solution)/shard_map/ppermute | solution.py:22
  40.6 3.3 %collective-permute-done.9.h1 = bf16[2,128,512]{2,1,0:T(8,128)(2,1)S(1)} collective-permute-done((bf16[2,128,512]{2,1,0:T(8,128)(2,1)S(1)}, bf16[2,128,512]{2,1,0:T(8,128)(2,1)S(1)}, u32[]{:S(2)}, u32[]{:S(2)}) %collective-permute-start.9) | collective-permute-done | bytes 262176 | tf_op jit(solution)/shard_map/ppermute | solution.py:22
  43.9 2.4 %collective-permute-done.10.h2 = bf16[2,128,512]{2,1,0:T(8,128)(2,1)S(1)} collective-permute-done((bf16[2,128,512]{2,1,0:T(8,128)(2,1)S(1)}, bf16[2,128,512]{2,1,0:T(8,128)(2,1)S(1)}, u32[]{:S(2)}, u32[]{:S(2)}) %collective-permute-start.10) | collective-permute-done | bytes 262176 | tf_op jit(solution)/shard_map/ppermute | solution.py:22
  46.2 3.3 %collective-permute-done.11.h3 = bf16[2,128,512]{2,1,0:T(8,128)(2,1)S(1)} collective-permute-done((bf16[2,128,512]{2,1,0:T(8,128)(2,1)S(1)}, bf16[2,128,512]{2,1,0:T(8,128)(2,1)S(1)}, u32[]{:S(2)}, u32[]{:S(2)}) %collective-permute-start.11) | collective-permute-done | bytes 262176 | tf_op jit(solution)/shard_map/ppermute | solution.py:22
  49.5 1.9 %shard_map.105 = (f32[4,2,128,512]{3,2,1,0:T(8,128)S(1)}, bf16[4,2,128,512]{3,2,1,0:T(8,128)(2,1)S(1)}) custom-call(s32[9]{0:T(128)S(1)} %stack.42.ids, s32[4,12]{1,0:T(4,128)S(1)} %maximum_convert_fusion.lists, bf16[1552,128]{1,0:T(8,128)(2,1)S(1)} %pad_maximum_fusion.a0, bf16[1552,128]{1,0:T(8,128)(2,1)S(1)} %collective-permute-done.3.a1, ...), custom_call_target="tpu_custom_call" | custom-call | flops 805306368 | bytes 5783780 | tf_op jit(solution)/shard_map/pallas_call | solution.py:36
  59.0 4.5 %collective-permute-done.18.o2 = bf16[128,512]{1,0:T(8,128)(2,1)S(1)} collective-permute-done((bf16[128,512]{1,0:T(8,128)(2,1)S(1)}, bf16[128,512]{1,0:T(8,128)(2,1)S(1)}, u32[]{:S(2)}, u32[]{:S(2)}) %collective-permute-start.18) | collective-permute-done | bytes 131104 | tf_op jit(solution)/shard_map/ppermute | solution.py:22
  64.7 2.6 %collective-permute-done.15.rest_4_ = bf16[272,512]{1,0:T(8,128)(2,1)S(1)} collective-permute-done((bf16[272,512]{1,0:T(8,128)(2,1)S(1)}, bf16[272,512]{1,0:T(8,128)(2,1)S(1)}, u32[]{:S(2)}, u32[]{:S(2)}) %collective-permute-start.15) | collective-permute-done | bytes 278560 | tf_op jit(solution)/shard_map/ppermute | solution.py:22
  74.8 2.1 %collective-permute-done.20.rest_6_ = bf16[272,512]{1,0:T(8,128)(2,1)S(1)} collective-permute-done((bf16[272,512]{1,0:T(8,128)(2,1)S(1)}, bf16[272,512]{1,0:T(8,128)(2,1)S(1)}, u32[]{:S(2)}, u32[]{:S(2)}) %collective-permute-start.20) | collective-permute-done | bytes 278560 | tf_op jit(solution)/shard_map/ppermute | solution.py:22
  78.4 4.5 %collective-permute-done.17.rest_5_ = bf16[272,512]{1,0:T(8,128)(2,1)S(1)} collective-permute-done((bf16[272,512]{1,0:T(8,128)(2,1)S(1)}, bf16[272,512]{1,0:T(8,128)(2,1)S(1)}, u32[]{:S(2)}, u32[]{:S(2)}) %collective-permute-start.17) | collective-permute-done | bytes 278560 | tf_op jit(solution)/shard_map/ppermute | solution.py:22
  82.8 4.2 %collective-permute-done.21.rest_7_ = bf16[272,512]{1,0:T(8,128)(2,1)S(1)} collective-permute-done((bf16[272,512]{1,0:T(8,128)(2,1)S(1)}, bf16[272,512]{1,0:T(8,128)(2,1)S(1)}, u32[]{:S(2)}, u32[]{:S(2)}) %collective-permute-start.21) | collective-permute-done | bytes 278560 | tf_op jit(solution)/shard_map/ppermute | solution.py:22
  89.4 2.6 %collective-permute-done.25.other = bf16[256,2048]{1,0:T(8,128)(2,1)S(1)} collective-permute-done((bf16[256,2048]{1,0:T(8,128)(2,1)S(1)}, bf16[256,2048]{1,0:T(8,128)(2,1)S(1)}, u32[]{:S(2)}, u32[]{:S(2)}) %collective-permute-start.25) | collective-permute-done | bytes 1048608 | tf_op jit(solution)/shard_map/ppermute | solution.py:22
  93.0 7.3 %shard_map.110 = (bf16[128,512]{1,0:T(8,128)(2,1)}, bf16[128,512]{1,0:T(8,128)(2,1)}, bf16[128,512]{1,0:T(8,128)(2,1)}, bf16[128,512]{1,0:T(8,128)(2,1)}, bf16[5...) custom-call(s32[9]{0:T(128)} %copy-done.9, bf16[256,2048]{1,0:T(8,128)(2,1)} %copy-done, ...), custom_call_target="tpu_custom_call" | custom-call | flops 2147483648 | bytes 9044004 | tf_op jit(solution)/shard_map/pallas_call | solution.py:36
  100.5 3.8 %shard_map.111 = (f32[4,128,512]{2,1,0:T(8,128)}, bf16[528,512]{1,0:T(8,128)(2,1)}, f32[16,512]{1,0:T(8,128)}) custom-call(s32[9]{0:T(128)} %copy-done.9, bf16[256,2048]{1,0:T(8,128)(2,1)} %copy-done, bf16[256,2048]{1,0:T(8,128)(2,1)} %copy-done.14, bf16[512,512]{1,0:T(8,128)(2,1)} %get-tuple-element.108.grads), custom_call_target="tpu_custom_call" | custom-call | flops 536870912 | bytes 4243492 | tf_op jit(solution)/shard_map/pallas_call | solution.py:36
  110.2 3.6 %shard_map.113 = (f32[4,128,512]{2,1,0:T(8,128)}, bf16[512,512]{1,0:T(8,128)(2,1)}) custom-call(s32[9]{0:T(128)} %copy-done.9, bf16[256,2048]{1,0:T(8,128)(2,1)} %copy-done, bf16[256,2048]{1,0:T(8,128)(2,1)} %copy-done.14, bf16[512,512]{1,0:T(8,128)(2,1)} %get-tuple-element.108.grads), custom_call_target="tpu_custom_call" | custom-call | flops 536870912 | bytes 4194340 | tf_op jit(solution)/shard_map/pallas_call | solution.py:36
  113.9 5.2 %collective-permute-done.28.received = bf16[528,512]{1,0:T(8,128)(2,1)S(1)} collective-permute-done((bf16[528,512]{1,0:T(8,128)(2,1)}, bf16[528,512]{1,0:T(8,128)(2,1)S(1)}, u32[]{:S(2)}, u32[]{:S(2)}) %collective-permute-start.28) | collective-permute-done | bytes 540704 | tf_op jit(solution)/shard_map/ppermute | solution.py:22
  119.6 2.4 %collective-permute-done.30.vxz = bf16[2,128,512]{2,1,0:T(8,128)(2,1)S(1)} collective-permute-done((bf16[2,128,512]{2,1,0:T(8,128)(2,1)S(1)}, bf16[2,128,512]{2,1,0:T(8,128)(2,1)S(1)}, u32[]{:S(2)}, u32[]{:S(2)}) %collective-permute-start.30) | collective-permute-done | bytes 262176 | tf_op jit(solution)/shard_map/ppermute | solution.py:22
  122.6 12.3 %collective-permute-done.35.rest_2_ = bf16[4,128,512]{2,1,0:T(8,128)(2,1)S(1)} collective-permute-done((bf16[4,128,512]{2,1,0:T(8,128)(2,1)S(1)}, bf16[4,128,512]{2,1,0:T(8,128)(2,1)S(1)}, u32[]{:S(2)}, u32[]{:S(2)}) %collective-permute-start.35) | collective-permute-done | bytes 524320 | tf_op jit(solution)/shard_map/ppermute | solution.py:22
  135.0 1.9 %collective-permute-done.37.rest_3_ = bf16[4,128,512]{2,1,0:T(8,128)(2,1)S(1)} collective-permute-done((bf16[4,128,512]{2,1,0:T(8,128)(2,1)S(1)}, bf16[4,128,512]{2,1,0:T(8,128)(2,1)S(1)}, u32[]{:S(2)}, u32[]{:S(2)}) %collective-permute-start.37) | collective-permute-done | bytes 524320 | tf_op jit(solution)/shard_map/ppermute | solution.py:22
  136.9 3.6 %shard_map.117 = bf16[8,128,512]{2,1,0:T(8,128)(2,1)} custom-call(s32[9]{0:T(128)S(1)} %copy-done.11, s32[4,12]{1,0:T(4,128)S(1)} %maximum_convert_fusion.lists, bf16[1552,128]{1,0:T(8,128)(2,1)S(1)} %pad_maximum_fusion.a0, bf16[1552,128]{1,0:T(8,128)(2,1)S(1)} %collective-permute-done.3.a1, bf16[1552,128]{1,0:T(8,128)(2,1)S(1)} %collective-permute-done.4.a2, ...), custom_call_target="tpu_custom_call" | custom-call | flops 805306368 | bytes 4735204 | tf_op jit(solution)/shard_map/pallas_call | solution.py:36
  140.5 4.7 %all-to-all-start = ((bf16[8,128,512]{2,1,0:T(8,128)(2,1)}), bf16[8,128,512]{2,1,0:T(8,128)(2,1)S(1)}, u32[]{:S(2)}, u32[]{:S(2)}) async-start(bf16[8,128,512]{2,1,0:T(8,128)(2,1)} %shard_map.117), calls=%async_computation | async-start | bytes 2097152 | tf_op jit(solution)/shard_map/all_to_all | solution.py:431
  145.7 13.4 %collective-permute-done.38.from_y = bf16[512,512]{1,0:T(8,128)(2,1)S(1)} collective-permute-done((bf16[512,512]{1,0:T(8,128)(2,1)}, bf16[512,512]{1,0:T(8,128)(2,1)S(1)}, u32[]{:S(2)}, u32[]{:S(2)}) %collective-permute-start.38) | collective-permute-done | bytes 524320 | tf_op jit(solution)/shard_map/ppermute | solution.py:22
  162.1 2.4 %collective-permute-start.40 = (bf16[144,512]{1,0:T(8,128)(2,1)S(1)}, bf16[144,512]{1,0:T(8,128)(2,1)S(1)}, u32[]{:S(2)}, u32[]{:S(2)}) collective-permute-start(bf16[144,512]{1,0:T(8,128)(2,1)S(1)} %get-tuple-element.131), channel_id=1, source_target_pairs={{0,16},{1,17},{2,18},{3,19},{4,20},{5,21},{6,22},{7,23},{8,24},{9,... | collective-permute-start | bytes 442376 | tf_op jit(solution)/shard_map/ppermute | solution.py:22
  166.5 4.5 %collective-permute-done.32.a2 = bf16[128,512]{1,0:T(8,128)(2,1)S(1)} collective-permute-done((bf16[128,512]{1,0:T(8,128)(2,1)S(1)}, bf16[128,512]{1,0:T(8,128)(2,1)S(1)}, u32[]{:S(2)}, u32[]{:S(2)}) %collective-permute-start.32) | collective-permute-done | bytes 131104 | tf_op jit(solution)/shard_map/ppermute | solution.py:22
  173.8 4.8 %all-to-all-done.terms = bf16[8,128,512]{2,1,0:T(8,128)(2,1)S(1)} async-done(((bf16[8,128,512]{2,1,0:T(8,128)(2,1)}), bf16[8,128,512]{2,1,0:T(8,128)(2,1)S(1)}, u32[]{:S(2)}, u32[]{:S(2)}) %all-to-all-start) | async-done | bytes 1048608 | tf_op jit(solution)/shard_map/all_to_all | solution.py:431
  179.6 2.2 %collective-permute-done.40.r2 = bf16[144,512]{1,0:T(8,128)(2,1)S(1)} collective-permute-done((bf16[144,512]{1,0:T(8,128)(2,1)S(1)}, bf16[144,512]{1,0:T(8,128)(2,1)S(1)}, u32[]{:S(2)}, u32[]{:S(2)}) %collective-permute-start.40) | collective-permute-done | bytes 147488 | tf_op jit(solution)/shard_map/ppermute | solution.py:22
  181.8 3.0 %collective-permute-done.41.r3 = bf16[144,512]{1,0:T(8,128)(2,1)S(1)} collective-permute-done((bf16[144,512]{1,0:T(8,128)(2,1)S(1)}, bf16[144,512]{1,0:T(8,128)(2,1)S(1)}, u32[]{:S(2)}, u32[]{:S(2)}) %collective-permute-start.41) | collective-permute-done | bytes 147488 | tf_op jit(solution)/shard_map/ppermute | solution.py:22
  (147 shorter events, 56.4 us)
Async XLA Ops:
  5.7 21.0 %collective-permute-start.4 = (bf16[1552,128]{1,0:T(8,128)(2,1)S(1)}, bf16[1552,128]{1,0:T(8,128)(2,1)S(1)}, u32[]{:S(2)}, u32[]{:S(2)}) collective-permute-start(bf16[1552,128]{1,0:T(8,128)(2,1)S(1)} %pad_maximum_fusion.a0), channel_id=1, source_target_pairs={{0,8},{1,9},{2,10},{3,11},{4,12},{5,13},{6,14},{7,15},{8,0},{9,1},... | collective-permute-start | bytes 1191944 | tf_op jit(solution)/shard_map/ppermute | solution.py:22
  8.6 26.2 %collective-permute-start.6 = (bf16[128,2048]{1,0:T(8,128)(2,1)}, bf16[128,2048]{1,0:T(8,128)(2,1)S(1)}, u32[]{:S(2)}, u32[]{:S(2)}) collective-permute-start(bf16[128,2048]{1,0:T(8,128)(2,1)} %bitcast.20), channel_id=1, source_target_pairs={{0,16},{1,17},{2,18},{3,19},{4,20},{5,21},{6,22},{7,23},{8,24},{9,... | collective-permute-start | bytes 1572872 | tf_op jit(solution)/shard_map/ppermute | solution.py:22
  17.3 12.9 %collective-permute-start.3 = (bf16[1552,128]{1,0:T(8,128)(2,1)S(1)}, bf16[1552,128]{1,0:T(8,128)(2,1)S(1)}, u32[]{:S(2)}, u32[]{:S(2)}) collective-permute-start(bf16[1552,128]{1,0:T(8,128)(2,1)S(1)} %pad_maximum_fusion.a0), channel_id=1, source_target_pairs={{0,4},{1,5},{2,6},{3,7},{4,0},{5,1},{6,2},{7,3},{8,12},{9,13},{10,... | collective-permute-start | bytes 1191944 | tf_op jit(solution)/shard_map/ppermute | solution.py:22
  18.5 18.5 %collective-permute-start.8 = (bf16[272,512]{1,0:T(8,128)(2,1)S(1)}, bf16[272,512]{1,0:T(8,128)(2,1)S(1)}, u32[]{:S(2)}, u32[]{:S(2)}) collective-permute-start(bf16[272,512]{1,0:T(8,128)(2,1)S(1)} %shard_map.104.rest_0_), channel_id=1, source_target_pairs={{0,8},{1,9},{2,10},{3,11},{4,12},{5,13},{6,14},{7,15},{8,0},{9,1},... | collective-permute-start | bytes 835592 | tf_op jit(solution)/shard_map/ppermute | solution.py:22
  26.7 13.8 %collective-permute-start.5 = (bf16[1552,128]{1,0:T(8,128)(2,1)S(1)}, bf16[1552,128]{1,0:T(8,128)(2,1)S(1)}, u32[]{:S(2)}, u32[]{:S(2)}) collective-permute-start(bf16[1552,128]{1,0:T(8,128)(2,1)S(1)} %collective-permute-done.4.a2), channel_id=1, source_target_pairs={{0,4},{1,5},{2,6},{3,7},{4,0},{5,1},{6,2},{7,3},{8,12},{9,13},{10,... | collective-permute-start | bytes 1191944 | tf_op jit(solution)/shard_map/ppermute | solution.py:22
  28.7 10.3 %collective-permute-start.7 = (bf16[272,512]{1,0:T(8,128)(2,1)S(1)}, bf16[272,512]{1,0:T(8,128)(2,1)S(1)}, u32[]{:S(2)}, u32[]{:S(2)}) collective-permute-start(bf16[272,512]{1,0:T(8,128)(2,1)S(1)} %shard_map.104.rest_0_), channel_id=1, source_target_pairs={{0,2},{1,3},{2,0},{3,1},{4,6},{5,7},{6,4},{7,5},{8,10},{9,11},{10,... | collective-permute-start | bytes 835592 | tf_op jit(solution)/shard_map/ppermute | solution.py:22
  35.5 8.4 %collective-permute-start.9 = (bf16[2,128,512]{2,1,0:T(8,128)(2,1)S(1)}, bf16[2,128,512]{2,1,0:T(8,128)(2,1)S(1)}, u32[]{:S(2)}, u32[]{:S(2)}) collective-permute-start(bf16[2,128,512]{2,1,0:T(8,128)(2,1)S(1)} %get-tuple-element.81), channel_id=1, source_target_pairs={{0,4},{1,5},{2,6},{3,7},{4,0},{5,1},{6,2},{7,3},{8,12},{9,13},{10,... | collective-permute-start | bytes 786440 | tf_op jit(solution)/shard_map/ppermute | solution.py:22
  37.0 9.2 %collective-permute-start.10 = (bf16[2,128,512]{2,1,0:T(8,128)(2,1)S(1)}, bf16[2,128,512]{2,1,0:T(8,128)(2,1)S(1)}, u32[]{:S(2)}, u32[]{:S(2)}) collective-permute-start(bf16[2,128,512]{2,1,0:T(8,128)(2,1)S(1)} %get-tuple-element.82), channel_id=1, source_target_pairs={{0,8},{1,9},{2,10},{3,11},{4,12},{5,13},{6,14},{7,15},{8,0},{9,1},... | collective-permute-start | bytes 786440 | tf_op jit(solution)/shard_map/ppermute | solution.py:22
  37.0 12.5 %collective-permute-start.11 = (bf16[2,128,512]{2,1,0:T(8,128)(2,1)S(1)}, bf16[2,128,512]{2,1,0:T(8,128)(2,1)S(1)}, u32[]{:S(2)}, u32[]{:S(2)}) collective-permute-start(bf16[2,128,512]{2,1,0:T(8,128)(2,1)S(1)} %get-tuple-element.83), channel_id=1, source_target_pairs={{0,12},{1,13},{2,14},{3,15},{4,8},{5,9},{6,10},{7,11},{8,4},{9,5},... | collective-permute-start | bytes 786440 | tf_op jit(solution)/shard_map/ppermute | solution.py:22
  39.0 12.4 %collective-permute-start.12 = (bf16[272,512]{1,0:T(8,128)(2,1)S(1)}, bf16[272,512]{1,0:T(8,128)(2,1)S(1)}, u32[]{:S(2)}, u32[]{:S(2)}) collective-permute-start(bf16[272,512]{1,0:T(8,128)(2,1)S(1)} %collective-permute-done.8.rest_2_), channel_id=1, source_target_pairs={{0,2},{1,3},{2,0},{3,1},{4,6},{5,7},{6,4},{7,5},{8,10},{9,11},{10,... | collective-permute-start | bytes 835592 | tf_op jit(solution)/shard_map/ppermute | solution.py:22
  51.5 15.8 %collective-permute-start.15 = (bf16[272,512]{1,0:T(8,128)(2,1)S(1)}, bf16[272,512]{1,0:T(8,128)(2,1)S(1)}, u32[]{:S(2)}, u32[]{:S(2)}) collective-permute-start(bf16[272,512]{1,0:T(8,128)(2,1)S(1)} %shard_map.104.rest_0_), channel_id=1, source_target_pairs={{0,16},{1,17},{2,18},{3,19},{4,20},{5,21},{6,22},{7,23},{8,24},{9,... | collective-permute-start | bytes 835592 | tf_op jit(solution)/shard_map/ppermute | solution.py:22
  55.0 14.0 %collective-permute-start.14 = (bf16[4,128,512]{2,1,0:T(8,128)(2,1)S(1)}, bf16[4,128,512]{2,1,0:T(8,128)(2,1)S(1)}, u32[]{:S(2)}, u32[]{:S(2)}) collective-permute-start(bf16[4,128,512]{2,1,0:T(8,128)(2,1)S(1)} %get-tuple-element.88), channel_id=1, source_target_pairs={{0,2},{1,3},{2,0},{3,1},{4,6},{5,7},{6,4},{7,5},{8,10},{9,11},{10,... | collective-permute-start | bytes 1572872 | tf_op jit(solution)/shard_map/ppermute | solution.py:22
  67.3 9.5 %collective-permute-start.20 = (bf16[272,512]{1,0:T(8,128)(2,1)S(1)}, bf16[272,512]{1,0:T(8,128)(2,1)S(1)}, u32[]{:S(2)}, u32[]{:S(2)}) collective-permute-start(bf16[272,512]{1,0:T(8,128)(2,1)S(1)} %collective-permute-done.15.rest_4_), channel_id=1, source_target_pairs={{0,8},{1,9},{2,10},{3,11},{4,12},{5,13},{6,14},{7,15},{8,0},{9,1},... | collective-permute-start | bytes 835592 | tf_op jit(solution)/shard_map/ppermute | solution.py:22
  69.7 17.4 %collective-permute-start.22 = (bf16[288,512]{1,0:T(8,128)(2,1)S(1)}, bf16[288,512]{1,0:T(8,128)(2,1)S(1)}, u32[]{:S(2)}, u32[]{:S(2)}) collective-permute-start(bf16[288,512]{1,0:T(8,128)(2,1)S(1)} %get-tuple-element.96.own), channel_id=1, source_target_pairs={{0,4},{1,5},{2,6},{3,7},{4,0},{5,1},{6,2},{7,3},{8,12},{9,13},{10,... | collective-permute-start | bytes 884744 | tf_op jit(solution)/shard_map/ppermute | solution.py:22
  71.2 15.8 %collective-permute-start.24 = (bf16[288,512]{1,0:T(8,128)(2,1)S(1)}, bf16[288,512]{1,0:T(8,128)(2,1)S(1)}, u32[]{:S(2)}, u32[]{:S(2)}) collective-permute-start(bf16[288,512]{1,0:T(8,128)(2,1)S(1)} %get-tuple-element.97), channel_id=1, source_target_pairs={{0,12},{1,13},{2,14},{3,15},{4,8},{5,9},{6,10},{7,11},{8,4},{9,5},... | collective-permute-start | bytes 884744 | tf_op jit(solution)/shard_map/ppermute | solution.py:22
  72.9 15.7 %collective-permute-start.23 = (bf16[288,512]{1,0:T(8,128)(2,1)S(1)}, bf16[288,512]{1,0:T(8,128)(2,1)S(1)}, u32[]{:S(2)}, u32[]{:S(2)}) collective-permute-start(bf16[288,512]{1,0:T(8,128)(2,1)S(1)} %get-tuple-element.97), channel_id=1, source_target_pairs={{0,8},{1,9},{2,10},{3,11},{4,12},{5,13},{6,14},{7,15},{8,0},{9,1},... | collective-permute-start | bytes 884744 | tf_op jit(solution)/shard_map/ppermute | solution.py:22
  73.2 9.6 %collective-permute-start.17 = (bf16[272,512]{1,0:T(8,128)(2,1)S(1)}, bf16[272,512]{1,0:T(8,128)(2,1)S(1)}, u32[]{:S(2)}, u32[]{:S(2)}) collective-permute-start(bf16[272,512]{1,0:T(8,128)(2,1)S(1)} %collective-permute-done.15.rest_4_), channel_id=1, source_target_pairs={{0,2},{1,3},{2,0},{3,1},{4,6},{5,7},{6,4},{7,5},{8,10},{9,11},{10,... | collective-permute-start | bytes 835592 | tf_op jit(solution)/shard_map/ppermute | solution.py:22
  76.8 10.2 %collective-permute-start.21 = (bf16[272,512]{1,0:T(8,128)(2,1)S(1)}, bf16[272,512]{1,0:T(8,128)(2,1)S(1)}, u32[]{:S(2)}, u32[]{:S(2)}) collective-permute-start(bf16[272,512]{1,0:T(8,128)(2,1)S(1)} %collective-permute-done.20.rest_6_), channel_id=1, source_target_pairs={{0,2},{1,3},{2,0},{3,1},{4,6},{5,7},{6,4},{7,5},{8,10},{9,11},{10,... | collective-permute-start | bytes 835592 | tf_op jit(solution)/shard_map/ppermute | solution.py:22
  104.3 14.8 %collective-permute-start.28 = (bf16[528,512]{1,0:T(8,128)(2,1)}, bf16[528,512]{1,0:T(8,128)(2,1)S(1)}, u32[]{:S(2)}, u32[]{:S(2)}) collective-permute-start(bf16[528,512]{1,0:T(8,128)(2,1)} %get-tuple-element.104), channel_id=1, source_target_pairs={{0,2},{1,3},{2,0},{3,1},{4,6},{5,7},{6,4},{7,5},{8,10},{9,11},{10,... | collective-permute-start | bytes 1622024 | tf_op jit(solution)/shard_map/ppermute | solution.py:22
  106.7 12.4 %collective-permute-start.27 = (bf16[2,128,512]{2,1,0:T(8,128)(2,1)S(1)}, bf16[2,128,512]{2,1,0:T(8,128)(2,1)S(1)}, u32[]{:S(2)}, u32[]{:S(2)}) collective-permute-start(bf16[2,128,512]{2,1,0:T(8,128)(2,1)S(1)} %get-tuple-element.107), channel_id=1, source_target_pairs={{0,4},{1,5},{2,6},{3,7},{4,0},{5,1},{6,2},{7,3},{8,12},{9,13},{10,... | collective-permute-start | bytes 786440 | tf_op jit(solution)/shard_map/ppermute | solution.py:22
  108.3 11.3 %collective-permute-start.29 = (bf16[2,128,512]{2,1,0:T(8,128)(2,1)S(1)}, bf16[2,128,512]{2,1,0:T(8,128)(2,1)S(1)}, u32[]{:S(2)}, u32[]{:S(2)}) collective-permute-start(bf16[2,128,512]{2,1,0:T(8,128)(2,1)S(1)} %get-tuple-element.111), channel_id=1, source_target_pairs={{0,8},{1,9},{2,10},{3,11},{4,12},{5,13},{6,14},{7,15},{8,0},{9,1},... | collective-permute-start | bytes 786440 | tf_op jit(solution)/shard_map/ppermute | solution.py:22
  108.5 13.4 %collective-permute-start.30 = (bf16[2,128,512]{2,1,0:T(8,128)(2,1)S(1)}, bf16[2,128,512]{2,1,0:T(8,128)(2,1)S(1)}, u32[]{:S(2)}, u32[]{:S(2)}) collective-permute-start(bf16[2,128,512]{2,1,0:T(8,128)(2,1)S(1)} %get-tuple-element.112), channel_id=1, source_target_pairs={{0,12},{1,13},{2,14},{3,15},{4,8},{5,9},{6,10},{7,11},{8,4},{9,5},... | collective-permute-start | bytes 786440 | tf_op jit(solution)/shard_map/ppermute | solution.py:22
  119.3 15.7 %collective-permute-start.36 = (bf16[528,512]{1,0:T(8,128)(2,1)S(1)}, bf16[528,512]{1,0:T(8,128)(2,1)S(1)}, u32[]{:S(2)}, u32[]{:S(2)}) collective-permute-start(bf16[528,512]{1,0:T(8,128)(2,1)S(1)} %get-tuple-element.121), channel_id=1, source_target_pairs={{0,8},{1,9},{2,10},{3,11},{4,12},{5,13},{6,14},{7,15},{8,0},{9,1},... | collective-permute-start | bytes 1622024 | tf_op jit(solution)/shard_map/ppermute | solution.py:22
  122.1 12.9 %collective-permute-start.35 = (bf16[4,128,512]{2,1,0:T(8,128)(2,1)S(1)}, bf16[4,128,512]{2,1,0:T(8,128)(2,1)S(1)}, u32[]{:S(2)}, u32[]{:S(2)}) collective-permute-start(bf16[4,128,512]{2,1,0:T(8,128)(2,1)S(1)} %shard_map.114.rest_0_), channel_id=1, source_target_pairs={{0,2},{1,3},{2,0},{3,1},{4,6},{5,7},{6,4},{7,5},{8,10},{9,11},{10,... | collective-permute-start | bytes 1572872 | tf_op jit(solution)/shard_map/ppermute | solution.py:22
  122.6 12.4 %collective-permute-start.34 = (bf16[4,128,512]{2,1,0:T(8,128)(2,1)S(1)}, bf16[4,128,512]{2,1,0:T(8,128)(2,1)S(1)}, u32[]{:S(2)}, u32[]{:S(2)}) collective-permute-start(bf16[4,128,512]{2,1,0:T(8,128)(2,1)S(1)} %shard_map.114.rest_0_), channel_id=1, source_target_pairs={{0,1},{1,0},{2,3},{3,2},{4,5},{5,4},{6,7},{7,6},{8,9},{9,8},{10,11... | collective-permute-start | bytes 1572872 | tf_op jit(solution)/shard_map/ppermute | solution.py:22
  140.5 38.2 %all-to-all-start = ((bf16[8,128,512]{2,1,0:T(8,128)(2,1)}), bf16[8,128,512]{2,1,0:T(8,128)(2,1)S(1)}, u32[]{:S(2)}, u32[]{:S(2)}) async-start(bf16[8,128,512]{2,1,0:T(8,128)(2,1)} %shard_map.117), calls=%async_computation | async-start | bytes 2097152 | tf_op jit(solution)/shard_map/all_to_all | solution.py:431
  145.2 14.0 %collective-permute-start.38 = (bf16[512,512]{1,0:T(8,128)(2,1)}, bf16[512,512]{1,0:T(8,128)(2,1)S(1)}, u32[]{:S(2)}, u32[]{:S(2)}) collective-permute-start(bf16[512,512]{1,0:T(8,128)(2,1)} %get-tuple-element.126), channel_id=1, source_target_pairs={{0,2},{1,3},{2,0},{3,1},{4,6},{5,7},{6,4},{7,5},{8,10},{9,11},{10,... | collective-permute-start | bytes 1572872 | tf_op jit(solution)/shard_map/ppermute | solution.py:22
  145.7 20.8 %collective-permute-start.31 = (bf16[128,512]{1,0:T(8,128)(2,1)}, bf16[128,512]{1,0:T(8,128)(2,1)S(1)}, u32[]{:S(2)}, u32[]{:S(2)}) collective-permute-start(bf16[128,512]{1,0:T(8,128)(2,1)} %get-tuple-element.113), channel_id=1, source_target_pairs={{0,1},{1,0},{2,3},{3,2},{4,5},{5,4},{6,7},{7,6},{8,9},{9,8},{10,11... | collective-permute-start | bytes 393224 | tf_op jit(solution)/shard_map/ppermute | solution.py:22
  160.5 19.1 %collective-permute-start.39 = (bf16[144,512]{1,0:T(8,128)(2,1)}, bf16[144,512]{1,0:T(8,128)(2,1)S(1)}, u32[]{:S(2)}, u32[]{:S(2)}) collective-permute-start(bf16[144,512]{1,0:T(8,128)(2,1)} %get-tuple-element.130), channel_id=1, source_target_pairs={{0,4},{1,5},{2,6},{3,7},{4,0},{5,1},{6,2},{7,3},{8,12},{9,13},{10,... | collective-permute-start | bytes 442376 | tf_op jit(solution)/shard_map/ppermute | solution.py:22
  162.1 19.7 %collective-permute-start.40 = (bf16[144,512]{1,0:T(8,128)(2,1)S(1)}, bf16[144,512]{1,0:T(8,128)(2,1)S(1)}, u32[]{:S(2)}, u32[]{:S(2)}) collective-permute-start(bf16[144,512]{1,0:T(8,128)(2,1)S(1)} %get-tuple-element.131), channel_id=1, source_target_pairs={{0,16},{1,17},{2,18},{3,19},{4,20},{5,21},{6,22},{7,23},{8,24},{9,... | collective-permute-start | bytes 442376 | tf_op jit(solution)/shard_map/ppermute | solution.py:22
  164.5 20.3 %collective-permute-start.41 = (bf16[144,512]{1,0:T(8,128)(2,1)S(1)}, bf16[144,512]{1,0:T(8,128)(2,1)S(1)}, u32[]{:S(2)}, u32[]{:S(2)}) collective-permute-start(bf16[144,512]{1,0:T(8,128)(2,1)S(1)} %get-tuple-element.132), channel_id=1, source_target_pairs={{0,20},{1,21},{2,22},{3,23},{4,16},{5,17},{6,18},{7,19},{8,28},{9,... | collective-permute-start | bytes 442376 | tf_op jit(solution)/shard_map/ppermute | solution.py:22
  164.9 6.1 %collective-permute-start.32 = (bf16[128,512]{1,0:T(8,128)(2,1)S(1)}, bf16[128,512]{1,0:T(8,128)(2,1)S(1)}, u32[]{:S(2)}, u32[]{:S(2)}) collective-permute-start(bf16[128,512]{1,0:T(8,128)(2,1)S(1)} %copy-done.23), channel_id=1, source_target_pairs={{0,4},{1,5},{2,6},{3,7},{4,0},{5,1},{6,2},{7,3},{8,12},{9,13},{10,... | collective-permute-start | bytes 393224 | tf_op jit(solution)/shard_map/ppermute | solution.py:22
  (40 other events, 566.3 us)

commit v4 on v3

--- a/solution.py
+++ b/solution.py
@@ -44,11 +44,18 @@
     )(*operands)
 
 
-def split_kernel(ids, value, row, *pieces):
+def split_kernel(ids, value, bias, *pieces):
     part = pieces[0].shape[-1]
+    many = bias.shape[1]
+    own, none = bias[...].astype(F32), jnp.zeros(bias.shape, F32)
+    row = jnp.where(
+        ids[1] == 0, jnp.concatenate([own, none], axis=1), jnp.concatenate([none, own], axis=1)
+    )
+    at = pl.ds(pl.multiple_of((ids[5] * 2 + ids[2]) * (2 * many), 2 * many), 2 * many)
     for i, piece in enumerate(pieces):
         piece[:-ROWS] = value[:, pl.ds(pl.multiple_of((ids[7] ^ i) * part, part), part)]
-        piece[-ROWS:] = row[...]
+        piece[-ROWS:] = jnp.zeros((ROWS, part), BF16)
+        piece[-ROWS:, at] = jnp.broadcast_to(row, (ROWS, 2 * many)).astype(BF16)
 
 
 def split_masked_kernel(ids, mask, value, *pieces):
@@ -63,7 +70,8 @@
 def block_kernel(ids, p0, p1, p2, p3, block):
     rows = p0.shape[0] - ROWS
     for i, piece in enumerate((p0, p1, p2, p3)):
-        block[pl.ds(pl.multiple_of((ids[7] ^ i) * rows, rows), rows), :] = piece[:rows]
+        at = (i >> 1) * 2 + (ids[1] ^ (i & 1))
+        block[pl.ds(pl.multiple_of(at * rows, rows), rows), :] = piece[:rows]
     block[4 * rows :] = p0[rows:] + p1[rows:] + p2[rows:] + p3[rows:]
 
 
@@ -122,26 +130,20 @@
         out[2 * nodes :, :] = jnp.zeros((out.shape[0] - 2 * nodes, out.shape[1]), BF16)
 
 
-def aggregate_kernel(ids, own, rx, rz, rxz, full):
-    member = ids[0]
-    nodes, part, half = full.shape[0] // 2, own.shape[1] // 2, full.shape[1] // 2
-    for i, term in enumerate((own, rx, rz, rxz)):
-        for j in range(2):
-            cols = pl.ds(pl.multiple_of(j * half + (member ^ i) * part, part), part)
-            for x in range(2):
-                full[x * nodes : (x + 1) * nodes, cols] = term[x * nodes : (x + 1) * nodes, j * part : (j + 1) * part]
-
-
-def dense_kernel(ids, own, other, o0, o1, o2, o3, *rest):
+def dense_kernel(ids, p0, p1, p2, p3, q0, q1, q2, q3, o0, o1, o2, o3, *rest):
     weights = rest[:8]
-    a0, a1, a2, a3, pre_grad, back_own, back_other, left, grads, acts = rest[8:]
-    y, z, x = ids[2], ids[3], ids[5]
-    pair, width = own.shape
-    nodes, block = pair // 2, width // 16
+    a0, a1, a2, a3, pre_grad, b0, b1, b2, b3, back_other, left, grads, acts = rest[8:]
+    back_own = (b0, b1, b2, b3)
+    y, high, z, x = ids[2], ids[4], ids[3], ids[5]
     part = pre_grad.shape[1]
-
-    def chip(i, other_x):
-        return pl.multiple_of(((z ^ (i >> 1)) * 4 + other_x * 2 + (y ^ (i & 1))) * block, block)
+    pair, block = b0.shape[0], part // 4
+    nodes = pair // 2
+
+    def lanes(i):
+        return pl.ds(pl.multiple_of(((high ^ (i >> 2)) * 2 + (y ^ (i & 1))) * block, block), block)
+
+    def quarter(i, j):
+        return (i & 2) + j
 
     def place(i):
         return pl.ds(pl.multiple_of((i & 1) * pair + (x ^ (i >> 1)) * nodes, nodes), nodes)
@@ -149,8 +151,8 @@
     for i in range(8):
         for j in range(2):
             cols = slice((2 * i + j) * block, (2 * i + j + 1) * block)
-            left[:pair, cols] = own[:, pl.ds(chip(i, j), block)]
-            left[pair:, cols] = other[:, pl.ds(chip(i, j), block)]
+            left[:pair, cols] = (p0, p1, p2, p3)[quarter(i, j)][:pair, lanes(i)]
+            left[pair:, cols] = (q0, q1, q2, q3)[quarter(i, j)][:pair, lanes(i)]
     for i, piece in enumerate((o0, o1, o2, o3)):
         grads[place(i), :] = piece[...]
     many = 2 * block
@@ -165,8 +167,7 @@
         sigmoid = 1.0 / (1.0 + jnp.exp(-pre))
         acts[:, cols] = (pre * sigmoid).astype(BF16)
         slope = sigmoid * (1.0 + pre * (1.0 - sigmoid))
-        grad = (grads[:, cols].astype(F32) * slope).astype(BF16)
-        pre_grad[:, cols] = grad
+        pre_grad[:, cols] = (grads[:, cols].astype(F32) * slope).astype(BF16)
     for i, piece in enumerate((a0, a1, a2, a3)):
         piece[...] = acts[place(i), :]
     for i, weight in enumerate(weights):
@@ -174,26 +175,25 @@
             pre_grad[...], weight[:many, :], (((1,), (1,)), ((), ())), preferred_element_type=F32
         )
         for j in range(2):
-            cols = pl.ds(chip(i, j), block)
-            back_own[:, cols] = back[:pair, j * block : (j + 1) * block]
-            back_other[:, cols] = back[pair:, j * block : (j + 1) * block].astype(BF16)
-
-
-def back_kernel(ids, own, received, v0, v1, v2, v3):
-    member = ids[0]
-    nodes, part, half = v0.shape[1], v0.shape[2] // 2, own.shape[1] // 2
-    for i, out in enumerate((v0, v1, v2, v3)):
-        for j in range(2):
-            cols = pl.ds(pl.multiple_of(j * half + (member ^ i) * part, part), part)
-            for x in range(2):
-                rows = slice(x * nodes, (x + 1) * nodes)
-                total = own[rows, cols] + received[rows, cols].astype(F32)
-                out[x, :, j * part : (j + 1) * part] = total.astype(out.dtype)
-
-
-def add_kernel(v0, vx, vz, vxz, out):
-    out[:2] = (v0[...] + vx[...].astype(F32)).astype(BF16)
-    out[2:] = (vz[...].astype(F32) + vxz[...].astype(F32)).astype(BF16)
+            cols = slice(j * block, (j + 1) * block)
+            back_own[quarter(i, j)][:, lanes(i)] = back[:pair, cols]
+            back_other[quarter(i, j), :, lanes(i)] = back[pair:, cols].astype(BF16)
+
+
+def back_kernel(b1, b2, b3, received, v1, v2, v3):
+    nodes = v1.shape[1]
+    for i, (own, out) in enumerate(((b1, v1), (b2, v2), (b3, v3))):
+        for x in range(2):
+            rows = slice(x * nodes, (x + 1) * nodes)
+            out[x] = (own[rows, :] + received[i + 1, rows, :].astype(F32)).astype(BF16)
+
+
+def add_kernel(own, received, vx, vz, vxz, out):
+    nodes = vx.shape[1]
+    for x in range(2):
+        rows = slice(x * nodes, (x + 1) * nodes)
+        out[x] = (own[rows, :] + received[0, rows, :].astype(F32) + vx[x].astype(F32)).astype(BF16)
+        out[2 + x] = (vz[x].astype(F32) + vxz[x].astype(F32)).astype(BF16)
 
 
 def spread_kernel(ids, lists, a0, a1, a2, a3, *rest):
@@ -235,20 +235,20 @@
             out[:, pl.ds(start + j * lanes, lanes)] = piece[:, j * lanes : (j + 1) * lanes] * mask[...]
 
 
-def weight_grad_kernel(far, ids, own, other, grads, keep, send, *rest):
-    y, low = ids[2], ids[6]
+def weight_grad_kernel(far, ids, own0, own1, other0, other1, grads, keep, send, *rest):
+    y, x = ids[2], ids[5]
     block = keep.shape[1]
     row, total = rest if far else (None,) + rest
-    z = 1 - low if far else low
-    for j in range(2):
-        cols = pl.ds(pl.multiple_of((j * 8 + z * 4) * block, block), 4 * block)
+    pair = grads.shape[0] // 2
+    for j, (own, other) in enumerate(((own0, other0), (own1, other1))):
         total[4 * j * block : 4 * (j + 1) * block, :] = lax.dot_general(
-            jnp.concatenate([own[:, cols], other[:, cols]], axis=0), grads[...],
+            jnp.concatenate([own[:pair, :], other[:pair, :]], axis=0), grads[...],
             (((0,), (0,)), ((), ())), preferred_element_type=F32,
         )
     for i in range(4):
-        keep[i] = total[pl.ds(pl.multiple_of((2 * i + y) * block, block), block), :]
-        value = total[pl.ds(pl.multiple_of((2 * i + 1 - y) * block, block), block), :]
+        at = ((i & 1) ^ x) * 4 + (i >> 1) * 2
+        keep[i] = total[pl.ds(pl.multiple_of((at + y) * block, block), block), :]
+        value = total[pl.ds(pl.multiple_of((at + 1 - y) * block, block), block), :]
         send[i * block : (i + 1) * block, :] = value.astype(BF16)
     if far:
         sums = jnp.sum(grads[...].astype(F32), axis=0, keepdims=True)
@@ -333,9 +333,7 @@
     shares = (CORE, X, X | CORE)
 
     own_rows = weight.shape[0]
-    at = (r & 1) * (quarter // 2) + c * own_rows
-    row = lax.dynamic_update_slice(jnp.zeros((ROWS, quarter), BF16), bias[None], (0, at))
-    pieces = call(split_kernel, [shape((own_rows + ROWS, quarter), BF16)] * 4, ids, weight, row)
+    pieces = call(split_kernel, [shape((own_rows + ROWS, quarter), BF16)] * 4, ids, weight, bias[None])
     pieces = [pieces[0]] + [swap(p, m) for p, m in zip(pieces[1:], shares)]
     (block,) = call(block_kernel, [shape((4 * own_rows + ROWS, quarter), BF16)], ids, *pieces)
 
@@ -374,42 +372,40 @@
     )
     received = after(swap(send, Y), y1, z2, grads[1])
     near, far = call(group_kernel, [shape((2 * tile + 2 * ROWS, quarter), BF16)] * 2, ids, mine, received)
-    (aggregate,) = call(
-        aggregate_kernel, [shape((2 * nodes, width), BF16)],
-        ids, after(near, y2, y3), swap(near, X), swap(far, Z), swap(far, X | Z),
-    )
-    aggregate_other = swap(aggregate, CORE)
-
-    *acts, pre_grad, back_own, back_other = call(
+    near = [near, swap(near, X), swap(far, Z), swap(far, X | Z)]
+    near[2] = after(near[2], y2, y3)
+    other = [swap(value, CORE) for value in near]
+
+    *acts, pre_grad, b0, b1, b2, b3, back_other = call(
         dense_kernel,
         [shape((nodes, quarter), BF16)] * 4
         + [shape((4 * nodes, quarter), BF16)]
-        + [shape((2 * nodes, width), F32), shape((2 * nodes, width), BF16)],
-        ids, aggregate, aggregate_other, *grads, *weights,
+        + [shape((2 * nodes, quarter), F32)] * 4 + [shape((4, 2 * nodes, quarter), BF16)],
+        ids, *near, *other, *grads, *weights,
         scratch=[pltpu.VMEM((4 * nodes, width), BF16)] + [pltpu.VMEM((4 * nodes, quarter), BF16)] * 2,
-        flops=16 * nodes * quarter * width, vmem=56,
+        flops=16 * nodes * quarter * width, vmem=40,
     )
 
     far, send_far, row = call(
         functools.partial(weight_grad_kernel, True),
         [shape((4, tile, quarter), F32), shape((4 * tile + ROWS, quarter), BF16), shape((ROWS, quarter), F32)],
-        ids, aggregate, aggregate_other, pre_grad,
-        scratch=[pltpu.VMEM((half, quarter), F32)], flops=4 * nodes * quarter * width, vmem=56,
-    )
-    v0, *others = call(
-        back_kernel, [shape((2, nodes, quarter), F32)] + [shape((2, nodes, quarter), BF16)] * 3,
-        ids, back_own, after(swap(back_other, CORE), send_far),
+        ids, *near[2:], *other[2:], pre_grad,
+        scratch=[pltpu.VMEM((half, quarter), F32)], flops=4 * nodes * quarter * width, vmem=28,
+    )
+    received = after(swap(back_other, CORE), send_far)
+    others = call(
+        back_kernel, [shape((2, nodes, quarter), BF16)] * 3, b1, b2, b3, received, smem=0
     )
     vx, vz, vxz = [swap(v, m) for v, m in zip(others, masks)]
     from_y = swap(send_far, Y)
-    near, send_near = call(
+    kept_near, send_near = call(
         functools.partial(weight_grad_kernel, False),
         [shape((4, tile, quarter), F32), shape((4 * tile, quarter), BF16)],
-        ids, aggregate, aggregate_other, after(pre_grad, v0),
-        scratch=[pltpu.VMEM((half, quarter), F32)], flops=4 * nodes * quarter * width, vmem=56,
-    )
-    vx, from_y, near = lax.optimization_barrier((vx, from_y, near))
-    grads_own = call(add_kernel, [shape((4, nodes, quarter), BF16)], v0, vx, vz, vxz, smem=0)[0]
+        ids, *near[:2], *other[:2], after(pre_grad, others[0]),
+        scratch=[pltpu.VMEM((half, quarter), F32)], flops=4 * nodes * quarter * width, vmem=28,
+    )
+    vx, from_y, kept_near = lax.optimization_barrier((vx, from_y, kept_near))
+    grads_own = call(add_kernel, [shape((4, nodes, quarter), BF16)], b0, received, vx, vz, vxz, smem=0)[0]
     grads_away = swap(grads_own, Y)
     send, row = call(
         fold_y_kernel, [shape((4 * tile + ROWS, quarter), BF16), shape((ROWS, quarter), F32)],
@@ -432,7 +428,7 @@
     own, row, *send = call(
         fold_low_kernel,
         [shape((tile, quarter), F32), shape((ROWS, quarter), F32)] + [shape((tile + ROWS, quarter), BF16)] * 3,
-        ids, near, row, from_y, from_z,
+        ids, kept_near, row, from_y, from_z,
     )
     received = [swap(s, m) for s, m in zip(send, (X, 2 * Z, 2 * Z | X))]
     (input_grad,) = call(finish_kernel, [shape((nodes, width), BF16)], spread_all, smem=0)

time: 189 us -> 180 us (0.952)
  Pallas kernels: 31.5 us -> 22.4 us
    pallas_call x20 -> x19, Pallas kernels: 31.5 us -> 22.4 us  [call(): pl.pallas_call(kernel, out_shape=outs, in_specs=[SMEM] * smem + [VMEM] *...]
    ppermute x43 -> x46, starting transfers between devices: 41.4 us -> 42.9 us  [swap(): return lax.ppermute(value, BOTH, [(i, i ^ mask) for i in range(total)])]
    ppermute x43 -> x46, waiting for transfers between devices: 100 us -> 101 us  [swap(): return lax.ppermute(value, BOTH, [(i, i ^ mask) for i in range(total)])]
  transfers between devices with their start and end apart: 44 -> 47, of which waited for: 29 -> 30; matrix products, arithmetic and copies ran while one was open for 1% -> 1% of each run, Pallas kernels for 9% -> 7%
where the time goes in v4:
time: 180 us
  waiting for transfers between devices  106 us (59%)
  starting transfers between devices  46.6 us (26%)
  Pallas kernels  22.4 us (12%)
  local copies, waits for them, and re-layouts  2.08 us (1%)
    ppermute x46, waiting for transfers between devices, swap(): return lax.ppermute(value, BOTH, [(i, i ^ mask) for i in range(total)])  101 us
    ppermute x46, starting transfers between devices, swap(): return lax.ppermute(value, BOTH, [(i, i ^ mask) for i in range(total)])  42.9 us
    pallas_call x19, Pallas kernels, call(): pl.pallas_call(kernel, out_shape=outs, in_specs=[SMEM] * smem + [VMEM] *...  22.4 us
    all_to_all x1, waiting for transfers between devices, chip_body(): spread_all = lax.all_to_all(spread, 'row', 0, 0, tiled=True)  4.65 us
    all_to_all x1, starting transfers between devices, chip_body(): spread_all = lax.all_to_all(spread, 'row', 0, 0, tiled=True)  3.66 us
  transfers between devices with their start and end apart: 47, of which 30 were waited for; matrix products, arithmetic and copies ran while one was open for 1% of the time, Pallas kernels for 7%

profile of v4, /device:TPU:0, one launch (start us, length us, event | category | flops | bytes accessed | tf_op | source)
XLA Modules:
  0.0 179.6 jit_solution(8728350487462770860)
XLA Ops:
  5.4 3.0 %collective-permute-start.4 = (bf16[1552,128]{1,0:T(8,128)(2,1)S(1)}, bf16[1552,128]{1,0:T(8,128)(2,1)S(1)}, u32[]{:S(2)}, u32[]{:S(2)}) collective-permute-start(bf16[1552,128]{1,0:T(8,128)(2,1)S(1)} %pad_maximum_fusion.a0), channel_id=1, source_target_pairs={{0,8},{1,9},{2,10},{3,11},{4,12},{5,13},{6,14},{7,15},{8,0},{9,1},... | collective-permute-start | bytes 1191944 | tf_op jit(solution)/shard_map/ppermute | solution.py:22
  8.4 2.6 %collective-permute-start.6 = (bf16[128,2048]{1,0:T(8,128)(2,1)}, bf16[128,2048]{1,0:T(8,128)(2,1)S(1)}, u32[]{:S(2)}, u32[]{:S(2)}) collective-permute-start(bf16[128,2048]{1,0:T(8,128)(2,1)} %bitcast.20), channel_id=1, source_target_pairs={{0,16},{1,17},{2,18},{3,19},{4,20},{5,21},{6,22},{7,23},{8,24},{9,... | collective-permute-start | bytes 1572872 | tf_op jit(solution)/shard_map/ppermute | solution.py:22
  12.5 2.9 %collective-permute-done.1.p2 = bf16[80,512]{1,0:T(8,128)(2,1)S(1)} collective-permute-done((bf16[80,512]{1,0:T(8,128)(2,1)S(1)}, bf16[80,512]{1,0:T(8,128)(2,1)S(1)}, u32[]{:S(2)}, u32[]{:S(2)}) %collective-permute-start.1) | collective-permute-done | bytes 81952 | tf_op jit(solution)/shard_map/ppermute | solution.py:22
  18.9 7.7 %collective-permute-done.4.a2 = bf16[1552,128]{1,0:T(8,128)(2,1)S(1)} collective-permute-done((bf16[1552,128]{1,0:T(8,128)(2,1)S(1)}, bf16[1552,128]{1,0:T(8,128)(2,1)S(1)}, u32[]{:S(2)}, u32[]{:S(2)}) %collective-permute-start.4) | collective-permute-done | bytes 397344 | tf_op jit(solution)/shard_map/ppermute | solution.py:22
  26.6 2.0 %collective-permute-start.5 = (bf16[1552,128]{1,0:T(8,128)(2,1)S(1)}, bf16[1552,128]{1,0:T(8,128)(2,1)S(1)}, u32[]{:S(2)}, u32[]{:S(2)}) collective-permute-start(bf16[1552,128]{1,0:T(8,128)(2,1)S(1)} %collective-permute-done.4.a2), channel_id=1, source_target_pairs={{0,4},{1,5},{2,6},{3,7},{4,0},{5,1},{6,2},{7,3},{8,12},{9,13},{10,... | collective-permute-start | bytes 1191944 | tf_op jit(solution)/shard_map/ppermute | solution.py:22
  30.1 4.5 %collective-permute-done.6.far = bf16[128,2048]{1,0:T(8,128)(2,1)S(1)} collective-permute-done((bf16[128,2048]{1,0:T(8,128)(2,1)}, bf16[128,2048]{1,0:T(8,128)(2,1)S(1)}, u32[]{:S(2)}, u32[]{:S(2)}) %collective-permute-start.6) | collective-permute-done | bytes 524320 | tf_op jit(solution)/shard_map/ppermute | solution.py:22
  36.9 2.0 %collective-permute-start.11 = (bf16[2,128,512]{2,1,0:T(8,128)(2,1)S(1)}, bf16[2,128,512]{2,1,0:T(8,128)(2,1)S(1)}, u32[]{:S(2)}, u32[]{:S(2)}) collective-permute-start(bf16[2,128,512]{2,1,0:T(8,128)(2,1)S(1)} %get-tuple-element.85), channel_id=1, source_target_pairs={{0,12},{1,13},{2,14},{3,15},{4,8},{5,9},{6,10},{7,11},{8,4},{9,5},... | collective-permute-start | bytes 786440 | tf_op jit(solution)/shard_map/ppermute | solution.py:22
  40.4 3.3 %collective-permute-done.9.h1 = bf16[2,128,512]{2,1,0:T(8,128)(2,1)S(1)} collective-permute-done((bf16[2,128,512]{2,1,0:T(8,128)(2,1)S(1)}, bf16[2,128,512]{2,1,0:T(8,128)(2,1)S(1)}, u32[]{:S(2)}, u32[]{:S(2)}) %collective-permute-start.9) | collective-permute-done | bytes 262176 | tf_op jit(solution)/shard_map/ppermute | solution.py:22
  43.7 2.4 %collective-permute-done.10.h2 = bf16[2,128,512]{2,1,0:T(8,128)(2,1)S(1)} collective-permute-done((bf16[2,128,512]{2,1,0:T(8,128)(2,1)S(1)}, bf16[2,128,512]{2,1,0:T(8,128)(2,1)S(1)}, u32[]{:S(2)}, u32[]{:S(2)}) %collective-permute-start.10) | collective-permute-done | bytes 262176 | tf_op jit(solution)/shard_map/ppermute | solution.py:22
  46.1 3.3 %collective-permute-done.11.h3 = bf16[2,128,512]{2,1,0:T(8,128)(2,1)S(1)} collective-permute-done((bf16[2,128,512]{2,1,0:T(8,128)(2,1)S(1)}, bf16[2,128,512]{2,1,0:T(8,128)(2,1)S(1)}, u32[]{:S(2)}, u32[]{:S(2)}) %collective-permute-start.11) | collective-permute-done | bytes 262176 | tf_op jit(solution)/shard_map/ppermute | solution.py:22
  49.4 1.9 %shard_map.105 = (f32[4,2,128,512]{3,2,1,0:T(8,128)S(1)}, bf16[4,2,128,512]{3,2,1,0:T(8,128)(2,1)S(1)}) custom-call(s32[9]{0:T(128)S(1)} %stack.42.ids, s32[4,12]{1,0:T(4,128)S(1)} %maximum_convert_fusion.lists, bf16[1552,128]{1,0:T(8,128)(2,1)S(1)} %pad_maximum_fusion.a0, bf16[1552,128]{1,0:T(8,128)(2,1)S(1)} %collective-permute-done.3.a1, ...), custom_call_target="tpu_custom_call" | custom-call | flops 805306368 | bytes 5783780 | tf_op jit(solution)/shard_map/pallas_call | solution.py:36
  58.7 4.5 %collective-permute-done.20.o2 = bf16[128,512]{1,0:T(8,128)(2,1)S(1)} collective-permute-done((bf16[128,512]{1,0:T(8,128)(2,1)S(1)}, bf16[128,512]{1,0:T(8,128)(2,1)S(1)}, u32[]{:S(2)}, u32[]{:S(2)}) %collective-permute-start.20) | collective-permute-done | bytes 131104 | tf_op jit(solution)/shard_map/ppermute | solution.py:22
  64.5 2.7 %collective-permute-done.15.rest_4_ = bf16[272,512]{1,0:T(8,128)(2,1)S(1)} collective-permute-done((bf16[272,512]{1,0:T(8,128)(2,1)S(1)}, bf16[272,512]{1,0:T(8,128)(2,1)S(1)}, u32[]{:S(2)}, u32[]{:S(2)}) %collective-permute-start.15) | collective-permute-done | bytes 278560 | tf_op jit(solution)/shard_map/ppermute | solution.py:22
  69.5 1.8 %collective-permute-start.18 = (bf16[288,512]{1,0:T(8,128)(2,1)S(1)}, bf16[288,512]{1,0:T(8,128)(2,1)S(1)}, u32[]{:S(2)}, u32[]{:S(2)}) collective-permute-start(bf16[288,512]{1,0:T(8,128)(2,1)S(1)} %get-tuple-element.95), channel_id=1, source_target_pairs={{0,8},{1,9},{2,10},{3,11},{4,12},{5,13},{6,14},{7,15},{8,0},{9,1},... | collective-permute-start | bytes 884744 | tf_op jit(solution)/shard_map/ppermute | solution.py:22
  74.5 2.2 %collective-permute-done.22.rest_6_ = bf16[272,512]{1,0:T(8,128)(2,1)S(1)} collective-permute-done((bf16[272,512]{1,0:T(8,128)(2,1)S(1)}, bf16[272,512]{1,0:T(8,128)(2,1)S(1)}, u32[]{:S(2)}, u32[]{:S(2)}) %collective-permute-start.22) | collective-permute-done | bytes 278560 | tf_op jit(solution)/shard_map/ppermute | solution.py:22
  78.2 4.4 %collective-permute-done.19.rest_5_ = bf16[272,512]{1,0:T(8,128)(2,1)S(1)} collective-permute-done((bf16[272,512]{1,0:T(8,128)(2,1)S(1)}, bf16[272,512]{1,0:T(8,128)(2,1)S(1)}, u32[]{:S(2)}, u32[]{:S(2)}) %collective-permute-start.19) | collective-permute-done | bytes 278560 | tf_op jit(solution)/shard_map/ppermute | solution.py:22
  82.6 4.3 %collective-permute-done.23.rest_7_ = bf16[272,512]{1,0:T(8,128)(2,1)S(1)} collective-permute-done((bf16[272,512]{1,0:T(8,128)(2,1)S(1)}, bf16[272,512]{1,0:T(8,128)(2,1)S(1)}, u32[]{:S(2)}, u32[]{:S(2)}) %collective-permute-start.23) | collective-permute-done | bytes 278560 | tf_op jit(solution)/shard_map/ppermute | solution.py:22
  87.0 2.4 %collective-permute-done.24.p3.own1 = bf16[288,512]{1,0:T(8,128)(2,1)S(1)} collective-permute-done((bf16[288,512]{1,0:T(8,128)(2,1)S(1)}, bf16[288,512]{1,0:T(8,128)(2,1)S(1)}, u32[]{:S(2)}, u32[]{:S(2)}) %collective-permute-start.24) | collective-permute-done | bytes 294944 | tf_op jit(solution)/shard_map/ppermute | solution.py:22
  91.4 4.0 %shard_map.109 = (bf16[128,512]{1,0:T(8,128)(2,1)S(1)}, bf16[128,512]{1,0:T(8,128)(2,1)}, bf16[128,512]{1,0:T(8,128)(2,1)S(1)}, bf16[128,512]{1,0:T(8,128)(2,1)S...) custom-call(s32[9]{0:T(128)S(1)} %stack.42.ids, ...), custom_call_target="tpu_custom_call" | custom-call | flops 2147483648 | bytes 9306148 | tf_op jit(solution)/shard_map/pallas_call | solution.py:36
  100.0 2.4 %collective-permute-start.33 = (bf16[2,128,512]{2,1,0:T(8,128)(2,1)S(1)}, bf16[2,128,512]{2,1,0:T(8,128)(2,1)S(1)}, u32[]{:S(2)}, u32[]{:S(2)}) collective-permute-start(bf16[2,128,512]{2,1,0:T(8,128)(2,1)S(1)} %get-tuple-element.116), channel_id=1, source_target_pairs={{0,12},{1,13},{2,14},{3,15},{4,8},{5,9},{6,10},{7,11},{8,4},{9,5},... | collective-permute-start | bytes 786440 | tf_op jit(solution)/shard_map/ppermute | solution.py:22
  103.8 7.9 %collective-permute-done.31.received = bf16[528,512]{1,0:T(8,128)(2,1)S(1)} collective-permute-done((bf16[528,512]{1,0:T(8,128)(2,1)S(1)}, bf16[528,512]{1,0:T(8,128)(2,1)S(1)}, u32[]{:S(2)}, u32[]{:S(2)}) %collective-permute-start.31) | collective-permute-done | bytes 540704 | tf_op jit(solution)/shard_map/ppermute | solution.py:22
  112.1 1.8 %collective-permute-done.33.vxz = bf16[2,128,512]{2,1,0:T(8,128)(2,1)S(1)} collective-permute-done((bf16[2,128,512]{2,1,0:T(8,128)(2,1)S(1)}, bf16[2,128,512]{2,1,0:T(8,128)(2,1)S(1)}, u32[]{:S(2)}, u32[]{:S(2)}) %collective-permute-start.33) | collective-permute-done | bytes 262176 | tf_op jit(solution)/shard_map/ppermute | solution.py:22
  115.2 11.7 %collective-permute-done.38.rest_2_ = bf16[4,128,512]{2,1,0:T(8,128)(2,1)S(1)} collective-permute-done((bf16[4,128,512]{2,1,0:T(8,128)(2,1)S(1)}, bf16[4,128,512]{2,1,0:T(8,128)(2,1)S(1)}, u32[]{:S(2)}, u32[]{:S(2)}) %collective-permute-start.38) | collective-permute-done | bytes 524320 | tf_op jit(solution)/shard_map/ppermute | solution.py:22
  127.0 1.9 %collective-permute-done.40.rest_3_ = bf16[4,128,512]{2,1,0:T(8,128)(2,1)S(1)} collective-permute-done((bf16[4,128,512]{2,1,0:T(8,128)(2,1)S(1)}, bf16[4,128,512]{2,1,0:T(8,128)(2,1)S(1)}, u32[]{:S(2)}, u32[]{:S(2)}) %collective-permute-start.40) | collective-permute-done | bytes 524320 | tf_op jit(solution)/shard_map/ppermute | solution.py:22
  128.9 3.7 %shard_map.116 = bf16[8,128,512]{2,1,0:T(8,128)(2,1)} custom-call(s32[9]{0:T(128)S(1)} %stack.42.ids, s32[4,12]{1,0:T(4,128)S(1)} %maximum_convert_fusion.lists, bf16[1552,128]{1,0:T(8,128)(2,1)S(1)} %pad_maximum_fusion.a0, bf16[1552,128]{1,0:T(8,128)(2,1)S(1)} %collective-permute-done.3.a1, bf16[1552,128]{1,0:T(8,128)(2,1)S(1)} %collective-permute-done.4.a2, ...), custom_call_target="tpu_custom_call" | custom-call | flops 805306368 | bytes 4735204 | tf_op jit(solution)/shard_map/pallas_call | solution.py:36
  132.5 3.7 %all-to-all-start = ((bf16[8,128,512]{2,1,0:T(8,128)(2,1)}), bf16[8,128,512]{2,1,0:T(8,128)(2,1)S(1)}, u32[]{:S(2)}, u32[]{:S(2)}) async-start(bf16[8,128,512]{2,1,0:T(8,128)(2,1)} %shard_map.116), calls=%async_computation | async-start | bytes 2097152 | tf_op jit(solution)/shard_map/all_to_all | solution.py:427
  137.4 13.0 %collective-permute-done.41.from_y = bf16[512,512]{1,0:T(8,128)(2,1)S(1)} collective-permute-done((bf16[512,512]{1,0:T(8,128)(2,1)}, bf16[512,512]{1,0:T(8,128)(2,1)S(1)}, u32[]{:S(2)}, u32[]{:S(2)}) %collective-permute-start.41) | collective-permute-done | bytes 524320 | tf_op jit(solution)/shard_map/ppermute | solution.py:22
  153.2 2.4 %collective-permute-start.43 = (bf16[144,512]{1,0:T(8,128)(2,1)S(1)}, bf16[144,512]{1,0:T(8,128)(2,1)S(1)}, u32[]{:S(2)}, u32[]{:S(2)}) collective-permute-start(bf16[144,512]{1,0:T(8,128)(2,1)S(1)} %get-tuple-element.135), channel_id=1, source_target_pairs={{0,16},{1,17},{2,18},{3,19},{4,20},{5,21},{6,22},{7,23},{8,24},{9,... | collective-permute-start | bytes 442376 | tf_op jit(solution)/shard_map/ppermute | solution.py:22
  157.6 4.9 %collective-permute-done.35.a2 = bf16[128,512]{1,0:T(8,128)(2,1)S(1)} collective-permute-done((bf16[128,512]{1,0:T(8,128)(2,1)S(1)}, bf16[128,512]{1,0:T(8,128)(2,1)S(1)}, u32[]{:S(2)}, u32[]{:S(2)}) %collective-permute-start.35) | collective-permute-done | bytes 131104 | tf_op jit(solution)/shard_map/ppermute | solution.py:22
  165.0 4.7 %all-to-all-done.terms = bf16[8,128,512]{2,1,0:T(8,128)(2,1)S(1)} async-done(((bf16[8,128,512]{2,1,0:T(8,128)(2,1)}), bf16[8,128,512]{2,1,0:T(8,128)(2,1)S(1)}, u32[]{:S(2)}, u32[]{:S(2)}) %all-to-all-start) | async-done | bytes 1048608 | tf_op jit(solution)/shard_map/all_to_all | solution.py:427
  170.6 2.2 %collective-permute-done.43.r2 = bf16[144,512]{1,0:T(8,128)(2,1)S(1)} collective-permute-done((bf16[144,512]{1,0:T(8,128)(2,1)S(1)}, bf16[144,512]{1,0:T(8,128)(2,1)S(1)}, u32[]{:S(2)}, u32[]{:S(2)}) %collective-permute-start.43) | collective-permute-done | bytes 147488 | tf_op jit(solution)/shard_map/ppermute | solution.py:22
  172.8 3.1 %collective-permute-done.44.r3 = bf16[144,512]{1,0:T(8,128)(2,1)S(1)} collective-permute-done((bf16[144,512]{1,0:T(8,128)(2,1)S(1)}, bf16[144,512]{1,0:T(8,128)(2,1)S(1)}, u32[]{:S(2)}, u32[]{:S(2)}) %collective-permute-start.44) | collective-permute-done | bytes 147488 | tf_op jit(solution)/shard_map/ppermute | solution.py:22
  (114 shorter events, 53.4 us)
Async XLA Ops:
  5.4 21.2 %collective-permute-start.4 = (bf16[1552,128]{1,0:T(8,128)(2,1)S(1)}, bf16[1552,128]{1,0:T(8,128)(2,1)S(1)}, u32[]{:S(2)}, u32[]{:S(2)}) collective-permute-start(bf16[1552,128]{1,0:T(8,128)(2,1)S(1)} %pad_maximum_fusion.a0), channel_id=1, source_target_pairs={{0,8},{1,9},{2,10},{3,11},{4,12},{5,13},{6,14},{7,15},{8,0},{9,1},... | collective-permute-start | bytes 1191944 | tf_op jit(solution)/shard_map/ppermute | solution.py:22
  8.4 26.2 %collective-permute-start.6 = (bf16[128,2048]{1,0:T(8,128)(2,1)}, bf16[128,2048]{1,0:T(8,128)(2,1)S(1)}, u32[]{:S(2)}, u32[]{:S(2)}) collective-permute-start(bf16[128,2048]{1,0:T(8,128)(2,1)} %bitcast.20), channel_id=1, source_target_pairs={{0,16},{1,17},{2,18},{3,19},{4,20},{5,21},{6,22},{7,23},{8,24},{9,... | collective-permute-start | bytes 1572872 | tf_op jit(solution)/shard_map/ppermute | solution.py:22
  17.2 12.9 %collective-permute-start.3 = (bf16[1552,128]{1,0:T(8,128)(2,1)S(1)}, bf16[1552,128]{1,0:T(8,128)(2,1)S(1)}, u32[]{:S(2)}, u32[]{:S(2)}) collective-permute-start(bf16[1552,128]{1,0:T(8,128)(2,1)S(1)} %pad_maximum_fusion.a0), channel_id=1, source_target_pairs={{0,4},{1,5},{2,6},{3,7},{4,0},{5,1},{6,2},{7,3},{8,12},{9,13},{10,... | collective-permute-start | bytes 1191944 | tf_op jit(solution)/shard_map/ppermute | solution.py:22
  18.4 18.5 %collective-permute-start.8 = (bf16[272,512]{1,0:T(8,128)(2,1)S(1)}, bf16[272,512]{1,0:T(8,128)(2,1)S(1)}, u32[]{:S(2)}, u32[]{:S(2)}) collective-permute-start(bf16[272,512]{1,0:T(8,128)(2,1)S(1)} %shard_map.104.rest_0_), channel_id=1, source_target_pairs={{0,8},{1,9},{2,10},{3,11},{4,12},{5,13},{6,14},{7,15},{8,0},{9,1},... | collective-permute-start | bytes 835592 | tf_op jit(solution)/shard_map/ppermute | solution.py:22
  26.6 13.8 %collective-permute-start.5 = (bf16[1552,128]{1,0:T(8,128)(2,1)S(1)}, bf16[1552,128]{1,0:T(8,128)(2,1)S(1)}, u32[]{:S(2)}, u32[]{:S(2)}) collective-permute-start(bf16[1552,128]{1,0:T(8,128)(2,1)S(1)} %collective-permute-done.4.a2), channel_id=1, source_target_pairs={{0,4},{1,5},{2,6},{3,7},{4,0},{5,1},{6,2},{7,3},{8,12},{9,13},{10,... | collective-permute-start | bytes 1191944 | tf_op jit(solution)/shard_map/ppermute | solution.py:22
  28.6 10.3 %collective-permute-start.7 = (bf16[272,512]{1,0:T(8,128)(2,1)S(1)}, bf16[272,512]{1,0:T(8,128)(2,1)S(1)}, u32[]{:S(2)}, u32[]{:S(2)}) collective-permute-start(bf16[272,512]{1,0:T(8,128)(2,1)S(1)} %shard_map.104.rest_0_), channel_id=1, source_target_pairs={{0,2},{1,3},{2,0},{3,1},{4,6},{5,7},{6,4},{7,5},{8,10},{9,11},{10,... | collective-permute-start | bytes 835592 | tf_op jit(solution)/shard_map/ppermute | solution.py:22
  35.3 8.4 %collective-permute-start.9 = (bf16[2,128,512]{2,1,0:T(8,128)(2,1)S(1)}, bf16[2,128,512]{2,1,0:T(8,128)(2,1)S(1)}, u32[]{:S(2)}, u32[]{:S(2)}) collective-permute-start(bf16[2,128,512]{2,1,0:T(8,128)(2,1)S(1)} %get-tuple-element.83), channel_id=1, source_target_pairs={{0,4},{1,5},{2,6},{3,7},{4,0},{5,1},{6,2},{7,3},{8,12},{9,13},{10,... | collective-permute-start | bytes 786440 | tf_op jit(solution)/shard_map/ppermute | solution.py:22
  36.9 9.2 %collective-permute-start.10 = (bf16[2,128,512]{2,1,0:T(8,128)(2,1)S(1)}, bf16[2,128,512]{2,1,0:T(8,128)(2,1)S(1)}, u32[]{:S(2)}, u32[]{:S(2)}) collective-permute-start(bf16[2,128,512]{2,1,0:T(8,128)(2,1)S(1)} %get-tuple-element.84), channel_id=1, source_target_pairs={{0,8},{1,9},{2,10},{3,11},{4,12},{5,13},{6,14},{7,15},{8,0},{9,1},... | collective-permute-start | bytes 786440 | tf_op jit(solution)/shard_map/ppermute | solution.py:22
  36.9 12.5 %collective-permute-start.11 = (bf16[2,128,512]{2,1,0:T(8,128)(2,1)S(1)}, bf16[2,128,512]{2,1,0:T(8,128)(2,1)S(1)}, u32[]{:S(2)}, u32[]{:S(2)}) collective-permute-start(bf16[2,128,512]{2,1,0:T(8,128)(2,1)S(1)} %get-tuple-element.85), channel_id=1, source_target_pairs={{0,12},{1,13},{2,14},{3,15},{4,8},{5,9},{6,10},{7,11},{8,4},{9,5},... | collective-permute-start | bytes 786440 | tf_op jit(solution)/shard_map/ppermute | solution.py:22
  38.9 12.5 %collective-permute-start.12 = (bf16[272,512]{1,0:T(8,128)(2,1)S(1)}, bf16[272,512]{1,0:T(8,128)(2,1)S(1)}, u32[]{:S(2)}, u32[]{:S(2)}) collective-permute-start(bf16[272,512]{1,0:T(8,128)(2,1)S(1)} %collective-permute-done.8.rest_2_), channel_id=1, source_target_pairs={{0,2},{1,3},{2,0},{3,1},{4,6},{5,7},{6,4},{7,5},{8,10},{9,11},{10,... | collective-permute-start | bytes 835592 | tf_op jit(solution)/shard_map/ppermute | solution.py:22
  51.4 15.8 %collective-permute-start.15 = (bf16[272,512]{1,0:T(8,128)(2,1)S(1)}, bf16[272,512]{1,0:T(8,128)(2,1)S(1)}, u32[]{:S(2)}, u32[]{:S(2)}) collective-permute-start(bf16[272,512]{1,0:T(8,128)(2,1)S(1)} %shard_map.104.rest_0_), channel_id=1, source_target_pairs={{0,16},{1,17},{2,18},{3,19},{4,20},{5,21},{6,22},{7,23},{8,24},{9,... | collective-permute-start | bytes 835592 | tf_op jit(solution)/shard_map/ppermute | solution.py:22
  54.8 14.0 %collective-permute-start.14 = (bf16[4,128,512]{2,1,0:T(8,128)(2,1)S(1)}, bf16[4,128,512]{2,1,0:T(8,128)(2,1)S(1)}, u32[]{:S(2)}, u32[]{:S(2)}) collective-permute-start(bf16[4,128,512]{2,1,0:T(8,128)(2,1)S(1)} %get-tuple-element.90), channel_id=1, source_target_pairs={{0,2},{1,3},{2,0},{3,1},{4,6},{5,7},{6,4},{7,5},{8,10},{9,11},{10,... | collective-permute-start | bytes 1572872 | tf_op jit(solution)/shard_map/ppermute | solution.py:22
  67.2 9.5 %collective-permute-start.22 = (bf16[272,512]{1,0:T(8,128)(2,1)S(1)}, bf16[272,512]{1,0:T(8,128)(2,1)S(1)}, u32[]{:S(2)}, u32[]{:S(2)}) collective-permute-start(bf16[272,512]{1,0:T(8,128)(2,1)S(1)} %collective-permute-done.15.rest_4_), channel_id=1, source_target_pairs={{0,8},{1,9},{2,10},{3,11},{4,12},{5,13},{6,14},{7,15},{8,0},{9,1},... | collective-permute-start | bytes 835592 | tf_op jit(solution)/shard_map/ppermute | solution.py:22
  69.5 17.5 %collective-permute-start.18 = (bf16[288,512]{1,0:T(8,128)(2,1)S(1)}, bf16[288,512]{1,0:T(8,128)(2,1)S(1)}, u32[]{:S(2)}, u32[]{:S(2)}) collective-permute-start(bf16[288,512]{1,0:T(8,128)(2,1)S(1)} %get-tuple-element.95), channel_id=1, source_target_pairs={{0,8},{1,9},{2,10},{3,11},{4,12},{5,13},{6,14},{7,15},{8,0},{9,1},... | collective-permute-start | bytes 884744 | tf_op jit(solution)/shard_map/ppermute | solution.py:22
  71.3 18.1 %collective-permute-start.24 = (bf16[288,512]{1,0:T(8,128)(2,1)S(1)}, bf16[288,512]{1,0:T(8,128)(2,1)S(1)}, u32[]{:S(2)}, u32[]{:S(2)}) collective-permute-start(bf16[288,512]{1,0:T(8,128)(2,1)S(1)} %get-tuple-element.95), channel_id=1, source_target_pairs={{0,12},{1,13},{2,14},{3,15},{4,8},{5,9},{6,10},{7,11},{8,4},{9,5},... | collective-permute-start | bytes 884744 | tf_op jit(solution)/shard_map/ppermute | solution.py:22
  72.5 16.9 %collective-permute-start.17 = (bf16[288,512]{1,0:T(8,128)(2,1)S(1)}, bf16[288,512]{1,0:T(8,128)(2,1)S(1)}, u32[]{:S(2)}, u32[]{:S(2)}) collective-permute-start(bf16[288,512]{1,0:T(8,128)(2,1)S(1)} %get-tuple-element.94.p0.own0), channel_id=1, source_target_pairs={{0,4},{1,5},{2,6},{3,7},{4,0},{5,1},{6,2},{7,3},{8,12},{9,13},{10,... | collective-permute-start | bytes 884744 | tf_op jit(solution)/shard_map/ppermute | solution.py:22
  73.0 9.6 %collective-permute-start.19 = (bf16[272,512]{1,0:T(8,128)(2,1)S(1)}, bf16[272,512]{1,0:T(8,128)(2,1)S(1)}, u32[]{:S(2)}, u32[]{:S(2)}) collective-permute-start(bf16[272,512]{1,0:T(8,128)(2,1)S(1)} %collective-permute-done.15.rest_4_), channel_id=1, source_target_pairs={{0,2},{1,3},{2,0},{3,1},{4,6},{5,7},{6,4},{7,5},{8,10},{9,11},{10,... | collective-permute-start | bytes 835592 | tf_op jit(solution)/shard_map/ppermute | solution.py:22
  76.7 10.2 %collective-permute-start.23 = (bf16[272,512]{1,0:T(8,128)(2,1)S(1)}, bf16[272,512]{1,0:T(8,128)(2,1)S(1)}, u32[]{:S(2)}, u32[]{:S(2)}) collective-permute-start(bf16[272,512]{1,0:T(8,128)(2,1)S(1)} %collective-permute-done.22.rest_6_), channel_id=1, source_target_pairs={{0,2},{1,3},{2,0},{3,1},{4,6},{5,7},{6,4},{7,5},{8,10},{9,11},{10,... | collective-permute-start | bytes 835592 | tf_op jit(solution)/shard_map/ppermute | solution.py:22
  82.6 7.3 %collective-permute-start.25 = (bf16[288,512]{1,0:T(8,128)(2,1)S(1)}, bf16[288,512]{1,0:T(8,128)(2,1)S(1)}, u32[]{:S(2)}, u32[]{:S(2)}) collective-permute-start(bf16[288,512]{1,0:T(8,128)(2,1)S(1)} %get-tuple-element.94.p0.own0), channel_id=1, source_target_pairs={{0,1},{1,0},{2,3},{3,2},{4,5},{5,4},{6,7},{7,6},{8,9},{9,8},{10,11... | collective-permute-start | bytes 884744 | tf_op jit(solution)/shard_map/ppermute | solution.py:22
  97.0 14.6 %collective-permute-start.31 = (bf16[528,512]{1,0:T(8,128)(2,1)S(1)}, bf16[528,512]{1,0:T(8,128)(2,1)S(1)}, u32[]{:S(2)}, u32[]{:S(2)}) collective-permute-start(bf16[528,512]{1,0:T(8,128)(2,1)S(1)} %get-tuple-element.106), channel_id=1, source_target_pairs={{0,2},{1,3},{2,0},{3,1},{4,6},{5,7},{6,4},{7,5},{8,10},{9,11},{10,... | collective-permute-start | bytes 1622024 | tf_op jit(solution)/shard_map/ppermute | solution.py:22
  98.8 12.8 %collective-permute-start.30 = (bf16[2,128,512]{2,1,0:T(8,128)(2,1)S(1)}, bf16[2,128,512]{2,1,0:T(8,128)(2,1)S(1)}, u32[]{:S(2)}, u32[]{:S(2)}) collective-permute-start(bf16[2,128,512]{2,1,0:T(8,128)(2,1)S(1)} %get-tuple-element.111), channel_id=1, source_target_pairs={{0,4},{1,5},{2,6},{3,7},{4,0},{5,1},{6,2},{7,3},{8,12},{9,13},{10,... | collective-permute-start | bytes 786440 | tf_op jit(solution)/shard_map/ppermute | solution.py:22
  99.4 12.7 %collective-permute-start.32 = (bf16[2,128,512]{2,1,0:T(8,128)(2,1)S(1)}, bf16[2,128,512]{2,1,0:T(8,128)(2,1)S(1)}, u32[]{:S(2)}, u32[]{:S(2)}) collective-permute-start(bf16[2,128,512]{2,1,0:T(8,128)(2,1)S(1)} %get-tuple-element.115), channel_id=1, source_target_pairs={{0,8},{1,9},{2,10},{3,11},{4,12},{5,13},{6,14},{7,15},{8,0},{9,1},... | collective-permute-start | bytes 786440 | tf_op jit(solution)/shard_map/ppermute | solution.py:22
  100.0 13.9 %collective-permute-start.33 = (bf16[2,128,512]{2,1,0:T(8,128)(2,1)S(1)}, bf16[2,128,512]{2,1,0:T(8,128)(2,1)S(1)}, u32[]{:S(2)}, u32[]{:S(2)}) collective-permute-start(bf16[2,128,512]{2,1,0:T(8,128)(2,1)S(1)} %get-tuple-element.116), channel_id=1, source_target_pairs={{0,12},{1,13},{2,14},{3,15},{4,8},{5,9},{6,10},{7,11},{8,4},{9,5},... | collective-permute-start | bytes 786440 | tf_op jit(solution)/shard_map/ppermute | solution.py:22
  111.8 15.2 %collective-permute-start.39 = (bf16[528,512]{1,0:T(8,128)(2,1)S(1)}, bf16[528,512]{1,0:T(8,128)(2,1)S(1)}, u32[]{:S(2)}, u32[]{:S(2)}) collective-permute-start(bf16[528,512]{1,0:T(8,128)(2,1)S(1)} %get-tuple-element.125), channel_id=1, source_target_pairs={{0,8},{1,9},{2,10},{3,11},{4,12},{5,13},{6,14},{7,15},{8,0},{9,1},... | collective-permute-start | bytes 1622024 | tf_op jit(solution)/shard_map/ppermute | solution.py:22
  114.1 12.8 %collective-permute-start.38 = (bf16[4,128,512]{2,1,0:T(8,128)(2,1)S(1)}, bf16[4,128,512]{2,1,0:T(8,128)(2,1)S(1)}, u32[]{:S(2)}, u32[]{:S(2)}) collective-permute-start(bf16[4,128,512]{2,1,0:T(8,128)(2,1)S(1)} %shard_map.113.rest_0_), channel_id=1, source_target_pairs={{0,2},{1,3},{2,0},{3,1},{4,6},{5,7},{6,4},{7,5},{8,10},{9,11},{10,... | collective-permute-start | bytes 1572872 | tf_op jit(solution)/shard_map/ppermute | solution.py:22
  115.2 11.7 %collective-permute-start.37 = (bf16[4,128,512]{2,1,0:T(8,128)(2,1)S(1)}, bf16[4,128,512]{2,1,0:T(8,128)(2,1)S(1)}, u32[]{:S(2)}, u32[]{:S(2)}) collective-permute-start(bf16[4,128,512]{2,1,0:T(8,128)(2,1)S(1)} %shard_map.113.rest_0_), channel_id=1, source_target_pairs={{0,1},{1,0},{2,3},{3,2},{4,5},{5,4},{6,7},{7,6},{8,9},{9,8},{10,11... | collective-permute-start | bytes 1572872 | tf_op jit(solution)/shard_map/ppermute | solution.py:22
  132.5 37.1 %all-to-all-start = ((bf16[8,128,512]{2,1,0:T(8,128)(2,1)}), bf16[8,128,512]{2,1,0:T(8,128)(2,1)S(1)}, u32[]{:S(2)}, u32[]{:S(2)}) async-start(bf16[8,128,512]{2,1,0:T(8,128)(2,1)} %shard_map.116), calls=%async_computation | async-start | bytes 2097152 | tf_op jit(solution)/shard_map/all_to_all | solution.py:427
  136.2 14.2 %collective-permute-start.41 = (bf16[512,512]{1,0:T(8,128)(2,1)}, bf16[512,512]{1,0:T(8,128)(2,1)S(1)}, u32[]{:S(2)}, u32[]{:S(2)}) collective-permute-start(bf16[512,512]{1,0:T(8,128)(2,1)} %copy-done.4), channel_id=1, source_target_pairs={{0,2},{1,3},{2,0},{3,1},{4,6},{5,7},{6,4},{7,5},{8,10},{9,11},{10,... | collective-permute-start | bytes 1572872 | tf_op jit(solution)/shard_map/ppermute | solution.py:22
  137.4 20.2 %collective-permute-start.34 = (bf16[128,512]{1,0:T(8,128)(2,1)}, bf16[128,512]{1,0:T(8,128)(2,1)S(1)}, u32[]{:S(2)}, u32[]{:S(2)}) collective-permute-start(bf16[128,512]{1,0:T(8,128)(2,1)} %get-tuple-element.117), channel_id=1, source_target_pairs={{0,1},{1,0},{2,3},{3,2},{4,5},{5,4},{6,7},{7,6},{8,9},{9,8},{10,11... | collective-permute-start | bytes 393224 | tf_op jit(solution)/shard_map/ppermute | solution.py:22
  151.7 18.9 %collective-permute-start.42 = (bf16[144,512]{1,0:T(8,128)(2,1)}, bf16[144,512]{1,0:T(8,128)(2,1)S(1)}, u32[]{:S(2)}, u32[]{:S(2)}) collective-permute-start(bf16[144,512]{1,0:T(8,128)(2,1)} %get-tuple-element.134), channel_id=1, source_target_pairs={{0,4},{1,5},{2,6},{3,7},{4,0},{5,1},{6,2},{7,3},{8,12},{9,13},{10,... | collective-permute-start | bytes 442376 | tf_op jit(solution)/shard_map/ppermute | solution.py:22
  153.2 19.6 %collective-permute-start.43 = (bf16[144,512]{1,0:T(8,128)(2,1)S(1)}, bf16[144,512]{1,0:T(8,128)(2,1)S(1)}, u32[]{:S(2)}, u32[]{:S(2)}) collective-permute-start(bf16[144,512]{1,0:T(8,128)(2,1)S(1)} %get-tuple-element.135), channel_id=1, source_target_pairs={{0,16},{1,17},{2,18},{3,19},{4,20},{5,21},{6,22},{7,23},{8,24},{9,... | collective-permute-start | bytes 442376 | tf_op jit(solution)/shard_map/ppermute | solution.py:22
  155.6 20.3 %collective-permute-start.44 = (bf16[144,512]{1,0:T(8,128)(2,1)S(1)}, bf16[144,512]{1,0:T(8,128)(2,1)S(1)}, u32[]{:S(2)}, u32[]{:S(2)}) collective-permute-start(bf16[144,512]{1,0:T(8,128)(2,1)S(1)} %get-tuple-element.136), channel_id=1, source_target_pairs={{0,20},{1,21},{2,22},{3,23},{4,16},{5,17},{6,18},{7,19},{8,28},{9,... | collective-permute-start | bytes 442376 | tf_op jit(solution)/shard_map/ppermute | solution.py:22
  (25 other events, 157.5 us)

commit v5 on v4

--- a/solution.py
+++ b/solution.py
@@ -196,27 +196,27 @@
         out[2 + x] = (vz[x].astype(F32) + vxz[x].astype(F32)).astype(BF16)
 
 
-def spread_kernel(ids, lists, a0, a1, a2, a3, *rest):
-    grads, (out, total) = rest[:4], rest[4:]
+def spread_kernel(near, ids, lists, a0, a1, a2, a3, same, cross, *rest):
+    start, out, total = (None,) + rest if near else rest
     core, y, x = ids[1], ids[2], ids[5]
     tile = out.shape[1]
-    total[...] = jnp.zeros_like(total)
+    total[...] = jnp.zeros_like(total) if near else start[...]
     for i, tiles in enumerate((a0, a1, a2, a3)):
-        for away in range(4):
-            m = (y ^ (away >> 1)) * 2 + (core ^ (away & 1))
+        for other, grads in enumerate((same, cross)):
+            m = (y if near else 1 - y) * 2 + (core ^ other)
             left = []
             for s in range(SLOTS):
                 slot = m * SLOTS + s
                 block = tiles[pl.ds(pl.multiple_of(slot * tile, tile), tile), :]
                 left.append(jnp.where(lists[i, slot] >= 0, block, jnp.zeros_like(block)))
             terms = lax.dot_general(
-                jnp.concatenate(left, axis=1), grads[away][2 * (i >> 1) + (x ^ (i & 1))],
+                jnp.concatenate(left, axis=1), grads[2 * (i >> 1) + (x ^ (i & 1))],
                 (((0,), (0,)), ((), ())), preferred_element_type=F32,
             )
             for s in range(SLOTS):
                 at = jnp.maximum(lists[i, m * SLOTS + s], 0)
                 total[at] += terms[s * tile : (s + 1) * tile]
-    out[...] = total[...].astype(BF16)
+    out[...] = total[...].astype(out.dtype)
 
 
 def finish_kernel(terms, out):
@@ -265,52 +265,28 @@
     send[4 * block :, :] = both[...].astype(BF16)
 
 
-def fold_low_kernel(ids, keep, row, from_y, from_z, own, sums, s1, s2, s3):
+def fold_low_kernel(ids, keep, row, from_y, from_z, own, s1, s2, s3):
     high, x, block = ids[4], ids[5], keep.shape[1]
-    sums[...] = row[...] + from_z[4 * block :, :].astype(F32)
+    sums = row[...] + from_z[4 * block :, :].astype(F32)
     for i, out in enumerate((own, s1, s2, s3)):
         at = (high ^ (i >> 1)) * 2 + (x ^ (i & 1))
         rows = pl.ds(pl.multiple_of(at * block, block), block)
         total = keep[at] + from_y[rows, :].astype(F32) + from_z[rows, :].astype(F32)
-        if out is own:
-            own[...] = total
-        else:
-            out[:block, :] = total.astype(BF16)
-            out[block:, :] = sums[...].astype(BF16)
-
-
-def fold_high_kernel(ids, own, row, r1, r2, r3, mine, sums, send):
-    core, block = ids[1], own.shape[0]
-    many = mine.shape[1]
-    for i in range(2):
-        for out, k in ((mine, core), (send, 1 - core)):
-            at = pl.ds(pl.multiple_of(k * many, many), many)
-            if i == 0:
-                value = own[at, :] + r2[at, :].astype(F32)
-            else:
-                value = r1[at, :].astype(F32) + r3[at, :].astype(F32)
-            if out is mine:
-                out[i] = value
-            else:
-                out[i * many : (i + 1) * many, :] = value
-    sums[0] = row[...] + r2[block:, :].astype(F32)
-    sums[1] = r1[block:, :].astype(F32) + r3[block:, :].astype(F32)
-    for i in range(2):
-        send[2 * many + i * ROWS : 2 * many + (i + 1) * ROWS, :] = sums[i]
-
-
-def weight_out_kernel(ids, mine, sums, received, out, bias):
-    many, part = mine.shape[1:]
+        out[:block, :] = total.astype(out.dtype)
+        out[block:, :] = sums.astype(out.dtype)
+
+
+def weight_out_kernel(ids, own, r1, r2, r3, own_c, r1_c, r2_c, r3_c, out, bias):
+    many, part = out.shape[0], own.shape[1]
     block = 2 * many
-    for i in range(2):
-        cols = pl.ds(pl.multiple_of((ids[7] ^ (2 * i)) * part, part), part)
-        out[:, cols] = mine[i]
-        cols = pl.ds(pl.multiple_of((ids[7] ^ (2 * i + 1)) * part, part), part)
-        out[:, cols] = received[i * many : (i + 1) * many, :]
-    quarters = (
-        sums[0], received[block : block + ROWS, :], sums[1], received[block + ROWS :, :],
-    )
-    total = sum(q * (ids[3] ^ ids[7] == i).astype(F32) for i, q in enumerate(quarters))
+    rows = pl.ds(pl.multiple_of(ids[1] * many, many), many)
+    pairs = ((own, r2), (own_c, r2_c), (r1, r3), (r1_c, r3_c))
+    total = 0.0
+    for i, (left, right) in enumerate(pairs):
+        cols = pl.ds(pl.multiple_of((ids[7] ^ i) * part, part), part)
+        out[:, cols] = left[rows, :].astype(F32) + right[rows, :].astype(F32)
+        quarter = left[block:, :].astype(F32) + right[block:, :].astype(F32)
+        total += quarter * (ids[3] ^ ids[7] == i).astype(F32)
     step = 2 * many
     picked = sum(
         total[:1, i * step : (i + 1) * step] * ((ids[5] * 2 + ids[2]) == i).astype(F32) for i in range(4)
@@ -416,32 +392,37 @@
     from_y = swap(after(send_near, grads_own), Y)
     acts = [acts[0]] + [swap(after(a, grads_own), m) for a, m in zip(acts[1:], shares)]
     (spread,) = call(
-        spread_kernel, [shape((rows, tile, quarter), BF16)],
-        ids, lists_of, *tiles_of,
-        grads_own, swap(grads_own, CORE), grads_away, swap(grads_away, CORE),
+        functools.partial(spread_kernel, True), [shape((rows, tile, quarter), F32)],
+        ids, lists_of, *tiles_of, grads_own, swap(grads_own, CORE),
         scratch=[pltpu.VMEM((rows, tile, quarter), F32)],
-        smem=2, flops=2 * GROUP * dests * slots * tile * tile * quarter,
-    )
-
-    pass
+        smem=2, flops=GROUP * dests * slots * tile * tile * quarter,
+    )
+    (spread,) = call(
+        functools.partial(spread_kernel, False), [shape((rows, tile, quarter), BF16)],
+        ids, lists_of, *tiles_of, grads_away, swap(grads_away, CORE), spread,
+        scratch=[pltpu.VMEM((rows, tile, quarter), F32)],
+        smem=2, flops=GROUP * dests * slots * tile * tile * quarter,
+    )
     spread_all = lax.all_to_all(spread, "row", 0, 0, tiled=True)
-    own, row, *send = call(
+    from_y = after(from_y, *acts[1:])
+    own, *send = call(
         fold_low_kernel,
-        [shape((tile, quarter), F32), shape((ROWS, quarter), F32)] + [shape((tile + ROWS, quarter), BF16)] * 3,
+        [shape((tile + ROWS, quarter), F32)] + [shape((tile + ROWS, quarter), BF16)] * 3,
         ids, kept_near, row, from_y, from_z,
     )
+    own_other = swap(own, CORE)
+    send[0] = after(send[0], own_other)
     received = [swap(s, m) for s, m in zip(send, (X, 2 * Z, 2 * Z | X))]
     (input_grad,) = call(finish_kernel, [shape((nodes, width), BF16)], spread_all, smem=0)
     (activations,) = call(act_kernel, [shape((nodes, width), BF16)], ids, lanes, *acts)
-    own = after(own, input_grad, activations)
-    own, rows_of, send = call(
-        fold_high_kernel,
-        [shape((2, own_rows, quarter), F32), shape((2, ROWS, quarter), F32), shape((2 * own_rows + 2 * ROWS, quarter), F32)],
-        ids, own, row, *received,
-    )
+    received_other = [
+        swap(received[0], CORE),
+        swap(after(received[1], input_grad, activations), CORE),
+        swap(received[2], CORE),
+    ]
     weight_grad, row = call(
         weight_out_kernel, [shape((own_rows, width), F32), shape((1, own_rows), F32)],
-        ids, own, rows_of, swap(send, CORE),
+        ids, own, *received, own_other, *received_other,
     )
     bias_grad = row.reshape(own_rows)
 

time: 180 us -> 177 us (0.983)
  waiting for transfers between devices: 106 us -> 99.3 us
  starting transfers between devices: 46.6 us -> 51.2 us
    all_to_all x1, waiting for transfers between devices: 4.65 us -> 0.01 us  [chip_body(): spread_all = lax.all_to_all(spread, 'row', 0, 0, tiled=True)]
    ppermute x46 -> x49, starting transfers between devices: 42.9 us -> 47.4 us  [swap(): return lax.ppermute(value, BOTH, [(i, i ^ mask) for i in range(total)])]
    ppermute x46 -> x49, waiting for transfers between devices: 101 us -> 99.3 us  [swap(): return lax.ppermute(value, BOTH, [(i, i ^ mask) for i in range(total)])]
  transfers between devices with their start and end apart: 47 -> 50, of which waited for: 30 -> 27; matrix products, arithmetic and copies ran while one was open for 1% -> 1% of each run, Pallas kernels for 7% -> 8%
where the time goes in v5:
time: 177 us
  waiting for transfers between devices  99.3 us (56%)
  starting transfers between devices  51.2 us (29%)
  Pallas kernels  21.7 us (12%)
  local copies, waits for them, and re-layouts  2.08 us (1%)
    ppermute x49, waiting for transfers between devices, swap(): return lax.ppermute(value, BOTH, [(i, i ^ mask) for i in range(total)])  99.3 us
    ppermute x49, starting transfers between devices, swap(): return lax.ppermute(value, BOTH, [(i, i ^ mask) for i in range(total)])  47.4 us
    pallas_call x19, Pallas kernels, call(): pl.pallas_call(kernel, out_shape=outs, in_specs=[SMEM] * smem + [VMEM] *...  21.7 us
    all_to_all x1, starting transfers between devices, chip_body(): spread_all = lax.all_to_all(spread, 'row', 0, 0, tiled=True)  3.81 us
  transfers between devices with their start and end apart: 50, of which 27 were waited for; matrix products, arithmetic and copies ran while one was open for 1% of the time, Pallas kernels for 8%

profile of v5, /device:TPU:0, one launch (start us, length us, event | category | flops | bytes accessed | tf_op | source)
XLA Modules:
  0.0 177.0 jit_solution(12161321080225315765)
XLA Ops:
  5.4 3.0 %collective-permute-start.4 = (bf16[1552,128]{1,0:T(8,128)(2,1)S(1)}, bf16[1552,128]{1,0:T(8,128)(2,1)S(1)}, u32[]{:S(2)}, u32[]{:S(2)}) collective-permute-start(bf16[1552,128]{1,0:T(8,128)(2,1)S(1)} %pad_maximum_fusion.a0), channel_id=1, source_target_pairs={{0,8},{1,9},{2,10},{3,11},{4,12},{5,13},{6,14},{7,15},{8,0},{9,1},... | collective-permute-start | bytes 1191944 | tf_op jit(solution)/shard_map/ppermute | solution.py:22
  8.4 2.6 %collective-permute-start.6 = (bf16[128,2048]{1,0:T(8,128)(2,1)}, bf16[128,2048]{1,0:T(8,128)(2,1)S(1)}, u32[]{:S(2)}, u32[]{:S(2)}) collective-permute-start(bf16[128,2048]{1,0:T(8,128)(2,1)} %bitcast.20), channel_id=1, source_target_pairs={{0,16},{1,17},{2,18},{3,19},{4,20},{5,21},{6,22},{7,23},{8,24},{9,... | collective-permute-start | bytes 1572872 | tf_op jit(solution)/shard_map/ppermute | solution.py:22
  12.5 2.9 %collective-permute-done.1.p2 = bf16[80,512]{1,0:T(8,128)(2,1)S(1)} collective-permute-done((bf16[80,512]{1,0:T(8,128)(2,1)S(1)}, bf16[80,512]{1,0:T(8,128)(2,1)S(1)}, u32[]{:S(2)}, u32[]{:S(2)}) %collective-permute-start.1) | collective-permute-done | bytes 81952 | tf_op jit(solution)/shard_map/ppermute | solution.py:22
  18.9 7.7 %collective-permute-done.4.a2 = bf16[1552,128]{1,0:T(8,128)(2,1)S(1)} collective-permute-done((bf16[1552,128]{1,0:T(8,128)(2,1)S(1)}, bf16[1552,128]{1,0:T(8,128)(2,1)S(1)}, u32[]{:S(2)}, u32[]{:S(2)}) %collective-permute-start.4) | collective-permute-done | bytes 397344 | tf_op jit(solution)/shard_map/ppermute | solution.py:22
  26.6 2.0 %collective-permute-start.5 = (bf16[1552,128]{1,0:T(8,128)(2,1)S(1)}, bf16[1552,128]{1,0:T(8,128)(2,1)S(1)}, u32[]{:S(2)}, u32[]{:S(2)}) collective-permute-start(bf16[1552,128]{1,0:T(8,128)(2,1)S(1)} %collective-permute-done.4.a2), channel_id=1, source_target_pairs={{0,4},{1,5},{2,6},{3,7},{4,0},{5,1},{6,2},{7,3},{8,12},{9,13},{10,... | collective-permute-start | bytes 1191944 | tf_op jit(solution)/shard_map/ppermute | solution.py:22
  30.1 4.5 %collective-permute-done.6.far = bf16[128,2048]{1,0:T(8,128)(2,1)S(1)} collective-permute-done((bf16[128,2048]{1,0:T(8,128)(2,1)}, bf16[128,2048]{1,0:T(8,128)(2,1)S(1)}, u32[]{:S(2)}, u32[]{:S(2)}) %collective-permute-start.6) | collective-permute-done | bytes 524320 | tf_op jit(solution)/shard_map/ppermute | solution.py:22
  36.9 2.0 %collective-permute-start.11 = (bf16[2,128,512]{2,1,0:T(8,128)(2,1)S(1)}, bf16[2,128,512]{2,1,0:T(8,128)(2,1)S(1)}, u32[]{:S(2)}, u32[]{:S(2)}) collective-permute-start(bf16[2,128,512]{2,1,0:T(8,128)(2,1)S(1)} %get-tuple-element.83), channel_id=1, source_target_pairs={{0,12},{1,13},{2,14},{3,15},{4,8},{5,9},{6,10},{7,11},{8,4},{9,5},... | collective-permute-start | bytes 786440 | tf_op jit(solution)/shard_map/ppermute | solution.py:22
  40.4 3.3 %collective-permute-done.9.h1 = bf16[2,128,512]{2,1,0:T(8,128)(2,1)S(1)} collective-permute-done((bf16[2,128,512]{2,1,0:T(8,128)(2,1)S(1)}, bf16[2,128,512]{2,1,0:T(8,128)(2,1)S(1)}, u32[]{:S(2)}, u32[]{:S(2)}) %collective-permute-start.9) | collective-permute-done | bytes 262176 | tf_op jit(solution)/shard_map/ppermute | solution.py:22
  43.7 2.4 %collective-permute-done.10.h2 = bf16[2,128,512]{2,1,0:T(8,128)(2,1)S(1)} collective-permute-done((bf16[2,128,512]{2,1,0:T(8,128)(2,1)S(1)}, bf16[2,128,512]{2,1,0:T(8,128)(2,1)S(1)}, u32[]{:S(2)}, u32[]{:S(2)}) %collective-permute-start.10) | collective-permute-done | bytes 262176 | tf_op jit(solution)/shard_map/ppermute | solution.py:22
  46.1 3.3 %collective-permute-done.11.h3 = bf16[2,128,512]{2,1,0:T(8,128)(2,1)S(1)} collective-permute-done((bf16[2,128,512]{2,1,0:T(8,128)(2,1)S(1)}, bf16[2,128,512]{2,1,0:T(8,128)(2,1)S(1)}, u32[]{:S(2)}, u32[]{:S(2)}) %collective-permute-start.11) | collective-permute-done | bytes 262176 | tf_op jit(solution)/shard_map/ppermute | solution.py:22
  49.4 1.9 %shard_map.105 = (f32[4,2,128,512]{3,2,1,0:T(8,128)S(1)}, bf16[4,2,128,512]{3,2,1,0:T(8,128)(2,1)S(1)}) custom-call(s32[9]{0:T(128)S(1)} %stack.42.ids, s32[4,12]{1,0:T(4,128)S(1)} %maximum_convert_fusion.lists, bf16[1552,128]{1,0:T(8,128)(2,1)S(1)} %pad_maximum_fusion.a0, bf16[1552,128]{1,0:T(8,128)(2,1)S(1)} %collective-permute-done.3.a1, ...), custom_call_target="tpu_custom_call" | custom-call | flops 805306368 | bytes 5783780 | tf_op jit(solution)/shard_map/pallas_call | solution.py:36
  58.7 4.5 %collective-permute-done.20.o2 = bf16[128,512]{1,0:T(8,128)(2,1)S(1)} collective-permute-done((bf16[128,512]{1,0:T(8,128)(2,1)S(1)}, bf16[128,512]{1,0:T(8,128)(2,1)S(1)}, u32[]{:S(2)}, u32[]{:S(2)}) %collective-permute-start.20) | collective-permute-done | bytes 131104 | tf_op jit(solution)/shard_map/ppermute | solution.py:22
  64.5 2.7 %collective-permute-done.15.rest_4_ = bf16[272,512]{1,0:T(8,128)(2,1)S(1)} collective-permute-done((bf16[272,512]{1,0:T(8,128)(2,1)S(1)}, bf16[272,512]{1,0:T(8,128)(2,1)S(1)}, u32[]{:S(2)}, u32[]{:S(2)}) %collective-permute-start.15) | collective-permute-done | bytes 278560 | tf_op jit(solution)/shard_map/ppermute | solution.py:22
  69.5 1.8 %collective-permute-start.18 = (bf16[288,512]{1,0:T(8,128)(2,1)S(1)}, bf16[288,512]{1,0:T(8,128)(2,1)S(1)}, u32[]{:S(2)}, u32[]{:S(2)}) collective-permute-start(bf16[288,512]{1,0:T(8,128)(2,1)S(1)} %get-tuple-element.93), channel_id=1, source_target_pairs={{0,8},{1,9},{2,10},{3,11},{4,12},{5,13},{6,14},{7,15},{8,0},{9,1},... | collective-permute-start | bytes 884744 | tf_op jit(solution)/shard_map/ppermute | solution.py:22
  74.5 2.2 %collective-permute-done.22.rest_6_ = bf16[272,512]{1,0:T(8,128)(2,1)S(1)} collective-permute-done((bf16[272,512]{1,0:T(8,128)(2,1)S(1)}, bf16[272,512]{1,0:T(8,128)(2,1)S(1)}, u32[]{:S(2)}, u32[]{:S(2)}) %collective-permute-start.22) | collective-permute-done | bytes 278560 | tf_op jit(solution)/shard_map/ppermute | solution.py:22
  78.2 4.4 %collective-permute-done.19.rest_5_ = bf16[272,512]{1,0:T(8,128)(2,1)S(1)} collective-permute-done((bf16[272,512]{1,0:T(8,128)(2,1)S(1)}, bf16[272,512]{1,0:T(8,128)(2,1)S(1)}, u32[]{:S(2)}, u32[]{:S(2)}) %collective-permute-start.19) | collective-permute-done | bytes 278560 | tf_op jit(solution)/shard_map/ppermute | solution.py:22
  82.6 4.3 %collective-permute-done.23.rest_7_ = bf16[272,512]{1,0:T(8,128)(2,1)S(1)} collective-permute-done((bf16[272,512]{1,0:T(8,128)(2,1)S(1)}, bf16[272,512]{1,0:T(8,128)(2,1)S(1)}, u32[]{:S(2)}, u32[]{:S(2)}) %collective-permute-start.23) | collective-permute-done | bytes 278560 | tf_op jit(solution)/shard_map/ppermute | solution.py:22
  87.0 2.4 %collective-permute-done.24.p3.own1 = bf16[288,512]{1,0:T(8,128)(2,1)S(1)} collective-permute-done((bf16[288,512]{1,0:T(8,128)(2,1)S(1)}, bf16[288,512]{1,0:T(8,128)(2,1)S(1)}, u32[]{:S(2)}, u32[]{:S(2)}) %collective-permute-start.24) | collective-permute-done | bytes 294944 | tf_op jit(solution)/shard_map/ppermute | solution.py:22
  91.4 3.5 %shard_map.109 = (bf16[128,512]{1,0:T(8,128)(2,1)S(1)}, bf16[128,512]{1,0:T(8,128)(2,1)S(1)}, bf16[128,512]{1,0:T(8,128)(2,1)S(1)}, bf16[128,512]{1,0:T(8,128)(2...) custom-call(s32[9]{0:T(128)S(1)} %stack.42.ids, ...), custom_call_target="tpu_custom_call" | custom-call | flops 2147483648 | bytes 9306148 | tf_op jit(solution)/shard_map/pallas_call | solution.py:36
  99.6 2.4 %collective-permute-start.33 = (bf16[2,128,512]{2,1,0:T(8,128)(2,1)S(1)}, bf16[2,128,512]{2,1,0:T(8,128)(2,1)S(1)}, u32[]{:S(2)}, u32[]{:S(2)}) collective-permute-start(bf16[2,128,512]{2,1,0:T(8,128)(2,1)S(1)} %get-tuple-element.114), channel_id=1, source_target_pairs={{0,12},{1,13},{2,14},{3,15},{4,8},{5,9},{6,10},{7,11},{8,4},{9,5},... | collective-permute-start | bytes 786440 | tf_op jit(solution)/shard_map/ppermute | solution.py:22
  103.4 7.9 %collective-permute-done.31.received = bf16[528,512]{1,0:T(8,128)(2,1)S(1)} collective-permute-done((bf16[528,512]{1,0:T(8,128)(2,1)S(1)}, bf16[528,512]{1,0:T(8,128)(2,1)S(1)}, u32[]{:S(2)}, u32[]{:S(2)}) %collective-permute-start.31) | collective-permute-done | bytes 540704 | tf_op jit(solution)/shard_map/ppermute | solution.py:22
  111.7 1.9 %collective-permute-done.33.vxz = bf16[2,128,512]{2,1,0:T(8,128)(2,1)S(1)} collective-permute-done((bf16[2,128,512]{2,1,0:T(8,128)(2,1)S(1)}, bf16[2,128,512]{2,1,0:T(8,128)(2,1)S(1)}, u32[]{:S(2)}, u32[]{:S(2)}) %collective-permute-start.33) | collective-permute-done | bytes 262176 | tf_op jit(solution)/shard_map/ppermute | solution.py:22
  114.9 11.7 %collective-permute-done.37.same = bf16[4,128,512]{2,1,0:T(8,128)(2,1)S(1)} collective-permute-done((bf16[4,128,512]{2,1,0:T(8,128)(2,1)S(1)}, bf16[4,128,512]{2,1,0:T(8,128)(2,1)S(1)}, u32[]{:S(2)}, u32[]{:S(2)}) %collective-permute-start.37) | collective-permute-done | bytes 524320 | tf_op jit(solution)/shard_map/ppermute | solution.py:22
  126.6 1.8 %shard_map.116.rest_0_ = f32[8,128,512]{2,1,0:T(8,128)S(1)} custom-call(s32[9]{0:T(128)S(1)} %stack.42.ids, s32[4,12]{1,0:T(4,128)S(1)} %maximum_convert_fusion.lists, bf16[1552,128]{1,0:T(8,128)(2,1)S(1)} %pad_maximum_fusion.a0, bf16[1552,128]{1,0:T(8,128)(2,1)S(1)} %collective-permute-done.3.a1, bf16[1552,128]{1,0:T(8,128)(2,1)S(1)} %collective-permute-done.4.a2, ...), custom_call_target="tpu_custom_call" | custom-call | flops 402653184 | bytes 4735204 | tf_op jit(solution)/shard_map/pallas_call | solution.py:36
  128.5 2.8 %shard_map.117 = bf16[8,128,512]{2,1,0:T(8,128)(2,1)} custom-call(s32[9]{0:T(128)S(1)} %stack.42.ids, s32[4,12]{1,0:T(4,128)S(1)} %maximum_convert_fusion.lists, bf16[1552,128]{1,0:T(8,128)(2,1)S(1)} %pad_maximum_fusion.a0, bf16[1552,128]{1,0:T(8,128)(2,1)S(1)} %collective-permute-done.3.a1, bf16[1552,128]{1,0:T(8,128)(2,1)S(1)} %collective-permute-done.4.a2, ...), custom_call_target="tpu_custom_call" | custom-call | flops 402653184 | bytes 5783780 | tf_op jit(solution)/shard_map/pallas_call | solution.py:36
  131.3 3.8 %all-to-all-start = ((bf16[8,128,512]{2,1,0:T(8,128)(2,1)}), bf16[8,128,512]{2,1,0:T(8,128)(2,1)S(1)}, u32[]{:S(2)}, u32[]{:S(2)}) async-start(bf16[8,128,512]{2,1,0:T(8,128)(2,1)} %shard_map.117), calls=%async_computation | async-start | bytes 2097152 | tf_op jit(solution)/shard_map/all_to_all | solution.py:406
  136.4 1.9 %collective-permute-start.35 = (bf16[128,512]{1,0:T(8,128)(2,1)}, bf16[128,512]{1,0:T(8,128)(2,1)S(1)}, u32[]{:S(2)}, u32[]{:S(2)}) collective-permute-start(bf16[128,512]{1,0:T(8,128)(2,1)} %copy-done.6), channel_id=1, source_target_pairs={{0,4},{1,5},{2,6},{3,7},{4,0},{5,1},{6,2},{7,3},{8,12},{9,13},{10,... | collective-permute-start | bytes 393224 | tf_op jit(solution)/shard_map/ppermute | solution.py:22
  138.4 11.2 %collective-permute-done.35.a2 = bf16[128,512]{1,0:T(8,128)(2,1)S(1)} collective-permute-done((bf16[128,512]{1,0:T(8,128)(2,1)}, bf16[128,512]{1,0:T(8,128)(2,1)S(1)}, u32[]{:S(2)}, u32[]{:S(2)}) %collective-permute-start.35) | collective-permute-done | bytes 131104 | tf_op jit(solution)/shard_map/ppermute | solution.py:22
  149.5 2.0 %collective-permute-done.36.a3 = bf16[128,512]{1,0:T(8,128)(2,1)S(1)} collective-permute-done((bf16[128,512]{1,0:T(8,128)(2,1)S(1)}, bf16[128,512]{1,0:T(8,128)(2,1)S(1)}, u32[]{:S(2)}, u32[]{:S(2)}) %collective-permute-start.36) | collective-permute-done | bytes 131104 | tf_op jit(solution)/shard_map/ppermute | solution.py:22
  153.3 4.9 %collective-permute-start.45 = (bf16[144,512]{1,0:T(8,128)(2,1)S(1)}, bf16[144,512]{1,0:T(8,128)(2,1)S(1)}, u32[]{:S(2)}, u32[]{:S(2)}) collective-permute-start(bf16[144,512]{1,0:T(8,128)(2,1)S(1)} %get-tuple-element.134), channel_id=1, source_target_pairs={{0,20},{1,21},{2,22},{3,23},{4,16},{5,17},{6,18},{7,19},{8,28},{9,... | collective-permute-start | bytes 442376 | tf_op jit(solution)/shard_map/ppermute | solution.py:22
  158.3 1.8 %collective-permute-start.44 = (bf16[144,512]{1,0:T(8,128)(2,1)S(1)}, bf16[144,512]{1,0:T(8,128)(2,1)S(1)}, u32[]{:S(2)}, u32[]{:S(2)}) collective-permute-start(bf16[144,512]{1,0:T(8,128)(2,1)S(1)} %get-tuple-element.133), channel_id=1, source_target_pairs={{0,16},{1,17},{2,18},{3,19},{4,20},{5,21},{6,22},{7,23},{8,24},{9,... | collective-permute-start | bytes 442376 | tf_op jit(solution)/shard_map/ppermute | solution.py:22
  161.5 11.1 %collective-permute-done.45.r3 = bf16[144,512]{1,0:T(8,128)(2,1)S(1)} collective-permute-done((bf16[144,512]{1,0:T(8,128)(2,1)S(1)}, bf16[144,512]{1,0:T(8,128)(2,1)S(1)}, u32[]{:S(2)}, u32[]{:S(2)}) %collective-permute-start.45) | collective-permute-done | bytes 147488 | tf_op jit(solution)/shard_map/ppermute | solution.py:22
  (118 shorter events, 49.5 us)
Async XLA Ops:
  5.4 21.2 %collective-permute-start.4 = (bf16[1552,128]{1,0:T(8,128)(2,1)S(1)}, bf16[1552,128]{1,0:T(8,128)(2,1)S(1)}, u32[]{:S(2)}, u32[]{:S(2)}) collective-permute-start(bf16[1552,128]{1,0:T(8,128)(2,1)S(1)} %pad_maximum_fusion.a0), channel_id=1, source_target_pairs={{0,8},{1,9},{2,10},{3,11},{4,12},{5,13},{6,14},{7,15},{8,0},{9,1},... | collective-permute-start | bytes 1191944 | tf_op jit(solution)/shard_map/ppermute | solution.py:22
  8.4 26.2 %collective-permute-start.6 = (bf16[128,2048]{1,0:T(8,128)(2,1)}, bf16[128,2048]{1,0:T(8,128)(2,1)S(1)}, u32[]{:S(2)}, u32[]{:S(2)}) collective-permute-start(bf16[128,2048]{1,0:T(8,128)(2,1)} %bitcast.20), channel_id=1, source_target_pairs={{0,16},{1,17},{2,18},{3,19},{4,20},{5,21},{6,22},{7,23},{8,24},{9,... | collective-permute-start | bytes 1572872 | tf_op jit(solution)/shard_map/ppermute | solution.py:22
  17.2 12.9 %collective-permute-start.3 = (bf16[1552,128]{1,0:T(8,128)(2,1)S(1)}, bf16[1552,128]{1,0:T(8,128)(2,1)S(1)}, u32[]{:S(2)}, u32[]{:S(2)}) collective-permute-start(bf16[1552,128]{1,0:T(8,128)(2,1)S(1)} %pad_maximum_fusion.a0), channel_id=1, source_target_pairs={{0,4},{1,5},{2,6},{3,7},{4,0},{5,1},{6,2},{7,3},{8,12},{9,13},{10,... | collective-permute-start | bytes 1191944 | tf_op jit(solution)/shard_map/ppermute | solution.py:22
  18.4 18.5 %collective-permute-start.8 = (bf16[272,512]{1,0:T(8,128)(2,1)S(1)}, bf16[272,512]{1,0:T(8,128)(2,1)S(1)}, u32[]{:S(2)}, u32[]{:S(2)}) collective-permute-start(bf16[272,512]{1,0:T(8,128)(2,1)S(1)} %shard_map.104.rest_0_), channel_id=1, source_target_pairs={{0,8},{1,9},{2,10},{3,11},{4,12},{5,13},{6,14},{7,15},{8,0},{9,1},... | collective-permute-start | bytes 835592 | tf_op jit(solution)/shard_map/ppermute | solution.py:22
  26.6 13.8 %collective-permute-start.5 = (bf16[1552,128]{1,0:T(8,128)(2,1)S(1)}, bf16[1552,128]{1,0:T(8,128)(2,1)S(1)}, u32[]{:S(2)}, u32[]{:S(2)}) collective-permute-start(bf16[1552,128]{1,0:T(8,128)(2,1)S(1)} %collective-permute-done.4.a2), channel_id=1, source_target_pairs={{0,4},{1,5},{2,6},{3,7},{4,0},{5,1},{6,2},{7,3},{8,12},{9,13},{10,... | collective-permute-start | bytes 1191944 | tf_op jit(solution)/shard_map/ppermute | solution.py:22
  28.6 10.3 %collective-permute-start.7 = (bf16[272,512]{1,0:T(8,128)(2,1)S(1)}, bf16[272,512]{1,0:T(8,128)(2,1)S(1)}, u32[]{:S(2)}, u32[]{:S(2)}) collective-permute-start(bf16[272,512]{1,0:T(8,128)(2,1)S(1)} %shard_map.104.rest_0_), channel_id=1, source_target_pairs={{0,2},{1,3},{2,0},{3,1},{4,6},{5,7},{6,4},{7,5},{8,10},{9,11},{10,... | collective-permute-start | bytes 835592 | tf_op jit(solution)/shard_map/ppermute | solution.py:22
  35.3 8.4 %collective-permute-start.9 = (bf16[2,128,512]{2,1,0:T(8,128)(2,1)S(1)}, bf16[2,128,512]{2,1,0:T(8,128)(2,1)S(1)}, u32[]{:S(2)}, u32[]{:S(2)}) collective-permute-start(bf16[2,128,512]{2,1,0:T(8,128)(2,1)S(1)} %get-tuple-element.81), channel_id=1, source_target_pairs={{0,4},{1,5},{2,6},{3,7},{4,0},{5,1},{6,2},{7,3},{8,12},{9,13},{10,... | collective-permute-start | bytes 786440 | tf_op jit(solution)/shard_map/ppermute | solution.py:22
  36.9 9.2 %collective-permute-start.10 = (bf16[2,128,512]{2,1,0:T(8,128)(2,1)S(1)}, bf16[2,128,512]{2,1,0:T(8,128)(2,1)S(1)}, u32[]{:S(2)}, u32[]{:S(2)}) collective-permute-start(bf16[2,128,512]{2,1,0:T(8,128)(2,1)S(1)} %get-tuple-element.82), channel_id=1, source_target_pairs={{0,8},{1,9},{2,10},{3,11},{4,12},{5,13},{6,14},{7,15},{8,0},{9,1},... | collective-permute-start | bytes 786440 | tf_op jit(solution)/shard_map/ppermute | solution.py:22
  36.9 12.5 %collective-permute-start.11 = (bf16[2,128,512]{2,1,0:T(8,128)(2,1)S(1)}, bf16[2,128,512]{2,1,0:T(8,128)(2,1)S(1)}, u32[]{:S(2)}, u32[]{:S(2)}) collective-permute-start(bf16[2,128,512]{2,1,0:T(8,128)(2,1)S(1)} %get-tuple-element.83), channel_id=1, source_target_pairs={{0,12},{1,13},{2,14},{3,15},{4,8},{5,9},{6,10},{7,11},{8,4},{9,5},... | collective-permute-start | bytes 786440 | tf_op jit(solution)/shard_map/ppermute | solution.py:22
  38.9 12.5 %collective-permute-start.12 = (bf16[272,512]{1,0:T(8,128)(2,1)S(1)}, bf16[272,512]{1,0:T(8,128)(2,1)S(1)}, u32[]{:S(2)}, u32[]{:S(2)}) collective-permute-start(bf16[272,512]{1,0:T(8,128)(2,1)S(1)} %collective-permute-done.8.rest_2_), channel_id=1, source_target_pairs={{0,2},{1,3},{2,0},{3,1},{4,6},{5,7},{6,4},{7,5},{8,10},{9,11},{10,... | collective-permute-start | bytes 835592 | tf_op jit(solution)/shard_map/ppermute | solution.py:22
  51.4 15.8 %collective-permute-start.15 = (bf16[272,512]{1,0:T(8,128)(2,1)S(1)}, bf16[272,512]{1,0:T(8,128)(2,1)S(1)}, u32[]{:S(2)}, u32[]{:S(2)}) collective-permute-start(bf16[272,512]{1,0:T(8,128)(2,1)S(1)} %shard_map.104.rest_0_), channel_id=1, source_target_pairs={{0,16},{1,17},{2,18},{3,19},{4,20},{5,21},{6,22},{7,23},{8,24},{9,... | collective-permute-start | bytes 835592 | tf_op jit(solution)/shard_map/ppermute | solution.py:22
  54.8 14.0 %collective-permute-start.14 = (bf16[4,128,512]{2,1,0:T(8,128)(2,1)S(1)}, bf16[4,128,512]{2,1,0:T(8,128)(2,1)S(1)}, u32[]{:S(2)}, u32[]{:S(2)}) collective-permute-start(bf16[4,128,512]{2,1,0:T(8,128)(2,1)S(1)} %get-tuple-element.88), channel_id=1, source_target_pairs={{0,2},{1,3},{2,0},{3,1},{4,6},{5,7},{6,4},{7,5},{8,10},{9,11},{10,... | collective-permute-start | bytes 1572872 | tf_op jit(solution)/shard_map/ppermute | solution.py:22
  67.2 9.5 %collective-permute-start.22 = (bf16[272,512]{1,0:T(8,128)(2,1)S(1)}, bf16[272,512]{1,0:T(8,128)(2,1)S(1)}, u32[]{:S(2)}, u32[]{:S(2)}) collective-permute-start(bf16[272,512]{1,0:T(8,128)(2,1)S(1)} %collective-permute-done.15.rest_4_), channel_id=1, source_target_pairs={{0,8},{1,9},{2,10},{3,11},{4,12},{5,13},{6,14},{7,15},{8,0},{9,1},... | collective-permute-start | bytes 835592 | tf_op jit(solution)/shard_map/ppermute | solution.py:22
  69.5 17.5 %collective-permute-start.18 = (bf16[288,512]{1,0:T(8,128)(2,1)S(1)}, bf16[288,512]{1,0:T(8,128)(2,1)S(1)}, u32[]{:S(2)}, u32[]{:S(2)}) collective-permute-start(bf16[288,512]{1,0:T(8,128)(2,1)S(1)} %get-tuple-element.93), channel_id=1, source_target_pairs={{0,8},{1,9},{2,10},{3,11},{4,12},{5,13},{6,14},{7,15},{8,0},{9,1},... | collective-permute-start | bytes 884744 | tf_op jit(solution)/shard_map/ppermute | solution.py:22
  71.3 18.1 %collective-permute-start.24 = (bf16[288,512]{1,0:T(8,128)(2,1)S(1)}, bf16[288,512]{1,0:T(8,128)(2,1)S(1)}, u32[]{:S(2)}, u32[]{:S(2)}) collective-permute-start(bf16[288,512]{1,0:T(8,128)(2,1)S(1)} %get-tuple-element.93), channel_id=1, source_target_pairs={{0,12},{1,13},{2,14},{3,15},{4,8},{5,9},{6,10},{7,11},{8,4},{9,5},... | collective-permute-start | bytes 884744 | tf_op jit(solution)/shard_map/ppermute | solution.py:22
  72.5 16.9 %collective-permute-start.17 = (bf16[288,512]{1,0:T(8,128)(2,1)S(1)}, bf16[288,512]{1,0:T(8,128)(2,1)S(1)}, u32[]{:S(2)}, u32[]{:S(2)}) collective-permute-start(bf16[288,512]{1,0:T(8,128)(2,1)S(1)} %get-tuple-element.92.p0.own0), channel_id=1, source_target_pairs={{0,4},{1,5},{2,6},{3,7},{4,0},{5,1},{6,2},{7,3},{8,12},{9,13},{10,... | collective-permute-start | bytes 884744 | tf_op jit(solution)/shard_map/ppermute | solution.py:22
  73.0 9.6 %collective-permute-start.19 = (bf16[272,512]{1,0:T(8,128)(2,1)S(1)}, bf16[272,512]{1,0:T(8,128)(2,1)S(1)}, u32[]{:S(2)}, u32[]{:S(2)}) collective-permute-start(bf16[272,512]{1,0:T(8,128)(2,1)S(1)} %collective-permute-done.15.rest_4_), channel_id=1, source_target_pairs={{0,2},{1,3},{2,0},{3,1},{4,6},{5,7},{6,4},{7,5},{8,10},{9,11},{10,... | collective-permute-start | bytes 835592 | tf_op jit(solution)/shard_map/ppermute | solution.py:22
  76.7 10.2 %collective-permute-start.23 = (bf16[272,512]{1,0:T(8,128)(2,1)S(1)}, bf16[272,512]{1,0:T(8,128)(2,1)S(1)}, u32[]{:S(2)}, u32[]{:S(2)}) collective-permute-start(bf16[272,512]{1,0:T(8,128)(2,1)S(1)} %collective-permute-done.22.rest_6_), channel_id=1, source_target_pairs={{0,2},{1,3},{2,0},{3,1},{4,6},{5,7},{6,4},{7,5},{8,10},{9,11},{10,... | collective-permute-start | bytes 835592 | tf_op jit(solution)/shard_map/ppermute | solution.py:22
  96.6 14.6 %collective-permute-start.31 = (bf16[528,512]{1,0:T(8,128)(2,1)S(1)}, bf16[528,512]{1,0:T(8,128)(2,1)S(1)}, u32[]{:S(2)}, u32[]{:S(2)}) collective-permute-start(bf16[528,512]{1,0:T(8,128)(2,1)S(1)} %get-tuple-element.104), channel_id=1, source_target_pairs={{0,2},{1,3},{2,0},{3,1},{4,6},{5,7},{6,4},{7,5},{8,10},{9,11},{10,... | collective-permute-start | bytes 1622024 | tf_op jit(solution)/shard_map/ppermute | solution.py:22
  98.4 12.8 %collective-permute-start.30 = (bf16[2,128,512]{2,1,0:T(8,128)(2,1)S(1)}, bf16[2,128,512]{2,1,0:T(8,128)(2,1)S(1)}, u32[]{:S(2)}, u32[]{:S(2)}) collective-permute-start(bf16[2,128,512]{2,1,0:T(8,128)(2,1)S(1)} %get-tuple-element.109), channel_id=1, source_target_pairs={{0,4},{1,5},{2,6},{3,7},{4,0},{5,1},{6,2},{7,3},{8,12},{9,13},{10,... | collective-permute-start | bytes 786440 | tf_op jit(solution)/shard_map/ppermute | solution.py:22
  99.0 12.7 %collective-permute-start.32 = (bf16[2,128,512]{2,1,0:T(8,128)(2,1)S(1)}, bf16[2,128,512]{2,1,0:T(8,128)(2,1)S(1)}, u32[]{:S(2)}, u32[]{:S(2)}) collective-permute-start(bf16[2,128,512]{2,1,0:T(8,128)(2,1)S(1)} %get-tuple-element.113), channel_id=1, source_target_pairs={{0,8},{1,9},{2,10},{3,11},{4,12},{5,13},{6,14},{7,15},{8,0},{9,1},... | collective-permute-start | bytes 786440 | tf_op jit(solution)/shard_map/ppermute | solution.py:22
  99.6 14.0 %collective-permute-start.33 = (bf16[2,128,512]{2,1,0:T(8,128)(2,1)S(1)}, bf16[2,128,512]{2,1,0:T(8,128)(2,1)S(1)}, u32[]{:S(2)}, u32[]{:S(2)}) collective-permute-start(bf16[2,128,512]{2,1,0:T(8,128)(2,1)S(1)} %get-tuple-element.114), channel_id=1, source_target_pairs={{0,12},{1,13},{2,14},{3,15},{4,8},{5,9},{6,10},{7,11},{8,4},{9,5},... | collective-permute-start | bytes 786440 | tf_op jit(solution)/shard_map/ppermute | solution.py:22
  111.4 15.2 %collective-permute-start.38 = (bf16[528,512]{1,0:T(8,128)(2,1)S(1)}, bf16[528,512]{1,0:T(8,128)(2,1)S(1)}, u32[]{:S(2)}, u32[]{:S(2)}) collective-permute-start(bf16[528,512]{1,0:T(8,128)(2,1)S(1)} %get-tuple-element.123), channel_id=1, source_target_pairs={{0,8},{1,9},{2,10},{3,11},{4,12},{5,13},{6,14},{7,15},{8,0},{9,1},... | collective-permute-start | bytes 1622024 | tf_op jit(solution)/shard_map/ppermute | solution.py:22
  113.7 12.8 %collective-permute-start.37 = (bf16[4,128,512]{2,1,0:T(8,128)(2,1)S(1)}, bf16[4,128,512]{2,1,0:T(8,128)(2,1)S(1)}, u32[]{:S(2)}, u32[]{:S(2)}) collective-permute-start(bf16[4,128,512]{2,1,0:T(8,128)(2,1)S(1)} %shard_map.113.same), channel_id=1, source_target_pairs={{0,2},{1,3},{2,0},{3,1},{4,6},{5,7},{6,4},{7,5},{8,10},{9,11},{10,... | collective-permute-start | bytes 1572872 | tf_op jit(solution)/shard_map/ppermute | solution.py:22
  114.9 11.7 %collective-permute-start.40 = (bf16[4,128,512]{2,1,0:T(8,128)(2,1)S(1)}, bf16[4,128,512]{2,1,0:T(8,128)(2,1)S(1)}, u32[]{:S(2)}, u32[]{:S(2)}) collective-permute-start(bf16[4,128,512]{2,1,0:T(8,128)(2,1)S(1)} %shard_map.113.same), channel_id=1, source_target_pairs={{0,1},{1,0},{2,3},{3,2},{4,5},{5,4},{6,7},{7,6},{8,9},{9,8},{10,11... | collective-permute-start | bytes 1572872 | tf_op jit(solution)/shard_map/ppermute | solution.py:22
  131.3 41.8 %all-to-all-start = ((bf16[8,128,512]{2,1,0:T(8,128)(2,1)}), bf16[8,128,512]{2,1,0:T(8,128)(2,1)S(1)}, u32[]{:S(2)}, u32[]{:S(2)}) async-start(bf16[8,128,512]{2,1,0:T(8,128)(2,1)} %shard_map.117), calls=%async_computation | async-start | bytes 2097152 | tf_op jit(solution)/shard_map/all_to_all | solution.py:406
  135.1 16.4 %collective-permute-start.41 = (bf16[512,512]{1,0:T(8,128)(2,1)S(1)}, bf16[512,512]{1,0:T(8,128)(2,1)S(1)}, u32[]{:S(2)}, u32[]{:S(2)}) collective-permute-start(bf16[512,512]{1,0:T(8,128)(2,1)S(1)} %copy-done.5), channel_id=1, source_target_pairs={{0,2},{1,3},{2,0},{3,1},{4,6},{5,7},{6,4},{7,5},{8,10},{9,11},{10,... | collective-permute-start | bytes 1572872 | tf_op jit(solution)/shard_map/ppermute | solution.py:22
  136.4 13.2 %collective-permute-start.35 = (bf16[128,512]{1,0:T(8,128)(2,1)}, bf16[128,512]{1,0:T(8,128)(2,1)S(1)}, u32[]{:S(2)}, u32[]{:S(2)}) collective-permute-start(bf16[128,512]{1,0:T(8,128)(2,1)} %copy-done.6), channel_id=1, source_target_pairs={{0,4},{1,5},{2,6},{3,7},{4,0},{5,1},{6,2},{7,3},{8,12},{9,13},{10,... | collective-permute-start | bytes 393224 | tf_op jit(solution)/shard_map/ppermute | solution.py:22
  138.2 13.3 %collective-permute-start.36 = (bf16[128,512]{1,0:T(8,128)(2,1)S(1)}, bf16[128,512]{1,0:T(8,128)(2,1)S(1)}, u32[]{:S(2)}, u32[]{:S(2)}) collective-permute-start(bf16[128,512]{1,0:T(8,128)(2,1)S(1)} %get-tuple-element.119), channel_id=1, source_target_pairs={{0,5},{1,4},{2,7},{3,6},{4,1},{5,0},{6,3},{7,2},{8,13},{9,12},{10,... | collective-permute-start | bytes 393224 | tf_op jit(solution)/shard_map/ppermute | solution.py:22
  153.3 19.3 %collective-permute-start.45 = (bf16[144,512]{1,0:T(8,128)(2,1)S(1)}, bf16[144,512]{1,0:T(8,128)(2,1)S(1)}, u32[]{:S(2)}, u32[]{:S(2)}) collective-permute-start(bf16[144,512]{1,0:T(8,128)(2,1)S(1)} %get-tuple-element.134), channel_id=1, source_target_pairs={{0,20},{1,21},{2,22},{3,23},{4,16},{5,17},{6,18},{7,19},{8,28},{9,... | collective-permute-start | bytes 442376 | tf_op jit(solution)/shard_map/ppermute | solution.py:22
  158.3 14.3 %collective-permute-start.43 = (bf16[144,512]{1,0:T(8,128)(2,1)S(1)}, bf16[144,512]{1,0:T(8,128)(2,1)S(1)}, u32[]{:S(2)}, u32[]{:S(2)}) collective-permute-start(bf16[144,512]{1,0:T(8,128)(2,1)S(1)} %get-tuple-element.132), channel_id=1, source_target_pairs={{0,4},{1,5},{2,6},{3,7},{4,0},{5,1},{6,2},{7,3},{8,12},{9,13},{10,... | collective-permute-start | bytes 442376 | tf_op jit(solution)/shard_map/ppermute | solution.py:22
  158.3 15.9 %collective-permute-start.44 = (bf16[144,512]{1,0:T(8,128)(2,1)S(1)}, bf16[144,512]{1,0:T(8,128)(2,1)S(1)}, u32[]{:S(2)}, u32[]{:S(2)}) collective-permute-start(bf16[144,512]{1,0:T(8,128)(2,1)S(1)} %get-tuple-element.133), channel_id=1, source_target_pairs={{0,16},{1,17},{2,18},{3,19},{4,20},{5,21},{6,22},{7,23},{8,24},{9,... | collective-permute-start | bytes 442376 | tf_op jit(solution)/shard_map/ppermute | solution.py:22
  (27 other events, 186.4 us)

commit v6 on v5

--- a/solution.py
+++ b/solution.py
@@ -110,7 +110,7 @@
                 if other == 0:
                     keep[member ^ i, pair] = total
                 else:
-                    send[member ^ i, pair] = total.astype(BF16)
+                    send[member ^ i, pair] = total.astype(send.dtype)
 
 
 def pair_sum_kernel(ids, kept, received, mine, send):
@@ -337,7 +337,7 @@
     source[0] = after(source[0], y0, z1)
     piece = (GROUP, dests // 2, tile, quarter)
     kept, sent = call(
-        gather_kernel, [shape(piece, F32), shape(piece, BF16)],
+        gather_kernel, [shape(piece, F32)] * 2,
         ids, lists_of, *tiles_of, *source,
         scratch=[pltpu.VMEM((rows, tile, quarter), BF16)],
         smem=2, flops=2 * GROUP * dests * slots * tile * tile * quarter,

time: 177 us -> 177 us (level)
  no operation moved by 1% of the time
where the time goes in v6:
time: 177 us
  waiting for transfers between devices  99.3 us (56%)
  starting transfers between devices  51.2 us (29%)
  Pallas kernels  21.8 us (12%)
  local copies, waits for them, and re-layouts  2.07 us (1%)
    ppermute x49, waiting for transfers between devices, swap(): return lax.ppermute(value, BOTH, [(i, i ^ mask) for i in range(total)])  99.3 us
    ppermute x49, starting transfers between devices, swap(): return lax.ppermute(value, BOTH, [(i, i ^ mask) for i in range(total)])  47.4 us
    pallas_call x19, Pallas kernels, call(): pl.pallas_call(kernel, out_shape=outs, in_specs=[SMEM] * smem + [VMEM] *...  21.8 us
    all_to_all x1, starting transfers between devices, chip_body(): spread_all = lax.all_to_all(spread, 'row', 0, 0, tiled=True)  3.77 us
  transfers between devices with their start and end apart: 50, of which 27 were waited for; matrix products, arithmetic and copies ran while one was open for 1% of the time, Pallas kernels for 8%

profile of v6, /device:TPU:0, one launch (start us, length us, event | category | flops | bytes accessed | tf_op | source)
XLA Modules:
  0.0 177.0 jit_solution(6428228498646274475)
XLA Ops:
  5.4 3.0 %collective-permute-start.4 = (bf16[1552,128]{1,0:T(8,128)(2,1)S(1)}, bf16[1552,128]{1,0:T(8,128)(2,1)S(1)}, u32[]{:S(2)}, u32[]{:S(2)}) collective-permute-start(bf16[1552,128]{1,0:T(8,128)(2,1)S(1)} %pad_maximum_fusion.a0), channel_id=1, source_target_pairs={{0,8},{1,9},{2,10},{3,11},{4,12},{5,13},{6,14},{7,15},{8,0},{9,1},... | collective-permute-start | bytes 1191944 | tf_op jit(solution)/shard_map/ppermute | solution.py:22
  8.4 2.6 %collective-permute-start.6 = (bf16[128,2048]{1,0:T(8,128)(2,1)}, bf16[128,2048]{1,0:T(8,128)(2,1)S(1)}, u32[]{:S(2)}, u32[]{:S(2)}) collective-permute-start(bf16[128,2048]{1,0:T(8,128)(2,1)} %bitcast.20), channel_id=1, source_target_pairs={{0,16},{1,17},{2,18},{3,19},{4,20},{5,21},{6,22},{7,23},{8,24},{9,... | collective-permute-start | bytes 1572872 | tf_op jit(solution)/shard_map/ppermute | solution.py:22
  12.5 2.9 %collective-permute-done.1.p2 = bf16[80,512]{1,0:T(8,128)(2,1)S(1)} collective-permute-done((bf16[80,512]{1,0:T(8,128)(2,1)S(1)}, bf16[80,512]{1,0:T(8,128)(2,1)S(1)}, u32[]{:S(2)}, u32[]{:S(2)}) %collective-permute-start.1) | collective-permute-done | bytes 81952 | tf_op jit(solution)/shard_map/ppermute | solution.py:22
  18.9 7.7 %collective-permute-done.4.a2 = bf16[1552,128]{1,0:T(8,128)(2,1)S(1)} collective-permute-done((bf16[1552,128]{1,0:T(8,128)(2,1)S(1)}, bf16[1552,128]{1,0:T(8,128)(2,1)S(1)}, u32[]{:S(2)}, u32[]{:S(2)}) %collective-permute-start.4) | collective-permute-done | bytes 397344 | tf_op jit(solution)/shard_map/ppermute | solution.py:22
  26.6 2.0 %collective-permute-start.5 = (bf16[1552,128]{1,0:T(8,128)(2,1)S(1)}, bf16[1552,128]{1,0:T(8,128)(2,1)S(1)}, u32[]{:S(2)}, u32[]{:S(2)}) collective-permute-start(bf16[1552,128]{1,0:T(8,128)(2,1)S(1)} %collective-permute-done.4.a2), channel_id=1, source_target_pairs={{0,4},{1,5},{2,6},{3,7},{4,0},{5,1},{6,2},{7,3},{8,12},{9,13},{10,... | collective-permute-start | bytes 1191944 | tf_op jit(solution)/shard_map/ppermute | solution.py:22
  30.1 4.5 %collective-permute-done.6.far = bf16[128,2048]{1,0:T(8,128)(2,1)S(1)} collective-permute-done((bf16[128,2048]{1,0:T(8,128)(2,1)}, bf16[128,2048]{1,0:T(8,128)(2,1)S(1)}, u32[]{:S(2)}, u32[]{:S(2)}) %collective-permute-start.6) | collective-permute-done | bytes 524320 | tf_op jit(solution)/shard_map/ppermute | solution.py:22
  36.9 2.0 %collective-permute-start.11 = (bf16[2,128,512]{2,1,0:T(8,128)(2,1)S(1)}, bf16[2,128,512]{2,1,0:T(8,128)(2,1)S(1)}, u32[]{:S(2)}, u32[]{:S(2)}) collective-permute-start(bf16[2,128,512]{2,1,0:T(8,128)(2,1)S(1)} %get-tuple-element.83), channel_id=1, source_target_pairs={{0,12},{1,13},{2,14},{3,15},{4,8},{5,9},{6,10},{7,11},{8,4},{9,5},... | collective-permute-start | bytes 786440 | tf_op jit(solution)/shard_map/ppermute | solution.py:22
  40.4 3.3 %collective-permute-done.9.h1 = bf16[2,128,512]{2,1,0:T(8,128)(2,1)S(1)} collective-permute-done((bf16[2,128,512]{2,1,0:T(8,128)(2,1)S(1)}, bf16[2,128,512]{2,1,0:T(8,128)(2,1)S(1)}, u32[]{:S(2)}, u32[]{:S(2)}) %collective-permute-start.9) | collective-permute-done | bytes 262176 | tf_op jit(solution)/shard_map/ppermute | solution.py:22
  43.7 2.4 %collective-permute-done.10.h2 = bf16[2,128,512]{2,1,0:T(8,128)(2,1)S(1)} collective-permute-done((bf16[2,128,512]{2,1,0:T(8,128)(2,1)S(1)}, bf16[2,128,512]{2,1,0:T(8,128)(2,1)S(1)}, u32[]{:S(2)}, u32[]{:S(2)}) %collective-permute-start.10) | collective-permute-done | bytes 262176 | tf_op jit(solution)/shard_map/ppermute | solution.py:22
  46.1 3.3 %collective-permute-done.11.h3 = bf16[2,128,512]{2,1,0:T(8,128)(2,1)S(1)} collective-permute-done((bf16[2,128,512]{2,1,0:T(8,128)(2,1)S(1)}, bf16[2,128,512]{2,1,0:T(8,128)(2,1)S(1)}, u32[]{:S(2)}, u32[]{:S(2)}) %collective-permute-start.11) | collective-permute-done | bytes 262176 | tf_op jit(solution)/shard_map/ppermute | solution.py:22
  49.4 1.9 %shard_map.105 = (f32[4,2,128,512]{3,2,1,0:T(8,128)S(1)}, f32[4,2,128,512]{3,2,1,0:T(8,128)S(1)}) custom-call(s32[9]{0:T(128)S(1)} %stack.42.ids, s32[4,12]{1,0:T(4,128)S(1)} %maximum_convert_fusion.lists, bf16[1552,128]{1,0:T(8,128)(2,1)S(1)} %pad_maximum_fusion.a0, bf16[1552,128]{1,0:T(8,128)(2,1)S(1)} %collective-permute-done.3.a1, ...), custom_call_target="tpu_custom_call" | custom-call | flops 805306368 | bytes 6832356 | tf_op jit(solution)/shard_map/pallas_call | solution.py:36
  52.8 2.8 %collective-permute-done.13.received = f32[4,2,128,512]{3,2,1,0:T(8,128)S(1)} collective-permute-done((f32[4,2,128,512]{3,2,1,0:T(8,128)S(1)}, f32[4,2,128,512]{3,2,1,0:T(8,128)S(1)}, u32[]{:S(2)}, u32[]{:S(2)}) %collective-permute-start.13) | collective-permute-done | bytes 2097184 | tf_op jit(solution)/shard_map/ppermute | solution.py:22
  60.3 4.5 %collective-permute-done.20.o2 = bf16[128,512]{1,0:T(8,128)(2,1)S(1)} collective-permute-done((bf16[128,512]{1,0:T(8,128)(2,1)S(1)}, bf16[128,512]{1,0:T(8,128)(2,1)S(1)}, u32[]{:S(2)}, u32[]{:S(2)}) %collective-permute-start.20) | collective-permute-done | bytes 131104 | tf_op jit(solution)/shard_map/ppermute | solution.py:22
  68.5 1.8 %collective-permute-done.14.received = bf16[4,128,512]{2,1,0:T(8,128)(2,1)S(1)} collective-permute-done((bf16[4,128,512]{2,1,0:T(8,128)(2,1)S(1)}, bf16[4,128,512]{2,1,0:T(8,128)(2,1)S(1)}, u32[]{:S(2)}, u32[]{:S(2)}) %collective-permute-start.14) | collective-permute-done | bytes 524320 | tf_op jit(solution)/shard_map/ppermute | solution.py:22
  71.3 2.7 %collective-permute-start.24 = (bf16[288,512]{1,0:T(8,128)(2,1)S(1)}, bf16[288,512]{1,0:T(8,128)(2,1)S(1)}, u32[]{:S(2)}, u32[]{:S(2)}) collective-permute-start(bf16[288,512]{1,0:T(8,128)(2,1)S(1)} %get-tuple-element.93), channel_id=1, source_target_pairs={{0,12},{1,13},{2,14},{3,15},{4,8},{5,9},{6,10},{7,11},{8,4},{9,5},... | collective-permute-start | bytes 884744 | tf_op jit(solution)/shard_map/ppermute | solution.py:22
  78.2 5.9 %collective-permute-done.19.rest_5_ = bf16[272,512]{1,0:T(8,128)(2,1)S(1)} collective-permute-done((bf16[272,512]{1,0:T(8,128)(2,1)S(1)}, bf16[272,512]{1,0:T(8,128)(2,1)S(1)}, u32[]{:S(2)}, u32[]{:S(2)}) %collective-permute-start.19) | collective-permute-done | bytes 278560 | tf_op jit(solution)/shard_map/ppermute | solution.py:22
  84.1 3.4 %collective-permute-done.23.rest_7_ = bf16[272,512]{1,0:T(8,128)(2,1)S(1)} collective-permute-done((bf16[272,512]{1,0:T(8,128)(2,1)S(1)}, bf16[272,512]{1,0:T(8,128)(2,1)S(1)}, u32[]{:S(2)}, u32[]{:S(2)}) %collective-permute-start.23) | collective-permute-done | bytes 278560 | tf_op jit(solution)/shard_map/ppermute | solution.py:22
  87.5 1.8 %collective-permute-done.24.p3.own1 = bf16[288,512]{1,0:T(8,128)(2,1)S(1)} collective-permute-done((bf16[288,512]{1,0:T(8,128)(2,1)S(1)}, bf16[288,512]{1,0:T(8,128)(2,1)S(1)}, u32[]{:S(2)}, u32[]{:S(2)}) %collective-permute-start.24) | collective-permute-done | bytes 294944 | tf_op jit(solution)/shard_map/ppermute | solution.py:22
  91.4 3.5 %shard_map.109 = (bf16[128,512]{1,0:T(8,128)(2,1)S(1)}, bf16[128,512]{1,0:T(8,128)(2,1)S(1)}, bf16[128,512]{1,0:T(8,128)(2,1)S(1)}, bf16[128,512]{1,0:T(8,128)(2...) custom-call(s32[9]{0:T(128)S(1)} %stack.42.ids, ...), custom_call_target="tpu_custom_call" | custom-call | flops 2147483648 | bytes 9306148 | tf_op jit(solution)/shard_map/pallas_call | solution.py:36
  99.6 2.4 %collective-permute-start.33 = (bf16[2,128,512]{2,1,0:T(8,128)(2,1)S(1)}, bf16[2,128,512]{2,1,0:T(8,128)(2,1)S(1)}, u32[]{:S(2)}, u32[]{:S(2)}) collective-permute-start(bf16[2,128,512]{2,1,0:T(8,128)(2,1)S(1)} %get-tuple-element.114), channel_id=1, source_target_pairs={{0,12},{1,13},{2,14},{3,15},{4,8},{5,9},{6,10},{7,11},{8,4},{9,5},... | collective-permute-start | bytes 786440 | tf_op jit(solution)/shard_map/ppermute | solution.py:22
  103.4 7.9 %collective-permute-done.31.received = bf16[528,512]{1,0:T(8,128)(2,1)S(1)} collective-permute-done((bf16[528,512]{1,0:T(8,128)(2,1)S(1)}, bf16[528,512]{1,0:T(8,128)(2,1)S(1)}, u32[]{:S(2)}, u32[]{:S(2)}) %collective-permute-start.31) | collective-permute-done | bytes 540704 | tf_op jit(solution)/shard_map/ppermute | solution.py:22
  111.7 1.9 %collective-permute-done.33.vxz = bf16[2,128,512]{2,1,0:T(8,128)(2,1)S(1)} collective-permute-done((bf16[2,128,512]{2,1,0:T(8,128)(2,1)S(1)}, bf16[2,128,512]{2,1,0:T(8,128)(2,1)S(1)}, u32[]{:S(2)}, u32[]{:S(2)}) %collective-permute-start.33) | collective-permute-done | bytes 262176 | tf_op jit(solution)/shard_map/ppermute | solution.py:22
  114.8 11.7 %collective-permute-done.37.same = bf16[4,128,512]{2,1,0:T(8,128)(2,1)S(1)} collective-permute-done((bf16[4,128,512]{2,1,0:T(8,128)(2,1)S(1)}, bf16[4,128,512]{2,1,0:T(8,128)(2,1)S(1)}, u32[]{:S(2)}, u32[]{:S(2)}) %collective-permute-start.37) | collective-permute-done | bytes 524320 | tf_op jit(solution)/shard_map/ppermute | solution.py:22
  126.6 1.8 %shard_map.116.rest_0_ = f32[8,128,512]{2,1,0:T(8,128)S(1)} custom-call(s32[9]{0:T(128)S(1)} %stack.42.ids, s32[4,12]{1,0:T(4,128)S(1)} %maximum_convert_fusion.lists, bf16[1552,128]{1,0:T(8,128)(2,1)S(1)} %pad_maximum_fusion.a0, bf16[1552,128]{1,0:T(8,128)(2,1)S(1)} %collective-permute-done.3.a1, bf16[1552,128]{1,0:T(8,128)(2,1)S(1)} %collective-permute-done.4.a2, ...), custom_call_target="tpu_custom_call" | custom-call | flops 402653184 | bytes 4735204 | tf_op jit(solution)/shard_map/pallas_call | solution.py:36
  128.5 2.8 %shard_map.117 = bf16[8,128,512]{2,1,0:T(8,128)(2,1)} custom-call(s32[9]{0:T(128)S(1)} %stack.42.ids, s32[4,12]{1,0:T(4,128)S(1)} %maximum_convert_fusion.lists, bf16[1552,128]{1,0:T(8,128)(2,1)S(1)} %pad_maximum_fusion.a0, bf16[1552,128]{1,0:T(8,128)(2,1)S(1)} %collective-permute-done.3.a1, bf16[1552,128]{1,0:T(8,128)(2,1)S(1)} %collective-permute-done.4.a2, ...), custom_call_target="tpu_custom_call" | custom-call | flops 402653184 | bytes 5783780 | tf_op jit(solution)/shard_map/pallas_call | solution.py:36
  131.3 3.8 %all-to-all-start = ((bf16[8,128,512]{2,1,0:T(8,128)(2,1)}), bf16[8,128,512]{2,1,0:T(8,128)(2,1)S(1)}, u32[]{:S(2)}, u32[]{:S(2)}) async-start(bf16[8,128,512]{2,1,0:T(8,128)(2,1)} %shard_map.117), calls=%async_computation | async-start | bytes 2097152 | tf_op jit(solution)/shard_map/all_to_all | solution.py:406
  136.3 1.9 %collective-permute-start.35 = (bf16[128,512]{1,0:T(8,128)(2,1)}, bf16[128,512]{1,0:T(8,128)(2,1)S(1)}, u32[]{:S(2)}, u32[]{:S(2)}) collective-permute-start(bf16[128,512]{1,0:T(8,128)(2,1)} %copy-done.6), channel_id=1, source_target_pairs={{0,4},{1,5},{2,6},{3,7},{4,0},{5,1},{6,2},{7,3},{8,12},{9,13},{10,... | collective-permute-start | bytes 393224 | tf_op jit(solution)/shard_map/ppermute | solution.py:22
  138.3 11.1 %collective-permute-done.35.a2 = bf16[128,512]{1,0:T(8,128)(2,1)S(1)} collective-permute-done((bf16[128,512]{1,0:T(8,128)(2,1)}, bf16[128,512]{1,0:T(8,128)(2,1)S(1)}, u32[]{:S(2)}, u32[]{:S(2)}) %collective-permute-start.35) | collective-permute-done | bytes 131104 | tf_op jit(solution)/shard_map/ppermute | solution.py:22
  149.4 2.1 %collective-permute-done.36.a3 = bf16[128,512]{1,0:T(8,128)(2,1)S(1)} collective-permute-done((bf16[128,512]{1,0:T(8,128)(2,1)S(1)}, bf16[128,512]{1,0:T(8,128)(2,1)S(1)}, u32[]{:S(2)}, u32[]{:S(2)}) %collective-permute-start.36) | collective-permute-done | bytes 131104 | tf_op jit(solution)/shard_map/ppermute | solution.py:22
  153.3 5.0 %collective-permute-start.45 = (bf16[144,512]{1,0:T(8,128)(2,1)S(1)}, bf16[144,512]{1,0:T(8,128)(2,1)S(1)}, u32[]{:S(2)}, u32[]{:S(2)}) collective-permute-start(bf16[144,512]{1,0:T(8,128)(2,1)S(1)} %get-tuple-element.134), channel_id=1, source_target_pairs={{0,20},{1,21},{2,22},{3,23},{4,16},{5,17},{6,18},{7,19},{8,28},{9,... | collective-permute-start | bytes 442376 | tf_op jit(solution)/shard_map/ppermute | solution.py:22
  158.3 1.8 %collective-permute-start.44 = (bf16[144,512]{1,0:T(8,128)(2,1)S(1)}, bf16[144,512]{1,0:T(8,128)(2,1)S(1)}, u32[]{:S(2)}, u32[]{:S(2)}) collective-permute-start(bf16[144,512]{1,0:T(8,128)(2,1)S(1)} %get-tuple-element.133), channel_id=1, source_target_pairs={{0,16},{1,17},{2,18},{3,19},{4,20},{5,21},{6,22},{7,23},{8,24},{9,... | collective-permute-start | bytes 442376 | tf_op jit(solution)/shard_map/ppermute | solution.py:22
  161.5 11.0 %collective-permute-done.45.r3 = bf16[144,512]{1,0:T(8,128)(2,1)S(1)} collective-permute-done((bf16[144,512]{1,0:T(8,128)(2,1)S(1)}, bf16[144,512]{1,0:T(8,128)(2,1)S(1)}, u32[]{:S(2)}, u32[]{:S(2)}) %collective-permute-start.45) | collective-permute-done | bytes 147488 | tf_op jit(solution)/shard_map/ppermute | solution.py:22
  (118 shorter events, 48.9 us)
Async XLA Ops:
  5.4 21.2 %collective-permute-start.4 = (bf16[1552,128]{1,0:T(8,128)(2,1)S(1)}, bf16[1552,128]{1,0:T(8,128)(2,1)S(1)}, u32[]{:S(2)}, u32[]{:S(2)}) collective-permute-start(bf16[1552,128]{1,0:T(8,128)(2,1)S(1)} %pad_maximum_fusion.a0), channel_id=1, source_target_pairs={{0,8},{1,9},{2,10},{3,11},{4,12},{5,13},{6,14},{7,15},{8,0},{9,1},... | collective-permute-start | bytes 1191944 | tf_op jit(solution)/shard_map/ppermute | solution.py:22
  8.4 26.2 %collective-permute-start.6 = (bf16[128,2048]{1,0:T(8,128)(2,1)}, bf16[128,2048]{1,0:T(8,128)(2,1)S(1)}, u32[]{:S(2)}, u32[]{:S(2)}) collective-permute-start(bf16[128,2048]{1,0:T(8,128)(2,1)} %bitcast.20), channel_id=1, source_target_pairs={{0,16},{1,17},{2,18},{3,19},{4,20},{5,21},{6,22},{7,23},{8,24},{9,... | collective-permute-start | bytes 1572872 | tf_op jit(solution)/shard_map/ppermute | solution.py:22
  17.2 12.9 %collective-permute-start.3 = (bf16[1552,128]{1,0:T(8,128)(2,1)S(1)}, bf16[1552,128]{1,0:T(8,128)(2,1)S(1)}, u32[]{:S(2)}, u32[]{:S(2)}) collective-permute-start(bf16[1552,128]{1,0:T(8,128)(2,1)S(1)} %pad_maximum_fusion.a0), channel_id=1, source_target_pairs={{0,4},{1,5},{2,6},{3,7},{4,0},{5,1},{6,2},{7,3},{8,12},{9,13},{10,... | collective-permute-start | bytes 1191944 | tf_op jit(solution)/shard_map/ppermute | solution.py:22
  18.4 18.5 %collective-permute-start.8 = (bf16[272,512]{1,0:T(8,128)(2,1)S(1)}, bf16[272,512]{1,0:T(8,128)(2,1)S(1)}, u32[]{:S(2)}, u32[]{:S(2)}) collective-permute-start(bf16[272,512]{1,0:T(8,128)(2,1)S(1)} %shard_map.104.rest_0_), channel_id=1, source_target_pairs={{0,8},{1,9},{2,10},{3,11},{4,12},{5,13},{6,14},{7,15},{8,0},{9,1},... | collective-permute-start | bytes 835592 | tf_op jit(solution)/shard_map/ppermute | solution.py:22
  26.6 13.8 %collective-permute-start.5 = (bf16[1552,128]{1,0:T(8,128)(2,1)S(1)}, bf16[1552,128]{1,0:T(8,128)(2,1)S(1)}, u32[]{:S(2)}, u32[]{:S(2)}) collective-permute-start(bf16[1552,128]{1,0:T(8,128)(2,1)S(1)} %collective-permute-done.4.a2), channel_id=1, source_target_pairs={{0,4},{1,5},{2,6},{3,7},{4,0},{5,1},{6,2},{7,3},{8,12},{9,13},{10,... | collective-permute-start | bytes 1191944 | tf_op jit(solution)/shard_map/ppermute | solution.py:22
  28.6 10.3 %collective-permute-start.7 = (bf16[272,512]{1,0:T(8,128)(2,1)S(1)}, bf16[272,512]{1,0:T(8,128)(2,1)S(1)}, u32[]{:S(2)}, u32[]{:S(2)}) collective-permute-start(bf16[272,512]{1,0:T(8,128)(2,1)S(1)} %shard_map.104.rest_0_), channel_id=1, source_target_pairs={{0,2},{1,3},{2,0},{3,1},{4,6},{5,7},{6,4},{7,5},{8,10},{9,11},{10,... | collective-permute-start | bytes 835592 | tf_op jit(solution)/shard_map/ppermute | solution.py:22
  35.3 8.4 %collective-permute-start.9 = (bf16[2,128,512]{2,1,0:T(8,128)(2,1)S(1)}, bf16[2,128,512]{2,1,0:T(8,128)(2,1)S(1)}, u32[]{:S(2)}, u32[]{:S(2)}) collective-permute-start(bf16[2,128,512]{2,1,0:T(8,128)(2,1)S(1)} %get-tuple-element.81), channel_id=1, source_target_pairs={{0,4},{1,5},{2,6},{3,7},{4,0},{5,1},{6,2},{7,3},{8,12},{9,13},{10,... | collective-permute-start | bytes 786440 | tf_op jit(solution)/shard_map/ppermute | solution.py:22
  36.9 9.2 %collective-permute-start.10 = (bf16[2,128,512]{2,1,0:T(8,128)(2,1)S(1)}, bf16[2,128,512]{2,1,0:T(8,128)(2,1)S(1)}, u32[]{:S(2)}, u32[]{:S(2)}) collective-permute-start(bf16[2,128,512]{2,1,0:T(8,128)(2,1)S(1)} %get-tuple-element.82), channel_id=1, source_target_pairs={{0,8},{1,9},{2,10},{3,11},{4,12},{5,13},{6,14},{7,15},{8,0},{9,1},... | collective-permute-start | bytes 786440 | tf_op jit(solution)/shard_map/ppermute | solution.py:22
  36.9 12.5 %collective-permute-start.11 = (bf16[2,128,512]{2,1,0:T(8,128)(2,1)S(1)}, bf16[2,128,512]{2,1,0:T(8,128)(2,1)S(1)}, u32[]{:S(2)}, u32[]{:S(2)}) collective-permute-start(bf16[2,128,512]{2,1,0:T(8,128)(2,1)S(1)} %get-tuple-element.83), channel_id=1, source_target_pairs={{0,12},{1,13},{2,14},{3,15},{4,8},{5,9},{6,10},{7,11},{8,4},{9,5},... | collective-permute-start | bytes 786440 | tf_op jit(solution)/shard_map/ppermute | solution.py:22
  38.9 12.4 %collective-permute-start.12 = (bf16[272,512]{1,0:T(8,128)(2,1)S(1)}, bf16[272,512]{1,0:T(8,128)(2,1)S(1)}, u32[]{:S(2)}, u32[]{:S(2)}) collective-permute-start(bf16[272,512]{1,0:T(8,128)(2,1)S(1)} %collective-permute-done.8.rest_2_), channel_id=1, source_target_pairs={{0,2},{1,3},{2,0},{3,1},{4,6},{5,7},{6,4},{7,5},{8,10},{9,11},{10,... | collective-permute-start | bytes 835592 | tf_op jit(solution)/shard_map/ppermute | solution.py:22
  51.4 15.8 %collective-permute-start.15 = (bf16[272,512]{1,0:T(8,128)(2,1)S(1)}, bf16[272,512]{1,0:T(8,128)(2,1)S(1)}, u32[]{:S(2)}, u32[]{:S(2)}) collective-permute-start(bf16[272,512]{1,0:T(8,128)(2,1)S(1)} %shard_map.104.rest_0_), channel_id=1, source_target_pairs={{0,16},{1,17},{2,18},{3,19},{4,20},{5,21},{6,22},{7,23},{8,24},{9,... | collective-permute-start | bytes 835592 | tf_op jit(solution)/shard_map/ppermute | solution.py:22
  56.3 14.0 %collective-permute-start.14 = (bf16[4,128,512]{2,1,0:T(8,128)(2,1)S(1)}, bf16[4,128,512]{2,1,0:T(8,128)(2,1)S(1)}, u32[]{:S(2)}, u32[]{:S(2)}) collective-permute-start(bf16[4,128,512]{2,1,0:T(8,128)(2,1)S(1)} %get-tuple-element.88), channel_id=1, source_target_pairs={{0,2},{1,3},{2,0},{3,1},{4,6},{5,7},{6,4},{7,5},{8,10},{9,11},{10,... | collective-permute-start | bytes 1572872 | tf_op jit(solution)/shard_map/ppermute | solution.py:22
  67.2 9.5 %collective-permute-start.22 = (bf16[272,512]{1,0:T(8,128)(2,1)S(1)}, bf16[272,512]{1,0:T(8,128)(2,1)S(1)}, u32[]{:S(2)}, u32[]{:S(2)}) collective-permute-start(bf16[272,512]{1,0:T(8,128)(2,1)S(1)} %collective-permute-done.15.rest_4_), channel_id=1, source_target_pairs={{0,8},{1,9},{2,10},{3,11},{4,12},{5,13},{6,14},{7,15},{8,0},{9,1},... | collective-permute-start | bytes 835592 | tf_op jit(solution)/shard_map/ppermute | solution.py:22
  71.0 16.6 %collective-permute-start.18 = (bf16[288,512]{1,0:T(8,128)(2,1)S(1)}, bf16[288,512]{1,0:T(8,128)(2,1)S(1)}, u32[]{:S(2)}, u32[]{:S(2)}) collective-permute-start(bf16[288,512]{1,0:T(8,128)(2,1)S(1)} %get-tuple-element.93), channel_id=1, source_target_pairs={{0,8},{1,9},{2,10},{3,11},{4,12},{5,13},{6,14},{7,15},{8,0},{9,1},... | collective-permute-start | bytes 884744 | tf_op jit(solution)/shard_map/ppermute | solution.py:22
  71.3 18.0 %collective-permute-start.24 = (bf16[288,512]{1,0:T(8,128)(2,1)S(1)}, bf16[288,512]{1,0:T(8,128)(2,1)S(1)}, u32[]{:S(2)}, u32[]{:S(2)}) collective-permute-start(bf16[288,512]{1,0:T(8,128)(2,1)S(1)} %get-tuple-element.93), channel_id=1, source_target_pairs={{0,12},{1,13},{2,14},{3,15},{4,8},{5,9},{6,10},{7,11},{8,4},{9,5},... | collective-permute-start | bytes 884744 | tf_op jit(solution)/shard_map/ppermute | solution.py:22
  74.0 15.4 %collective-permute-start.17 = (bf16[288,512]{1,0:T(8,128)(2,1)S(1)}, bf16[288,512]{1,0:T(8,128)(2,1)S(1)}, u32[]{:S(2)}, u32[]{:S(2)}) collective-permute-start(bf16[288,512]{1,0:T(8,128)(2,1)S(1)} %get-tuple-element.92.p0.own0), channel_id=1, source_target_pairs={{0,4},{1,5},{2,6},{3,7},{4,0},{5,1},{6,2},{7,3},{8,12},{9,13},{10,... | collective-permute-start | bytes 884744 | tf_op jit(solution)/shard_map/ppermute | solution.py:22
  74.5 9.6 %collective-permute-start.19 = (bf16[272,512]{1,0:T(8,128)(2,1)S(1)}, bf16[272,512]{1,0:T(8,128)(2,1)S(1)}, u32[]{:S(2)}, u32[]{:S(2)}) collective-permute-start(bf16[272,512]{1,0:T(8,128)(2,1)S(1)} %collective-permute-done.15.rest_4_), channel_id=1, source_target_pairs={{0,2},{1,3},{2,0},{3,1},{4,6},{5,7},{6,4},{7,5},{8,10},{9,11},{10,... | collective-permute-start | bytes 835592 | tf_op jit(solution)/shard_map/ppermute | solution.py:22
  76.7 10.8 %collective-permute-start.23 = (bf16[272,512]{1,0:T(8,128)(2,1)S(1)}, bf16[272,512]{1,0:T(8,128)(2,1)S(1)}, u32[]{:S(2)}, u32[]{:S(2)}) collective-permute-start(bf16[272,512]{1,0:T(8,128)(2,1)S(1)} %collective-permute-done.22.rest_6_), channel_id=1, source_target_pairs={{0,2},{1,3},{2,0},{3,1},{4,6},{5,7},{6,4},{7,5},{8,10},{9,11},{10,... | collective-permute-start | bytes 835592 | tf_op jit(solution)/shard_map/ppermute | solution.py:22
  96.6 14.6 %collective-permute-start.31 = (bf16[528,512]{1,0:T(8,128)(2,1)S(1)}, bf16[528,512]{1,0:T(8,128)(2,1)S(1)}, u32[]{:S(2)}, u32[]{:S(2)}) collective-permute-start(bf16[528,512]{1,0:T(8,128)(2,1)S(1)} %get-tuple-element.104), channel_id=1, source_target_pairs={{0,2},{1,3},{2,0},{3,1},{4,6},{5,7},{6,4},{7,5},{8,10},{9,11},{10,... | collective-permute-start | bytes 1622024 | tf_op jit(solution)/shard_map/ppermute | solution.py:22
  98.4 12.8 %collective-permute-start.30 = (bf16[2,128,512]{2,1,0:T(8,128)(2,1)S(1)}, bf16[2,128,512]{2,1,0:T(8,128)(2,1)S(1)}, u32[]{:S(2)}, u32[]{:S(2)}) collective-permute-start(bf16[2,128,512]{2,1,0:T(8,128)(2,1)S(1)} %get-tuple-element.109), channel_id=1, source_target_pairs={{0,4},{1,5},{2,6},{3,7},{4,0},{5,1},{6,2},{7,3},{8,12},{9,13},{10,... | collective-permute-start | bytes 786440 | tf_op jit(solution)/shard_map/ppermute | solution.py:22
  99.0 12.7 %collective-permute-start.32 = (bf16[2,128,512]{2,1,0:T(8,128)(2,1)S(1)}, bf16[2,128,512]{2,1,0:T(8,128)(2,1)S(1)}, u32[]{:S(2)}, u32[]{:S(2)}) collective-permute-start(bf16[2,128,512]{2,1,0:T(8,128)(2,1)S(1)} %get-tuple-element.113), channel_id=1, source_target_pairs={{0,8},{1,9},{2,10},{3,11},{4,12},{5,13},{6,14},{7,15},{8,0},{9,1},... | collective-permute-start | bytes 786440 | tf_op jit(solution)/shard_map/ppermute | solution.py:22
  99.6 14.0 %collective-permute-start.33 = (bf16[2,128,512]{2,1,0:T(8,128)(2,1)S(1)}, bf16[2,128,512]{2,1,0:T(8,128)(2,1)S(1)}, u32[]{:S(2)}, u32[]{:S(2)}) collective-permute-start(bf16[2,128,512]{2,1,0:T(8,128)(2,1)S(1)} %get-tuple-element.114), channel_id=1, source_target_pairs={{0,12},{1,13},{2,14},{3,15},{4,8},{5,9},{6,10},{7,11},{8,4},{9,5},... | collective-permute-start | bytes 786440 | tf_op jit(solution)/shard_map/ppermute | solution.py:22
  111.4 15.2 %collective-permute-start.38 = (bf16[528,512]{1,0:T(8,128)(2,1)S(1)}, bf16[528,512]{1,0:T(8,128)(2,1)S(1)}, u32[]{:S(2)}, u32[]{:S(2)}) collective-permute-start(bf16[528,512]{1,0:T(8,128)(2,1)S(1)} %get-tuple-element.123), channel_id=1, source_target_pairs={{0,8},{1,9},{2,10},{3,11},{4,12},{5,13},{6,14},{7,15},{8,0},{9,1},... | collective-permute-start | bytes 1622024 | tf_op jit(solution)/shard_map/ppermute | solution.py:22
  113.7 12.8 %collective-permute-start.37 = (bf16[4,128,512]{2,1,0:T(8,128)(2,1)S(1)}, bf16[4,128,512]{2,1,0:T(8,128)(2,1)S(1)}, u32[]{:S(2)}, u32[]{:S(2)}) collective-permute-start(bf16[4,128,512]{2,1,0:T(8,128)(2,1)S(1)} %shard_map.113.same), channel_id=1, source_target_pairs={{0,2},{1,3},{2,0},{3,1},{4,6},{5,7},{6,4},{7,5},{8,10},{9,11},{10,... | collective-permute-start | bytes 1572872 | tf_op jit(solution)/shard_map/ppermute | solution.py:22
  114.8 11.7 %collective-permute-start.40 = (bf16[4,128,512]{2,1,0:T(8,128)(2,1)S(1)}, bf16[4,128,512]{2,1,0:T(8,128)(2,1)S(1)}, u32[]{:S(2)}, u32[]{:S(2)}) collective-permute-start(bf16[4,128,512]{2,1,0:T(8,128)(2,1)S(1)} %shard_map.113.same), channel_id=1, source_target_pairs={{0,1},{1,0},{2,3},{3,2},{4,5},{5,4},{6,7},{7,6},{8,9},{9,8},{10,11... | collective-permute-start | bytes 1572872 | tf_op jit(solution)/shard_map/ppermute | solution.py:22
  131.3 41.8 %all-to-all-start = ((bf16[8,128,512]{2,1,0:T(8,128)(2,1)}), bf16[8,128,512]{2,1,0:T(8,128)(2,1)S(1)}, u32[]{:S(2)}, u32[]{:S(2)}) async-start(bf16[8,128,512]{2,1,0:T(8,128)(2,1)} %shard_map.117), calls=%async_computation | async-start | bytes 2097152 | tf_op jit(solution)/shard_map/all_to_all | solution.py:406
  135.1 16.5 %collective-permute-start.41 = (bf16[512,512]{1,0:T(8,128)(2,1)S(1)}, bf16[512,512]{1,0:T(8,128)(2,1)S(1)}, u32[]{:S(2)}, u32[]{:S(2)}) collective-permute-start(bf16[512,512]{1,0:T(8,128)(2,1)S(1)} %copy-done.5), channel_id=1, source_target_pairs={{0,2},{1,3},{2,0},{3,1},{4,6},{5,7},{6,4},{7,5},{8,10},{9,11},{10,... | collective-permute-start | bytes 1572872 | tf_op jit(solution)/shard_map/ppermute | solution.py:22
  136.3 13.1 %collective-permute-start.35 = (bf16[128,512]{1,0:T(8,128)(2,1)}, bf16[128,512]{1,0:T(8,128)(2,1)S(1)}, u32[]{:S(2)}, u32[]{:S(2)}) collective-permute-start(bf16[128,512]{1,0:T(8,128)(2,1)} %copy-done.6), channel_id=1, source_target_pairs={{0,4},{1,5},{2,6},{3,7},{4,0},{5,1},{6,2},{7,3},{8,12},{9,13},{10,... | collective-permute-start | bytes 393224 | tf_op jit(solution)/shard_map/ppermute | solution.py:22
  138.2 13.4 %collective-permute-start.36 = (bf16[128,512]{1,0:T(8,128)(2,1)S(1)}, bf16[128,512]{1,0:T(8,128)(2,1)S(1)}, u32[]{:S(2)}, u32[]{:S(2)}) collective-permute-start(bf16[128,512]{1,0:T(8,128)(2,1)S(1)} %get-tuple-element.119), channel_id=1, source_target_pairs={{0,5},{1,4},{2,7},{3,6},{4,1},{5,0},{6,3},{7,2},{8,13},{9,12},{10,... | collective-permute-start | bytes 393224 | tf_op jit(solution)/shard_map/ppermute | solution.py:22
  153.3 19.3 %collective-permute-start.45 = (bf16[144,512]{1,0:T(8,128)(2,1)S(1)}, bf16[144,512]{1,0:T(8,128)(2,1)S(1)}, u32[]{:S(2)}, u32[]{:S(2)}) collective-permute-start(bf16[144,512]{1,0:T(8,128)(2,1)S(1)} %get-tuple-element.134), channel_id=1, source_target_pairs={{0,20},{1,21},{2,22},{3,23},{4,16},{5,17},{6,18},{7,19},{8,28},{9,... | collective-permute-start | bytes 442376 | tf_op jit(solution)/shard_map/ppermute | solution.py:22
  158.3 14.3 %collective-permute-start.43 = (bf16[144,512]{1,0:T(8,128)(2,1)S(1)}, bf16[144,512]{1,0:T(8,128)(2,1)S(1)}, u32[]{:S(2)}, u32[]{:S(2)}) collective-permute-start(bf16[144,512]{1,0:T(8,128)(2,1)S(1)} %get-tuple-element.132), channel_id=1, source_target_pairs={{0,4},{1,5},{2,6},{3,7},{4,0},{5,1},{6,2},{7,3},{8,12},{9,13},{10,... | collective-permute-start | bytes 442376 | tf_op jit(solution)/shard_map/ppermute | solution.py:22
  158.3 15.9 %collective-permute-start.44 = (bf16[144,512]{1,0:T(8,128)(2,1)S(1)}, bf16[144,512]{1,0:T(8,128)(2,1)S(1)}, u32[]{:S(2)}, u32[]{:S(2)}) collective-permute-start(bf16[144,512]{1,0:T(8,128)(2,1)S(1)} %get-tuple-element.133), channel_id=1, source_target_pairs={{0,16},{1,17},{2,18},{3,19},{4,20},{5,21},{6,22},{7,23},{8,24},{9,... | collective-permute-start | bytes 442376 | tf_op jit(solution)/shard_map/ppermute | solution.py:22
  (27 other events, 180.3 us)

commit v7 on v6

--- a/solution.py
+++ b/solution.py
@@ -117,7 +117,7 @@
     y = ids[2]
     for g in range(GROUP):
         mine[g] = kept[g, y] + received[g, y].astype(F32)
-        send[g] = (kept[g, 1 - y] + received[g, 1 - y].astype(F32)).astype(BF16)
+        send[g] = (kept[g, 1 - y] + received[g, 1 - y].astype(F32)).astype(send.dtype)
 
 
 def group_kernel(ids, mine, received, near, far):
@@ -343,7 +343,7 @@
         smem=2, flops=2 * GROUP * dests * slots * tile * tile * quarter,
     )
     mine, send = call(
-        pair_sum_kernel, [shape((GROUP, tile, quarter), F32), shape((GROUP, tile, quarter), BF16)],
+        pair_sum_kernel, [shape((GROUP, tile, quarter), F32)] * 2,
         ids, kept, swap(after(sent, y1), CORE),
     )
     received = after(swap(send, Y), y1, z2, grads[1])

time: 177 us -> 188 us (1.062)
  waiting for transfers between devices: 99.3 us -> 110 us
    ppermute x49, waiting for transfers between devices: 99.3 us -> 110 us  [swap(): return lax.ppermute(value, BOTH, [(i, i ^ mask) for i in range(total)])]
  transfers between devices with their start and end apart: 50 -> 50, of which waited for: 27 -> 27; matrix products, arithmetic and copies ran while one was open for 1% -> 1% of each run, Pallas kernels for 8% -> 7%
where the time goes in v7:
time: 188 us
  waiting for transfers between devices  110 us (59%)
  starting transfers between devices  51.4 us (27%)
  Pallas kernels  21.8 us (12%)
  local copies, waits for them, and re-layouts  2.07 us (1%)
    ppermute x49, waiting for transfers between devices, swap(): return lax.ppermute(value, BOTH, [(i, i ^ mask) for i in range(total)])  110 us
    ppermute x49, starting transfers between devices, swap(): return lax.ppermute(value, BOTH, [(i, i ^ mask) for i in range(total)])  46.5 us
    pallas_call x19, Pallas kernels, call(): pl.pallas_call(kernel, out_shape=outs, in_specs=[SMEM] * smem + [VMEM] *...  21.8 us
    all_to_all x1, starting transfers between devices, chip_body(): spread_all = lax.all_to_all(spread, 'row', 0, 0, tiled=True)  4.86 us
  transfers between devices with their start and end apart: 50, of which 27 were waited for; matrix products, arithmetic and copies ran while one was open for 1% of the time, Pallas kernels for 7%

profile of v7, /device:TPU:0, one launch (start us, length us, event | category | flops | bytes accessed | tf_op | source)
XLA Modules:
  0.0 187.8 jit_solution(858919420716129796)
XLA Ops:
  5.4 3.0 %collective-permute-start.4 = (bf16[1552,128]{1,0:T(8,128)(2,1)S(1)}, bf16[1552,128]{1,0:T(8,128)(2,1)S(1)}, u32[]{:S(2)}, u32[]{:S(2)}) collective-permute-start(bf16[1552,128]{1,0:T(8,128)(2,1)S(1)} %pad_maximum_fusion.a0), channel_id=1, source_target_pairs={{0,8},{1,9},{2,10},{3,11},{4,12},{5,13},{6,14},{7,15},{8,0},{9,1},... | collective-permute-start | bytes 1191944 | tf_op jit(solution)/shard_map/ppermute | solution.py:22
  8.4 2.6 %collective-permute-start.6 = (bf16[128,2048]{1,0:T(8,128)(2,1)}, bf16[128,2048]{1,0:T(8,128)(2,1)S(1)}, u32[]{:S(2)}, u32[]{:S(2)}) collective-permute-start(bf16[128,2048]{1,0:T(8,128)(2,1)} %bitcast.20), channel_id=1, source_target_pairs={{0,16},{1,17},{2,18},{3,19},{4,20},{5,21},{6,22},{7,23},{8,24},{9,... | collective-permute-start | bytes 1572872 | tf_op jit(solution)/shard_map/ppermute | solution.py:22
  12.5 2.9 %collective-permute-done.1.p2 = bf16[80,512]{1,0:T(8,128)(2,1)S(1)} collective-permute-done((bf16[80,512]{1,0:T(8,128)(2,1)S(1)}, bf16[80,512]{1,0:T(8,128)(2,1)S(1)}, u32[]{:S(2)}, u32[]{:S(2)}) %collective-permute-start.1) | collective-permute-done | bytes 81952 | tf_op jit(solution)/shard_map/ppermute | solution.py:22
  15.5 1.8 collective-permute-done.2.p3
  18.9 7.7 %collective-permute-done.4.a2 = bf16[1552,128]{1,0:T(8,128)(2,1)S(1)} collective-permute-done((bf16[1552,128]{1,0:T(8,128)(2,1)S(1)}, bf16[1552,128]{1,0:T(8,128)(2,1)S(1)}, u32[]{:S(2)}, u32[]{:S(2)}) %collective-permute-start.4) | collective-permute-done | bytes 397344 | tf_op jit(solution)/shard_map/ppermute | solution.py:22
  26.6 2.0 %collective-permute-start.5 = (bf16[1552,128]{1,0:T(8,128)(2,1)S(1)}, bf16[1552,128]{1,0:T(8,128)(2,1)S(1)}, u32[]{:S(2)}, u32[]{:S(2)}) collective-permute-start(bf16[1552,128]{1,0:T(8,128)(2,1)S(1)} %collective-permute-done.4.a2), channel_id=1, source_target_pairs={{0,4},{1,5},{2,6},{3,7},{4,0},{5,1},{6,2},{7,3},{8,12},{9,13},{10,... | collective-permute-start | bytes 1191944 | tf_op jit(solution)/shard_map/ppermute | solution.py:22
  30.1 4.5 %collective-permute-done.6.far = bf16[128,2048]{1,0:T(8,128)(2,1)S(1)} collective-permute-done((bf16[128,2048]{1,0:T(8,128)(2,1)}, bf16[128,2048]{1,0:T(8,128)(2,1)S(1)}, u32[]{:S(2)}, u32[]{:S(2)}) %collective-permute-start.6) | collective-permute-done | bytes 524320 | tf_op jit(solution)/shard_map/ppermute | solution.py:22
  36.9 2.0 %collective-permute-start.11 = (bf16[2,128,512]{2,1,0:T(8,128)(2,1)S(1)}, bf16[2,128,512]{2,1,0:T(8,128)(2,1)S(1)}, u32[]{:S(2)}, u32[]{:S(2)}) collective-permute-start(bf16[2,128,512]{2,1,0:T(8,128)(2,1)S(1)} %get-tuple-element.83), channel_id=1, source_target_pairs={{0,12},{1,13},{2,14},{3,15},{4,8},{5,9},{6,10},{7,11},{8,4},{9,5},... | collective-permute-start | bytes 786440 | tf_op jit(solution)/shard_map/ppermute | solution.py:22
  40.4 3.3 %collective-permute-done.9.h1 = bf16[2,128,512]{2,1,0:T(8,128)(2,1)S(1)} collective-permute-done((bf16[2,128,512]{2,1,0:T(8,128)(2,1)S(1)}, bf16[2,128,512]{2,1,0:T(8,128)(2,1)S(1)}, u32[]{:S(2)}, u32[]{:S(2)}) %collective-permute-start.9) | collective-permute-done | bytes 262176 | tf_op jit(solution)/shard_map/ppermute | solution.py:22
  43.7 2.4 %collective-permute-done.10.h2 = bf16[2,128,512]{2,1,0:T(8,128)(2,1)S(1)} collective-permute-done((bf16[2,128,512]{2,1,0:T(8,128)(2,1)S(1)}, bf16[2,128,512]{2,1,0:T(8,128)(2,1)S(1)}, u32[]{:S(2)}, u32[]{:S(2)}) %collective-permute-start.10) | collective-permute-done | bytes 262176 | tf_op jit(solution)/shard_map/ppermute | solution.py:22
  46.1 3.3 %collective-permute-done.11.h3 = bf16[2,128,512]{2,1,0:T(8,128)(2,1)S(1)} collective-permute-done((bf16[2,128,512]{2,1,0:T(8,128)(2,1)S(1)}, bf16[2,128,512]{2,1,0:T(8,128)(2,1)S(1)}, u32[]{:S(2)}, u32[]{:S(2)}) %collective-permute-start.11) | collective-permute-done | bytes 262176 | tf_op jit(solution)/shard_map/ppermute | solution.py:22
  49.4 1.9 %shard_map.105 = (f32[4,2,128,512]{3,2,1,0:T(8,128)S(1)}, f32[4,2,128,512]{3,2,1,0:T(8,128)S(1)}) custom-call(s32[9]{0:T(128)S(1)} %stack.42.ids, s32[4,12]{1,0:T(4,128)S(1)} %maximum_convert_fusion.lists, bf16[1552,128]{1,0:T(8,128)(2,1)S(1)} %pad_maximum_fusion.a0, bf16[1552,128]{1,0:T(8,128)(2,1)S(1)} %collective-permute-done.3.a1, ...), custom_call_target="tpu_custom_call" | custom-call | flops 805306368 | bytes 6832356 | tf_op jit(solution)/shard_map/pallas_call | solution.py:36
  51.4 4.1 %collective-permute-done.13.received = f32[4,2,128,512]{3,2,1,0:T(8,128)S(1)} collective-permute-done((f32[4,2,128,512]{3,2,1,0:T(8,128)S(1)}, f32[4,2,128,512]{3,2,1,0:T(8,128)S(1)}, u32[]{:S(2)}, u32[]{:S(2)}) %collective-permute-start.13) | collective-permute-done | bytes 2097184 | tf_op jit(solution)/shard_map/ppermute | solution.py:22
  61.6 4.0 %collective-permute-done.20.o2 = bf16[128,512]{1,0:T(8,128)(2,1)S(1)} collective-permute-done((bf16[128,512]{1,0:T(8,128)(2,1)S(1)}, bf16[128,512]{1,0:T(8,128)(2,1)S(1)}, u32[]{:S(2)}, u32[]{:S(2)}) %collective-permute-start.20) | collective-permute-done | bytes 131104 | tf_op jit(solution)/shard_map/ppermute | solution.py:22
  65.6 1.8 collective-permute-done.21.o3
  67.3 5.7 %collective-permute-done.15.rest_4_ = bf16[272,512]{1,0:T(8,128)(2,1)S(1)} collective-permute-done((bf16[272,512]{1,0:T(8,128)(2,1)S(1)}, bf16[272,512]{1,0:T(8,128)(2,1)S(1)}, u32[]{:S(2)}, u32[]{:S(2)}) %collective-permute-start.15) | collective-permute-done | bytes 278560 | tf_op jit(solution)/shard_map/ppermute | solution.py:22
  74.4 7.2 %collective-permute-done.14.received = f32[4,128,512]{2,1,0:T(8,128)S(1)} collective-permute-done((f32[4,128,512]{2,1,0:T(8,128)S(1)}, f32[4,128,512]{2,1,0:T(8,128)S(1)}, u32[]{:S(2)}, u32[]{:S(2)}) %collective-permute-start.14) | collective-permute-done | bytes 1048608 | tf_op jit(solution)/shard_map/ppermute | solution.py:22
  82.6 2.7 %collective-permute-start.24 = (bf16[288,512]{1,0:T(8,128)(2,1)S(1)}, bf16[288,512]{1,0:T(8,128)(2,1)S(1)}, u32[]{:S(2)}, u32[]{:S(2)}) collective-permute-start(bf16[288,512]{1,0:T(8,128)(2,1)S(1)} %get-tuple-element.93), channel_id=1, source_target_pairs={{0,12},{1,13},{2,14},{3,15},{4,8},{5,9},{6,10},{7,11},{8,4},{9,5},... | collective-permute-start | bytes 884744 | tf_op jit(solution)/shard_map/ppermute | solution.py:22
  87.8 7.6 %collective-permute-done.19.rest_5_ = bf16[272,512]{1,0:T(8,128)(2,1)S(1)} collective-permute-done((bf16[272,512]{1,0:T(8,128)(2,1)S(1)}, bf16[272,512]{1,0:T(8,128)(2,1)S(1)}, u32[]{:S(2)}, u32[]{:S(2)}) %collective-permute-start.19) | collective-permute-done | bytes 278560 | tf_op jit(solution)/shard_map/ppermute | solution.py:22
  95.4 3.4 %collective-permute-done.23.rest_7_ = bf16[272,512]{1,0:T(8,128)(2,1)S(1)} collective-permute-done((bf16[272,512]{1,0:T(8,128)(2,1)S(1)}, bf16[272,512]{1,0:T(8,128)(2,1)S(1)}, u32[]{:S(2)}, u32[]{:S(2)}) %collective-permute-start.23) | collective-permute-done | bytes 278560 | tf_op jit(solution)/shard_map/ppermute | solution.py:22
  101.2 3.5 %shard_map.109 = (bf16[128,512]{1,0:T(8,128)(2,1)S(1)}, bf16[128,512]{1,0:T(8,128)(2,1)S(1)}, bf16[128,512]{1,0:T(8,128)(2,1)S(1)}, bf16[128,512]{1,0:T(8,128)(2...) custom-call(s32[9]{0:T(128)S(1)} %stack.42.ids, ...), custom_call_target="tpu_custom_call" | custom-call | flops 2147483648 | bytes 9306148 | tf_op jit(solution)/shard_map/pallas_call | solution.py:36
  113.2 7.9 %collective-permute-done.31.received = bf16[528,512]{1,0:T(8,128)(2,1)S(1)} collective-permute-done((bf16[528,512]{1,0:T(8,128)(2,1)S(1)}, bf16[528,512]{1,0:T(8,128)(2,1)S(1)}, u32[]{:S(2)}, u32[]{:S(2)}) %collective-permute-start.31) | collective-permute-done | bytes 540704 | tf_op jit(solution)/shard_map/ppermute | solution.py:22
  121.6 1.8 collective-permute-done.33.vxz
  124.7 11.7 %collective-permute-done.37.same = bf16[4,128,512]{2,1,0:T(8,128)(2,1)S(1)} collective-permute-done((bf16[4,128,512]{2,1,0:T(8,128)(2,1)S(1)}, bf16[4,128,512]{2,1,0:T(8,128)(2,1)S(1)}, u32[]{:S(2)}, u32[]{:S(2)}) %collective-permute-start.37) | collective-permute-done | bytes 524320 | tf_op jit(solution)/shard_map/ppermute | solution.py:22
  136.4 1.8 shard_map.116.rest_0_
  138.3 2.8 %shard_map.117 = bf16[8,128,512]{2,1,0:T(8,128)(2,1)} custom-call(s32[9]{0:T(128)S(1)} %stack.42.ids, s32[4,12]{1,0:T(4,128)S(1)} %maximum_convert_fusion.lists, bf16[1552,128]{1,0:T(8,128)(2,1)S(1)} %pad_maximum_fusion.a0, bf16[1552,128]{1,0:T(8,128)(2,1)S(1)} %collective-permute-done.3.a1, bf16[1552,128]{1,0:T(8,128)(2,1)S(1)} %collective-permute-done.4.a2, ...), custom_call_target="tpu_custom_call" | custom-call | flops 402653184 | bytes 5783780 | tf_op jit(solution)/shard_map/pallas_call | solution.py:36
  141.1 4.9 %all-to-all-start = ((bf16[8,128,512]{2,1,0:T(8,128)(2,1)}), bf16[8,128,512]{2,1,0:T(8,128)(2,1)S(1)}, u32[]{:S(2)}, u32[]{:S(2)}) async-start(bf16[8,128,512]{2,1,0:T(8,128)(2,1)} %shard_map.117), calls=%async_computation | async-start | bytes 2097152 | tf_op jit(solution)/shard_map/all_to_all | solution.py:406
  147.1 2.0 %collective-permute-start.35 = (bf16[128,512]{1,0:T(8,128)(2,1)}, bf16[128,512]{1,0:T(8,128)(2,1)S(1)}, u32[]{:S(2)}, u32[]{:S(2)}) collective-permute-start(bf16[128,512]{1,0:T(8,128)(2,1)} %copy-done.6), channel_id=1, source_target_pairs={{0,4},{1,5},{2,6},{3,7},{4,0},{5,1},{6,2},{7,3},{8,12},{9,13},{10,... | collective-permute-start | bytes 393224 | tf_op jit(solution)/shard_map/ppermute | solution.py:22
  149.2 11.4 %collective-permute-done.35.a2 = bf16[128,512]{1,0:T(8,128)(2,1)S(1)} collective-permute-done((bf16[128,512]{1,0:T(8,128)(2,1)}, bf16[128,512]{1,0:T(8,128)(2,1)S(1)}, u32[]{:S(2)}, u32[]{:S(2)}) %collective-permute-start.35) | collective-permute-done | bytes 131104 | tf_op jit(solution)/shard_map/ppermute | solution.py:22
  164.3 4.8 %collective-permute-start.45 = (bf16[144,512]{1,0:T(8,128)(2,1)S(1)}, bf16[144,512]{1,0:T(8,128)(2,1)S(1)}, u32[]{:S(2)}, u32[]{:S(2)}) collective-permute-start(bf16[144,512]{1,0:T(8,128)(2,1)S(1)} %get-tuple-element.134), channel_id=1, source_target_pairs={{0,20},{1,21},{2,22},{3,23},{4,16},{5,17},{6,18},{7,19},{8,28},{9,... | collective-permute-start | bytes 442376 | tf_op jit(solution)/shard_map/ppermute | solution.py:22
  169.1 1.8 collective-permute-start.44
  172.3 11.2 %collective-permute-done.45.r3 = bf16[144,512]{1,0:T(8,128)(2,1)S(1)} collective-permute-done((bf16[144,512]{1,0:T(8,128)(2,1)S(1)}, bf16[144,512]{1,0:T(8,128)(2,1)S(1)}, u32[]{:S(2)}, u32[]{:S(2)}) %collective-permute-start.45) | collective-permute-done | bytes 147488 | tf_op jit(solution)/shard_map/ppermute | solution.py:22
  (118 shorter events, 47.7 us)
Async XLA Ops:
  5.4 21.2 %collective-permute-start.4 = (bf16[1552,128]{1,0:T(8,128)(2,1)S(1)}, bf16[1552,128]{1,0:T(8,128)(2,1)S(1)}, u32[]{:S(2)}, u32[]{:S(2)}) collective-permute-start(bf16[1552,128]{1,0:T(8,128)(2,1)S(1)} %pad_maximum_fusion.a0), channel_id=1, source_target_pairs={{0,8},{1,9},{2,10},{3,11},{4,12},{5,13},{6,14},{7,15},{8,0},{9,1},... | collective-permute-start | bytes 1191944 | tf_op jit(solution)/shard_map/ppermute | solution.py:22
  8.4 26.2 %collective-permute-start.6 = (bf16[128,2048]{1,0:T(8,128)(2,1)}, bf16[128,2048]{1,0:T(8,128)(2,1)S(1)}, u32[]{:S(2)}, u32[]{:S(2)}) collective-permute-start(bf16[128,2048]{1,0:T(8,128)(2,1)} %bitcast.20), channel_id=1, source_target_pairs={{0,16},{1,17},{2,18},{3,19},{4,20},{5,21},{6,22},{7,23},{8,24},{9,... | collective-permute-start | bytes 1572872 | tf_op jit(solution)/shard_map/ppermute | solution.py:22
  17.2 12.9 %collective-permute-start.3 = (bf16[1552,128]{1,0:T(8,128)(2,1)S(1)}, bf16[1552,128]{1,0:T(8,128)(2,1)S(1)}, u32[]{:S(2)}, u32[]{:S(2)}) collective-permute-start(bf16[1552,128]{1,0:T(8,128)(2,1)S(1)} %pad_maximum_fusion.a0), channel_id=1, source_target_pairs={{0,4},{1,5},{2,6},{3,7},{4,0},{5,1},{6,2},{7,3},{8,12},{9,13},{10,... | collective-permute-start | bytes 1191944 | tf_op jit(solution)/shard_map/ppermute | solution.py:22
  18.4 18.5 %collective-permute-start.8 = (bf16[272,512]{1,0:T(8,128)(2,1)S(1)}, bf16[272,512]{1,0:T(8,128)(2,1)S(1)}, u32[]{:S(2)}, u32[]{:S(2)}) collective-permute-start(bf16[272,512]{1,0:T(8,128)(2,1)S(1)} %shard_map.104.rest_0_), channel_id=1, source_target_pairs={{0,8},{1,9},{2,10},{3,11},{4,12},{5,13},{6,14},{7,15},{8,0},{9,1},... | collective-permute-start | bytes 835592 | tf_op jit(solution)/shard_map/ppermute | solution.py:22
  26.6 13.8 %collective-permute-start.5 = (bf16[1552,128]{1,0:T(8,128)(2,1)S(1)}, bf16[1552,128]{1,0:T(8,128)(2,1)S(1)}, u32[]{:S(2)}, u32[]{:S(2)}) collective-permute-start(bf16[1552,128]{1,0:T(8,128)(2,1)S(1)} %collective-permute-done.4.a2), channel_id=1, source_target_pairs={{0,4},{1,5},{2,6},{3,7},{4,0},{5,1},{6,2},{7,3},{8,12},{9,13},{10,... | collective-permute-start | bytes 1191944 | tf_op jit(solution)/shard_map/ppermute | solution.py:22
  28.6 10.3 %collective-permute-start.7 = (bf16[272,512]{1,0:T(8,128)(2,1)S(1)}, bf16[272,512]{1,0:T(8,128)(2,1)S(1)}, u32[]{:S(2)}, u32[]{:S(2)}) collective-permute-start(bf16[272,512]{1,0:T(8,128)(2,1)S(1)} %shard_map.104.rest_0_), channel_id=1, source_target_pairs={{0,2},{1,3},{2,0},{3,1},{4,6},{5,7},{6,4},{7,5},{8,10},{9,11},{10,... | collective-permute-start | bytes 835592 | tf_op jit(solution)/shard_map/ppermute | solution.py:22
  35.3 8.4 %collective-permute-start.9 = (bf16[2,128,512]{2,1,0:T(8,128)(2,1)S(1)}, bf16[2,128,512]{2,1,0:T(8,128)(2,1)S(1)}, u32[]{:S(2)}, u32[]{:S(2)}) collective-permute-start(bf16[2,128,512]{2,1,0:T(8,128)(2,1)S(1)} %get-tuple-element.81), channel_id=1, source_target_pairs={{0,4},{1,5},{2,6},{3,7},{4,0},{5,1},{6,2},{7,3},{8,12},{9,13},{10,... | collective-permute-start | bytes 786440 | tf_op jit(solution)/shard_map/ppermute | solution.py:22
  36.9 9.2 %collective-permute-start.10 = (bf16[2,128,512]{2,1,0:T(8,128)(2,1)S(1)}, bf16[2,128,512]{2,1,0:T(8,128)(2,1)S(1)}, u32[]{:S(2)}, u32[]{:S(2)}) collective-permute-start(bf16[2,128,512]{2,1,0:T(8,128)(2,1)S(1)} %get-tuple-element.82), channel_id=1, source_target_pairs={{0,8},{1,9},{2,10},{3,11},{4,12},{5,13},{6,14},{7,15},{8,0},{9,1},... | collective-permute-start | bytes 786440 | tf_op jit(solution)/shard_map/ppermute | solution.py:22
  36.9 12.5 %collective-permute-start.11 = (bf16[2,128,512]{2,1,0:T(8,128)(2,1)S(1)}, bf16[2,128,512]{2,1,0:T(8,128)(2,1)S(1)}, u32[]{:S(2)}, u32[]{:S(2)}) collective-permute-start(bf16[2,128,512]{2,1,0:T(8,128)(2,1)S(1)} %get-tuple-element.83), channel_id=1, source_target_pairs={{0,12},{1,13},{2,14},{3,15},{4,8},{5,9},{6,10},{7,11},{8,4},{9,5},... | collective-permute-start | bytes 786440 | tf_op jit(solution)/shard_map/ppermute | solution.py:22
  38.9 12.4 %collective-permute-start.12 = (bf16[272,512]{1,0:T(8,128)(2,1)S(1)}, bf16[272,512]{1,0:T(8,128)(2,1)S(1)}, u32[]{:S(2)}, u32[]{:S(2)}) collective-permute-start(bf16[272,512]{1,0:T(8,128)(2,1)S(1)} %collective-permute-done.8.rest_2_), channel_id=1, source_target_pairs={{0,2},{1,3},{2,0},{3,1},{4,6},{5,7},{6,4},{7,5},{8,10},{9,11},{10,... | collective-permute-start | bytes 835592 | tf_op jit(solution)/shard_map/ppermute | solution.py:22
  56.3 25.3 %collective-permute-start.14 = (f32[4,128,512]{2,1,0:T(8,128)S(1)}, f32[4,128,512]{2,1,0:T(8,128)S(1)}, u32[]{:S(2)}, u32[]{:S(2)}) collective-permute-start(f32[4,128,512]{2,1,0:T(8,128)S(1)} %get-tuple-element.88), channel_id=1, source_target_pairs={{0,2},{1,3},{2,0},{3,1},{4,6},{5,7},{6,4},{7,5},{8,10},{9,11},{10,... | collective-permute-start | bytes 3145736 | tf_op jit(solution)/shard_map/ppermute | solution.py:22
  57.9 15.1 %collective-permute-start.15 = (bf16[272,512]{1,0:T(8,128)(2,1)S(1)}, bf16[272,512]{1,0:T(8,128)(2,1)S(1)}, u32[]{:S(2)}, u32[]{:S(2)}) collective-permute-start(bf16[272,512]{1,0:T(8,128)(2,1)S(1)} %shard_map.104.rest_0_), channel_id=1, source_target_pairs={{0,16},{1,17},{2,18},{3,19},{4,20},{5,21},{6,22},{7,23},{8,24},{9,... | collective-permute-start | bytes 835592 | tf_op jit(solution)/shard_map/ppermute | solution.py:22
  73.0 14.3 %collective-permute-start.22 = (bf16[272,512]{1,0:T(8,128)(2,1)S(1)}, bf16[272,512]{1,0:T(8,128)(2,1)S(1)}, u32[]{:S(2)}, u32[]{:S(2)}) collective-permute-start(bf16[272,512]{1,0:T(8,128)(2,1)S(1)} %collective-permute-done.15.rest_4_), channel_id=1, source_target_pairs={{0,8},{1,9},{2,10},{3,11},{4,12},{5,13},{6,14},{7,15},{8,0},{9,1},... | collective-permute-start | bytes 835592 | tf_op jit(solution)/shard_map/ppermute | solution.py:22
  82.2 16.6 %collective-permute-start.18 = (bf16[288,512]{1,0:T(8,128)(2,1)S(1)}, bf16[288,512]{1,0:T(8,128)(2,1)S(1)}, u32[]{:S(2)}, u32[]{:S(2)}) collective-permute-start(bf16[288,512]{1,0:T(8,128)(2,1)S(1)} %get-tuple-element.93), channel_id=1, source_target_pairs={{0,8},{1,9},{2,10},{3,11},{4,12},{5,13},{6,14},{7,15},{8,0},{9,1},... | collective-permute-start | bytes 884744 | tf_op jit(solution)/shard_map/ppermute | solution.py:22
  82.6 16.2 %collective-permute-start.24 = (bf16[288,512]{1,0:T(8,128)(2,1)S(1)}, bf16[288,512]{1,0:T(8,128)(2,1)S(1)}, u32[]{:S(2)}, u32[]{:S(2)}) collective-permute-start(bf16[288,512]{1,0:T(8,128)(2,1)S(1)} %get-tuple-element.93), channel_id=1, source_target_pairs={{0,12},{1,13},{2,14},{3,15},{4,8},{5,9},{6,10},{7,11},{8,4},{9,5},... | collective-permute-start | bytes 884744 | tf_op jit(solution)/shard_map/ppermute | solution.py:22
  85.3 14.0 %collective-permute-start.17 = (bf16[288,512]{1,0:T(8,128)(2,1)S(1)}, bf16[288,512]{1,0:T(8,128)(2,1)S(1)}, u32[]{:S(2)}, u32[]{:S(2)}) collective-permute-start(bf16[288,512]{1,0:T(8,128)(2,1)S(1)} %get-tuple-element.92.p0.own0), channel_id=1, source_target_pairs={{0,4},{1,5},{2,6},{3,7},{4,0},{5,1},{6,2},{7,3},{8,12},{9,13},{10,... | collective-permute-start | bytes 884744 | tf_op jit(solution)/shard_map/ppermute | solution.py:22
  85.8 9.6 %collective-permute-start.19 = (bf16[272,512]{1,0:T(8,128)(2,1)S(1)}, bf16[272,512]{1,0:T(8,128)(2,1)S(1)}, u32[]{:S(2)}, u32[]{:S(2)}) collective-permute-start(bf16[272,512]{1,0:T(8,128)(2,1)S(1)} %collective-permute-done.15.rest_4_), channel_id=1, source_target_pairs={{0,2},{1,3},{2,0},{3,1},{4,6},{5,7},{6,4},{7,5},{8,10},{9,11},{10,... | collective-permute-start | bytes 835592 | tf_op jit(solution)/shard_map/ppermute | solution.py:22
  87.3 11.5 %collective-permute-start.23 = (bf16[272,512]{1,0:T(8,128)(2,1)S(1)}, bf16[272,512]{1,0:T(8,128)(2,1)S(1)}, u32[]{:S(2)}, u32[]{:S(2)}) collective-permute-start(bf16[272,512]{1,0:T(8,128)(2,1)S(1)} %collective-permute-done.22.rest_6_), channel_id=1, source_target_pairs={{0,2},{1,3},{2,0},{3,1},{4,6},{5,7},{6,4},{7,5},{8,10},{9,11},{10,... | collective-permute-start | bytes 835592 | tf_op jit(solution)/shard_map/ppermute | solution.py:22
  106.4 14.6 %collective-permute-start.31 = (bf16[528,512]{1,0:T(8,128)(2,1)S(1)}, bf16[528,512]{1,0:T(8,128)(2,1)S(1)}, u32[]{:S(2)}, u32[]{:S(2)}) collective-permute-start(bf16[528,512]{1,0:T(8,128)(2,1)S(1)} %get-tuple-element.104), channel_id=1, source_target_pairs={{0,2},{1,3},{2,0},{3,1},{4,6},{5,7},{6,4},{7,5},{8,10},{9,11},{10,... | collective-permute-start | bytes 1622024 | tf_op jit(solution)/shard_map/ppermute | solution.py:22
  108.2 12.8 %collective-permute-start.30 = (bf16[2,128,512]{2,1,0:T(8,128)(2,1)S(1)}, bf16[2,128,512]{2,1,0:T(8,128)(2,1)S(1)}, u32[]{:S(2)}, u32[]{:S(2)}) collective-permute-start(bf16[2,128,512]{2,1,0:T(8,128)(2,1)S(1)} %get-tuple-element.109), channel_id=1, source_target_pairs={{0,4},{1,5},{2,6},{3,7},{4,0},{5,1},{6,2},{7,3},{8,12},{9,13},{10,... | collective-permute-start | bytes 786440 | tf_op jit(solution)/shard_map/ppermute | solution.py:22
  109.8 11.8 %collective-permute-start.32 = (bf16[2,128,512]{2,1,0:T(8,128)(2,1)S(1)}, bf16[2,128,512]{2,1,0:T(8,128)(2,1)S(1)}, u32[]{:S(2)}, u32[]{:S(2)}) collective-permute-start(bf16[2,128,512]{2,1,0:T(8,128)(2,1)S(1)} %get-tuple-element.113), channel_id=1, source_target_pairs={{0,8},{1,9},{2,10},{3,11},{4,12},{5,13},{6,14},{7,15},{8,0},{9,1},... | collective-permute-start | bytes 786440 | tf_op jit(solution)/shard_map/ppermute | solution.py:22
  110.2 13.2 %collective-permute-start.33 = (bf16[2,128,512]{2,1,0:T(8,128)(2,1)S(1)}, bf16[2,128,512]{2,1,0:T(8,128)(2,1)S(1)}, u32[]{:S(2)}, u32[]{:S(2)}) collective-permute-start(bf16[2,128,512]{2,1,0:T(8,128)(2,1)S(1)} %get-tuple-element.114), channel_id=1, source_target_pairs={{0,12},{1,13},{2,14},{3,15},{4,8},{5,9},{6,10},{7,11},{8,4},{9,5},... | collective-permute-start | bytes 786440 | tf_op jit(solution)/shard_map/ppermute | solution.py:22
  121.2 15.2 %collective-permute-start.38 = (bf16[528,512]{1,0:T(8,128)(2,1)S(1)}, bf16[528,512]{1,0:T(8,128)(2,1)S(1)}, u32[]{:S(2)}, u32[]{:S(2)}) collective-permute-start(bf16[528,512]{1,0:T(8,128)(2,1)S(1)} %get-tuple-element.123), channel_id=1, source_target_pairs={{0,8},{1,9},{2,10},{3,11},{4,12},{5,13},{6,14},{7,15},{8,0},{9,1},... | collective-permute-start | bytes 1622024 | tf_op jit(solution)/shard_map/ppermute | solution.py:22
  123.6 12.8 %collective-permute-start.37 = (bf16[4,128,512]{2,1,0:T(8,128)(2,1)S(1)}, bf16[4,128,512]{2,1,0:T(8,128)(2,1)S(1)}, u32[]{:S(2)}, u32[]{:S(2)}) collective-permute-start(bf16[4,128,512]{2,1,0:T(8,128)(2,1)S(1)} %shard_map.113.same), channel_id=1, source_target_pairs={{0,2},{1,3},{2,0},{3,1},{4,6},{5,7},{6,4},{7,5},{8,10},{9,11},{10,... | collective-permute-start | bytes 1572872 | tf_op jit(solution)/shard_map/ppermute | solution.py:22
  124.7 11.7 %collective-permute-start.40 = (bf16[4,128,512]{2,1,0:T(8,128)(2,1)S(1)}, bf16[4,128,512]{2,1,0:T(8,128)(2,1)S(1)}, u32[]{:S(2)}, u32[]{:S(2)}) collective-permute-start(bf16[4,128,512]{2,1,0:T(8,128)(2,1)S(1)} %shard_map.113.same), channel_id=1, source_target_pairs={{0,1},{1,0},{2,3},{3,2},{4,5},{5,4},{6,7},{7,6},{8,9},{9,8},{10,11... | collective-permute-start | bytes 1572872 | tf_op jit(solution)/shard_map/ppermute | solution.py:22
  141.1 42.9 %all-to-all-start = ((bf16[8,128,512]{2,1,0:T(8,128)(2,1)}), bf16[8,128,512]{2,1,0:T(8,128)(2,1)S(1)}, u32[]{:S(2)}, u32[]{:S(2)}) async-start(bf16[8,128,512]{2,1,0:T(8,128)(2,1)} %shard_map.117), calls=%async_computation | async-start | bytes 2097152 | tf_op jit(solution)/shard_map/all_to_all | solution.py:406
  146.0 16.3 %collective-permute-start.41 = (bf16[512,512]{1,0:T(8,128)(2,1)S(1)}, bf16[512,512]{1,0:T(8,128)(2,1)S(1)}, u32[]{:S(2)}, u32[]{:S(2)}) collective-permute-start(bf16[512,512]{1,0:T(8,128)(2,1)S(1)} %copy-done.5), channel_id=1, source_target_pairs={{0,2},{1,3},{2,0},{3,1},{4,6},{5,7},{6,4},{7,5},{8,10},{9,11},{10,... | collective-permute-start | bytes 1572872 | tf_op jit(solution)/shard_map/ppermute | solution.py:22
  147.1 13.5 %collective-permute-start.35 = (bf16[128,512]{1,0:T(8,128)(2,1)}, bf16[128,512]{1,0:T(8,128)(2,1)S(1)}, u32[]{:S(2)}, u32[]{:S(2)}) collective-permute-start(bf16[128,512]{1,0:T(8,128)(2,1)} %copy-done.6), channel_id=1, source_target_pairs={{0,4},{1,5},{2,6},{3,7},{4,0},{5,1},{6,2},{7,3},{8,12},{9,13},{10,... | collective-permute-start | bytes 393224 | tf_op jit(solution)/shard_map/ppermute | solution.py:22
  149.1 13.1 %collective-permute-start.36 = (bf16[128,512]{1,0:T(8,128)(2,1)S(1)}, bf16[128,512]{1,0:T(8,128)(2,1)S(1)}, u32[]{:S(2)}, u32[]{:S(2)}) collective-permute-start(bf16[128,512]{1,0:T(8,128)(2,1)S(1)} %get-tuple-element.119), channel_id=1, source_target_pairs={{0,5},{1,4},{2,7},{3,6},{4,1},{5,0},{6,3},{7,2},{8,13},{9,12},{10,... | collective-permute-start | bytes 393224 | tf_op jit(solution)/shard_map/ppermute | solution.py:22
  164.3 19.2 %collective-permute-start.45 = (bf16[144,512]{1,0:T(8,128)(2,1)S(1)}, bf16[144,512]{1,0:T(8,128)(2,1)S(1)}, u32[]{:S(2)}, u32[]{:S(2)}) collective-permute-start(bf16[144,512]{1,0:T(8,128)(2,1)S(1)} %get-tuple-element.134), channel_id=1, source_target_pairs={{0,20},{1,21},{2,22},{3,23},{4,16},{5,17},{6,18},{7,19},{8,28},{9,... | collective-permute-start | bytes 442376 | tf_op jit(solution)/shard_map/ppermute | solution.py:22
  169.0 14.4 %collective-permute-start.43 = (bf16[144,512]{1,0:T(8,128)(2,1)S(1)}, bf16[144,512]{1,0:T(8,128)(2,1)S(1)}, u32[]{:S(2)}, u32[]{:S(2)}) collective-permute-start(bf16[144,512]{1,0:T(8,128)(2,1)S(1)} %get-tuple-element.132), channel_id=1, source_target_pairs={{0,4},{1,5},{2,6},{3,7},{4,0},{5,1},{6,2},{7,3},{8,12},{9,13},{10,... | collective-permute-start | bytes 442376 | tf_op jit(solution)/shard_map/ppermute | solution.py:22
  169.1 15.9 %collective-permute-start.44 = (bf16[144,512]{1,0:T(8,128)(2,1)S(1)}, bf16[144,512]{1,0:T(8,128)(2,1)S(1)}, u32[]{:S(2)}, u32[]{:S(2)}) collective-permute-start(bf16[144,512]{1,0:T(8,128)(2,1)S(1)} %get-tuple-element.133), channel_id=1, source_target_pairs={{0,16},{1,17},{2,18},{3,19},{4,20},{5,21},{6,22},{7,23},{8,24},{9,... | collective-permute-start | bytes 442376 | tf_op jit(solution)/shard_map/ppermute | solution.py:22
  (27 other events, 180.4 us)

commit v8 on v6

--- a/solution.py
+++ b/solution.py
@@ -314,7 +314,6 @@
     (block,) = call(block_kernel, [shape((4 * own_rows + ROWS, quarter), BF16)], ids, *pieces)
 
     lists = jnp.pad(lists.reshape(1, -1), ((0, 15), (0, tile - dests * slots))).astype(BF16)
-    tiles, lists = lax.optimization_barrier((tiles, lists, pieces[1]))[:2]
     tiles = jnp.concatenate([tiles.reshape(-1, tile), lists], axis=0)
     tiles_of = [tiles, swap(after(tiles, *pieces[2:]), X), swap(tiles, Z)]
     tiles_of.append(swap(tiles_of[2], X))

time: 177 us -> 176 us (level)
  waiting for transfers between devices: 99.3 us -> 97.1 us
    ppermute x49, waiting for transfers between devices: 99.3 us -> 97.1 us  [swap(): return lax.ppermute(value, BOTH, [(i, i ^ mask) for i in range(total)])]
  transfers between devices with their start and end apart: 50 -> 50, of which waited for: 27 -> 28; matrix products, arithmetic and copies ran while one was open for 1% -> 0% of each run, Pallas kernels for 8% -> 8%
where the time goes in v8:
time: 176 us; the launch traced here: 175 us
  waiting for transfers between devices  97.1 us (55%)
  starting transfers between devices  50.7 us (29%)
  Pallas kernels  21.8 us (12%)
  local copies, waits for them, and re-layouts  3.05 us (2%)
    ppermute x49, waiting for transfers between devices, swap(): return lax.ppermute(value, BOTH, [(i, i ^ mask) for i in range(total)])  97.1 us
    ppermute x49, starting transfers between devices, swap(): return lax.ppermute(value, BOTH, [(i, i ^ mask) for i in range(total)])  47 us
    pallas_call x19, Pallas kernels, call(): pl.pallas_call(kernel, out_shape=outs, in_specs=[SMEM] * smem + [VMEM] *...  21.8 us
    all_to_all x1, starting transfers between devices, chip_body(): spread_all = lax.all_to_all(spread, 'row', 0, 0, tiled=True)  3.69 us
  transfers between devices with their start and end apart: 50, of which 28 were waited for; matrix products, arithmetic and copies ran while one was open for 0% of the time, Pallas kernels for 8%

profile of v8, /device:TPU:0, one launch (start us, length us, event | category | flops | bytes accessed | tf_op | source)
XLA Modules:
  0.0 175.3 jit_solution(637588807990276818)
XLA Ops:
  2.5 3.1 %collective-permute-start.3 = (bf16[1552,128]{1,0:T(8,128)(2,1)S(1)}, bf16[1552,128]{1,0:T(8,128)(2,1)S(1)}, u32[]{:S(2)}, u32[]{:S(2)}) collective-permute-start(bf16[1552,128]{1,0:T(8,128)(2,1)S(1)} %fusion.1.a0), channel_id=1, source_target_pairs={{0,8},{1,9},{2,10},{3,11},{4,12},{5,13},{6,14},{7,15},{8,0},{9,1},... | collective-permute-start | bytes 1191944 | tf_op jit(solution)/shard_map/ppermute | solution.py:22
  5.6 2.6 %collective-permute-start.5 = (bf16[128,2048]{1,0:T(8,128)(2,1)}, bf16[128,2048]{1,0:T(8,128)(2,1)S(1)}, u32[]{:S(2)}, u32[]{:S(2)}) collective-permute-start(bf16[128,2048]{1,0:T(8,128)(2,1)} %bitcast.19), channel_id=1, source_target_pairs={{0,16},{1,17},{2,18},{3,19},{4,20},{5,21},{6,22},{7,23},{8,24},{9,... | collective-permute-start | bytes 1572872 | tf_op jit(solution)/shard_map/ppermute | solution.py:22
  12.1 2.9 %collective-permute-done.p2 = bf16[80,512]{1,0:T(8,128)(2,1)S(1)} collective-permute-done((bf16[80,512]{1,0:T(8,128)(2,1)S(1)}, bf16[80,512]{1,0:T(8,128)(2,1)S(1)}, u32[]{:S(2)}, u32[]{:S(2)}) %collective-permute-start) | collective-permute-done | bytes 81952 | tf_op jit(solution)/shard_map/ppermute | solution.py:22
  15.0 1.8 %collective-permute-done.1.p3 = bf16[80,512]{1,0:T(8,128)(2,1)S(1)} collective-permute-done((bf16[80,512]{1,0:T(8,128)(2,1)S(1)}, bf16[80,512]{1,0:T(8,128)(2,1)S(1)}, u32[]{:S(2)}, u32[]{:S(2)}) %collective-permute-start.1) | collective-permute-done | bytes 81952 | tf_op jit(solution)/shard_map/ppermute | solution.py:22
  20.1 3.4 %collective-permute-done.3.a2 = bf16[1552,128]{1,0:T(8,128)(2,1)S(1)} collective-permute-done((bf16[1552,128]{1,0:T(8,128)(2,1)S(1)}, bf16[1552,128]{1,0:T(8,128)(2,1)S(1)}, u32[]{:S(2)}, u32[]{:S(2)}) %collective-permute-start.3) | collective-permute-done | bytes 397344 | tf_op jit(solution)/shard_map/ppermute | solution.py:22
  23.4 2.4 %collective-permute-start.4 = (bf16[1552,128]{1,0:T(8,128)(2,1)S(1)}, bf16[1552,128]{1,0:T(8,128)(2,1)S(1)}, u32[]{:S(2)}, u32[]{:S(2)}) collective-permute-start(bf16[1552,128]{1,0:T(8,128)(2,1)S(1)} %collective-permute-done.3.a2), channel_id=1, source_target_pairs={{0,4},{1,5},{2,6},{3,7},{4,0},{5,1},{6,2},{7,3},{8,12},{9,13},{10,... | collective-permute-start | bytes 1191944 | tf_op jit(solution)/shard_map/ppermute | solution.py:22
  28.8 2.7 %collective-permute-done.5.far = bf16[128,2048]{1,0:T(8,128)(2,1)S(1)} collective-permute-done((bf16[128,2048]{1,0:T(8,128)(2,1)}, bf16[128,2048]{1,0:T(8,128)(2,1)S(1)}, u32[]{:S(2)}, u32[]{:S(2)}) %collective-permute-start.5) | collective-permute-done | bytes 524320 | tf_op jit(solution)/shard_map/ppermute | solution.py:22
  34.8 2.0 %collective-permute-start.11 = (bf16[2,128,512]{2,1,0:T(8,128)(2,1)S(1)}, bf16[2,128,512]{2,1,0:T(8,128)(2,1)S(1)}, u32[]{:S(2)}, u32[]{:S(2)}) collective-permute-start(bf16[2,128,512]{2,1,0:T(8,128)(2,1)S(1)} %get-tuple-element.79), channel_id=1, source_target_pairs={{0,12},{1,13},{2,14},{3,15},{4,8},{5,9},{6,10},{7,11},{8,4},{9,5},... | collective-permute-start | bytes 786440 | tf_op jit(solution)/shard_map/ppermute | solution.py:22
  38.4 9.3 %collective-permute-done.9.h1 = bf16[2,128,512]{2,1,0:T(8,128)(2,1)S(1)} collective-permute-done((bf16[2,128,512]{2,1,0:T(8,128)(2,1)S(1)}, bf16[2,128,512]{2,1,0:T(8,128)(2,1)S(1)}, u32[]{:S(2)}, u32[]{:S(2)}) %collective-permute-start.9) | collective-permute-done | bytes 262176 | tf_op jit(solution)/shard_map/ppermute | solution.py:22
  47.7 1.9 %shard_map.105 = (f32[4,2,128,512]{3,2,1,0:T(8,128)S(1)}, f32[4,2,128,512]{3,2,1,0:T(8,128)S(1)}) custom-call(s32[9]{0:T(128)S(1)} %stack.42.ids, s32[4,12]{1,0:T(4,128)S(1)} %maximum_convert_fusion.lists, bf16[1552,128]{1,0:T(8,128)(2,1)S(1)} %fusion.1.a0, bf16[1552,128]{1,0:T(8,128)(2,1)S(1)} %collective-permute-done.2.a1, ...), custom_call_target="tpu_custom_call" | custom-call | flops 805306368 | bytes 6832356 | tf_op jit(solution)/shard_map/pallas_call | solution.py:36
  50.3 3.5 %collective-permute-done.13.received = f32[4,2,128,512]{3,2,1,0:T(8,128)S(1)} collective-permute-done((f32[4,2,128,512]{3,2,1,0:T(8,128)S(1)}, f32[4,2,128,512]{3,2,1,0:T(8,128)S(1)}, u32[]{:S(2)}, u32[]{:S(2)}) %collective-permute-start.13) | collective-permute-done | bytes 2097184 | tf_op jit(solution)/shard_map/ppermute | solution.py:22
  58.5 4.6 %collective-permute-done.20.o2 = bf16[128,512]{1,0:T(8,128)(2,1)S(1)} collective-permute-done((bf16[128,512]{1,0:T(8,128)(2,1)S(1)}, bf16[128,512]{1,0:T(8,128)(2,1)S(1)}, u32[]{:S(2)}, u32[]{:S(2)}) %collective-permute-start.20) | collective-permute-done | bytes 131104 | tf_op jit(solution)/shard_map/ppermute | solution.py:22
  66.9 1.8 collective-permute-done.14.received
  69.8 2.5 %collective-permute-start.24 = (bf16[288,512]{1,0:T(8,128)(2,1)S(1)}, bf16[288,512]{1,0:T(8,128)(2,1)S(1)}, u32[]{:S(2)}, u32[]{:S(2)}) collective-permute-start(bf16[288,512]{1,0:T(8,128)(2,1)S(1)} %get-tuple-element.89), channel_id=1, source_target_pairs={{0,12},{1,13},{2,14},{3,15},{4,8},{5,9},{6,10},{7,11},{8,4},{9,5},... | collective-permute-start | bytes 884744 | tf_op jit(solution)/shard_map/ppermute | solution.py:22
  76.6 5.9 %collective-permute-done.19.rest_5_ = bf16[272,512]{1,0:T(8,128)(2,1)S(1)} collective-permute-done((bf16[272,512]{1,0:T(8,128)(2,1)S(1)}, bf16[272,512]{1,0:T(8,128)(2,1)S(1)}, u32[]{:S(2)}, u32[]{:S(2)}) %collective-permute-start.19) | collective-permute-done | bytes 278560 | tf_op jit(solution)/shard_map/ppermute | solution.py:22
  82.4 3.4 %collective-permute-done.23.rest_7_ = bf16[272,512]{1,0:T(8,128)(2,1)S(1)} collective-permute-done((bf16[272,512]{1,0:T(8,128)(2,1)S(1)}, bf16[272,512]{1,0:T(8,128)(2,1)S(1)}, u32[]{:S(2)}, u32[]{:S(2)}) %collective-permute-start.23) | collective-permute-done | bytes 278560 | tf_op jit(solution)/shard_map/ppermute | solution.py:22
  85.9 1.9 %collective-permute-done.24.p3.own1 = bf16[288,512]{1,0:T(8,128)(2,1)S(1)} collective-permute-done((bf16[288,512]{1,0:T(8,128)(2,1)S(1)}, bf16[288,512]{1,0:T(8,128)(2,1)S(1)}, u32[]{:S(2)}, u32[]{:S(2)}) %collective-permute-start.24) | collective-permute-done | bytes 294944 | tf_op jit(solution)/shard_map/ppermute | solution.py:22
  89.7 3.5 %shard_map.109 = (bf16[128,512]{1,0:T(8,128)(2,1)S(1)}, bf16[128,512]{1,0:T(8,128)(2,1)S(1)}, bf16[128,512]{1,0:T(8,128)(2,1)S(1)}, bf16[128,512]{1,0:T(8,128)(2...) custom-call(s32[9]{0:T(128)S(1)} %stack.42.ids, ...), custom_call_target="tpu_custom_call" | custom-call | flops 2147483648 | bytes 9306148 | tf_op jit(solution)/shard_map/pallas_call | solution.py:36
  94.9 1.6 collective-permute-start.31
  97.9 2.4 %collective-permute-start.33 = (bf16[2,128,512]{2,1,0:T(8,128)(2,1)S(1)}, bf16[2,128,512]{2,1,0:T(8,128)(2,1)S(1)}, u32[]{:S(2)}, u32[]{:S(2)}) collective-permute-start(bf16[2,128,512]{2,1,0:T(8,128)(2,1)S(1)} %get-tuple-element.110), channel_id=1, source_target_pairs={{0,12},{1,13},{2,14},{3,15},{4,8},{5,9},{6,10},{7,11},{8,4},{9,5},... | collective-permute-start | bytes 786440 | tf_op jit(solution)/shard_map/ppermute | solution.py:22
  101.7 7.9 %collective-permute-done.31.received = bf16[528,512]{1,0:T(8,128)(2,1)S(1)} collective-permute-done((bf16[528,512]{1,0:T(8,128)(2,1)S(1)}, bf16[528,512]{1,0:T(8,128)(2,1)S(1)}, u32[]{:S(2)}, u32[]{:S(2)}) %collective-permute-start.31) | collective-permute-done | bytes 540704 | tf_op jit(solution)/shard_map/ppermute | solution.py:22
  110.0 1.8 %collective-permute-done.33.vxz = bf16[2,128,512]{2,1,0:T(8,128)(2,1)S(1)} collective-permute-done((bf16[2,128,512]{2,1,0:T(8,128)(2,1)S(1)}, bf16[2,128,512]{2,1,0:T(8,128)(2,1)S(1)}, u32[]{:S(2)}, u32[]{:S(2)}) %collective-permute-start.33) | collective-permute-done | bytes 262176 | tf_op jit(solution)/shard_map/ppermute | solution.py:22
  113.1 11.7 %collective-permute-done.37.same = bf16[4,128,512]{2,1,0:T(8,128)(2,1)S(1)} collective-permute-done((bf16[4,128,512]{2,1,0:T(8,128)(2,1)S(1)}, bf16[4,128,512]{2,1,0:T(8,128)(2,1)S(1)}, u32[]{:S(2)}, u32[]{:S(2)}) %collective-permute-start.37) | collective-permute-done | bytes 524320 | tf_op jit(solution)/shard_map/ppermute | solution.py:22
  124.8 1.8 %shard_map.116.rest_0_ = f32[8,128,512]{2,1,0:T(8,128)S(1)} custom-call(s32[9]{0:T(128)S(1)} %stack.42.ids, s32[4,12]{1,0:T(4,128)S(1)} %maximum_convert_fusion.lists, bf16[1552,128]{1,0:T(8,128)(2,1)S(1)} %fusion.1.a0, bf16[1552,128]{1,0:T(8,128)(2,1)S(1)} %collective-permute-done.2.a1, bf16[1552,128]{1,0:T(8,128)(2,1)S(1)} %collective-permute-done.3.a2, ...), custom_call_target="tpu_custom_call" | custom-call | flops 402653184 | bytes 4735204 | tf_op jit(solution)/shard_map/pallas_call | solution.py:36
  126.7 2.8 %shard_map.117 = bf16[8,128,512]{2,1,0:T(8,128)(2,1)} custom-call(s32[9]{0:T(128)S(1)} %stack.42.ids, s32[4,12]{1,0:T(4,128)S(1)} %maximum_convert_fusion.lists, bf16[1552,128]{1,0:T(8,128)(2,1)S(1)} %fusion.1.a0, bf16[1552,128]{1,0:T(8,128)(2,1)S(1)} %collective-permute-done.2.a1, bf16[1552,128]{1,0:T(8,128)(2,1)S(1)} %collective-permute-done.3.a2, ...), custom_call_target="tpu_custom_call" | custom-call | flops 402653184 | bytes 5783780 | tf_op jit(solution)/shard_map/pallas_call | solution.py:36
  129.6 3.7 %all-to-all-start = ((bf16[8,128,512]{2,1,0:T(8,128)(2,1)}), bf16[8,128,512]{2,1,0:T(8,128)(2,1)S(1)}, u32[]{:S(2)}, u32[]{:S(2)}) async-start(bf16[8,128,512]{2,1,0:T(8,128)(2,1)} %shard_map.117), calls=%async_computation | async-start | bytes 2097152 | tf_op jit(solution)/shard_map/all_to_all | solution.py:405
  134.6 1.7 collective-permute-start.35
  136.4 10.8 %collective-permute-done.35.a2 = bf16[128,512]{1,0:T(8,128)(2,1)S(1)} collective-permute-done((bf16[128,512]{1,0:T(8,128)(2,1)}, bf16[128,512]{1,0:T(8,128)(2,1)S(1)}, u32[]{:S(2)}, u32[]{:S(2)}) %collective-permute-start.35) | collective-permute-done | bytes 131104 | tf_op jit(solution)/shard_map/ppermute | solution.py:22
  147.2 2.8 %collective-permute-done.36.a3 = bf16[128,512]{1,0:T(8,128)(2,1)S(1)} collective-permute-done((bf16[128,512]{1,0:T(8,128)(2,1)S(1)}, bf16[128,512]{1,0:T(8,128)(2,1)S(1)}, u32[]{:S(2)}, u32[]{:S(2)}) %collective-permute-start.36) | collective-permute-done | bytes 131104 | tf_op jit(solution)/shard_map/ppermute | solution.py:22
  151.4 5.1 %collective-permute-start.45 = (bf16[144,512]{1,0:T(8,128)(2,1)S(1)}, bf16[144,512]{1,0:T(8,128)(2,1)S(1)}, u32[]{:S(2)}, u32[]{:S(2)}) collective-permute-start(bf16[144,512]{1,0:T(8,128)(2,1)S(1)} %get-tuple-element.130), channel_id=1, source_target_pairs={{0,20},{1,21},{2,22},{3,23},{4,16},{5,17},{6,18},{7,19},{8,28},{9,... | collective-permute-start | bytes 442376 | tf_op jit(solution)/shard_map/ppermute | solution.py:22
  156.5 1.8 %collective-permute-start.44 = (bf16[144,512]{1,0:T(8,128)(2,1)S(1)}, bf16[144,512]{1,0:T(8,128)(2,1)S(1)}, u32[]{:S(2)}, u32[]{:S(2)}) collective-permute-start(bf16[144,512]{1,0:T(8,128)(2,1)S(1)} %get-tuple-element.129), channel_id=1, source_target_pairs={{0,16},{1,17},{2,18},{3,19},{4,20},{5,21},{6,22},{7,23},{8,24},{9,... | collective-permute-start | bytes 442376 | tf_op jit(solution)/shard_map/ppermute | solution.py:22
  159.8 10.9 %collective-permute-done.45.r3 = bf16[144,512]{1,0:T(8,128)(2,1)S(1)} collective-permute-done((bf16[144,512]{1,0:T(8,128)(2,1)S(1)}, bf16[144,512]{1,0:T(8,128)(2,1)S(1)}, u32[]{:S(2)}, u32[]{:S(2)}) %collective-permute-start.45) | collective-permute-done | bytes 147488 | tf_op jit(solution)/shard_map/ppermute | solution.py:22
  (116 shorter events, 48.5 us)
Async XLA Ops:
  2.5 20.9 %collective-permute-start.3 = (bf16[1552,128]{1,0:T(8,128)(2,1)S(1)}, bf16[1552,128]{1,0:T(8,128)(2,1)S(1)}, u32[]{:S(2)}, u32[]{:S(2)}) collective-permute-start(bf16[1552,128]{1,0:T(8,128)(2,1)S(1)} %fusion.1.a0), channel_id=1, source_target_pairs={{0,8},{1,9},{2,10},{3,11},{4,12},{5,13},{6,14},{7,15},{8,0},{9,1},... | collective-permute-start | bytes 1191944 | tf_op jit(solution)/shard_map/ppermute | solution.py:22
  5.6 25.9 %collective-permute-start.5 = (bf16[128,2048]{1,0:T(8,128)(2,1)}, bf16[128,2048]{1,0:T(8,128)(2,1)S(1)}, u32[]{:S(2)}, u32[]{:S(2)}) collective-permute-start(bf16[128,2048]{1,0:T(8,128)(2,1)} %bitcast.19), channel_id=1, source_target_pairs={{0,16},{1,17},{2,18},{3,19},{4,20},{5,21},{6,22},{7,23},{8,24},{9,... | collective-permute-start | bytes 1572872 | tf_op jit(solution)/shard_map/ppermute | solution.py:22
  16.8 12.1 %collective-permute-start.2 = (bf16[1552,128]{1,0:T(8,128)(2,1)S(1)}, bf16[1552,128]{1,0:T(8,128)(2,1)S(1)}, u32[]{:S(2)}, u32[]{:S(2)}) collective-permute-start(bf16[1552,128]{1,0:T(8,128)(2,1)S(1)} %fusion.1.a0), channel_id=1, source_target_pairs={{0,4},{1,5},{2,6},{3,7},{4,0},{5,1},{6,2},{7,3},{8,12},{9,13},{10,... | collective-permute-start | bytes 1191944 | tf_op jit(solution)/shard_map/ppermute | solution.py:22
  19.5 15.3 %collective-permute-start.8 = (bf16[272,512]{1,0:T(8,128)(2,1)S(1)}, bf16[272,512]{1,0:T(8,128)(2,1)S(1)}, u32[]{:S(2)}, u32[]{:S(2)}) collective-permute-start(bf16[272,512]{1,0:T(8,128)(2,1)S(1)} %shard_map.104.rest_0_), channel_id=1, source_target_pairs={{0,8},{1,9},{2,10},{3,11},{4,12},{5,13},{6,14},{7,15},{8,0},{9,1},... | collective-permute-start | bytes 835592 | tf_op jit(solution)/shard_map/ppermute | solution.py:22
  23.4 14.9 %collective-permute-start.4 = (bf16[1552,128]{1,0:T(8,128)(2,1)S(1)}, bf16[1552,128]{1,0:T(8,128)(2,1)S(1)}, u32[]{:S(2)}, u32[]{:S(2)}) collective-permute-start(bf16[1552,128]{1,0:T(8,128)(2,1)S(1)} %collective-permute-done.3.a2), channel_id=1, source_target_pairs={{0,4},{1,5},{2,6},{3,7},{4,0},{5,1},{6,2},{7,3},{8,12},{9,13},{10,... | collective-permute-start | bytes 1191944 | tf_op jit(solution)/shard_map/ppermute | solution.py:22
  25.8 11.0 %collective-permute-start.7 = (bf16[272,512]{1,0:T(8,128)(2,1)S(1)}, bf16[272,512]{1,0:T(8,128)(2,1)S(1)}, u32[]{:S(2)}, u32[]{:S(2)}) collective-permute-start(bf16[272,512]{1,0:T(8,128)(2,1)S(1)} %shard_map.104.rest_0_), channel_id=1, source_target_pairs={{0,2},{1,3},{2,0},{3,1},{4,6},{5,7},{6,4},{7,5},{8,10},{9,11},{10,... | collective-permute-start | bytes 835592 | tf_op jit(solution)/shard_map/ppermute | solution.py:22
  33.2 14.5 %collective-permute-start.9 = (bf16[2,128,512]{2,1,0:T(8,128)(2,1)S(1)}, bf16[2,128,512]{2,1,0:T(8,128)(2,1)S(1)}, u32[]{:S(2)}, u32[]{:S(2)}) collective-permute-start(bf16[2,128,512]{2,1,0:T(8,128)(2,1)S(1)} %get-tuple-element.77), channel_id=1, source_target_pairs={{0,4},{1,5},{2,6},{3,7},{4,0},{5,1},{6,2},{7,3},{8,12},{9,13},{10,... | collective-permute-start | bytes 786440 | tf_op jit(solution)/shard_map/ppermute | solution.py:22
  34.8 12.9 %collective-permute-start.10 = (bf16[2,128,512]{2,1,0:T(8,128)(2,1)S(1)}, bf16[2,128,512]{2,1,0:T(8,128)(2,1)S(1)}, u32[]{:S(2)}, u32[]{:S(2)}) collective-permute-start(bf16[2,128,512]{2,1,0:T(8,128)(2,1)S(1)} %get-tuple-element.78), channel_id=1, source_target_pairs={{0,8},{1,9},{2,10},{3,11},{4,12},{5,13},{6,14},{7,15},{8,0},{9,1},... | collective-permute-start | bytes 786440 | tf_op jit(solution)/shard_map/ppermute | solution.py:22
  34.8 12.9 %collective-permute-start.11 = (bf16[2,128,512]{2,1,0:T(8,128)(2,1)S(1)}, bf16[2,128,512]{2,1,0:T(8,128)(2,1)S(1)}, u32[]{:S(2)}, u32[]{:S(2)}) collective-permute-start(bf16[2,128,512]{2,1,0:T(8,128)(2,1)S(1)} %get-tuple-element.79), channel_id=1, source_target_pairs={{0,12},{1,13},{2,14},{3,15},{4,8},{5,9},{6,10},{7,11},{8,4},{9,5},... | collective-permute-start | bytes 786440 | tf_op jit(solution)/shard_map/ppermute | solution.py:22
  36.8 12.8 %collective-permute-start.12 = (bf16[272,512]{1,0:T(8,128)(2,1)S(1)}, bf16[272,512]{1,0:T(8,128)(2,1)S(1)}, u32[]{:S(2)}, u32[]{:S(2)}) collective-permute-start(bf16[272,512]{1,0:T(8,128)(2,1)S(1)} %collective-permute-done.8.rest_2_), channel_id=1, source_target_pairs={{0,2},{1,3},{2,0},{3,1},{4,6},{5,7},{6,4},{7,5},{8,10},{9,11},{10,... | collective-permute-start | bytes 835592 | tf_op jit(solution)/shard_map/ppermute | solution.py:22
  49.7 15.8 %collective-permute-start.15 = (bf16[272,512]{1,0:T(8,128)(2,1)S(1)}, bf16[272,512]{1,0:T(8,128)(2,1)S(1)}, u32[]{:S(2)}, u32[]{:S(2)}) collective-permute-start(bf16[272,512]{1,0:T(8,128)(2,1)S(1)} %shard_map.104.rest_0_), channel_id=1, source_target_pairs={{0,16},{1,17},{2,18},{3,19},{4,20},{5,21},{6,22},{7,23},{8,24},{9,... | collective-permute-start | bytes 835592 | tf_op jit(solution)/shard_map/ppermute | solution.py:22
  54.6 14.0 %collective-permute-start.14 = (bf16[4,128,512]{2,1,0:T(8,128)(2,1)S(1)}, bf16[4,128,512]{2,1,0:T(8,128)(2,1)S(1)}, u32[]{:S(2)}, u32[]{:S(2)}) collective-permute-start(bf16[4,128,512]{2,1,0:T(8,128)(2,1)S(1)} %get-tuple-element.84), channel_id=1, source_target_pairs={{0,2},{1,3},{2,0},{3,1},{4,6},{5,7},{6,4},{7,5},{8,10},{9,11},{10,... | collective-permute-start | bytes 1572872 | tf_op jit(solution)/shard_map/ppermute | solution.py:22
  65.5 9.5 %collective-permute-start.22 = (bf16[272,512]{1,0:T(8,128)(2,1)S(1)}, bf16[272,512]{1,0:T(8,128)(2,1)S(1)}, u32[]{:S(2)}, u32[]{:S(2)}) collective-permute-start(bf16[272,512]{1,0:T(8,128)(2,1)S(1)} %collective-permute-done.15.rest_4_), channel_id=1, source_target_pairs={{0,8},{1,9},{2,10},{3,11},{4,12},{5,13},{6,14},{7,15},{8,0},{9,1},... | collective-permute-start | bytes 835592 | tf_op jit(solution)/shard_map/ppermute | solution.py:22
  69.3 16.6 %collective-permute-start.18 = (bf16[288,512]{1,0:T(8,128)(2,1)S(1)}, bf16[288,512]{1,0:T(8,128)(2,1)S(1)}, u32[]{:S(2)}, u32[]{:S(2)}) collective-permute-start(bf16[288,512]{1,0:T(8,128)(2,1)S(1)} %get-tuple-element.89), channel_id=1, source_target_pairs={{0,8},{1,9},{2,10},{3,11},{4,12},{5,13},{6,14},{7,15},{8,0},{9,1},... | collective-permute-start | bytes 884744 | tf_op jit(solution)/shard_map/ppermute | solution.py:22
  69.8 17.9 %collective-permute-start.24 = (bf16[288,512]{1,0:T(8,128)(2,1)S(1)}, bf16[288,512]{1,0:T(8,128)(2,1)S(1)}, u32[]{:S(2)}, u32[]{:S(2)}) collective-permute-start(bf16[288,512]{1,0:T(8,128)(2,1)S(1)} %get-tuple-element.89), channel_id=1, source_target_pairs={{0,12},{1,13},{2,14},{3,15},{4,8},{5,9},{6,10},{7,11},{8,4},{9,5},... | collective-permute-start | bytes 884744 | tf_op jit(solution)/shard_map/ppermute | solution.py:22
  72.3 15.4 %collective-permute-start.17 = (bf16[288,512]{1,0:T(8,128)(2,1)S(1)}, bf16[288,512]{1,0:T(8,128)(2,1)S(1)}, u32[]{:S(2)}, u32[]{:S(2)}) collective-permute-start(bf16[288,512]{1,0:T(8,128)(2,1)S(1)} %get-tuple-element.88.p0.own0), channel_id=1, source_target_pairs={{0,4},{1,5},{2,6},{3,7},{4,0},{5,1},{6,2},{7,3},{8,12},{9,13},{10,... | collective-permute-start | bytes 884744 | tf_op jit(solution)/shard_map/ppermute | solution.py:22
  72.8 9.6 %collective-permute-start.19 = (bf16[272,512]{1,0:T(8,128)(2,1)S(1)}, bf16[272,512]{1,0:T(8,128)(2,1)S(1)}, u32[]{:S(2)}, u32[]{:S(2)}) collective-permute-start(bf16[272,512]{1,0:T(8,128)(2,1)S(1)} %collective-permute-done.15.rest_4_), channel_id=1, source_target_pairs={{0,2},{1,3},{2,0},{3,1},{4,6},{5,7},{6,4},{7,5},{8,10},{9,11},{10,... | collective-permute-start | bytes 835592 | tf_op jit(solution)/shard_map/ppermute | solution.py:22
  75.1 10.8 %collective-permute-start.23 = (bf16[272,512]{1,0:T(8,128)(2,1)S(1)}, bf16[272,512]{1,0:T(8,128)(2,1)S(1)}, u32[]{:S(2)}, u32[]{:S(2)}) collective-permute-start(bf16[272,512]{1,0:T(8,128)(2,1)S(1)} %collective-permute-done.22.rest_6_), channel_id=1, source_target_pairs={{0,2},{1,3},{2,0},{3,1},{4,6},{5,7},{6,4},{7,5},{8,10},{9,11},{10,... | collective-permute-start | bytes 835592 | tf_op jit(solution)/shard_map/ppermute | solution.py:22
  94.9 14.6 %collective-permute-start.31 = (bf16[528,512]{1,0:T(8,128)(2,1)S(1)}, bf16[528,512]{1,0:T(8,128)(2,1)S(1)}, u32[]{:S(2)}, u32[]{:S(2)}) collective-permute-start(bf16[528,512]{1,0:T(8,128)(2,1)S(1)} %get-tuple-element.100), channel_id=1, source_target_pairs={{0,2},{1,3},{2,0},{3,1},{4,6},{5,7},{6,4},{7,5},{8,10},{9,11},{10,... | collective-permute-start | bytes 1622024 | tf_op jit(solution)/shard_map/ppermute | solution.py:22
  96.7 12.9 %collective-permute-start.30 = (bf16[2,128,512]{2,1,0:T(8,128)(2,1)S(1)}, bf16[2,128,512]{2,1,0:T(8,128)(2,1)S(1)}, u32[]{:S(2)}, u32[]{:S(2)}) collective-permute-start(bf16[2,128,512]{2,1,0:T(8,128)(2,1)S(1)} %get-tuple-element.105), channel_id=1, source_target_pairs={{0,4},{1,5},{2,6},{3,7},{4,0},{5,1},{6,2},{7,3},{8,12},{9,13},{10,... | collective-permute-start | bytes 786440 | tf_op jit(solution)/shard_map/ppermute | solution.py:22
  97.4 12.7 %collective-permute-start.32 = (bf16[2,128,512]{2,1,0:T(8,128)(2,1)S(1)}, bf16[2,128,512]{2,1,0:T(8,128)(2,1)S(1)}, u32[]{:S(2)}, u32[]{:S(2)}) collective-permute-start(bf16[2,128,512]{2,1,0:T(8,128)(2,1)S(1)} %get-tuple-element.109), channel_id=1, source_target_pairs={{0,8},{1,9},{2,10},{3,11},{4,12},{5,13},{6,14},{7,15},{8,0},{9,1},... | collective-permute-start | bytes 786440 | tf_op jit(solution)/shard_map/ppermute | solution.py:22
  97.9 13.9 %collective-permute-start.33 = (bf16[2,128,512]{2,1,0:T(8,128)(2,1)S(1)}, bf16[2,128,512]{2,1,0:T(8,128)(2,1)S(1)}, u32[]{:S(2)}, u32[]{:S(2)}) collective-permute-start(bf16[2,128,512]{2,1,0:T(8,128)(2,1)S(1)} %get-tuple-element.110), channel_id=1, source_target_pairs={{0,12},{1,13},{2,14},{3,15},{4,8},{5,9},{6,10},{7,11},{8,4},{9,5},... | collective-permute-start | bytes 786440 | tf_op jit(solution)/shard_map/ppermute | solution.py:22
  109.7 15.1 %collective-permute-start.38 = (bf16[528,512]{1,0:T(8,128)(2,1)S(1)}, bf16[528,512]{1,0:T(8,128)(2,1)S(1)}, u32[]{:S(2)}, u32[]{:S(2)}) collective-permute-start(bf16[528,512]{1,0:T(8,128)(2,1)S(1)} %get-tuple-element.119), channel_id=1, source_target_pairs={{0,8},{1,9},{2,10},{3,11},{4,12},{5,13},{6,14},{7,15},{8,0},{9,1},... | collective-permute-start | bytes 1622024 | tf_op jit(solution)/shard_map/ppermute | solution.py:22
  112.0 12.8 %collective-permute-start.37 = (bf16[4,128,512]{2,1,0:T(8,128)(2,1)S(1)}, bf16[4,128,512]{2,1,0:T(8,128)(2,1)S(1)}, u32[]{:S(2)}, u32[]{:S(2)}) collective-permute-start(bf16[4,128,512]{2,1,0:T(8,128)(2,1)S(1)} %shard_map.113.same), channel_id=1, source_target_pairs={{0,2},{1,3},{2,0},{3,1},{4,6},{5,7},{6,4},{7,5},{8,10},{9,11},{10,... | collective-permute-start | bytes 1572872 | tf_op jit(solution)/shard_map/ppermute | solution.py:22
  113.1 11.7 %collective-permute-start.40 = (bf16[4,128,512]{2,1,0:T(8,128)(2,1)S(1)}, bf16[4,128,512]{2,1,0:T(8,128)(2,1)S(1)}, u32[]{:S(2)}, u32[]{:S(2)}) collective-permute-start(bf16[4,128,512]{2,1,0:T(8,128)(2,1)S(1)} %shard_map.113.same), channel_id=1, source_target_pairs={{0,1},{1,0},{2,3},{3,2},{4,5},{5,4},{6,7},{7,6},{8,9},{9,8},{10,11... | collective-permute-start | bytes 1572872 | tf_op jit(solution)/shard_map/ppermute | solution.py:22
  129.6 41.7 %all-to-all-start = ((bf16[8,128,512]{2,1,0:T(8,128)(2,1)}), bf16[8,128,512]{2,1,0:T(8,128)(2,1)S(1)}, u32[]{:S(2)}, u32[]{:S(2)}) async-start(bf16[8,128,512]{2,1,0:T(8,128)(2,1)} %shard_map.117), calls=%async_computation | async-start | bytes 2097152 | tf_op jit(solution)/shard_map/all_to_all | solution.py:405
  133.3 16.8 %collective-permute-start.41 = (bf16[512,512]{1,0:T(8,128)(2,1)S(1)}, bf16[512,512]{1,0:T(8,128)(2,1)S(1)}, u32[]{:S(2)}, u32[]{:S(2)}) collective-permute-start(bf16[512,512]{1,0:T(8,128)(2,1)S(1)} %copy-done.5), channel_id=1, source_target_pairs={{0,2},{1,3},{2,0},{3,1},{4,6},{5,7},{6,4},{7,5},{8,10},{9,11},{10,... | collective-permute-start | bytes 1572872 | tf_op jit(solution)/shard_map/ppermute | solution.py:22
  134.6 12.6 %collective-permute-start.35 = (bf16[128,512]{1,0:T(8,128)(2,1)}, bf16[128,512]{1,0:T(8,128)(2,1)S(1)}, u32[]{:S(2)}, u32[]{:S(2)}) collective-permute-start(bf16[128,512]{1,0:T(8,128)(2,1)} %copy-done.6), channel_id=1, source_target_pairs={{0,4},{1,5},{2,6},{3,7},{4,0},{5,1},{6,2},{7,3},{8,12},{9,13},{10,... | collective-permute-start | bytes 393224 | tf_op jit(solution)/shard_map/ppermute | solution.py:22
  136.3 13.7 %collective-permute-start.36 = (bf16[128,512]{1,0:T(8,128)(2,1)S(1)}, bf16[128,512]{1,0:T(8,128)(2,1)S(1)}, u32[]{:S(2)}, u32[]{:S(2)}) collective-permute-start(bf16[128,512]{1,0:T(8,128)(2,1)S(1)} %get-tuple-element.115), channel_id=1, source_target_pairs={{0,5},{1,4},{2,7},{3,6},{4,1},{5,0},{6,3},{7,2},{8,13},{9,12},{10,... | collective-permute-start | bytes 393224 | tf_op jit(solution)/shard_map/ppermute | solution.py:22
  151.4 19.3 %collective-permute-start.45 = (bf16[144,512]{1,0:T(8,128)(2,1)S(1)}, bf16[144,512]{1,0:T(8,128)(2,1)S(1)}, u32[]{:S(2)}, u32[]{:S(2)}) collective-permute-start(bf16[144,512]{1,0:T(8,128)(2,1)S(1)} %get-tuple-element.130), channel_id=1, source_target_pairs={{0,20},{1,21},{2,22},{3,23},{4,16},{5,17},{6,18},{7,19},{8,28},{9,... | collective-permute-start | bytes 442376 | tf_op jit(solution)/shard_map/ppermute | solution.py:22
  156.5 14.2 %collective-permute-start.43 = (bf16[144,512]{1,0:T(8,128)(2,1)S(1)}, bf16[144,512]{1,0:T(8,128)(2,1)S(1)}, u32[]{:S(2)}, u32[]{:S(2)}) collective-permute-start(bf16[144,512]{1,0:T(8,128)(2,1)S(1)} %get-tuple-element.128), channel_id=1, source_target_pairs={{0,4},{1,5},{2,6},{3,7},{4,0},{5,1},{6,2},{7,3},{8,12},{9,13},{10,... | collective-permute-start | bytes 442376 | tf_op jit(solution)/shard_map/ppermute | solution.py:22
  156.5 15.9 %collective-permute-start.44 = (bf16[144,512]{1,0:T(8,128)(2,1)S(1)}, bf16[144,512]{1,0:T(8,128)(2,1)S(1)}, u32[]{:S(2)}, u32[]{:S(2)}) collective-permute-start(bf16[144,512]{1,0:T(8,128)(2,1)S(1)} %get-tuple-element.129), channel_id=1, source_target_pairs={{0,16},{1,17},{2,18},{3,19},{4,20},{5,21},{6,22},{7,23},{8,24},{9,... | collective-permute-start | bytes 442376 | tf_op jit(solution)/shard_map/ppermute | solution.py:22
  (27 other events, 147.3 us)

commit v9 on v7

--- a/solution.py
+++ b/solution.py
@@ -314,7 +314,6 @@
     (block,) = call(block_kernel, [shape((4 * own_rows + ROWS, quarter), BF16)], ids, *pieces)
 
     lists = jnp.pad(lists.reshape(1, -1), ((0, 15), (0, tile - dests * slots))).astype(BF16)
-    tiles, lists = lax.optimization_barrier((tiles, lists, pieces[1]))[:2]
     tiles = jnp.concatenate([tiles.reshape(-1, tile), lists], axis=0)
     tiles_of = [tiles, swap(after(tiles, *pieces[2:]), X), swap(tiles, Z)]
     tiles_of.append(swap(tiles_of[2], X))

time: 188 us -> 186 us (0.989)
  waiting for transfers between devices: 110 us -> 107 us
    ppermute x49, waiting for transfers between devices: 110 us -> 107 us  [swap(): return lax.ppermute(value, BOTH, [(i, i ^ mask) for i in range(total)])]
  transfers between devices with their start and end apart: 50 -> 50, of which waited for: 27 -> 27; matrix products, arithmetic and copies ran while one was open for 1% -> 0% of each run, Pallas kernels for 7% -> 7%
where the time goes in v9:
time: 186 us; the launch traced here: 185 us
  waiting for transfers between devices  107 us (58%)
  starting transfers between devices  50.7 us (27%)
  Pallas kernels  21.8 us (12%)
  local copies, waits for them, and re-layouts  3.05 us (2%)
    ppermute x49, waiting for transfers between devices, swap(): return lax.ppermute(value, BOTH, [(i, i ^ mask) for i in range(total)])  107 us
    ppermute x49, starting transfers between devices, swap(): return lax.ppermute(value, BOTH, [(i, i ^ mask) for i in range(total)])  46.6 us
    pallas_call x19, Pallas kernels, call(): pl.pallas_call(kernel, out_shape=outs, in_specs=[SMEM] * smem + [VMEM] *...  21.8 us
    all_to_all x1, starting transfers between devices, chip_body(): spread_all = lax.all_to_all(spread, 'row', 0, 0, tiled=True)  4.08 us
  transfers between devices with their start and end apart: 50, of which 27 were waited for; matrix products, arithmetic and copies ran while one was open for 0% of the time, Pallas kernels for 7%

profile of v9, /device:TPU:0, one launch (start us, length us, event | category | flops | bytes accessed | tf_op | source)
XLA Modules:
  0.0 185.3 jit_solution(10710214805095612358)
XLA Ops:
  2.5 3.1 %collective-permute-start.3 = (bf16[1552,128]{1,0:T(8,128)(2,1)S(1)}, bf16[1552,128]{1,0:T(8,128)(2,1)S(1)}, u32[]{:S(2)}, u32[]{:S(2)}) collective-permute-start(bf16[1552,128]{1,0:T(8,128)(2,1)S(1)} %fusion.1.a0), channel_id=1, source_target_pairs={{0,8},{1,9},{2,10},{3,11},{4,12},{5,13},{6,14},{7,15},{8,0},{9,1},... | collective-permute-start | bytes 1191944 | tf_op jit(solution)/shard_map/ppermute | solution.py:22
  5.6 2.6 %collective-permute-start.5 = (bf16[128,2048]{1,0:T(8,128)(2,1)}, bf16[128,2048]{1,0:T(8,128)(2,1)S(1)}, u32[]{:S(2)}, u32[]{:S(2)}) collective-permute-start(bf16[128,2048]{1,0:T(8,128)(2,1)} %bitcast.19), channel_id=1, source_target_pairs={{0,16},{1,17},{2,18},{3,19},{4,20},{5,21},{6,22},{7,23},{8,24},{9,... | collective-permute-start | bytes 1572872 | tf_op jit(solution)/shard_map/ppermute | solution.py:22
  12.1 2.9 %collective-permute-done.p2 = bf16[80,512]{1,0:T(8,128)(2,1)S(1)} collective-permute-done((bf16[80,512]{1,0:T(8,128)(2,1)S(1)}, bf16[80,512]{1,0:T(8,128)(2,1)S(1)}, u32[]{:S(2)}, u32[]{:S(2)}) %collective-permute-start) | collective-permute-done | bytes 81952 | tf_op jit(solution)/shard_map/ppermute | solution.py:22
  15.0 1.8 collective-permute-done.1.p3
  20.1 3.4 %collective-permute-done.3.a2 = bf16[1552,128]{1,0:T(8,128)(2,1)S(1)} collective-permute-done((bf16[1552,128]{1,0:T(8,128)(2,1)S(1)}, bf16[1552,128]{1,0:T(8,128)(2,1)S(1)}, u32[]{:S(2)}, u32[]{:S(2)}) %collective-permute-start.3) | collective-permute-done | bytes 397344 | tf_op jit(solution)/shard_map/ppermute | solution.py:22
  23.4 2.4 %collective-permute-start.4 = (bf16[1552,128]{1,0:T(8,128)(2,1)S(1)}, bf16[1552,128]{1,0:T(8,128)(2,1)S(1)}, u32[]{:S(2)}, u32[]{:S(2)}) collective-permute-start(bf16[1552,128]{1,0:T(8,128)(2,1)S(1)} %collective-permute-done.3.a2), channel_id=1, source_target_pairs={{0,4},{1,5},{2,6},{3,7},{4,0},{5,1},{6,2},{7,3},{8,12},{9,13},{10,... | collective-permute-start | bytes 1191944 | tf_op jit(solution)/shard_map/ppermute | solution.py:22
  28.8 2.7 %collective-permute-done.5.far = bf16[128,2048]{1,0:T(8,128)(2,1)S(1)} collective-permute-done((bf16[128,2048]{1,0:T(8,128)(2,1)}, bf16[128,2048]{1,0:T(8,128)(2,1)S(1)}, u32[]{:S(2)}, u32[]{:S(2)}) %collective-permute-start.5) | collective-permute-done | bytes 524320 | tf_op jit(solution)/shard_map/ppermute | solution.py:22
  34.8 2.0 %collective-permute-start.11 = (bf16[2,128,512]{2,1,0:T(8,128)(2,1)S(1)}, bf16[2,128,512]{2,1,0:T(8,128)(2,1)S(1)}, u32[]{:S(2)}, u32[]{:S(2)}) collective-permute-start(bf16[2,128,512]{2,1,0:T(8,128)(2,1)S(1)} %get-tuple-element.79), channel_id=1, source_target_pairs={{0,12},{1,13},{2,14},{3,15},{4,8},{5,9},{6,10},{7,11},{8,4},{9,5},... | collective-permute-start | bytes 786440 | tf_op jit(solution)/shard_map/ppermute | solution.py:22
  38.4 9.3 %collective-permute-done.9.h1 = bf16[2,128,512]{2,1,0:T(8,128)(2,1)S(1)} collective-permute-done((bf16[2,128,512]{2,1,0:T(8,128)(2,1)S(1)}, bf16[2,128,512]{2,1,0:T(8,128)(2,1)S(1)}, u32[]{:S(2)}, u32[]{:S(2)}) %collective-permute-start.9) | collective-permute-done | bytes 262176 | tf_op jit(solution)/shard_map/ppermute | solution.py:22
  47.7 1.9 %shard_map.105 = (f32[4,2,128,512]{3,2,1,0:T(8,128)S(1)}, f32[4,2,128,512]{3,2,1,0:T(8,128)S(1)}) custom-call(s32[9]{0:T(128)S(1)} %stack.42.ids, s32[4,12]{1,0:T(4,128)S(1)} %maximum_convert_fusion.lists, bf16[1552,128]{1,0:T(8,128)(2,1)S(1)} %fusion.1.a0, bf16[1552,128]{1,0:T(8,128)(2,1)S(1)} %collective-permute-done.2.a1, ...), custom_call_target="tpu_custom_call" | custom-call | flops 805306368 | bytes 6832356 | tf_op jit(solution)/shard_map/pallas_call | solution.py:36
  49.7 4.1 %collective-permute-done.13.received = f32[4,2,128,512]{3,2,1,0:T(8,128)S(1)} collective-permute-done((f32[4,2,128,512]{3,2,1,0:T(8,128)S(1)}, f32[4,2,128,512]{3,2,1,0:T(8,128)S(1)}, u32[]{:S(2)}, u32[]{:S(2)}) %collective-permute-start.13) | collective-permute-done | bytes 2097184 | tf_op jit(solution)/shard_map/ppermute | solution.py:22
  59.1 4.0 %collective-permute-done.20.o2 = bf16[128,512]{1,0:T(8,128)(2,1)S(1)} collective-permute-done((bf16[128,512]{1,0:T(8,128)(2,1)S(1)}, bf16[128,512]{1,0:T(8,128)(2,1)S(1)}, u32[]{:S(2)}, u32[]{:S(2)}) %collective-permute-start.20) | collective-permute-done | bytes 131104 | tf_op jit(solution)/shard_map/ppermute | solution.py:22
  63.1 1.8 collective-permute-done.21.o3
  64.9 6.5 %collective-permute-done.15.rest_4_ = bf16[272,512]{1,0:T(8,128)(2,1)S(1)} collective-permute-done((bf16[272,512]{1,0:T(8,128)(2,1)S(1)}, bf16[272,512]{1,0:T(8,128)(2,1)S(1)}, u32[]{:S(2)}, u32[]{:S(2)}) %collective-permute-start.15) | collective-permute-done | bytes 278560 | tf_op jit(solution)/shard_map/ppermute | solution.py:22
  72.7 7.2 %collective-permute-done.14.received = f32[4,128,512]{2,1,0:T(8,128)S(1)} collective-permute-done((f32[4,128,512]{2,1,0:T(8,128)S(1)}, f32[4,128,512]{2,1,0:T(8,128)S(1)}, u32[]{:S(2)}, u32[]{:S(2)}) %collective-permute-start.14) | collective-permute-done | bytes 1048608 | tf_op jit(solution)/shard_map/ppermute | solution.py:22
  81.1 2.5 %collective-permute-start.24 = (bf16[288,512]{1,0:T(8,128)(2,1)S(1)}, bf16[288,512]{1,0:T(8,128)(2,1)S(1)}, u32[]{:S(2)}, u32[]{:S(2)}) collective-permute-start(bf16[288,512]{1,0:T(8,128)(2,1)S(1)} %get-tuple-element.89), channel_id=1, source_target_pairs={{0,12},{1,13},{2,14},{3,15},{4,8},{5,9},{6,10},{7,11},{8,4},{9,5},... | collective-permute-start | bytes 884744 | tf_op jit(solution)/shard_map/ppermute | solution.py:22
  86.1 7.6 %collective-permute-done.19.rest_5_ = bf16[272,512]{1,0:T(8,128)(2,1)S(1)} collective-permute-done((bf16[272,512]{1,0:T(8,128)(2,1)S(1)}, bf16[272,512]{1,0:T(8,128)(2,1)S(1)}, u32[]{:S(2)}, u32[]{:S(2)}) %collective-permute-start.19) | collective-permute-done | bytes 278560 | tf_op jit(solution)/shard_map/ppermute | solution.py:22
  93.7 3.4 %collective-permute-done.23.rest_7_ = bf16[272,512]{1,0:T(8,128)(2,1)S(1)} collective-permute-done((bf16[272,512]{1,0:T(8,128)(2,1)S(1)}, bf16[272,512]{1,0:T(8,128)(2,1)S(1)}, u32[]{:S(2)}, u32[]{:S(2)}) %collective-permute-start.23) | collective-permute-done | bytes 278560 | tf_op jit(solution)/shard_map/ppermute | solution.py:22
  99.5 3.5 %shard_map.109 = (bf16[128,512]{1,0:T(8,128)(2,1)S(1)}, bf16[128,512]{1,0:T(8,128)(2,1)S(1)}, bf16[128,512]{1,0:T(8,128)(2,1)S(1)}, bf16[128,512]{1,0:T(8,128)(2...) custom-call(s32[9]{0:T(128)S(1)} %stack.42.ids, ...), custom_call_target="tpu_custom_call" | custom-call | flops 2147483648 | bytes 9306148 | tf_op jit(solution)/shard_map/pallas_call | solution.py:36
  104.8 1.6 collective-permute-start.31
  111.5 7.9 %collective-permute-done.31.received = bf16[528,512]{1,0:T(8,128)(2,1)S(1)} collective-permute-done((bf16[528,512]{1,0:T(8,128)(2,1)S(1)}, bf16[528,512]{1,0:T(8,128)(2,1)S(1)}, u32[]{:S(2)}, u32[]{:S(2)}) %collective-permute-start.31) | collective-permute-done | bytes 540704 | tf_op jit(solution)/shard_map/ppermute | solution.py:22
  120.0 1.7 collective-permute-done.33.vxz
  123.0 11.7 %collective-permute-done.37.same = bf16[4,128,512]{2,1,0:T(8,128)(2,1)S(1)} collective-permute-done((bf16[4,128,512]{2,1,0:T(8,128)(2,1)S(1)}, bf16[4,128,512]{2,1,0:T(8,128)(2,1)S(1)}, u32[]{:S(2)}, u32[]{:S(2)}) %collective-permute-start.37) | collective-permute-done | bytes 524320 | tf_op jit(solution)/shard_map/ppermute | solution.py:22
  134.7 1.8 shard_map.116.rest_0_
  136.6 2.8 %shard_map.117 = bf16[8,128,512]{2,1,0:T(8,128)(2,1)} custom-call(s32[9]{0:T(128)S(1)} %stack.42.ids, s32[4,12]{1,0:T(4,128)S(1)} %maximum_convert_fusion.lists, bf16[1552,128]{1,0:T(8,128)(2,1)S(1)} %fusion.1.a0, bf16[1552,128]{1,0:T(8,128)(2,1)S(1)} %collective-permute-done.2.a1, bf16[1552,128]{1,0:T(8,128)(2,1)S(1)} %collective-permute-done.3.a2, ...), custom_call_target="tpu_custom_call" | custom-call | flops 402653184 | bytes 5783780 | tf_op jit(solution)/shard_map/pallas_call | solution.py:36
  139.4 4.1 %all-to-all-start = ((bf16[8,128,512]{2,1,0:T(8,128)(2,1)}), bf16[8,128,512]{2,1,0:T(8,128)(2,1)S(1)}, u32[]{:S(2)}, u32[]{:S(2)}) async-start(bf16[8,128,512]{2,1,0:T(8,128)(2,1)} %shard_map.117), calls=%async_computation | async-start | bytes 2097152 | tf_op jit(solution)/shard_map/all_to_all | solution.py:405
  144.7 2.0 %collective-permute-start.35 = (bf16[128,512]{1,0:T(8,128)(2,1)}, bf16[128,512]{1,0:T(8,128)(2,1)S(1)}, u32[]{:S(2)}, u32[]{:S(2)}) collective-permute-start(bf16[128,512]{1,0:T(8,128)(2,1)} %copy-done.6), channel_id=1, source_target_pairs={{0,4},{1,5},{2,6},{3,7},{4,0},{5,1},{6,2},{7,3},{8,12},{9,13},{10,... | collective-permute-start | bytes 393224 | tf_op jit(solution)/shard_map/ppermute | solution.py:22
  146.8 11.3 %collective-permute-done.35.a2 = bf16[128,512]{1,0:T(8,128)(2,1)S(1)} collective-permute-done((bf16[128,512]{1,0:T(8,128)(2,1)}, bf16[128,512]{1,0:T(8,128)(2,1)S(1)}, u32[]{:S(2)}, u32[]{:S(2)}) %collective-permute-start.35) | collective-permute-done | bytes 131104 | tf_op jit(solution)/shard_map/ppermute | solution.py:22
  158.1 1.6 collective-permute-done.36.a3
  161.8 4.8 %collective-permute-start.45 = (bf16[144,512]{1,0:T(8,128)(2,1)S(1)}, bf16[144,512]{1,0:T(8,128)(2,1)S(1)}, u32[]{:S(2)}, u32[]{:S(2)}) collective-permute-start(bf16[144,512]{1,0:T(8,128)(2,1)S(1)} %get-tuple-element.130), channel_id=1, source_target_pairs={{0,20},{1,21},{2,22},{3,23},{4,16},{5,17},{6,18},{7,19},{8,28},{9,... | collective-permute-start | bytes 442376 | tf_op jit(solution)/shard_map/ppermute | solution.py:22
  166.6 1.8 collective-permute-start.44
  169.8 11.2 %collective-permute-done.45.r3 = bf16[144,512]{1,0:T(8,128)(2,1)S(1)} collective-permute-done((bf16[144,512]{1,0:T(8,128)(2,1)S(1)}, bf16[144,512]{1,0:T(8,128)(2,1)S(1)}, u32[]{:S(2)}, u32[]{:S(2)}) %collective-permute-start.45) | collective-permute-done | bytes 147488 | tf_op jit(solution)/shard_map/ppermute | solution.py:22
  (116 shorter events, 47.5 us)
Async XLA Ops:
  2.5 20.9 %collective-permute-start.3 = (bf16[1552,128]{1,0:T(8,128)(2,1)S(1)}, bf16[1552,128]{1,0:T(8,128)(2,1)S(1)}, u32[]{:S(2)}, u32[]{:S(2)}) collective-permute-start(bf16[1552,128]{1,0:T(8,128)(2,1)S(1)} %fusion.1.a0), channel_id=1, source_target_pairs={{0,8},{1,9},{2,10},{3,11},{4,12},{5,13},{6,14},{7,15},{8,0},{9,1},... | collective-permute-start | bytes 1191944 | tf_op jit(solution)/shard_map/ppermute | solution.py:22
  5.6 25.9 %collective-permute-start.5 = (bf16[128,2048]{1,0:T(8,128)(2,1)}, bf16[128,2048]{1,0:T(8,128)(2,1)S(1)}, u32[]{:S(2)}, u32[]{:S(2)}) collective-permute-start(bf16[128,2048]{1,0:T(8,128)(2,1)} %bitcast.19), channel_id=1, source_target_pairs={{0,16},{1,17},{2,18},{3,19},{4,20},{5,21},{6,22},{7,23},{8,24},{9,... | collective-permute-start | bytes 1572872 | tf_op jit(solution)/shard_map/ppermute | solution.py:22
  16.8 12.1 %collective-permute-start.2 = (bf16[1552,128]{1,0:T(8,128)(2,1)S(1)}, bf16[1552,128]{1,0:T(8,128)(2,1)S(1)}, u32[]{:S(2)}, u32[]{:S(2)}) collective-permute-start(bf16[1552,128]{1,0:T(8,128)(2,1)S(1)} %fusion.1.a0), channel_id=1, source_target_pairs={{0,4},{1,5},{2,6},{3,7},{4,0},{5,1},{6,2},{7,3},{8,12},{9,13},{10,... | collective-permute-start | bytes 1191944 | tf_op jit(solution)/shard_map/ppermute | solution.py:22
  19.5 15.3 %collective-permute-start.8 = (bf16[272,512]{1,0:T(8,128)(2,1)S(1)}, bf16[272,512]{1,0:T(8,128)(2,1)S(1)}, u32[]{:S(2)}, u32[]{:S(2)}) collective-permute-start(bf16[272,512]{1,0:T(8,128)(2,1)S(1)} %shard_map.104.rest_0_), channel_id=1, source_target_pairs={{0,8},{1,9},{2,10},{3,11},{4,12},{5,13},{6,14},{7,15},{8,0},{9,1},... | collective-permute-start | bytes 835592 | tf_op jit(solution)/shard_map/ppermute | solution.py:22
  23.4 14.9 %collective-permute-start.4 = (bf16[1552,128]{1,0:T(8,128)(2,1)S(1)}, bf16[1552,128]{1,0:T(8,128)(2,1)S(1)}, u32[]{:S(2)}, u32[]{:S(2)}) collective-permute-start(bf16[1552,128]{1,0:T(8,128)(2,1)S(1)} %collective-permute-done.3.a2), channel_id=1, source_target_pairs={{0,4},{1,5},{2,6},{3,7},{4,0},{5,1},{6,2},{7,3},{8,12},{9,13},{10,... | collective-permute-start | bytes 1191944 | tf_op jit(solution)/shard_map/ppermute | solution.py:22
  25.8 11.0 %collective-permute-start.7 = (bf16[272,512]{1,0:T(8,128)(2,1)S(1)}, bf16[272,512]{1,0:T(8,128)(2,1)S(1)}, u32[]{:S(2)}, u32[]{:S(2)}) collective-permute-start(bf16[272,512]{1,0:T(8,128)(2,1)S(1)} %shard_map.104.rest_0_), channel_id=1, source_target_pairs={{0,2},{1,3},{2,0},{3,1},{4,6},{5,7},{6,4},{7,5},{8,10},{9,11},{10,... | collective-permute-start | bytes 835592 | tf_op jit(solution)/shard_map/ppermute | solution.py:22
  33.2 14.5 %collective-permute-start.9 = (bf16[2,128,512]{2,1,0:T(8,128)(2,1)S(1)}, bf16[2,128,512]{2,1,0:T(8,128)(2,1)S(1)}, u32[]{:S(2)}, u32[]{:S(2)}) collective-permute-start(bf16[2,128,512]{2,1,0:T(8,128)(2,1)S(1)} %get-tuple-element.77), channel_id=1, source_target_pairs={{0,4},{1,5},{2,6},{3,7},{4,0},{5,1},{6,2},{7,3},{8,12},{9,13},{10,... | collective-permute-start | bytes 786440 | tf_op jit(solution)/shard_map/ppermute | solution.py:22
  34.8 12.9 %collective-permute-start.10 = (bf16[2,128,512]{2,1,0:T(8,128)(2,1)S(1)}, bf16[2,128,512]{2,1,0:T(8,128)(2,1)S(1)}, u32[]{:S(2)}, u32[]{:S(2)}) collective-permute-start(bf16[2,128,512]{2,1,0:T(8,128)(2,1)S(1)} %get-tuple-element.78), channel_id=1, source_target_pairs={{0,8},{1,9},{2,10},{3,11},{4,12},{5,13},{6,14},{7,15},{8,0},{9,1},... | collective-permute-start | bytes 786440 | tf_op jit(solution)/shard_map/ppermute | solution.py:22
  34.8 12.9 %collective-permute-start.11 = (bf16[2,128,512]{2,1,0:T(8,128)(2,1)S(1)}, bf16[2,128,512]{2,1,0:T(8,128)(2,1)S(1)}, u32[]{:S(2)}, u32[]{:S(2)}) collective-permute-start(bf16[2,128,512]{2,1,0:T(8,128)(2,1)S(1)} %get-tuple-element.79), channel_id=1, source_target_pairs={{0,12},{1,13},{2,14},{3,15},{4,8},{5,9},{6,10},{7,11},{8,4},{9,5},... | collective-permute-start | bytes 786440 | tf_op jit(solution)/shard_map/ppermute | solution.py:22
  36.8 12.8 %collective-permute-start.12 = (bf16[272,512]{1,0:T(8,128)(2,1)S(1)}, bf16[272,512]{1,0:T(8,128)(2,1)S(1)}, u32[]{:S(2)}, u32[]{:S(2)}) collective-permute-start(bf16[272,512]{1,0:T(8,128)(2,1)S(1)} %collective-permute-done.8.rest_2_), channel_id=1, source_target_pairs={{0,2},{1,3},{2,0},{3,1},{4,6},{5,7},{6,4},{7,5},{8,10},{9,11},{10,... | collective-permute-start | bytes 835592 | tf_op jit(solution)/shard_map/ppermute | solution.py:22
  54.6 25.3 %collective-permute-start.14 = (f32[4,128,512]{2,1,0:T(8,128)S(1)}, f32[4,128,512]{2,1,0:T(8,128)S(1)}, u32[]{:S(2)}, u32[]{:S(2)}) collective-permute-start(f32[4,128,512]{2,1,0:T(8,128)S(1)} %get-tuple-element.84), channel_id=1, source_target_pairs={{0,2},{1,3},{2,0},{3,1},{4,6},{5,7},{6,4},{7,5},{8,10},{9,11},{10,... | collective-permute-start | bytes 3145736 | tf_op jit(solution)/shard_map/ppermute | solution.py:22
  56.2 15.2 %collective-permute-start.15 = (bf16[272,512]{1,0:T(8,128)(2,1)S(1)}, bf16[272,512]{1,0:T(8,128)(2,1)S(1)}, u32[]{:S(2)}, u32[]{:S(2)}) collective-permute-start(bf16[272,512]{1,0:T(8,128)(2,1)S(1)} %shard_map.104.rest_0_), channel_id=1, source_target_pairs={{0,16},{1,17},{2,18},{3,19},{4,20},{5,21},{6,22},{7,23},{8,24},{9,... | collective-permute-start | bytes 835592 | tf_op jit(solution)/shard_map/ppermute | solution.py:22
  71.4 14.2 %collective-permute-start.22 = (bf16[272,512]{1,0:T(8,128)(2,1)S(1)}, bf16[272,512]{1,0:T(8,128)(2,1)S(1)}, u32[]{:S(2)}, u32[]{:S(2)}) collective-permute-start(bf16[272,512]{1,0:T(8,128)(2,1)S(1)} %collective-permute-done.15.rest_4_), channel_id=1, source_target_pairs={{0,8},{1,9},{2,10},{3,11},{4,12},{5,13},{6,14},{7,15},{8,0},{9,1},... | collective-permute-start | bytes 835592 | tf_op jit(solution)/shard_map/ppermute | solution.py:22
  80.5 16.6 %collective-permute-start.18 = (bf16[288,512]{1,0:T(8,128)(2,1)S(1)}, bf16[288,512]{1,0:T(8,128)(2,1)S(1)}, u32[]{:S(2)}, u32[]{:S(2)}) collective-permute-start(bf16[288,512]{1,0:T(8,128)(2,1)S(1)} %get-tuple-element.89), channel_id=1, source_target_pairs={{0,8},{1,9},{2,10},{3,11},{4,12},{5,13},{6,14},{7,15},{8,0},{9,1},... | collective-permute-start | bytes 884744 | tf_op jit(solution)/shard_map/ppermute | solution.py:22
  81.1 16.0 %collective-permute-start.24 = (bf16[288,512]{1,0:T(8,128)(2,1)S(1)}, bf16[288,512]{1,0:T(8,128)(2,1)S(1)}, u32[]{:S(2)}, u32[]{:S(2)}) collective-permute-start(bf16[288,512]{1,0:T(8,128)(2,1)S(1)} %get-tuple-element.89), channel_id=1, source_target_pairs={{0,12},{1,13},{2,14},{3,15},{4,8},{5,9},{6,10},{7,11},{8,4},{9,5},... | collective-permute-start | bytes 884744 | tf_op jit(solution)/shard_map/ppermute | solution.py:22
  83.5 14.1 %collective-permute-start.17 = (bf16[288,512]{1,0:T(8,128)(2,1)S(1)}, bf16[288,512]{1,0:T(8,128)(2,1)S(1)}, u32[]{:S(2)}, u32[]{:S(2)}) collective-permute-start(bf16[288,512]{1,0:T(8,128)(2,1)S(1)} %get-tuple-element.88.p0.own0), channel_id=1, source_target_pairs={{0,4},{1,5},{2,6},{3,7},{4,0},{5,1},{6,2},{7,3},{8,12},{9,13},{10,... | collective-permute-start | bytes 884744 | tf_op jit(solution)/shard_map/ppermute | solution.py:22
  84.1 9.6 %collective-permute-start.19 = (bf16[272,512]{1,0:T(8,128)(2,1)S(1)}, bf16[272,512]{1,0:T(8,128)(2,1)S(1)}, u32[]{:S(2)}, u32[]{:S(2)}) collective-permute-start(bf16[272,512]{1,0:T(8,128)(2,1)S(1)} %collective-permute-done.15.rest_4_), channel_id=1, source_target_pairs={{0,2},{1,3},{2,0},{3,1},{4,6},{5,7},{6,4},{7,5},{8,10},{9,11},{10,... | collective-permute-start | bytes 835592 | tf_op jit(solution)/shard_map/ppermute | solution.py:22
  85.6 11.5 %collective-permute-start.23 = (bf16[272,512]{1,0:T(8,128)(2,1)S(1)}, bf16[272,512]{1,0:T(8,128)(2,1)S(1)}, u32[]{:S(2)}, u32[]{:S(2)}) collective-permute-start(bf16[272,512]{1,0:T(8,128)(2,1)S(1)} %collective-permute-done.22.rest_6_), channel_id=1, source_target_pairs={{0,2},{1,3},{2,0},{3,1},{4,6},{5,7},{6,4},{7,5},{8,10},{9,11},{10,... | collective-permute-start | bytes 835592 | tf_op jit(solution)/shard_map/ppermute | solution.py:22
  104.8 14.6 %collective-permute-start.31 = (bf16[528,512]{1,0:T(8,128)(2,1)S(1)}, bf16[528,512]{1,0:T(8,128)(2,1)S(1)}, u32[]{:S(2)}, u32[]{:S(2)}) collective-permute-start(bf16[528,512]{1,0:T(8,128)(2,1)S(1)} %get-tuple-element.100), channel_id=1, source_target_pairs={{0,2},{1,3},{2,0},{3,1},{4,6},{5,7},{6,4},{7,5},{8,10},{9,11},{10,... | collective-permute-start | bytes 1622024 | tf_op jit(solution)/shard_map/ppermute | solution.py:22
  106.6 12.8 %collective-permute-start.30 = (bf16[2,128,512]{2,1,0:T(8,128)(2,1)S(1)}, bf16[2,128,512]{2,1,0:T(8,128)(2,1)S(1)}, u32[]{:S(2)}, u32[]{:S(2)}) collective-permute-start(bf16[2,128,512]{2,1,0:T(8,128)(2,1)S(1)} %get-tuple-element.105), channel_id=1, source_target_pairs={{0,4},{1,5},{2,6},{3,7},{4,0},{5,1},{6,2},{7,3},{8,12},{9,13},{10,... | collective-permute-start | bytes 786440 | tf_op jit(solution)/shard_map/ppermute | solution.py:22
  108.1 11.9 %collective-permute-start.32 = (bf16[2,128,512]{2,1,0:T(8,128)(2,1)S(1)}, bf16[2,128,512]{2,1,0:T(8,128)(2,1)S(1)}, u32[]{:S(2)}, u32[]{:S(2)}) collective-permute-start(bf16[2,128,512]{2,1,0:T(8,128)(2,1)S(1)} %get-tuple-element.109), channel_id=1, source_target_pairs={{0,8},{1,9},{2,10},{3,11},{4,12},{5,13},{6,14},{7,15},{8,0},{9,1},... | collective-permute-start | bytes 786440 | tf_op jit(solution)/shard_map/ppermute | solution.py:22
  108.5 13.2 %collective-permute-start.33 = (bf16[2,128,512]{2,1,0:T(8,128)(2,1)S(1)}, bf16[2,128,512]{2,1,0:T(8,128)(2,1)S(1)}, u32[]{:S(2)}, u32[]{:S(2)}) collective-permute-start(bf16[2,128,512]{2,1,0:T(8,128)(2,1)S(1)} %get-tuple-element.110), channel_id=1, source_target_pairs={{0,12},{1,13},{2,14},{3,15},{4,8},{5,9},{6,10},{7,11},{8,4},{9,5},... | collective-permute-start | bytes 786440 | tf_op jit(solution)/shard_map/ppermute | solution.py:22
  119.5 15.2 %collective-permute-start.38 = (bf16[528,512]{1,0:T(8,128)(2,1)S(1)}, bf16[528,512]{1,0:T(8,128)(2,1)S(1)}, u32[]{:S(2)}, u32[]{:S(2)}) collective-permute-start(bf16[528,512]{1,0:T(8,128)(2,1)S(1)} %get-tuple-element.119), channel_id=1, source_target_pairs={{0,8},{1,9},{2,10},{3,11},{4,12},{5,13},{6,14},{7,15},{8,0},{9,1},... | collective-permute-start | bytes 1622024 | tf_op jit(solution)/shard_map/ppermute | solution.py:22
  121.9 12.8 %collective-permute-start.37 = (bf16[4,128,512]{2,1,0:T(8,128)(2,1)S(1)}, bf16[4,128,512]{2,1,0:T(8,128)(2,1)S(1)}, u32[]{:S(2)}, u32[]{:S(2)}) collective-permute-start(bf16[4,128,512]{2,1,0:T(8,128)(2,1)S(1)} %shard_map.113.same), channel_id=1, source_target_pairs={{0,2},{1,3},{2,0},{3,1},{4,6},{5,7},{6,4},{7,5},{8,10},{9,11},{10,... | collective-permute-start | bytes 1572872 | tf_op jit(solution)/shard_map/ppermute | solution.py:22
  123.0 11.7 %collective-permute-start.40 = (bf16[4,128,512]{2,1,0:T(8,128)(2,1)S(1)}, bf16[4,128,512]{2,1,0:T(8,128)(2,1)S(1)}, u32[]{:S(2)}, u32[]{:S(2)}) collective-permute-start(bf16[4,128,512]{2,1,0:T(8,128)(2,1)S(1)} %shard_map.113.same), channel_id=1, source_target_pairs={{0,1},{1,0},{2,3},{3,2},{4,5},{5,4},{6,7},{7,6},{8,9},{9,8},{10,11... | collective-permute-start | bytes 1572872 | tf_op jit(solution)/shard_map/ppermute | solution.py:22
  139.4 42.1 %all-to-all-start = ((bf16[8,128,512]{2,1,0:T(8,128)(2,1)}), bf16[8,128,512]{2,1,0:T(8,128)(2,1)S(1)}, u32[]{:S(2)}, u32[]{:S(2)}) async-start(bf16[8,128,512]{2,1,0:T(8,128)(2,1)} %shard_map.117), calls=%async_computation | async-start | bytes 2097152 | tf_op jit(solution)/shard_map/all_to_all | solution.py:405
  143.5 16.3 %collective-permute-start.41 = (bf16[512,512]{1,0:T(8,128)(2,1)S(1)}, bf16[512,512]{1,0:T(8,128)(2,1)S(1)}, u32[]{:S(2)}, u32[]{:S(2)}) collective-permute-start(bf16[512,512]{1,0:T(8,128)(2,1)S(1)} %copy-done.5), channel_id=1, source_target_pairs={{0,2},{1,3},{2,0},{3,1},{4,6},{5,7},{6,4},{7,5},{8,10},{9,11},{10,... | collective-permute-start | bytes 1572872 | tf_op jit(solution)/shard_map/ppermute | solution.py:22
  144.7 13.4 %collective-permute-start.35 = (bf16[128,512]{1,0:T(8,128)(2,1)}, bf16[128,512]{1,0:T(8,128)(2,1)S(1)}, u32[]{:S(2)}, u32[]{:S(2)}) collective-permute-start(bf16[128,512]{1,0:T(8,128)(2,1)} %copy-done.6), channel_id=1, source_target_pairs={{0,4},{1,5},{2,6},{3,7},{4,0},{5,1},{6,2},{7,3},{8,12},{9,13},{10,... | collective-permute-start | bytes 393224 | tf_op jit(solution)/shard_map/ppermute | solution.py:22
  146.6 13.1 %collective-permute-start.36 = (bf16[128,512]{1,0:T(8,128)(2,1)S(1)}, bf16[128,512]{1,0:T(8,128)(2,1)S(1)}, u32[]{:S(2)}, u32[]{:S(2)}) collective-permute-start(bf16[128,512]{1,0:T(8,128)(2,1)S(1)} %get-tuple-element.115), channel_id=1, source_target_pairs={{0,5},{1,4},{2,7},{3,6},{4,1},{5,0},{6,3},{7,2},{8,13},{9,12},{10,... | collective-permute-start | bytes 393224 | tf_op jit(solution)/shard_map/ppermute | solution.py:22
  161.8 19.2 %collective-permute-start.45 = (bf16[144,512]{1,0:T(8,128)(2,1)S(1)}, bf16[144,512]{1,0:T(8,128)(2,1)S(1)}, u32[]{:S(2)}, u32[]{:S(2)}) collective-permute-start(bf16[144,512]{1,0:T(8,128)(2,1)S(1)} %get-tuple-element.130), channel_id=1, source_target_pairs={{0,20},{1,21},{2,22},{3,23},{4,16},{5,17},{6,18},{7,19},{8,28},{9,... | collective-permute-start | bytes 442376 | tf_op jit(solution)/shard_map/ppermute | solution.py:22
  166.6 14.4 %collective-permute-start.43 = (bf16[144,512]{1,0:T(8,128)(2,1)S(1)}, bf16[144,512]{1,0:T(8,128)(2,1)S(1)}, u32[]{:S(2)}, u32[]{:S(2)}) collective-permute-start(bf16[144,512]{1,0:T(8,128)(2,1)S(1)} %get-tuple-element.128), channel_id=1, source_target_pairs={{0,4},{1,5},{2,6},{3,7},{4,0},{5,1},{6,2},{7,3},{8,12},{9,13},{10,... | collective-permute-start | bytes 442376 | tf_op jit(solution)/shard_map/ppermute | solution.py:22
  166.6 15.9 %collective-permute-start.44 = (bf16[144,512]{1,0:T(8,128)(2,1)S(1)}, bf16[144,512]{1,0:T(8,128)(2,1)S(1)}, u32[]{:S(2)}, u32[]{:S(2)}) collective-permute-start(bf16[144,512]{1,0:T(8,128)(2,1)S(1)} %get-tuple-element.129), channel_id=1, source_target_pairs={{0,16},{1,17},{2,18},{3,19},{4,20},{5,21},{6,22},{7,23},{8,24},{9,... | collective-permute-start | bytes 442376 | tf_op jit(solution)/shard_map/ppermute | solution.py:22
  (27 other events, 145.4 us)
